TPU v7x, 32 devices: a whole 2x2x4 slice. The times are simulated.
32 devices in a mesh: branch: 1, dap: 32 (over z, y, x, core).
Axes of the slice: x: 2, y: 2, z: 4, core: 2. Of those that a mesh axis runs over, the one named last changes fastest.
Arguments:
- alignment: bfloat16 [256, 256, 256], P('dap'), may hold values from -24 to 24
- pair_rep: bfloat16 [256, 256, 128], P('dap', 'branch'), may hold values from -6 to 6
- align_mask: int32 [256, 256], replicated, may hold values from 0 to 1, as said below
- residue_mask: int32 [256], replicated, may hold values from 0 to 1, as said below
- bias_weight: bfloat16 [128, 8], replicated, may hold values from -1 to 1
- row_proj_weight: bfloat16 [4, 256, 256], P(None, None, 'branch'), may hold values from -0.375 to 0.375
- row_out_weight: bfloat16 [256, 256], replicated, may hold values from -1 to 1
- column_proj_weight: bfloat16 [4, 256, 256], P(None, None, 'branch'), may hold values from -0.375 to 0.375
- column_out_weight: bfloat16 [256, 256], replicated, may hold values from -1 to 1
- outer_factor_weight: bfloat16 [256, 64], replicated, may hold values from -0.375 to 0.375
- outer_out: bfloat16 [1024, 128], replicated, may hold values from -0.375 to 0.375
Outputs:
- updated_alignment: bfloat16 [256, 256, 256], P(None, 'dap')
- pair_out: bfloat16 [256, 256, 128], P('dap', 'branch')
Inputs may be any that keep to these rules, and one draw needn't show every extreme that they name: `align_mask`: the first alignment is all ones; in every other alignment the ones form one contiguous run of residues that is never empty. `residue_mask`: ones on a leading run of residues and zeros after it; both values occur.
All inputs are finite; a program needn't handle non-finite values.
Results may differ from a plain program's by a relative error of at most 0.0085.
Values may be sent and summed in bfloat16 or wider, within the bound.
No kernel may reach another device: no remote copies, remote signals or barrier semaphores. Data moves between devices by JAX's collectives and lax.ppermute only.
A program may use at most 128 MiB of HBM per device.

v0:
```python
import math

import jax
import jax.numpy as jnp
from jax import lax
from jax.sharding import PartitionSpec as P

ATTN_HEAD_COUNT = 8
HEAD_CHANNELS = 32
FACTOR_CHANNELS = 32


norm_eps = 1e-05
count_eps = 0.001


def layer_normalize(values):
    centre = jnp.mean(values, axis=-1, keepdims=True)
    centred = values - centre
    spread = jnp.mean(centred * centred, axis=-1, keepdims=True)
    return centred * lax.rsqrt(spread + norm_eps)


def attend_heads(inputs, key_mask, proj_weight, out_weight, score_bias):
    batch = inputs.shape[0]
    length = inputs.shape[1]
    local_width = proj_weight.shape[2]
    local_heads = local_width // HEAD_CHANNELS
    normed = layer_normalize(inputs.astype(jnp.float32)).astype(jnp.bfloat16)
    projected = jnp.einsum("blc,kcd->kbld", normed, proj_weight, preferred_element_type=jnp.float32)
    triple = (
        projected[:3].astype(jnp.bfloat16).reshape(3, batch, length, local_heads, HEAD_CHANNELS)
    )
    gating = jax.nn.sigmoid(projected[3])

    def attend_one(operands):
        queries, key_rows, value_rows, mask_row = operands
        scores = jnp.einsum(
            "ihd,jhd->hij", queries, key_rows, preferred_element_type=jnp.float32
        ) / math.sqrt(HEAD_CHANNELS)
        if score_bias is not None:
            scores = scores + score_bias.astype(jnp.float32)
        raised = jnp.exp(scores) * mask_row[None, None, :]
        weights = (raised / jnp.sum(raised, axis=-1, keepdims=True)).astype(jnp.bfloat16)
        return jnp.einsum("hij,jhd->ihd", weights, value_rows, preferred_element_type=jnp.float32)

    attended_rows = lax.map(attend_one, (triple[0], triple[1], triple[2], key_mask))
    heads_out = (attended_rows.reshape(batch, length, local_width) * gating).astype(jnp.bfloat16)
    gathered = lax.all_gather(heads_out, "branch", axis=2, tiled=True)
    update = jnp.einsum("blf,fc->blc", gathered, out_weight, preferred_element_type=jnp.float32)
    return (inputs.astype(jnp.float32) + update).astype(jnp.bfloat16)


def per_device(
    alignment,
    pair_rep,
    align_mask,
    residue_mask,
    bias_weight,
    row_proj_weight,
    row_out_weight,
    column_proj_weight,
    column_out_weight,
    outer_factor_weight,
    outer_out,
):
    branch_count = lax.axis_size("branch")
    dap_count = lax.axis_size("dap")
    branch_index = lax.axis_index("branch")
    dap_index = lax.axis_index("dap")
    seq_dev = alignment.shape[0]
    res_dev = pair_rep.shape[0]
    quarter = pair_rep.shape[1]
    total_seqs = align_mask.shape[0]
    local_heads = ATTN_HEAD_COUNT // branch_count
    float_mask = align_mask.astype(jnp.float32)
    res_float = residue_mask.astype(jnp.float32)
    pair_normed = layer_normalize(pair_rep.astype(jnp.float32)).astype(jnp.bfloat16)
    bias_block = jnp.einsum(
        "ijc,ch->hij", pair_normed, bias_weight, preferred_element_type=jnp.float32
    ).astype(jnp.bfloat16)
    bias_wide = lax.all_gather(bias_block, "branch", axis=2, tiled=True)
    bias_full = lax.all_gather(bias_wide, "dap", axis=1, tiled=True)
    pair_score_bias = lax.dynamic_slice_in_dim(
        bias_full, branch_index * local_heads, local_heads, 0
    )
    sequence_row_mask = lax.dynamic_slice_in_dim(float_mask, dap_index * seq_dev, seq_dev, 0)
    row_alignment = attend_heads(
        alignment, sequence_row_mask, row_proj_weight, row_out_weight, pair_score_bias
    )
    send_mask = sequence_row_mask.astype(jnp.bfloat16)
    blocked_rows = row_alignment.reshape(seq_dev, dap_count, res_dev, row_alignment.shape[2])
    blocked_mask = send_mask.reshape(seq_dev, dap_count, res_dev)
    moved_rows = lax.all_to_all(blocked_rows, "dap", split_axis=1, concat_axis=0, tiled=True)
    moved_mask = lax.all_to_all(blocked_mask, "dap", split_axis=1, concat_axis=0, tiled=True)
    seq_total = moved_rows.shape[0]
    items = moved_rows.shape[2]
    flat_rows = moved_rows.reshape(seq_total, items, moved_rows.shape[3])
    flat_mask = moved_mask.reshape(seq_total, items)
    transposed_rows = jnp.swapaxes(flat_rows, 0, 1)
    key_mask = jnp.swapaxes(flat_mask, 0, 1).astype(jnp.float32)
    attended_rows = attend_heads(
        transposed_rows, key_mask, column_proj_weight, column_out_weight, None
    )
    column_alignment = jnp.swapaxes(attended_rows, 0, 1)
    outer_mean_normed = layer_normalize(column_alignment.astype(jnp.float32)).astype(jnp.bfloat16)
    projected = jnp.einsum(
        "src,ce->sre", outer_mean_normed, outer_factor_weight, preferred_element_type=jnp.float32
    )
    factor_pairs = (projected * flat_mask.astype(jnp.float32)[:, :, None]).astype(jnp.bfloat16)
    column_alignment, factor_pairs = (column_alignment, factor_pairs)
    blocked_out = column_alignment.reshape(seq_total, 1, items, column_alignment.shape[2])
    blocked_factors = factor_pairs.reshape(seq_total, 1, items, factor_pairs.shape[2])
    updated_alignment = blocked_out.reshape(total_seqs, res_dev, blocked_out.shape[3])
    factor_pairs = blocked_factors.reshape(total_seqs, res_dev, blocked_factors.shape[3])
    left_side = factor_pairs[:, :, :FACTOR_CHANNELS]
    right_local = factor_pairs[:, :, FACTOR_CHANNELS:]
    col_start = branch_index * quarter
    row_start = dap_index * res_dev
    mask_rows = lax.dynamic_slice_in_dim(align_mask, row_start, res_dev, 1).astype(jnp.bfloat16)
    mask_cols = lax.dynamic_slice_in_dim(align_mask, col_start, quarter, 1).astype(jnp.bfloat16)
    counts = jnp.einsum("si,sj->ij", mask_rows, mask_cols, preferred_element_type=jnp.float32)
    live_rows = lax.dynamic_slice_in_dim(res_float, row_start, res_dev, 0)
    live_cols = lax.dynamic_slice_in_dim(res_float, col_start, quarter, 0)
    outer_weight = outer_out.astype(jnp.float32)
    right_all = lax.all_gather(right_local, "dap", axis=1, tiled=True)
    right_mine = lax.dynamic_slice_in_dim(right_all, col_start, quarter, 1)
    outer_sums = jnp.einsum(
        "sic,sje->ijce", left_side, right_mine, preferred_element_type=jnp.float32
    )
    outer_sums = outer_sums.reshape(res_dev, quarter, FACTOR_CHANNELS * FACTOR_CHANNELS)
    update = jnp.einsum("ijf,fz->ijz", outer_sums, outer_weight, precision=lax.Precision.HIGHEST)
    live = live_rows[:, None] * live_cols[None, :]
    update = update / (counts[:, :, None] + count_eps) * live[:, :, None]
    pair_out = (pair_rep.astype(jnp.float32) + update).astype(jnp.bfloat16)
    return (updated_alignment, pair_out)


def solution(mesh):
    placed = (
        P("dap", None, None),
        P("dap", "branch", None),
        P(),
        P(),
        P(),
        P(None, None, "branch"),
        P(),
        P(None, None, "branch"),
        P(),
        P(),
        P(),
    )
    return jax.shard_map(
        per_device,
        mesh=mesh,
        in_specs=placed,
        out_specs=(P(None, "dap", None), P("dap", "branch", None)),
        check_vma=False,
    )
```

profile of v0, /device:TPU:0, one launch (start us, length us, event | category | flops | bytes accessed | tf_op | source)
XLA Modules:
  0.0 269.4 jit_solution(9048823718636560808)
XLA Ops:
  10.3 2.4 fusion.58
  13.6 7.3 %all-to-all-start.1 = ((bf16[8,32,8]{2,0,1:T(8,128)(2,1)}), bf16[8,32,8]{2,0,1:T(8,128)(2,1)S(1)}, u32[]{:S(2)}, u32[]{:S(2)}) async-start(bf16[8,32,8]{2,0,1:T(8,128)(2,1)} %copy.80), calls=%async_computation.1 | async-start | bytes 131072 | tf_op jit(solution)/shard_map/all_to_all | solution.py:95
  21.9 4.2 %fusion.85 = (bf16[4,8,256,256]{2,3,0,1:T(8,128)(2,1)S(1)}, f32[4,8,256,256]{2,3,0,1:T(8,128)}) fusion(bf16[4,256,256]{2,1,0:T(8,128)(2,1)S(1)} %copy-done, bf16[8,256,256]{2,1,0:T(8,128)(2,1)S(1)} %copy-done.2, f32[8,256]{1,0:T(8,128)S(1)} %add_rsqrt_fusion.3, f32[8,256]{1,0:T(8,128)S(1)} %broadcast_multiply_fusion.4), kind=kOutput, calls=%fused_computation.121 | convolution fusion | flops 1077936128 | bytes 14172160 | tf_op jit(solution)/shard_map/blc,kcd->kbld/dot_general | solution.py:30
  27.9 41.4 %all-gather.3.cloned.1.call-done = bf16[8,256,256]{2,0,1:T(8,128)(2,1)} async-done(((bf16[8,8,256]{2,0,1:T(8,128)(2,1)}), bf16[8,256,256]{2,0,1:T(8,128)(2,1)}) %all-gather.3.cloned.1.call-update) | async-done | bytes 1048592 | tf_op jit(solution)/shard_map/all_gather | solution.py:83
  72.5 29.2 %while.20 = (s32[]{:T(128)}, f32[8,256,8,32]{1,3,2,0:T(8,128)}, bf16[8,256,8,32]{1,3,2,0:T(8,128)(2,1)}, bf16[8,256,8,32]{1,3,2,0:T(8,128)(2,1)}, bf16[8,256,8,3...) while((s32[]{:T(128)}, f32[8,256,8,32]{1,3,2,0:T(8,128)}, ...), condition=%wide.region_6.7_spmd, body=%wide.region_4.6_spmd.sunk | while | flops 70256896 | bytes 8000601 | solution.py:47
  74.2 2.0 fusion.103
  77.8 2.0 fusion.103
  81.5 2.0 fusion.103
  85.1 2.0 fusion.103
  88.8 2.0 fusion.103
  92.4 2.0 fusion.103
  96.1 2.0 fusion.103
  99.7 2.0 fusion.103
  101.7 2.9 %fusion.50 = bf16[8,256,256]{1,2,0:T(8,128)(2,1)S(1)} fusion(f32[4,8,256,256]{2,3,0,1:T(8,128)} %get-tuple-element.146, f32[8,256,8,32]{1,3,2,0:T(8,128)} %get-tuple-element.71), kind=kLoop, calls=%fused_computation.68 | loop fusion | flops 2621440 | bytes 5242880 | tf_op jit(solution)/shard_map/convert_element_type | solution.py:48
  106.2 3.6 %all-to-all-start = ((bf16[8,32,8,256]{3,2,0,1:T(8,128)(2,1)}), bf16[8,32,8,256]{3,2,0,1:T(8,128)(2,1)S(1)}, u32[]{:S(2)}, u32[]{:S(2)}) async-start(bf16[8,32,8,256]{3,2,0,1:T(8,128)(2,1)} %copy.73), calls=%async_computation | async-start | bytes 2097152 | tf_op jit(solution)/shard_map/all_to_all | solution.py:94
  110.1 25.9 %all-to-all-done = bf16[8,32,8,256]{3,2,0,1:T(8,128)(2,1)S(1)} async-done(((bf16[8,32,8,256]{3,2,0,1:T(8,128)(2,1)}), bf16[8,32,8,256]{3,2,0,1:T(8,128)(2,1)S(1)}, u32[]{:S(2)}, u32[]{:S(2)}) %all-to-all-start) | async-done | bytes 1048608 | tf_op jit(solution)/shard_map/all_to_all | solution.py:94
  138.6 4.5 %fusion.86 = (bf16[4,8,256,256]{2,3,0,1:T(8,128)(2,1)S(1)}, f32[4,8,256,256]{2,3,0,1:T(8,128)}) fusion(bf16[4,256,256]{2,1,0:T(8,128)(2,1)S(1)} %copy-done.6, bf16[8,256,256,1]{2,0,1,3:T(8,128)(2,1)S(1)} %fusion.61), kind=kOutput, calls=%fused_computation.122 | convolution fusion | flops 1075838976 | bytes 14155776 | tf_op jit(solution)/shard_map/blc,kcd->kbld/dot_general | solution.py:30
  146.3 29.5 %while.21 = (s32[]{:T(128)}, f32[8,256,8,32]{1,3,2,0:T(8,128)}, bf16[8,256,8,32]{1,3,2,0:T(8,128)(2,1)}, bf16[8,256,8,32]{1,3,2,0:T(8,128)(2,1)}, bf16[8,256,8,3...) while((s32[]{:T(128)}, f32[8,256,8,32]{1,3,2,0:T(8,128)}, ...), condition=%wide.region_11.12_spmd, body=%wide.region_9.11_spmd.sunk | while | flops 70776832 | bytes 4872273 | solution.py:47
  147.9 2.2 fusion.106
  151.6 2.2 fusion.106
  155.2 2.2 fusion.106
  158.9 2.2 fusion.106
  162.6 2.1 fusion.106
  166.3 2.1 fusion.106
  170.0 2.2 fusion.106
  173.7 2.1 fusion.106
  175.8 1.8 copy.84
  177.7 2.9 %fusion.51 = bf16[8,256,256]{1,2,0:T(8,128)(2,1)S(1)} fusion(f32[4,8,256,256]{2,3,0,1:T(8,128)} %get-tuple-element.148, f32[8,256,8,32]{1,3,2,0:T(8,128)} %get-tuple-element.72), kind=kLoop, calls=%fused_computation.69 | loop fusion | flops 2621440 | bytes 5242880 | tf_op jit(solution)/shard_map/convert_element_type | solution.py:48
  184.9 59.0 %all-gather.5.cloned.1.call-done = bf16[256,256,32]{0,2,1:T(8,128)(2,1)} async-done(((bf16[256,8,32]{0,2,1:T(8,128)(2,1)}), bf16[256,256,32]{0,2,1:T(8,128)(2,1)}) %all-gather.5.cloned.1.call-update) | async-done | bytes 4194320 | tf_op jit(solution)/shard_map/all_gather | solution.py:126
  243.9 5.2 %fusion.27 = f32[8,256,32,32]{1,2,0,3:T(8,128)S(1)} fusion(bf16[256,256,32,1]{0,2,1,3:T(8,128)(2,1)} %bitcast.164, bf16[256,8,64]{0,2,1:T(8,128)(2,1)S(1)} %fusion.57), kind=kOutput, calls=%fused_computation.37 | convolution fusion | flops 1073741824 | bytes 12713984 | tf_op jit(solution)/shard_map/sic,sje->ijce/dot_general | solution.py:128
  249.2 4.8 %copy.87 = f32[8,256,32,32]{1,3,2,0:T(8,128)S(1)} copy(f32[8,256,32,32]{1,2,0,3:T(8,128)S(1)} %fusion.27) | data formatting | bytes 16777216 | tf_op jit(solution)/shard_map/sic,sje->ijce/transpose | solution.py:128
  254.0 8.5 %fusion.54 = bf16[8,256,128]{2,1,0:T(8,128)(2,1)} fusion(f32[8,256,1024]{1,2,0:T(8,128)S(1)} %bitcast.163, bf16[8,256,128]{2,1,0:T(8,128)(2,1)S(1)} %copy-done.5, f32[8,256]{1,0:T(8,128)S(1)} %broadcast_multiply_fusion, f32[8,256]{1,0:T(8,128)S(1)} %convolution_add_fusion, bf16[1024,128]{1,0:T(8,128)(2,1)S(1)} %copy-done.8), kind=kOutput, calls=%fused_computation.76 | convolution fusion | flops 3222536192 | bytes 9715712 | tf_op jit(solution)/shard_map/ijf,fz->ijz/dot_general | solution.py:132
  (104 shorter events, 47.0 us)
Async XLA Ops:
  7.2 14.7 %copy-start = (bf16[4,256,256]{2,1,0:T(8,128)(2,1)S(1)}, bf16[4,256,256]{2,1,0:T(8,128)(2,1)}, u32[]{:S(2)}) copy-start(bf16[4,256,256]{2,1,0:T(8,128)(2,1)} %param.20) | copy-start | bytes 1572868
  7.2 5.6 %copy-start.7 = (s32[256,256]{1,0:T(8,128)S(1)}, s32[256,256]{1,0:T(8,128)}, u32[]{:S(2)}) copy-start(s32[256,256]{1,0:T(8,128)} %param.17) | copy-start | bytes 786436
  7.2 13.7 %copy-start.2 = (bf16[8,256,256]{2,1,0:T(8,128)(2,1)S(1)}, bf16[8,256,256]{2,1,0:T(8,128)(2,1)}, u32[]{:S(2)}) copy-start(bf16[8,256,256]{2,1,0:T(8,128)(2,1)} %param.15) | copy-start | bytes 3145732
  7.2 62.0 %all-gather.3.cloned.1.call-start = ((), (), s32[]{:S(2)}) async-start(), calls=%async_computation.2 | async-start | bytes 1081344 | tf_op jit(solution)/shard_map/all_gather | solution.py:83
  13.6 92.7 %all-to-all-start.1 = ((bf16[8,32,8]{2,0,1:T(8,128)(2,1)}), bf16[8,32,8]{2,0,1:T(8,128)(2,1)S(1)}, u32[]{:S(2)}, u32[]{:S(2)}) async-start(bf16[8,32,8]{2,0,1:T(8,128)(2,1)} %copy.80), calls=%async_computation.1 | async-start | bytes 131072 | tf_op jit(solution)/shard_map/all_to_all | solution.py:95
  101.7 2.9 %copy-start.3 = (bf16[8,256,256]{2,1,0:T(8,128)(2,1)S(1)}, bf16[8,256,256]{2,1,0:T(8,128)(2,1)}, u32[]{:S(2)}) copy-start(bf16[8,256,256]{2,1,0:T(8,128)(2,1)} %param.15) | copy-start | bytes 3145732
  101.7 2.9 %copy-start.9 = (bf16[256,256]{1,0:T(8,128)(2,1)S(1)}, bf16[256,256]{1,0:T(8,128)(2,1)}, u32[]{:S(2)}) copy-start(bf16[256,256]{1,0:T(8,128)(2,1)} %param.21) | copy-start | bytes 393220
  106.2 29.8 %all-to-all-start = ((bf16[8,32,8,256]{3,2,0,1:T(8,128)(2,1)}), bf16[8,32,8,256]{3,2,0,1:T(8,128)(2,1)S(1)}, u32[]{:S(2)}, u32[]{:S(2)}) async-start(bf16[8,32,8,256]{3,2,0,1:T(8,128)(2,1)} %copy.73), calls=%async_computation | async-start | bytes 2097152 | tf_op jit(solution)/shard_map/all_to_all | solution.py:94
  109.8 134.1 %all-gather.5.cloned.1.call-start = ((), (), s32[]{:S(2)}) async-start(), calls=%async_computation.3 | async-start | bytes 4325376 | tf_op jit(solution)/shard_map/all_gather | solution.py:126
  137.5 1.1 copy-start.6
  177.7 2.9 %copy-start.4 = (f32[256,8,256]{0,2,1:T(8,128)S(1)}, f32[256,8,256]{0,2,1:T(8,128)}, u32[]{:S(2)}) copy-start(f32[256,8,256]{0,2,1:T(8,128)} %copy.84) | copy-start | bytes 6291460
  177.7 2.9 %copy-start.10 = (bf16[256,256]{1,0:T(8,128)(2,1)S(1)}, bf16[256,256]{1,0:T(8,128)(2,1)}, u32[]{:S(2)}) copy-start(bf16[256,256]{1,0:T(8,128)(2,1)} %param.23) | copy-start | bytes 393220
  180.6 0.9 copy-start.12
  181.2 1.5 copy-start.11
  249.1 4.8 %copy-start.5 = (bf16[8,256,128]{2,1,0:T(8,128)(2,1)S(1)}, bf16[8,256,128]{2,1,0:T(8,128)(2,1)}, u32[]{:S(2)}) copy-start(bf16[8,256,128]{2,1,0:T(8,128)(2,1)} %param.16) | copy-start | bytes 1572868
  249.2 4.8 %copy-start.8 = (bf16[1024,128]{1,0:T(8,128)(2,1)S(1)}, bf16[1024,128]{1,0:T(8,128)(2,1)}, u32[]{:S(2)}) copy-start(bf16[1024,128]{1,0:T(8,128)(2,1)} %param.25) | copy-start | bytes 786436
  254.0 8.5 %copy-start.1 = (bf16[4,256,256]{2,1,0:T(8,128)(2,1)S(1)}, bf16[4,256,256]{2,1,0:T(8,128)(2,1)}, u32[]{:S(2)}) copy-start(bf16[4,256,256]{2,1,0:T(8,128)(2,1)} %param.20) | copy-start | bytes 1572868
Sparse Core Ops, SparseCore 0:
  12.9 56.3 all-gather.2
  182.8 61.0 all-gather.4
where the time goes:
time: 270 us; the launch traced here: 269 us
  waiting for transfers between devices  126 us (47%)
  matrix products  85.1 us (32%)
  local copies, waits for them, and re-layouts  19.8 us (7%)
  between operations  14.4 us (5%)
  other arithmetic  12.4 us (5%)
  starting transfers between devices  11.1 us (4%)
    all_gather x1, waiting for transfers between devices, per_device(): right_all = lax.all_gather(right_local, 'dap', axis=1, tiled=True)  59 us
    all_gather x1, waiting for transfers between devices, per_device(): bias_full = lax.all_gather(bias_wide, 'dap', axis=1, tiled=True)  41.4 us
    dot_general x16, matrix products, attend_one(): jnp.einsum('hij,jhd->ihd', weights, value_rows, preferred_element_type=jn...  33.3 us
    all_to_all x1, waiting for transfers between devices, per_device(): lax.all_to_all(blocked_rows, 'dap', split_axis=1, concat_axis=0, tiled=True)  25.9 us
    dot_general x16, matrix products, attend_one(): jnp.einsum('ihd,jhd->hij', queries, key_rows, preferred_element_type=jnp....  25.2 us
    dot_general x2, matrix products, attend_heads(): jnp.einsum('blc,kcd->kbld', normed, proj_weight, preferred_element_type=j...  8.77 us
    dot_general x1, matrix products, per_device(): jnp.einsum('ijf,fz->ijz', outer_sums, outer_weight, precision=lax.Precisi...  8.52 us
    all_to_all x1, starting transfers between devices, per_device(): lax.all_to_all(blocked_mask, 'dap', split_axis=1, concat_axis=0, tiled=True)  7.3 us
  transfers between devices with their start and end apart: 4, of which 3 were waited for; matrix products, arithmetic and copies ran while one was open for 17% of the time, Pallas kernels for 0%

commit v1 on v0

--- a/solution.py
+++ b/solution.py
@@ -1,8 +1,11 @@
+import functools
 import math
 
 import jax
 import jax.numpy as jnp
 from jax import lax
+from jax.experimental import pallas as pl
+from jax.experimental.pallas import tpu as pltpu
 from jax.sharding import PartitionSpec as P
 
 ATTN_HEAD_COUNT = 8
@@ -51,7 +54,7 @@
     return (inputs.astype(jnp.float32) + update).astype(jnp.bfloat16)
 
 
-def per_device(
+def per_device_general(
     alignment,
     pair_rep,
     align_mask,
@@ -136,6 +139,394 @@
     return (updated_alignment, pair_out)
 
 
+LANES = 128
+LOG2E = math.log2(math.e)
+VALUE_SCALE = 1.0 / 128.0
+BF16 = jnp.bfloat16
+F32 = jnp.float32
+MIB = 1024 * 1024
+
+
+def nt_dot(a, b):
+    return lax.dot_general(a, b, (((1,), (1,)), ((), ())), preferred_element_type=F32)
+
+
+def nn_dot(a, b):
+    return jnp.dot(a, b, preferred_element_type=F32)
+
+
+def full_spec(shape):
+    zeros = (0,) * len(shape)
+    return pl.BlockSpec(shape, lambda *_: zeros)
+
+
+def params(mib):
+    return pltpu.CompilerParams(vmem_limit_bytes=mib * MIB)
+
+
+def tiled_scratch(rows, cols):
+    return pltpu.VMEM((cols // LANES, rows, LANES), F32)
+
+
+def store_strided(held, first, stride, values):
+    rows = values.shape[0]
+    for t in range(held.shape[0]):
+        held[t, pl.ds(first, rows, stride=stride), :] = values[:, t * LANES : (t + 1) * LANES]
+
+
+def load_strided(held, first, stride, rows):
+    parts = [held[t, pl.ds(first, rows, stride=stride), :] for t in range(held.shape[0])]
+    return jnp.concatenate(parts, axis=1)
+
+
+def joined_tiles(held):
+    return jnp.concatenate([held[t] for t in range(held.shape[0])], axis=1)
+
+
+def head_lanes(length):
+    lane = lax.broadcasted_iota(jnp.int32, (length, LANES), 1) // HEAD_CHANNELS
+    return [
+        jnp.where(lane == t, 1.0, 0.0).astype(BF16) for t in range(LANES // HEAD_CHANNELS)
+    ]
+
+
+def attend_block(query, key, value, live, lanes, bias_of):
+    pieces = []
+    per_tile = LANES // HEAD_CHANNELS
+    for tile in range(query.shape[1] // LANES):
+        cut = slice(tile * LANES, (tile + 1) * LANES)
+        query_t, key_t = query[:, cut], key[:, cut]
+        value_t = value[:, cut] * live
+        total = None
+        for t in range(per_tile):
+            scores = nt_dot(query_t * lanes[t], key_t)
+            if bias_of is not None:
+                scores = scores + bias_of(tile * per_tile + t)
+            raised = jnp.exp2(scores).astype(BF16)
+            side = jnp.concatenate([value_t * lanes[t], live * lanes[t]], axis=1)
+            part = nn_dot(raised, side)
+            total = part if total is None else total + part
+        pieces.append(total[:, :LANES] / total[:, LANES:])
+    return jnp.concatenate(pieces, axis=1)
+
+
+def project(normed, weight_ref):
+    scale = LOG2E / math.sqrt(HEAD_CHANNELS)
+    query = (nn_dot(normed, weight_ref[0]) * scale).astype(BF16)
+    key = nn_dot(normed, weight_ref[1]).astype(BF16)
+    value = (nn_dot(normed, weight_ref[2]) * VALUE_SCALE).astype(BF16)
+    gate = jax.nn.sigmoid(nn_dot(normed, weight_ref[3])) * (1.0 / VALUE_SCALE)
+    return query, key, value, gate
+
+
+def bias_kernel(pair_ref, weight_ref, out_ref, held):
+    rows, cols, width = pair_ref.shape
+    normed = layer_normalize(pair_ref[...].astype(F32)).astype(BF16).reshape(rows * cols, width)
+    bias = nt_dot(weight_ref[...], normed)[:ATTN_HEAD_COUNT] * LOG2E
+    for i in range(rows):
+        store_strided(held, i, rows, bias[:, i * cols : (i + 1) * cols])
+    out_ref[...] = joined_tiles(held).astype(BF16)
+
+
+def pair_bias_block(pair_rep, bias_weight):
+    rows, cols, width = pair_rep.shape
+    weight = jnp.pad(bias_weight.T, ((0, 16 - ATTN_HEAD_COUNT), (0, 0)))
+    out = jax.ShapeDtypeStruct((ATTN_HEAD_COUNT * rows, cols), BF16)
+    return pl.pallas_call(
+        bias_kernel,
+        out_shape=out,
+        scratch_shapes=[tiled_scratch(*out.shape)],
+        compiler_params=params(32),
+        name="pair_bias",
+    )(pair_rep, weight)
+
+
+def row_project_kernel(x_ref, weight_ref, q_ref, k_ref, v_ref, g_ref):
+    for s in range(x_ref.shape[0]):
+        normed = layer_normalize(x_ref[s].astype(F32)).astype(BF16)
+        q_ref[s], k_ref[s], v_ref[s], g_ref[s] = project(normed, weight_ref)
+
+
+def row_project(alignment, weight):
+    seqs, length, width = alignment.shape
+    step = 2
+    block = pl.BlockSpec((step, length, width), lambda i: (i, 0, 0))
+    small = jax.ShapeDtypeStruct(alignment.shape, BF16)
+    return pl.pallas_call(
+        row_project_kernel,
+        grid=(seqs // step,),
+        in_specs=[block, full_spec(weight.shape)],
+        out_specs=[block] * 4,
+        out_shape=[small, small, small, jax.ShapeDtypeStruct(alignment.shape, F32)],
+        compiler_params=params(48),
+        name="row_project",
+    )(alignment, weight)
+
+
+def row_attend_kernel(group, step, me_ref, x_ref, q_ref, k_ref, v_ref, g_ref, live_ref, out_w_ref, *rest):
+    bias_refs, out_ref, bias_all = rest[:group], rest[group], rest[group + 1]
+    heads, length, _ = bias_all.shape
+    outer = bias_refs[0].shape[0]
+
+    @pl.when(pl.program_id(0) == 0)
+    def _():
+        here = me_ref[0]
+        for k in range(group):
+            for z in range(outer):
+                rows = bias_refs[k].shape[1] // heads
+                owner = here ^ (z * group + k)
+                at = pl.ds(pl.multiple_of(owner * rows, rows), rows)
+                block = bias_refs[k][z].astype(F32).reshape(heads, rows, length)
+                bias_all[:, at, :] = block
+
+    lanes = head_lanes(length)
+    results = []
+    for s in range(step):
+        heads_out = attend_block(
+            q_ref[s], k_ref[s], v_ref[s], live_ref[s], lanes, lambda h: bias_all[h]
+        )
+        heads_out = (heads_out * g_ref[s]).astype(BF16)
+        total = x_ref[s].astype(F32) + nn_dot(heads_out, out_w_ref[...])
+        parts, rows = out_ref.shape[0], out_ref.shape[1]
+        results.append(total.reshape(parts, 1, rows // step, total.shape[1]))
+    joined = jnp.concatenate(results, axis=1)
+    out_ref[...] = joined.reshape(out_ref.shape).astype(BF16)
+
+
+def row_attend(me, alignment, projected, live, out_weight, bias_parts, dap_count):
+    seqs, length, width = alignment.shape
+    rows = length // dap_count
+    step = 2
+    block = pl.BlockSpec((step, length, width), lambda i: (i, 0, 0))
+    return pl.pallas_call(
+        functools.partial(row_attend_kernel, len(bias_parts), step),
+        grid=(seqs // step,),
+        in_specs=[pl.BlockSpec(memory_space=pltpu.SMEM)]
+        + [block] * 5
+        + [pl.BlockSpec((step, length, LANES), lambda i: (i, 0, 0)), full_spec(out_weight.shape)]
+        + [full_spec(b.shape) for b in bias_parts],
+        out_specs=pl.BlockSpec((dap_count, step * rows, width), lambda i: (0, i, 0)),
+        out_shape=jax.ShapeDtypeStruct((dap_count, seqs * rows, width), BF16),
+        scratch_shapes=[pltpu.VMEM((ATTN_HEAD_COUNT, length, length), F32)],
+        compiler_params=params(56),
+        name="row_attend",
+    )(me, alignment, *projected, live, out_weight, *bias_parts)
+
+
+def column_kernel(
+    items, x_ref, live_ref, mask_ref, weight_ref, out_w_ref, factor_ref,
+    out_ref, left_ref, right_ref, held, right_held,
+):
+    step = pl.program_id(0)
+    total_rows = held.shape[1]
+    length = total_rows // items
+
+    @pl.when(step == 0)
+    def _():
+        for t in range(held.shape[0]):
+            part = x_ref[:, :, t * LANES : (t + 1) * LANES].astype(F32)
+            held[t] = part.reshape(total_rows, LANES)
+
+    lanes = head_lanes(length)
+    current = load_strided(held, step, items, length)
+    normed = layer_normalize(current).astype(BF16)
+    query, key, value, gate = project(normed, weight_ref)
+    heads_out = attend_block(query, key, value, live_ref[0], lanes, None)
+    heads_out = (heads_out * gate).astype(BF16)
+    updated = (current + nn_dot(heads_out, out_w_ref[...])).astype(BF16).astype(F32)
+    store_strided(held, step, items, updated)
+    normed = layer_normalize(updated).astype(BF16)
+    factors = nt_dot(factor_ref[...], normed) * mask_ref[pl.ds(step, 1), :]
+    left_at = pl.ds(pl.multiple_of(step * FACTOR_CHANNELS, FACTOR_CHANNELS), FACTOR_CHANNELS)
+    left_ref[left_at, :] = factors[:FACTOR_CHANNELS].astype(BF16)
+    store_strided(right_held, step, items, factors[FACTOR_CHANNELS:])
+
+    @pl.when(step == items - 1)
+    def _():
+        for t in range(held.shape[0]):
+            part = held[t].reshape(out_ref.shape[:2] + (LANES,))
+            out_ref[:, :, t * LANES : (t + 1) * LANES] = part.astype(BF16)
+        right_ref[...] = joined_tiles(right_held).astype(BF16)
+
+
+def column_attend(moved, live, mask_rows, weight, out_weight, factor_weight, items):
+    width = moved.shape[2]
+    total_rows = moved.shape[0] * moved.shape[1]
+    length = total_rows // items
+    factor_t = factor_weight.T
+    side = jax.ShapeDtypeStruct((items * FACTOR_CHANNELS, length), BF16)
+    out = jax.ShapeDtypeStruct((length, items, width), BF16)
+    return pl.pallas_call(
+        functools.partial(column_kernel, items),
+        grid=(items,),
+        in_specs=[
+            full_spec(moved.shape),
+            pl.BlockSpec((1, length, LANES), lambda i: (i, 0, 0)),
+            full_spec(mask_rows.shape),
+            full_spec(weight.shape),
+            full_spec(out_weight.shape),
+            full_spec(factor_t.shape),
+        ],
+        out_specs=[full_spec(out.shape), full_spec(side.shape), full_spec(side.shape)],
+        out_shape=[out, side, side],
+        scratch_shapes=[tiled_scratch(total_rows, width), tiled_scratch(*side.shape)],
+        compiler_params=params(56),
+        name="column_attend",
+    )(moved, live, mask_rows, weight, out_weight, factor_t)
+
+
+def outer_kernel(group, outer, items, *refs):
+    lefts, rights = refs[:group], refs[group : group + outer]
+    weight_ref = refs[group + outer]
+    outs = refs[group + outer + 1 : 2 * group + outer + 1]
+    held = refs[-1]
+    feat = FACTOR_CHANNELS
+    quad = LANES // feat
+    tiles = items * feat // LANES
+    cols = outer * items
+    right = jnp.concatenate([r[...] for r in rights], axis=0)
+    for k in range(group):
+        sums = nt_dot(right, lefts[k][...])
+        sums = sums.reshape(outer, feat, items, sums.shape[1])
+        sums = jnp.transpose(sums, (1, 0, 2, 3)).reshape(feat, cols, sums.shape[3]).astype(BF16)
+        for t in range(tiles):
+            at = slice((k * tiles + t) * cols, (k * tiles + t + 1) * cols)
+            for e in range(feat):
+                held[at, e * LANES : (e + 1) * LANES] = sums[e, :, t * LANES : (t + 1) * LANES]
+    update = nn_dot(held[...], weight_ref[...])
+    width = update.shape[1] // quad
+    for k in range(group):
+        for t in range(tiles):
+            rows = update[(k * tiles + t) * cols : (k * tiles + t + 1) * cols]
+            for i in range(quad):
+                outs[k][t * quad + i] = rows[:, i * width : (i + 1) * width].astype(BF16)
+
+
+def outer_product(lefts, rights, weight, items):
+    group, outer = len(lefts), len(rights)
+    cols = outer * items
+    width = weight.shape[1] * FACTOR_CHANNELS // LANES
+    out = jax.ShapeDtypeStruct((items, cols, width), BF16)
+    tiles = items * FACTOR_CHANNELS // LANES
+    return pl.pallas_call(
+        functools.partial(outer_kernel, group, outer, items),
+        out_shape=[out] * group,
+        scratch_shapes=[pltpu.VMEM((group * tiles * cols, weight.shape[0]), BF16)],
+        compiler_params=params(56),
+        name="outer_product",
+    )(*lefts, *rights, weight)
+
+
+def finish_kernel(group, outer, items, me_ref, pair_ref, scale_ref, *refs):
+    parts, out_ref = refs[:group], refs[group]
+    here = me_ref[0]
+    odd = (here & 1) == 1
+    for pairing in range(group // 2):
+        for i in range(items):
+            first = parts[2 * pairing][i].astype(F32)
+            second = parts[2 * pairing + 1][i].astype(F32)
+            low = jnp.where(odd, second, first)
+            high = jnp.where(odd, first, second)
+            for z in range(outer):
+                owner = here ^ (z * group + 2 * pairing)
+                start = pl.multiple_of((owner >> 1) * (2 * items), 2 * items)
+                at = pl.ds(start, 2 * items)
+                cut = slice(z * items, (z + 1) * items)
+                update = jnp.concatenate([low[cut], high[cut]], axis=0)
+                update = update * scale_ref[at, i : i + 1]
+                out_ref[i, at, :] = (pair_ref[i, at, :].astype(F32) + update).astype(BF16)
+
+
+def finish(me, pair_rep, scale, parts, outer):
+    items = pair_rep.shape[0]
+    return pl.pallas_call(
+        functools.partial(finish_kernel, len(parts), outer, items),
+        in_specs=[pl.BlockSpec(memory_space=pltpu.SMEM), full_spec(pair_rep.shape), full_spec(scale.shape)]
+        + [full_spec(p.shape) for p in parts],
+        out_specs=full_spec(pair_rep.shape),
+        out_shape=jax.ShapeDtypeStruct(pair_rep.shape, BF16),
+        compiler_params=params(48),
+        name="finish",
+    )(me, pair_rep, scale, *parts)
+
+
+def exchange(block, count, offset):
+    pairs = [(i, i ^ offset) for i in range(count)]
+    return lax.ppermute(block, "dap", pairs)
+
+
+def per_device_fast(
+    alignment,
+    pair_rep,
+    align_mask,
+    residue_mask,
+    bias_weight,
+    row_proj_weight,
+    row_out_weight,
+    column_proj_weight,
+    column_out_weight,
+    outer_factor_weight,
+    outer_out,
+):
+    dap_count = lax.axis_size("dap")
+    group = inner_size(dap_count)
+    outer = dap_count // group
+    dap_index = lax.axis_index("dap")
+    me = jnp.reshape(dap_index, (1,)).astype(jnp.int32)
+    seq_dev = alignment.shape[0]
+    items = pair_rep.shape[0]
+    width = alignment.shape[2]
+    total_seqs, total_res = align_mask.shape
+
+    bias = pair_bias_block(pair_rep, bias_weight)
+    column = [bias] + [exchange(bias, dap_count, z * group) for z in range(1, outer)]
+    projected = row_project(alignment, row_proj_weight)
+    column = jnp.stack(column)
+    bias_parts = [column] + [exchange(column, dap_count, k) for k in range(1, group)]
+
+    mask = align_mask.astype(F32)
+    own_seqs = lax.dynamic_slice_in_dim(align_mask, dap_index * seq_dev, seq_dev, 0)
+    own_res = lax.dynamic_slice_in_dim(align_mask, dap_index * items, items, 1)
+    row_live = jnp.broadcast_to(own_seqs.astype(BF16)[:, :, None], (seq_dev, total_res, LANES))
+    col_live = jnp.broadcast_to(own_res.T.astype(BF16)[:, :, None], (items, total_seqs, LANES))
+    counts = jnp.einsum(
+        "si,sj->ji", own_res.astype(BF16), mask.astype(BF16), preferred_element_type=F32
+    )
+    res_float = residue_mask.astype(F32)
+    live_rows = lax.dynamic_slice_in_dim(res_float, dap_index * items, items, 0)
+    scale = live_rows[None, :] * res_float[:, None] / (counts + count_eps)
+
+    quad = LANES // FACTOR_CHANNELS
+    weight = outer_out.reshape(FACTOR_CHANNELS, FACTOR_CHANNELS, -1).swapaxes(0, 1)
+    spread = jnp.eye(quad, dtype=BF16)[None, :, None, :, None] * weight[:, None, :, None, :]
+    spread = spread.reshape(FACTOR_CHANNELS * LANES, quad * weight.shape[2])
+
+    row_out = row_attend(me, alignment, projected, row_live, row_out_weight, bias_parts, dap_count)
+    moved = lax.all_to_all(row_out, "dap", split_axis=0, concat_axis=0, tiled=True)
+    updated, left, right = column_attend(
+        moved,
+        col_live,
+        own_res.T.astype(F32),
+        column_proj_weight,
+        column_out_weight,
+        outer_factor_weight,
+        items,
+    )
+    rights = [right] + [exchange(right, dap_count, z * group) for z in range(1, outer)]
+    lefts = [left] + [exchange(left, dap_count, k) for k in range(1, group)]
+    parts = outer_product(lefts, rights, spread, items)
+    parts = [parts[0]] + [exchange(parts[k], dap_count, k) for k in range(1, group)]
+    pair_out = finish(me, pair_rep, scale, parts, outer)
+    return updated, pair_out
+
+
+def inner_size(count):
+    size = 1
+    while 2 * size * size < count * 2 and count % (2 * size) == 0:
+        size *= 2
+    return size
+
+
 def solution(mesh):
     placed = (
         P("dap", None, None),
@@ -150,6 +541,15 @@
         P(),
         P(),
     )
+    count = mesh.shape["dap"]
+    whole_heads = mesh.shape["branch"] == 1 and count & (count - 1) == 0
+
+    def per_device(*operands):
+        alignment, pair_rep = operands[0], operands[1]
+        tile = 8
+        fits = whole_heads and alignment.shape[0] == tile and pair_rep.shape[0] == tile
+        return (per_device_fast if fits else per_device_general)(*operands)
+
     return jax.shard_map(
         per_device,
         mesh=mesh,

time: 270 us -> 135 us (0.50)
  matrix products: 85.1 us -> 0.23 us
  waiting for transfers between devices: 126 us -> 44.6 us
  Pallas kernels: 0 us -> 39.4 us
  starting transfers between devices: 11.1 us -> 32.9 us
  between operations: 14.4 us -> 0.99 us
  other arithmetic: 12.4 us -> 2.99 us
  local copies, waits for them, and re-layouts: 19.8 us -> 13.8 us
    all_gather x2 -> x0, waiting for transfers between devices: 100 us -> none  [the longest x1 59 us: per_device(): right_all = lax.all_gather(right_local, 'dap', axis=1, tiled=True)]
    dot_general x41 -> x1, matrix products: 85.1 us -> 0.23 us  [per_device_fast(): jnp.einsum('si,sj->ji', own_res.astype(BF16), mask.astype(BF16), preferre...]
    pallas_call x0 -> x6, Pallas kernels: none -> 39.4 us  [the longest x1 16.7 us: column_attend(): pl.pallas_call(functools.partial(column_kernel, items), grid=(items,), in...]
    ppermute x0 -> x27, starting transfers between devices: none -> 30 us  [exchange(): return lax.ppermute(block, 'dap', pairs)]
    ppermute x0 -> x27, waiting for transfers between devices: none -> 19.3 us  [exchange(): return lax.ppermute(block, 'dap', pairs)]
    unnamed x27 -> x62, local copies, waits for them, and re-layouts: 1.87 us -> 10.6 us
    all_to_all x2 -> x1, starting transfers between devices: 10.8 us -> 2.97 us  [per_device_fast(): lax.all_to_all(row_out, 'dap', split_axis=0, concat_axis=0, tiled=True)]
    convert_element_type x7 -> x4, other arithmetic: 6.94 us -> 1.32 us  [the longest x1 0.7 us: per_device_fast(): own_seqs.astype(BF16)[:, :, None]]
  transfers between devices with their start and end apart: 4 -> 28, of which waited for: 3 -> 11; matrix products, arithmetic and copies ran while one was open for 17% -> 5% of each run, Pallas kernels for 0% -> 3%
where the time goes in v1:
time: 135 us
  waiting for transfers between devices  44.6 us (33%)
  Pallas kernels  39.4 us (29%)
  starting transfers between devices  32.9 us (24%)
  local copies, waits for them, and re-layouts  13.8 us (10%)
  other arithmetic  2.99 us (2%)
    ppermute x27, starting transfers between devices, exchange(): return lax.ppermute(block, 'dap', pairs)  30 us
    all_to_all x1, waiting for transfers between devices, per_device_fast(): lax.all_to_all(row_out, 'dap', split_axis=0, concat_axis=0, tiled=True)  25.2 us
    ppermute x27, waiting for transfers between devices, exchange(): return lax.ppermute(block, 'dap', pairs)  19.3 us
    pallas_call x1, Pallas kernels, column_attend(): pl.pallas_call(functools.partial(column_kernel, items), grid=(items,), in...  16.7 us
    unnamed x62, local copies, waits for them, and re-layouts  10.6 us
    pallas_call x1, Pallas kernels, row_attend(): pl.pallas_call(functools.partial(row_attend_kernel, len(bias_parts), step...  9.99 us
    pallas_call x1, Pallas kernels, outer_product(): pl.pallas_call(functools.partial(outer_kernel, group, outer, items), out_...  6.92 us
    pallas_call x1, Pallas kernels, row_project(): pl.pallas_call(row_project_kernel, grid=(seqs // step,), in_specs=[block,...  3.76 us
  transfers between devices with their start and end apart: 28, of which 11 were waited for; matrix products, arithmetic and copies ran while one was open for 5% of the time, Pallas kernels for 3%

profile of v1, /device:TPU:0, one launch (start us, length us, event | category | flops | bytes accessed | tf_op | source)
XLA Modules:
  0.0 135.0 jit_solution(7709694389965595957)
XLA Ops:
  3.1 3.1 %collective-permute-start = (bf16[64,256]{1,0:T(8,128)(2,1)S(1)}, bf16[64,256]{1,0:T(8,128)(2,1)S(1)}, u32[]{:S(2)}, u32[]{:S(2)}) collective-permute-start(bf16[64,256]{1,0:T(8,128)(2,1)S(1)} %pair_bias.1), channel_id=1, source_target_pairs={{0,8},{1,9},{2,10},{3,11},{4,12},{5,13},{6,14},{7,15},{8,0},{9,1},... | collective-permute-start | bytes 98312 | tf_op jit(solution)/shard_map/ppermute | solution.py:455
  6.2 2.6 %collective-permute-start.1 = (bf16[64,256]{1,0:T(8,128)(2,1)S(1)}, bf16[64,256]{1,0:T(8,128)(2,1)S(1)}, u32[]{:S(2)}, u32[]{:S(2)}) collective-permute-start(bf16[64,256]{1,0:T(8,128)(2,1)S(1)} %pair_bias.1), channel_id=1, source_target_pairs={{0,16},{1,17},{2,18},{3,19},{4,20},{5,21},{6,22},{7,23},{8,24},{9,... | collective-permute-start | bytes 98312 | tf_op jit(solution)/shard_map/ppermute | solution.py:455
  8.8 2.8 %collective-permute-done.1 = bf16[64,256]{1,0:T(8,128)(2,1)S(1)} collective-permute-done((bf16[64,256]{1,0:T(8,128)(2,1)S(1)}, bf16[64,256]{1,0:T(8,128)(2,1)S(1)}, u32[]{:S(2)}, u32[]{:S(2)}) %collective-permute-start.1) | collective-permute-done | bytes 32800 | tf_op jit(solution)/shard_map/ppermute | solution.py:455
  11.6 2.9 %collective-permute-done.2 = bf16[64,256]{1,0:T(8,128)(2,1)S(1)} collective-permute-done((bf16[64,256]{1,0:T(8,128)(2,1)S(1)}, bf16[64,256]{1,0:T(8,128)(2,1)S(1)}, u32[]{:S(2)}, u32[]{:S(2)}) %collective-permute-start.2) | collective-permute-done | bytes 32800 | tf_op jit(solution)/shard_map/ppermute | solution.py:455
  14.6 1.6 %collective-permute-start.4 = (bf16[4,64,256]{2,1,0:T(8,128)(2,1)S(1)}, bf16[4,64,256]{2,1,0:T(8,128)(2,1)S(1)}, u32[]{:S(2)}, u32[]{:S(2)}) collective-permute-start(bf16[4,64,256]{2,1,0:T(8,128)(2,1)S(1)} %pad_maximum_fusion.rest_0_), channel_id=1, source_target_pairs={{0,2},{1,3},{2,0},{3,1},{4,6},{5,7},{6,4},{7,5},{8,10},{9,11},{10,... | collective-permute-start | bytes 393224 | tf_op jit(solution)/shard_map/ppermute | solution.py:455
  16.5 1.5 %collective-permute-start.6 = (bf16[4,64,256]{2,1,0:T(8,128)(2,1)S(1)}, bf16[4,64,256]{2,1,0:T(8,128)(2,1)S(1)}, u32[]{:S(2)}, u32[]{:S(2)}) collective-permute-start(bf16[4,64,256]{2,1,0:T(8,128)(2,1)S(1)} %pad_maximum_fusion.rest_0_), channel_id=1, source_target_pairs={{0,4},{1,5},{2,6},{3,7},{4,0},{5,1},{6,2},{7,3},{8,12},{9,13},{10,... | collective-permute-start | bytes 393224 | tf_op jit(solution)/shard_map/ppermute | solution.py:455
  18.2 2.4 %collective-permute-start.8 = (bf16[4,64,256]{2,1,0:T(8,128)(2,1)S(1)}, bf16[4,64,256]{2,1,0:T(8,128)(2,1)S(1)}, u32[]{:S(2)}, u32[]{:S(2)}) collective-permute-start(bf16[4,64,256]{2,1,0:T(8,128)(2,1)S(1)} %pad_maximum_fusion.rest_0_), channel_id=1, source_target_pairs={{0,6},{1,7},{2,4},{3,5},{4,2},{5,3},{6,0},{7,1},{8,14},{9,15},{10,... | collective-permute-start | bytes 393224 | tf_op jit(solution)/shard_map/ppermute | solution.py:455
  21.0 1.3 collective-permute-start.9
  22.2 1.2 copy-done
  24.5 3.8 %row_project.1 = (bf16[8,256,256]{2,1,0:T(8,128)(2,1)S(1)}, bf16[8,256,256]{2,1,0:T(8,128)(2,1)S(1)}, bf16[8,256,256]{2,1,0:T(8,128)(2,1)S(1)}, f32[8,256,256]{2,1,0:T(8,128)}) custom-call(bf16[8,256,256]{2,1,0:T(8,128)(2,1)S(1)} %copy-done, bf16[4,256,256]{2,1,0:T(8,128)(2,1)S(1)} %copy-done.6), custom_call_target="tpu_custom_call" | custom-call | tf_op jit(solution)/shard_map/row_project/pallas_call | solution.py:255
  33.2 10.0 %row_attend.1 = bf16[32,64,256]{2,1,0:T(8,128)(2,1)} custom-call(s32[1]{0:T(128)} %bitcast.me_ref, bf16[8,256,256]{2,1,0:T(8,128)(2,1)} %x_ref.3, bf16[8,256,256]{2,1,0:T(8,128)(2,1)} %copy-done.3, bf16[8,256,256]{2,1,0:T(8,128)(2,1)} %copy-done.4, bf16[8,256,256]{2,1,0:T(8,128)(2,1)} %copy-done.5, f32[8,256,256]{2,1,0:T(8,128)} %get-tuple-element.20.g_ref, ...), custom_call_target="tpu_custom_call" | custom-call | tf_op jit(solution)/shard_map/row_attend/pallas_call | solution.py:301
  43.2 3.0 %all-to-all-start = ((bf16[32,64,256]{2,1,0:T(8,128)(2,1)}), bf16[32,64,256]{2,1,0:T(8,128)(2,1)S(1)}, u32[]{:S(2)}, u32[]{:S(2)}) async-start(bf16[32,64,256]{2,1,0:T(8,128)(2,1)} %row_attend.1), calls=%async_computation | async-start | bytes 2097152 | tf_op jit(solution)/shard_map/all_to_all | solution.py:505
  47.0 25.2 %all-to-all-done.x_ref = bf16[32,64,256]{2,1,0:T(8,128)(2,1)S(1)} async-done(((bf16[32,64,256]{2,1,0:T(8,128)(2,1)}), bf16[32,64,256]{2,1,0:T(8,128)(2,1)S(1)}, u32[]{:S(2)}, u32[]{:S(2)}) %all-to-all-start) | async-done | bytes 1048608 | tf_op jit(solution)/shard_map/all_to_all | solution.py:505
  72.2 1.1 broadcast_in_dim.5.live_ref
  73.4 16.7 %column_attend.1 = (bf16[256,8,256]{2,1,0:T(8,128)(2,1)}, bf16[256,256]{1,0:T(8,128)(2,1)}, bf16[256,256]{1,0:T(8,128)(2,1)}) custom-call(bf16[32,64,256]{2,1,0:T(8,128)(2,1)} %copy-done.8, bf16[8,256,128]{2,1,0:T(8,128)(2,1)} %broadcast_in_dim.5.live_ref, f32[8,256]{1,0:T(8,128)} %get-tuple-element.32.mask_ref, bf16[4,256,256]{2,1,0:T(8,128)(2,1)} %weight_ref.3, ...), custom_call_target="tpu_custom_call" | custom-call | tf_op jit(solution)/shard_map/column_attend/pallas_call | solution.py:359
  90.1 1.5 %collective-permute-start.11 = (bf16[256,256]{1,0:T(8,128)(2,1)}, bf16[256,256]{1,0:T(8,128)(2,1)S(1)}, u32[]{:S(2)}, u32[]{:S(2)}) collective-permute-start(bf16[256,256]{1,0:T(8,128)(2,1)} %get-tuple-element.22.refs_0_), channel_id=1, source_target_pairs={{0,2},{1,3},{2,0},{3,1},{4,6},{5,7},{6,4},{7,5},{8,10},{9,11},{10,... | collective-permute-start | bytes 393224 | tf_op jit(solution)/shard_map/ppermute | solution.py:455
  92.0 1.5 %collective-permute-start.13 = (bf16[256,256]{1,0:T(8,128)(2,1)}, bf16[256,256]{1,0:T(8,128)(2,1)S(1)}, u32[]{:S(2)}, u32[]{:S(2)}) collective-permute-start(bf16[256,256]{1,0:T(8,128)(2,1)} %get-tuple-element.22.refs_0_), channel_id=1, source_target_pairs={{0,4},{1,5},{2,6},{3,7},{4,0},{5,1},{6,2},{7,3},{8,12},{9,13},{10,... | collective-permute-start | bytes 393224 | tf_op jit(solution)/shard_map/ppermute | solution.py:455
  93.8 2.5 %collective-permute-start.15 = (bf16[256,256]{1,0:T(8,128)(2,1)}, bf16[256,256]{1,0:T(8,128)(2,1)S(1)}, u32[]{:S(2)}, u32[]{:S(2)}) collective-permute-start(bf16[256,256]{1,0:T(8,128)(2,1)} %get-tuple-element.22.refs_0_), channel_id=1, source_target_pairs={{0,6},{1,7},{2,4},{3,5},{4,2},{5,3},{6,0},{7,1},{8,14},{9,15},{10,... | collective-permute-start | bytes 393224 | tf_op jit(solution)/shard_map/ppermute | solution.py:455
  96.7 1.3 collective-permute-start.16
  100.6 5.2 %collective-permute-done.14.refs_5_ = bf16[256,256]{1,0:T(8,128)(2,1)S(1)} collective-permute-done((bf16[256,256]{1,0:T(8,128)(2,1)}, bf16[256,256]{1,0:T(8,128)(2,1)S(1)}, u32[]{:S(2)}, u32[]{:S(2)}) %collective-permute-start.14) | collective-permute-done | bytes 131104 | tf_op jit(solution)/shard_map/ppermute | solution.py:455
  105.8 1.4 %collective-permute-start.19 = (bf16[256,256]{1,0:T(8,128)(2,1)}, bf16[256,256]{1,0:T(8,128)(2,1)S(1)}, u32[]{:S(2)}, u32[]{:S(2)}) collective-permute-start(bf16[256,256]{1,0:T(8,128)(2,1)} %get-tuple-element.23.refs_8_), channel_id=1, source_target_pairs={{0,24},{1,25},{2,26},{3,27},{4,28},{5,29},{6,30},{7,31},{8,16},{9,... | collective-permute-start | bytes 393224 | tf_op jit(solution)/shard_map/ppermute | solution.py:455
  107.1 1.6 %broadcast_multiply_fusion = bf16[32,4,32,4,128]{4,3,2,1,0:T(4,128)(2,1)S(1)} fusion(bf16[32,32,128]{2,1,0:T(8,128)(2,1)S(1)} %copy.19, bf16[4,4]{1,0:T(4,128)(2,1)S(1)} %fusion.3), kind=kLoop, calls=%fused_computation.1 | loop fusion | flops 2097152 | bytes 4456480 | tf_op jit(solution)/shard_map/mul | solution.py:501
  108.8 2.7 %copy.24 = bf16[512,8,4,128]{3,1,2,0:T(8,128)(2,1)} copy(bf16[512,8,4,128]{3,2,1,0:T(4,128)(2,1)S(1)} %bitcast.25) | data formatting | bytes 8388608
  111.6 2.3 %collective-permute-done.19.refs_11_ = bf16[256,256]{1,0:T(8,128)(2,1)S(1)} collective-permute-done((bf16[256,256]{1,0:T(8,128)(2,1)}, bf16[256,256]{1,0:T(8,128)(2,1)S(1)}, u32[]{:S(2)}, u32[]{:S(2)}) %collective-permute-start.19) | collective-permute-done | bytes 131104 | tf_op jit(solution)/shard_map/ppermute | solution.py:455
  114.6 6.9 %outer_product.1 = (bf16[8,32,128]{2,1,0:T(8,128)(2,1)}, bf16[8,32,128]{2,1,0:T(8,128)(2,1)}, bf16[8,32,128]{2,1,0:T(8,128)(2,1)}, bf16[8,32,128]{2,1,0:T(8,128)...) custom-call(bf16[256,256]{1,0:T(8,128)(2,1)} %get-tuple-element.22.r, ...), custom_call_target="tpu_custom_call" | custom-call | tf_op jit(solution)/shard_map/outer_product/pallas_call | solution.py:411
  121.6 1.6 %collective-permute-start.21 = (bf16[8,32,128]{2,1,0:T(8,128)(2,1)}, bf16[8,32,128]{2,1,0:T(8,128)(2,1)S(1)}, u32[]{:S(2)}, u32[]{:S(2)}) collective-permute-start(bf16[8,32,128]{2,1,0:T(8,128)(2,1)} %get-tuple-element.26), channel_id=1, source_target_pairs={{0,2},{1,3},{2,0},{3,1},{4,6},{5,7},{6,4},{7,5},{8,10},{9,11},{10,... | collective-permute-start | bytes 196616 | tf_op jit(solution)/shard_map/ppermute | solution.py:455
  123.5 1.5 %collective-permute-start.23 = (bf16[8,32,128]{2,1,0:T(8,128)(2,1)}, bf16[8,32,128]{2,1,0:T(8,128)(2,1)S(1)}, u32[]{:S(2)}, u32[]{:S(2)}) collective-permute-start(bf16[8,32,128]{2,1,0:T(8,128)(2,1)} %get-tuple-element.28), channel_id=1, source_target_pairs={{0,4},{1,5},{2,6},{3,7},{4,0},{5,1},{6,2},{7,3},{8,12},{9,13},{10,... | collective-permute-start | bytes 196616 | tf_op jit(solution)/shard_map/ppermute | solution.py:455
  125.2 2.4 %collective-permute-start.25 = (bf16[8,32,128]{2,1,0:T(8,128)(2,1)}, bf16[8,32,128]{2,1,0:T(8,128)(2,1)S(1)}, u32[]{:S(2)}, u32[]{:S(2)}) collective-permute-start(bf16[8,32,128]{2,1,0:T(8,128)(2,1)} %get-tuple-element.30), channel_id=1, source_target_pairs={{0,6},{1,7},{2,4},{3,5},{4,2},{5,3},{6,0},{7,1},{8,14},{9,15},{10,... | collective-permute-start | bytes 196616 | tf_op jit(solution)/shard_map/ppermute | solution.py:455
  128.2 1.1 collective-permute-done.24.refs_5_
  129.4 1.5 %collective-permute-done.25.refs_6_ = bf16[8,32,128]{2,1,0:T(8,128)(2,1)S(1)} collective-permute-done((bf16[8,32,128]{2,1,0:T(8,128)(2,1)}, bf16[8,32,128]{2,1,0:T(8,128)(2,1)S(1)}, u32[]{:S(2)}, u32[]{:S(2)}) %collective-permute-start.25) | collective-permute-done | bytes 65568 | tf_op jit(solution)/shard_map/ppermute | solution.py:455
  130.9 2.0 %collective-permute-done.26.refs_7_ = bf16[8,32,128]{2,1,0:T(8,128)(2,1)S(1)} collective-permute-done((bf16[8,32,128]{2,1,0:T(8,128)(2,1)}, bf16[8,32,128]{2,1,0:T(8,128)(2,1)S(1)}, u32[]{:S(2)}, u32[]{:S(2)}) %collective-permute-start.26) | collective-permute-done | bytes 65568 | tf_op jit(solution)/shard_map/ppermute | solution.py:455
  133.7 1.3 finish.1
  (105 shorter events, 16.4 us)
Async XLA Ops:
  3.1 5.7 %collective-permute-start = (bf16[64,256]{1,0:T(8,128)(2,1)S(1)}, bf16[64,256]{1,0:T(8,128)(2,1)S(1)}, u32[]{:S(2)}, u32[]{:S(2)}) collective-permute-start(bf16[64,256]{1,0:T(8,128)(2,1)S(1)} %pair_bias.1), channel_id=1, source_target_pairs={{0,8},{1,9},{2,10},{3,11},{4,12},{5,13},{6,14},{7,15},{8,0},{9,1},... | collective-permute-start | bytes 98312 | tf_op jit(solution)/shard_map/ppermute | solution.py:455
  6.2 5.4 %collective-permute-start.1 = (bf16[64,256]{1,0:T(8,128)(2,1)S(1)}, bf16[64,256]{1,0:T(8,128)(2,1)S(1)}, u32[]{:S(2)}, u32[]{:S(2)}) collective-permute-start(bf16[64,256]{1,0:T(8,128)(2,1)S(1)} %pair_bias.1), channel_id=1, source_target_pairs={{0,16},{1,17},{2,18},{3,19},{4,20},{5,21},{6,22},{7,23},{8,24},{9,... | collective-permute-start | bytes 98312 | tf_op jit(solution)/shard_map/ppermute | solution.py:455
  8.8 5.7 %collective-permute-start.2 = (bf16[64,256]{1,0:T(8,128)(2,1)S(1)}, bf16[64,256]{1,0:T(8,128)(2,1)S(1)}, u32[]{:S(2)}, u32[]{:S(2)}) collective-permute-start(bf16[64,256]{1,0:T(8,128)(2,1)S(1)} %pair_bias.1), channel_id=1, source_target_pairs={{0,24},{1,25},{2,26},{3,27},{4,28},{5,29},{6,30},{7,31},{8,16},{9,... | collective-permute-start | bytes 98312 | tf_op jit(solution)/shard_map/ppermute | solution.py:455
  14.5 18.6 %copy-start.9 = (bf16[4,64,256]{2,1,0:T(8,128)(2,1)}, bf16[4,64,256]{2,1,0:T(8,128)(2,1)S(1)}, u32[]{:S(2)}) copy-start(bf16[4,64,256]{2,1,0:T(8,128)(2,1)S(1)} %pad_maximum_fusion.rest_0_) | copy-start | bytes 393220
  14.5 3.6 %collective-permute-start.3 = (bf16[4,64,256]{2,1,0:T(8,128)(2,1)S(1)}, bf16[4,64,256]{2,1,0:T(8,128)(2,1)S(1)}, u32[]{:S(2)}, u32[]{:S(2)}) collective-permute-start(bf16[4,64,256]{2,1,0:T(8,128)(2,1)S(1)} %pad_maximum_fusion.rest_0_), channel_id=1, source_target_pairs={{0,1},{1,0},{2,3},{3,2},{4,5},{5,4},{6,7},{7,6},{8,9},{9,8},{10,11... | collective-permute-start | bytes 393224 | tf_op jit(solution)/shard_map/ppermute | solution.py:455
  14.6 6.4 %collective-permute-start.4 = (bf16[4,64,256]{2,1,0:T(8,128)(2,1)S(1)}, bf16[4,64,256]{2,1,0:T(8,128)(2,1)S(1)}, u32[]{:S(2)}, u32[]{:S(2)}) collective-permute-start(bf16[4,64,256]{2,1,0:T(8,128)(2,1)S(1)} %pad_maximum_fusion.rest_0_), channel_id=1, source_target_pairs={{0,2},{1,3},{2,0},{3,1},{4,6},{5,7},{6,4},{7,5},{8,10},{9,11},{10,... | collective-permute-start | bytes 393224 | tf_op jit(solution)/shard_map/ppermute | solution.py:455
  16.2 15.8 %collective-permute-start.5 = (bf16[4,64,256]{2,1,0:T(8,128)(2,1)S(1)}, bf16[4,64,256]{2,1,0:T(8,128)(2,1)S(1)}, u32[]{:S(2)}, u32[]{:S(2)}) collective-permute-start(bf16[4,64,256]{2,1,0:T(8,128)(2,1)S(1)} %pad_maximum_fusion.rest_0_), channel_id=1, source_target_pairs={{0,3},{1,2},{2,1},{3,0},{4,7},{5,6},{6,5},{7,4},{8,11},{9,10},{10,... | collective-permute-start | bytes 393224 | tf_op jit(solution)/shard_map/ppermute | solution.py:455
  16.5 15.5 %collective-permute-start.6 = (bf16[4,64,256]{2,1,0:T(8,128)(2,1)S(1)}, bf16[4,64,256]{2,1,0:T(8,128)(2,1)S(1)}, u32[]{:S(2)}, u32[]{:S(2)}) collective-permute-start(bf16[4,64,256]{2,1,0:T(8,128)(2,1)S(1)} %pad_maximum_fusion.rest_0_), channel_id=1, source_target_pairs={{0,4},{1,5},{2,6},{3,7},{4,0},{5,1},{6,2},{7,3},{8,12},{9,13},{10,... | collective-permute-start | bytes 393224 | tf_op jit(solution)/shard_map/ppermute | solution.py:455
  18.0 14.0 %collective-permute-start.7 = (bf16[4,64,256]{2,1,0:T(8,128)(2,1)S(1)}, bf16[4,64,256]{2,1,0:T(8,128)(2,1)S(1)}, u32[]{:S(2)}, u32[]{:S(2)}) collective-permute-start(bf16[4,64,256]{2,1,0:T(8,128)(2,1)S(1)} %pad_maximum_fusion.rest_0_), channel_id=1, source_target_pairs={{0,5},{1,4},{2,7},{3,6},{4,1},{5,0},{6,3},{7,2},{8,13},{9,12},{10,... | collective-permute-start | bytes 393224 | tf_op jit(solution)/shard_map/ppermute | solution.py:455
  18.2 13.8 %collective-permute-start.8 = (bf16[4,64,256]{2,1,0:T(8,128)(2,1)S(1)}, bf16[4,64,256]{2,1,0:T(8,128)(2,1)S(1)}, u32[]{:S(2)}, u32[]{:S(2)}) collective-permute-start(bf16[4,64,256]{2,1,0:T(8,128)(2,1)S(1)} %pad_maximum_fusion.rest_0_), channel_id=1, source_target_pairs={{0,6},{1,7},{2,4},{3,5},{4,2},{5,3},{6,0},{7,1},{8,14},{9,15},{10,... | collective-permute-start | bytes 393224 | tf_op jit(solution)/shard_map/ppermute | solution.py:455
  21.0 11.0 %collective-permute-start.9 = (bf16[4,64,256]{2,1,0:T(8,128)(2,1)S(1)}, bf16[4,64,256]{2,1,0:T(8,128)(2,1)S(1)}, u32[]{:S(2)}, u32[]{:S(2)}) collective-permute-start(bf16[4,64,256]{2,1,0:T(8,128)(2,1)S(1)} %pad_maximum_fusion.rest_0_), channel_id=1, source_target_pairs={{0,7},{1,6},{2,5},{3,4},{4,3},{5,2},{6,1},{7,0},{8,15},{9,14},{10,... | collective-permute-start | bytes 393224 | tf_op jit(solution)/shard_map/ppermute | solution.py:455
  43.2 50.5 %copy-start.10 = (bf16[1024,128]{1,0:T(8,128)(2,1)S(1)}, bf16[1024,128]{1,0:T(8,128)(2,1)}, u32[]{:S(2)}) copy-start(bf16[1024,128]{1,0:T(8,128)(2,1)} %param.21) | copy-start | bytes 786436
  43.2 29.0 %all-to-all-start = ((bf16[32,64,256]{2,1,0:T(8,128)(2,1)}), bf16[32,64,256]{2,1,0:T(8,128)(2,1)S(1)}, u32[]{:S(2)}, u32[]{:S(2)}) async-start(bf16[32,64,256]{2,1,0:T(8,128)(2,1)} %row_attend.1), calls=%async_computation | async-start | bytes 2097152 | tf_op jit(solution)/shard_map/all_to_all | solution.py:505
  90.1 3.7 %collective-permute-start.10 = (bf16[256,256]{1,0:T(8,128)(2,1)}, bf16[256,256]{1,0:T(8,128)(2,1)S(1)}, u32[]{:S(2)}, u32[]{:S(2)}) collective-permute-start(bf16[256,256]{1,0:T(8,128)(2,1)} %get-tuple-element.22.refs_0_), channel_id=1, source_target_pairs={{0,1},{1,0},{2,3},{3,2},{4,5},{5,4},{6,7},{7,6},{8,9},{9,8},{10,11... | collective-permute-start | bytes 393224 | tf_op jit(solution)/shard_map/ppermute | solution.py:455
  90.1 6.6 %collective-permute-start.11 = (bf16[256,256]{1,0:T(8,128)(2,1)}, bf16[256,256]{1,0:T(8,128)(2,1)S(1)}, u32[]{:S(2)}, u32[]{:S(2)}) collective-permute-start(bf16[256,256]{1,0:T(8,128)(2,1)} %get-tuple-element.22.refs_0_), channel_id=1, source_target_pairs={{0,2},{1,3},{2,0},{3,1},{4,6},{5,7},{6,4},{7,5},{8,10},{9,11},{10,... | collective-permute-start | bytes 393224 | tf_op jit(solution)/shard_map/ppermute | solution.py:455
  91.6 7.0 %collective-permute-start.12 = (bf16[256,256]{1,0:T(8,128)(2,1)}, bf16[256,256]{1,0:T(8,128)(2,1)S(1)}, u32[]{:S(2)}, u32[]{:S(2)}) collective-permute-start(bf16[256,256]{1,0:T(8,128)(2,1)} %get-tuple-element.22.refs_0_), channel_id=1, source_target_pairs={{0,3},{1,2},{2,1},{3,0},{4,7},{5,6},{6,5},{7,4},{8,11},{9,10},{10,... | collective-permute-start | bytes 393224 | tf_op jit(solution)/shard_map/ppermute | solution.py:455
  92.0 7.6 %collective-permute-start.13 = (bf16[256,256]{1,0:T(8,128)(2,1)}, bf16[256,256]{1,0:T(8,128)(2,1)S(1)}, u32[]{:S(2)}, u32[]{:S(2)}) collective-permute-start(bf16[256,256]{1,0:T(8,128)(2,1)} %get-tuple-element.22.refs_0_), channel_id=1, source_target_pairs={{0,4},{1,5},{2,6},{3,7},{4,0},{5,1},{6,2},{7,3},{8,12},{9,13},{10,... | collective-permute-start | bytes 393224 | tf_op jit(solution)/shard_map/ppermute | solution.py:455
  93.5 12.3 %collective-permute-start.14 = (bf16[256,256]{1,0:T(8,128)(2,1)}, bf16[256,256]{1,0:T(8,128)(2,1)S(1)}, u32[]{:S(2)}, u32[]{:S(2)}) collective-permute-start(bf16[256,256]{1,0:T(8,128)(2,1)} %get-tuple-element.22.refs_0_), channel_id=1, source_target_pairs={{0,5},{1,4},{2,7},{3,6},{4,1},{5,0},{6,3},{7,2},{8,13},{9,12},{10,... | collective-permute-start | bytes 393224 | tf_op jit(solution)/shard_map/ppermute | solution.py:455
  93.8 17.7 %copy-start.18 = (bf16[256,256]{1,0:T(8,128)(2,1)}, bf16[256,256]{1,0:T(8,128)(2,1)S(1)}, u32[]{:S(2)}) copy-start(bf16[256,256]{1,0:T(8,128)(2,1)S(1)} %collective-permute-done.10.refs_1_) | copy-start | bytes 393220
  93.8 17.8 %collective-permute-start.15 = (bf16[256,256]{1,0:T(8,128)(2,1)}, bf16[256,256]{1,0:T(8,128)(2,1)S(1)}, u32[]{:S(2)}, u32[]{:S(2)}) collective-permute-start(bf16[256,256]{1,0:T(8,128)(2,1)} %get-tuple-element.22.refs_0_), channel_id=1, source_target_pairs={{0,6},{1,7},{2,4},{3,5},{4,2},{5,3},{6,0},{7,1},{8,14},{9,15},{10,... | collective-permute-start | bytes 393224 | tf_op jit(solution)/shard_map/ppermute | solution.py:455
  96.7 14.9 %collective-permute-start.16 = (bf16[256,256]{1,0:T(8,128)(2,1)}, bf16[256,256]{1,0:T(8,128)(2,1)S(1)}, u32[]{:S(2)}, u32[]{:S(2)}) collective-permute-start(bf16[256,256]{1,0:T(8,128)(2,1)} %get-tuple-element.22.refs_0_), channel_id=1, source_target_pairs={{0,7},{1,6},{2,5},{3,4},{4,3},{5,2},{6,1},{7,0},{8,15},{9,14},{10,... | collective-permute-start | bytes 393224 | tf_op jit(solution)/shard_map/ppermute | solution.py:455
  98.6 13.0 %collective-permute-start.17 = (bf16[256,256]{1,0:T(8,128)(2,1)}, bf16[256,256]{1,0:T(8,128)(2,1)S(1)}, u32[]{:S(2)}, u32[]{:S(2)}) collective-permute-start(bf16[256,256]{1,0:T(8,128)(2,1)} %get-tuple-element.23.refs_8_), channel_id=1, source_target_pairs={{0,8},{1,9},{2,10},{3,11},{4,12},{5,13},{6,14},{7,15},{8,0},{9,1},... | collective-permute-start | bytes 393224 | tf_op jit(solution)/shard_map/ppermute | solution.py:455
  99.6 12.1 %collective-permute-start.18 = (bf16[256,256]{1,0:T(8,128)(2,1)}, bf16[256,256]{1,0:T(8,128)(2,1)S(1)}, u32[]{:S(2)}, u32[]{:S(2)}) collective-permute-start(bf16[256,256]{1,0:T(8,128)(2,1)} %get-tuple-element.23.refs_8_), channel_id=1, source_target_pairs={{0,16},{1,17},{2,18},{3,19},{4,20},{5,21},{6,22},{7,23},{8,24},{9,... | collective-permute-start | bytes 393224 | tf_op jit(solution)/shard_map/ppermute | solution.py:455
  105.8 8.2 %collective-permute-start.19 = (bf16[256,256]{1,0:T(8,128)(2,1)}, bf16[256,256]{1,0:T(8,128)(2,1)S(1)}, u32[]{:S(2)}, u32[]{:S(2)}) collective-permute-start(bf16[256,256]{1,0:T(8,128)(2,1)} %get-tuple-element.23.refs_8_), channel_id=1, source_target_pairs={{0,24},{1,25},{2,26},{3,27},{4,28},{5,29},{6,30},{7,31},{8,16},{9,... | collective-permute-start | bytes 393224 | tf_op jit(solution)/shard_map/ppermute | solution.py:455
  111.6 21.3 %copy-start.2 = (bf16[8,256,128]{2,1,0:T(8,128)(2,1)S(1)}, bf16[8,256,128]{2,1,0:T(8,128)(2,1)}, u32[]{:S(2)}) copy-start(bf16[8,256,128]{2,1,0:T(8,128)(2,1)} %pair_ref.3) | copy-start | bytes 1572868
  121.5 3.7 %collective-permute-start.20 = (bf16[8,32,128]{2,1,0:T(8,128)(2,1)}, bf16[8,32,128]{2,1,0:T(8,128)(2,1)S(1)}, u32[]{:S(2)}, u32[]{:S(2)}) collective-permute-start(bf16[8,32,128]{2,1,0:T(8,128)(2,1)} %get-tuple-element.25), channel_id=1, source_target_pairs={{0,1},{1,0},{2,3},{3,2},{4,5},{5,4},{6,7},{7,6},{8,9},{9,8},{10,11... | collective-permute-start | bytes 196616 | tf_op jit(solution)/shard_map/ppermute | solution.py:455
  121.6 6.1 %collective-permute-start.21 = (bf16[8,32,128]{2,1,0:T(8,128)(2,1)}, bf16[8,32,128]{2,1,0:T(8,128)(2,1)S(1)}, u32[]{:S(2)}, u32[]{:S(2)}) collective-permute-start(bf16[8,32,128]{2,1,0:T(8,128)(2,1)} %get-tuple-element.26), channel_id=1, source_target_pairs={{0,2},{1,3},{2,0},{3,1},{4,6},{5,7},{6,4},{7,5},{8,10},{9,11},{10,... | collective-permute-start | bytes 196616 | tf_op jit(solution)/shard_map/ppermute | solution.py:455
  123.2 5.0 %collective-permute-start.22 = (bf16[8,32,128]{2,1,0:T(8,128)(2,1)}, bf16[8,32,128]{2,1,0:T(8,128)(2,1)S(1)}, u32[]{:S(2)}, u32[]{:S(2)}) collective-permute-start(bf16[8,32,128]{2,1,0:T(8,128)(2,1)} %get-tuple-element.27), channel_id=1, source_target_pairs={{0,3},{1,2},{2,1},{3,0},{4,7},{5,6},{6,5},{7,4},{8,11},{9,10},{10,... | collective-permute-start | bytes 196616 | tf_op jit(solution)/shard_map/ppermute | solution.py:455
  123.5 4.7 %collective-permute-start.23 = (bf16[8,32,128]{2,1,0:T(8,128)(2,1)}, bf16[8,32,128]{2,1,0:T(8,128)(2,1)S(1)}, u32[]{:S(2)}, u32[]{:S(2)}) collective-permute-start(bf16[8,32,128]{2,1,0:T(8,128)(2,1)} %get-tuple-element.28), channel_id=1, source_target_pairs={{0,4},{1,5},{2,6},{3,7},{4,0},{5,1},{6,2},{7,3},{8,12},{9,13},{10,... | collective-permute-start | bytes 196616 | tf_op jit(solution)/shard_map/ppermute | solution.py:455
  125.0 4.4 %collective-permute-start.24 = (bf16[8,32,128]{2,1,0:T(8,128)(2,1)}, bf16[8,32,128]{2,1,0:T(8,128)(2,1)S(1)}, u32[]{:S(2)}, u32[]{:S(2)}) collective-permute-start(bf16[8,32,128]{2,1,0:T(8,128)(2,1)} %get-tuple-element.29), channel_id=1, source_target_pairs={{0,5},{1,4},{2,7},{3,6},{4,1},{5,0},{6,3},{7,2},{8,13},{9,12},{10,... | collective-permute-start | bytes 196616 | tf_op jit(solution)/shard_map/ppermute | solution.py:455
  125.2 5.7 %collective-permute-start.25 = (bf16[8,32,128]{2,1,0:T(8,128)(2,1)}, bf16[8,32,128]{2,1,0:T(8,128)(2,1)S(1)}, u32[]{:S(2)}, u32[]{:S(2)}) collective-permute-start(bf16[8,32,128]{2,1,0:T(8,128)(2,1)} %get-tuple-element.30), channel_id=1, source_target_pairs={{0,6},{1,7},{2,4},{3,5},{4,2},{5,3},{6,0},{7,1},{8,14},{9,15},{10,... | collective-permute-start | bytes 196616 | tf_op jit(solution)/shard_map/ppermute | solution.py:455
  127.6 5.2 %collective-permute-start.26 = (bf16[8,32,128]{2,1,0:T(8,128)(2,1)}, bf16[8,32,128]{2,1,0:T(8,128)(2,1)S(1)}, u32[]{:S(2)}, u32[]{:S(2)}) collective-permute-start(bf16[8,32,128]{2,1,0:T(8,128)(2,1)} %get-tuple-element.31), channel_id=1, source_target_pairs={{0,7},{1,6},{2,5},{3,4},{4,3},{5,2},{6,1},{7,0},{8,15},{9,14},{10,... | collective-permute-start | bytes 196616 | tf_op jit(solution)/shard_map/ppermute | solution.py:455
  (26 other events, 121.7 us)

commit v2 on v1

--- a/solution.py
+++ b/solution.py
@@ -193,19 +193,28 @@
 def attend_block(query, key, value, live, lanes, bias_of):
     pieces = []
     per_tile = LANES // HEAD_CHANNELS
+    length = query.shape[0]
     for tile in range(query.shape[1] // LANES):
         cut = slice(tile * LANES, (tile + 1) * LANES)
         query_t, key_t = query[:, cut], key[:, cut]
         value_t = value[:, cut] * live
-        total = None
-        for t in range(per_tile):
-            scores = nt_dot(query_t * lanes[t], key_t)
-            if bias_of is not None:
-                scores = scores + bias_of(tile * per_tile + t)
-            raised = jnp.exp2(scores).astype(BF16)
-            side = jnp.concatenate([value_t * lanes[t], live * lanes[t]], axis=1)
-            part = nn_dot(raised, side)
-            total = part if total is None else total + part
+        if bias_of is None:
+            all_scores = [nt_dot(query_t * lanes[t], key_t) for t in range(per_tile)]
+        else:
+            stacked = jnp.concatenate([query_t * lanes[t] for t in range(per_tile)], axis=0)
+            stacked = nt_dot(stacked, key_t)
+            all_scores = [
+                stacked[t * length : (t + 1) * length] + bias_of(tile * per_tile + t)
+                for t in range(per_tile)
+            ]
+        raised = [jnp.exp2(scores).astype(BF16) for scores in all_scores]
+        sides = [
+            jnp.concatenate([value_t * lanes[t], live * lanes[t]], axis=1) for t in range(per_tile)
+        ]
+        if bias_of is None:
+            total = sum(nn_dot(r, s) for r, s in zip(raised, sides))
+        else:
+            total = nn_dot(jnp.concatenate(raised, axis=1), jnp.concatenate(sides, axis=0))
         pieces.append(total[:, :LANES] / total[:, LANES:])
     return jnp.concatenate(pieces, axis=1)
 
@@ -236,7 +245,7 @@
         bias_kernel,
         out_shape=out,
         scratch_shapes=[tiled_scratch(*out.shape)],
-        compiler_params=params(32),
+        compiler_params=params(12),
         name="pair_bias",
     )(pair_rep, weight)
 
@@ -258,26 +267,23 @@
         in_specs=[block, full_spec(weight.shape)],
         out_specs=[block] * 4,
         out_shape=[small, small, small, jax.ShapeDtypeStruct(alignment.shape, F32)],
-        compiler_params=params(48),
+        compiler_params=params(24),
         name="row_project",
     )(alignment, weight)
 
 
-def row_attend_kernel(group, step, me_ref, x_ref, q_ref, k_ref, v_ref, g_ref, live_ref, out_w_ref, *rest):
-    bias_refs, out_ref, bias_all = rest[:group], rest[group], rest[group + 1]
+def row_attend_kernel(step, x_ref, q_ref, k_ref, v_ref, g_ref, live_ref, out_w_ref, bias_ref, out_ref, bias_all):
     heads, length, _ = bias_all.shape
-    outer = bias_refs[0].shape[0]
+    group, outer, block_rows, _ = bias_ref.shape
+    rows = block_rows // heads
 
     @pl.when(pl.program_id(0) == 0)
     def _():
-        here = me_ref[0]
         for k in range(group):
             for z in range(outer):
-                rows = bias_refs[k].shape[1] // heads
-                owner = here ^ (z * group + k)
-                at = pl.ds(pl.multiple_of(owner * rows, rows), rows)
-                block = bias_refs[k][z].astype(F32).reshape(heads, rows, length)
-                bias_all[:, at, :] = block
+                owner = z * group + k
+                block = bias_ref[k, z].astype(F32).reshape(heads, rows, length)
+                bias_all[:, owner * rows : (owner + 1) * rows, :] = block
 
     lanes = head_lanes(length)
     results = []
@@ -293,29 +299,28 @@
     out_ref[...] = joined.reshape(out_ref.shape).astype(BF16)
 
 
-def row_attend(me, alignment, projected, live, out_weight, bias_parts, dap_count):
+def row_attend(alignment, projected, live, out_weight, bias, dap_count):
     seqs, length, width = alignment.shape
     rows = length // dap_count
     step = 2
     block = pl.BlockSpec((step, length, width), lambda i: (i, 0, 0))
     return pl.pallas_call(
-        functools.partial(row_attend_kernel, len(bias_parts), step),
+        functools.partial(row_attend_kernel, step),
         grid=(seqs // step,),
-        in_specs=[pl.BlockSpec(memory_space=pltpu.SMEM)]
-        + [block] * 5
+        in_specs=[block] * 5
         + [pl.BlockSpec((step, length, LANES), lambda i: (i, 0, 0)), full_spec(out_weight.shape)]
-        + [full_spec(b.shape) for b in bias_parts],
+        + [full_spec(bias.shape)],
         out_specs=pl.BlockSpec((dap_count, step * rows, width), lambda i: (0, i, 0)),
         out_shape=jax.ShapeDtypeStruct((dap_count, seqs * rows, width), BF16),
         scratch_shapes=[pltpu.VMEM((ATTN_HEAD_COUNT, length, length), F32)],
-        compiler_params=params(56),
+        compiler_params=params(28),
         name="row_attend",
-    )(me, alignment, *projected, live, out_weight, *bias_parts)
+    )(alignment, *projected, live, out_weight, bias)
 
 
 def column_kernel(
-    items, x_ref, live_ref, mask_ref, weight_ref, out_w_ref, factor_ref,
-    out_ref, left_ref, right_ref, held, right_held,
+    items, each, x_ref, live_ref, mask_ref, weight_ref, out_w_ref, factor_ref,
+    out_ref, left_ref, right_ref, held, left_held, right_held,
 ):
     step = pl.program_id(0)
     total_rows = held.shape[1]
@@ -328,65 +333,90 @@
             held[t] = part.reshape(total_rows, LANES)
 
     lanes = head_lanes(length)
-    current = load_strided(held, step, items, length)
-    normed = layer_normalize(current).astype(BF16)
-    query, key, value, gate = project(normed, weight_ref)
-    heads_out = attend_block(query, key, value, live_ref[0], lanes, None)
-    heads_out = (heads_out * gate).astype(BF16)
-    updated = (current + nn_dot(heads_out, out_w_ref[...])).astype(BF16).astype(F32)
-    store_strided(held, step, items, updated)
-    normed = layer_normalize(updated).astype(BF16)
-    factors = nt_dot(factor_ref[...], normed) * mask_ref[pl.ds(step, 1), :]
-    left_at = pl.ds(pl.multiple_of(step * FACTOR_CHANNELS, FACTOR_CHANNELS), FACTOR_CHANNELS)
-    left_ref[left_at, :] = factors[:FACTOR_CHANNELS].astype(BF16)
-    store_strided(right_held, step, items, factors[FACTOR_CHANNELS:])
-
-    @pl.when(step == items - 1)
+    for n in range(each):
+        item = step * each + n
+        current = load_strided(held, item, items, length)
+        normed = layer_normalize(current).astype(BF16)
+        query, key, value, gate = project(normed, weight_ref)
+        heads_out = attend_block(query, key, value, live_ref[n], lanes, None)
+        heads_out = (heads_out * gate).astype(BF16)
+        updated = (current + nn_dot(heads_out, out_w_ref[...])).astype(BF16).astype(F32)
+        store_strided(held, item, items, updated)
+        normed = layer_normalize(updated).astype(BF16)
+        factors = nt_dot(factor_ref[...], normed) * mask_ref[pl.ds(item, 1), :]
+        left_at = pl.ds(pl.multiple_of(item * FACTOR_CHANNELS, FACTOR_CHANNELS), FACTOR_CHANNELS)
+        left_held[left_at, :] = factors[:FACTOR_CHANNELS].astype(BF16)
+        store_strided(right_held, item, items, factors[FACTOR_CHANNELS:])
+
+    @pl.when(step == items // each - 1)
     def _():
         for t in range(held.shape[0]):
             part = held[t].reshape(out_ref.shape[:2] + (LANES,))
             out_ref[:, :, t * LANES : (t + 1) * LANES] = part.astype(BF16)
-        right_ref[...] = joined_tiles(right_held).astype(BF16)
-
-
-def column_attend(moved, live, mask_rows, weight, out_weight, factor_weight, items):
+        right = joined_tiles(right_held).astype(BF16)
+        for k in range(right_ref.shape[0]):
+            right_ref[k] = right
+        for k in range(left_ref.shape[0]):
+            left_ref[k] = left_held[...]
+
+
+def column_attend(moved, live, mask_rows, weight, out_weight, factor_weight, items, group, outer):
     width = moved.shape[2]
     total_rows = moved.shape[0] * moved.shape[1]
     length = total_rows // items
     factor_t = factor_weight.T
-    side = jax.ShapeDtypeStruct((items * FACTOR_CHANNELS, length), BF16)
+    each = 2
+    side = (items * FACTOR_CHANNELS, length)
+    left = jax.ShapeDtypeStruct((group,) + side, BF16)
+    right = jax.ShapeDtypeStruct((outer,) + side, BF16)
     out = jax.ShapeDtypeStruct((length, items, width), BF16)
     return pl.pallas_call(
-        functools.partial(column_kernel, items),
-        grid=(items,),
+        functools.partial(column_kernel, items, each),
+        grid=(items // each,),
         in_specs=[
             full_spec(moved.shape),
-            pl.BlockSpec((1, length, LANES), lambda i: (i, 0, 0)),
+            pl.BlockSpec((each, length, LANES), lambda i: (i, 0, 0)),
             full_spec(mask_rows.shape),
             full_spec(weight.shape),
             full_spec(out_weight.shape),
             full_spec(factor_t.shape),
         ],
-        out_specs=[full_spec(out.shape), full_spec(side.shape), full_spec(side.shape)],
-        out_shape=[out, side, side],
-        scratch_shapes=[tiled_scratch(total_rows, width), tiled_scratch(*side.shape)],
-        compiler_params=params(56),
+        out_specs=[full_spec(out.shape), full_spec(left.shape), full_spec(right.shape)],
+        out_shape=[out, left, right],
+        scratch_shapes=[tiled_scratch(total_rows, width), pltpu.VMEM(side, BF16), tiled_scratch(*side)],
+        compiler_params=params(28),
         name="column_attend",
     )(moved, live, mask_rows, weight, out_weight, factor_t)
 
 
-def outer_kernel(group, outer, items, *refs):
-    lefts, rights = refs[:group], refs[group : group + outer]
-    weight_ref = refs[group + outer]
-    outs = refs[group + outer + 1 : 2 * group + outer + 1]
-    held = refs[-1]
+def spread_kernel(weight_ref, out_ref):
+    feat = weight_ref.shape[1]
+    width = weight_ref.shape[2]
+    out_ref[...] = jnp.zeros_like(out_ref)
+    for e in range(weight_ref.shape[0]):
+        for i in range(LANES // feat):
+            start = e * LANES + i * feat
+            out_ref[start : start + feat, i * width : (i + 1) * width] = weight_ref[e]
+
+
+def spread_weight(outer_out):
+    weight = outer_out.reshape(FACTOR_CHANNELS, FACTOR_CHANNELS, -1).swapaxes(0, 1)
+    quad = LANES // FACTOR_CHANNELS
+    out = jax.ShapeDtypeStruct((FACTOR_CHANNELS * LANES, quad * weight.shape[2]), BF16)
+    return pl.pallas_call(
+        spread_kernel, out_shape=out, compiler_params=params(12), name="spread_weight"
+    )(weight)
+
+
+def outer_kernel(items, left_ref, right_ref, weight_ref, out_ref, held):
+    group, outer = left_ref.shape[0], right_ref.shape[0]
     feat = FACTOR_CHANNELS
     quad = LANES // feat
     tiles = items * feat // LANES
     cols = outer * items
-    right = jnp.concatenate([r[...] for r in rights], axis=0)
+    right = right_ref[...].reshape(outer * right_ref.shape[1], right_ref.shape[2])
     for k in range(group):
-        sums = nt_dot(right, lefts[k][...])
+        sums = nt_dot(right, left_ref[k])
         sums = sums.reshape(outer, feat, items, sums.shape[1])
         sums = jnp.transpose(sums, (1, 0, 2, 3)).reshape(feat, cols, sums.shape[3]).astype(BF16)
         for t in range(tiles):
@@ -399,60 +429,45 @@
         for t in range(tiles):
             rows = update[(k * tiles + t) * cols : (k * tiles + t + 1) * cols]
             for i in range(quad):
-                outs[k][t * quad + i] = rows[:, i * width : (i + 1) * width].astype(BF16)
+                out_ref[k, t * quad + i] = rows[:, i * width : (i + 1) * width].astype(BF16)
 
 
 def outer_product(lefts, rights, weight, items):
-    group, outer = len(lefts), len(rights)
+    group, outer = lefts.shape[0], rights.shape[0]
     cols = outer * items
     width = weight.shape[1] * FACTOR_CHANNELS // LANES
-    out = jax.ShapeDtypeStruct((items, cols, width), BF16)
     tiles = items * FACTOR_CHANNELS // LANES
     return pl.pallas_call(
-        functools.partial(outer_kernel, group, outer, items),
-        out_shape=[out] * group,
+        functools.partial(outer_kernel, items),
+        out_shape=jax.ShapeDtypeStruct((group, items, cols, width), BF16),
         scratch_shapes=[pltpu.VMEM((group * tiles * cols, weight.shape[0]), BF16)],
-        compiler_params=params(56),
+        compiler_params=params(28),
         name="outer_product",
-    )(*lefts, *rights, weight)
-
-
-def finish_kernel(group, outer, items, me_ref, pair_ref, scale_ref, *refs):
-    parts, out_ref = refs[:group], refs[group]
-    here = me_ref[0]
-    odd = (here & 1) == 1
+    )(lefts, rights, weight)
+
+
+def finish_kernel(pair_ref, scale_ref, parts_ref, out_ref):
+    group, items, cols, width = parts_ref.shape
+    outer = cols // items
     for pairing in range(group // 2):
         for i in range(items):
-            first = parts[2 * pairing][i].astype(F32)
-            second = parts[2 * pairing + 1][i].astype(F32)
-            low = jnp.where(odd, second, first)
-            high = jnp.where(odd, first, second)
+            low = parts_ref[2 * pairing, i].astype(F32).reshape(outer, 1, items, width)
+            high = parts_ref[2 * pairing + 1, i].astype(F32).reshape(outer, 1, items, width)
+            both = jnp.concatenate([low, high], axis=1).reshape(outer, 2 * items, width)
             for z in range(outer):
-                owner = here ^ (z * group + 2 * pairing)
-                start = pl.multiple_of((owner >> 1) * (2 * items), 2 * items)
-                at = pl.ds(start, 2 * items)
-                cut = slice(z * items, (z + 1) * items)
-                update = jnp.concatenate([low[cut], high[cut]], axis=0)
-                update = update * scale_ref[at, i : i + 1]
+                start = (z * group + 2 * pairing) * items
+                at = slice(start, start + 2 * items)
+                update = both[z] * scale_ref[at, i : i + 1]
                 out_ref[i, at, :] = (pair_ref[i, at, :].astype(F32) + update).astype(BF16)
 
 
-def finish(me, pair_rep, scale, parts, outer):
-    items = pair_rep.shape[0]
-    return pl.pallas_call(
-        functools.partial(finish_kernel, len(parts), outer, items),
-        in_specs=[pl.BlockSpec(memory_space=pltpu.SMEM), full_spec(pair_rep.shape), full_spec(scale.shape)]
-        + [full_spec(p.shape) for p in parts],
-        out_specs=full_spec(pair_rep.shape),
+def finish(pair_rep, scale, parts):
+    return pl.pallas_call(
+        finish_kernel,
         out_shape=jax.ShapeDtypeStruct(pair_rep.shape, BF16),
-        compiler_params=params(48),
+        compiler_params=params(16),
         name="finish",
-    )(me, pair_rep, scale, *parts)
-
-
-def exchange(block, count, offset):
-    pairs = [(i, i ^ offset) for i in range(count)]
-    return lax.ppermute(block, "dap", pairs)
+    )(pair_rep, scale, parts)
 
 
 def per_device_fast(
@@ -472,17 +487,17 @@
     group = inner_size(dap_count)
     outer = dap_count // group
     dap_index = lax.axis_index("dap")
-    me = jnp.reshape(dap_index, (1,)).astype(jnp.int32)
+    plane = [[z * group + k for k in range(group)] for z in range(outer)]
+    line = [[z * group + k for z in range(outer)] for k in range(group)]
     seq_dev = alignment.shape[0]
     items = pair_rep.shape[0]
     width = alignment.shape[2]
     total_seqs, total_res = align_mask.shape
 
     bias = pair_bias_block(pair_rep, bias_weight)
-    column = [bias] + [exchange(bias, dap_count, z * group) for z in range(1, outer)]
+    bias = lax.all_gather(bias, "dap", axis_index_groups=line)
     projected = row_project(alignment, row_proj_weight)
-    column = jnp.stack(column)
-    bias_parts = [column] + [exchange(column, dap_count, k) for k in range(1, group)]
+    bias = lax.all_gather(bias, "dap", axis_index_groups=plane)
 
     mask = align_mask.astype(F32)
     own_seqs = lax.dynamic_slice_in_dim(align_mask, dap_index * seq_dev, seq_dev, 0)
@@ -496,12 +511,10 @@
     live_rows = lax.dynamic_slice_in_dim(res_float, dap_index * items, items, 0)
     scale = live_rows[None, :] * res_float[:, None] / (counts + count_eps)
 
-    quad = LANES // FACTOR_CHANNELS
-    weight = outer_out.reshape(FACTOR_CHANNELS, FACTOR_CHANNELS, -1).swapaxes(0, 1)
-    spread = jnp.eye(quad, dtype=BF16)[None, :, None, :, None] * weight[:, None, :, None, :]
-    spread = spread.reshape(FACTOR_CHANNELS * LANES, quad * weight.shape[2])
-
-    row_out = row_attend(me, alignment, projected, row_live, row_out_weight, bias_parts, dap_count)
+    spread = spread_weight(outer_out)
+    spread, scale, col_live = lax.optimization_barrier((spread, scale, col_live))
+
+    row_out = row_attend(alignment, projected, row_live, row_out_weight, bias, dap_count)
     moved = lax.all_to_all(row_out, "dap", split_axis=0, concat_axis=0, tiled=True)
     updated, left, right = column_attend(
         moved,
@@ -511,13 +524,20 @@
         column_out_weight,
         outer_factor_weight,
         items,
-    )
-    rights = [right] + [exchange(right, dap_count, z * group) for z in range(1, outer)]
-    lefts = [left] + [exchange(left, dap_count, k) for k in range(1, group)]
-    parts = outer_product(lefts, rights, spread, items)
-    parts = [parts[0]] + [exchange(parts[k], dap_count, k) for k in range(1, group)]
-    pair_out = finish(me, pair_rep, scale, parts, outer)
+        group,
+        outer,
+    )
+    rights = grouped_exchange(right, line)
+    lefts = grouped_exchange(left, plane)
+    parts = grouped_exchange(outer_product(lefts, rights, spread, items), plane)
+    pair_out = finish(pair_rep, scale, parts)
     return updated, pair_out
+
+
+def grouped_exchange(blocks, groups):
+    return lax.all_to_all(
+        blocks, "dap", split_axis=0, concat_axis=0, tiled=True, axis_index_groups=groups
+    )
 
 
 def inner_size(count):

time: 135 us -> 170 us (1.26)
  blocking collectives: 0 us -> 64.1 us
  starting transfers between devices: 32.9 us -> 4.64 us
  between operations: 0.99 us -> 14.2 us
  Pallas kernels: 39.4 us -> 30.8 us
  waiting for transfers between devices: 44.6 us -> 39.9 us
  other arithmetic: 2.99 us -> 0.71 us
    all_to_all x0 -> x3, blocking collectives: none -> 48.3 us  [grouped_exchange(): lax.all_to_all(blocks, 'dap', split_axis=0, concat_axis=0, tiled=True, ax...]
    ppermute x27 -> x0, starting transfers between devices: 30 us -> none  [exchange(): return lax.ppermute(block, 'dap', pairs)]
    ppermute x27 -> x0, waiting for transfers between devices: 19.3 us -> none  [exchange(): return lax.ppermute(block, 'dap', pairs)]
    all_gather x0 -> x1, waiting for transfers between devices: none -> 16.9 us  [per_device_fast(): bias = lax.all_gather(bias, 'dap', axis_index_groups=plane)]
    all_gather x0 -> x1, blocking collectives: none -> 15.8 us  [per_device_fast(): bias = lax.all_gather(bias, 'dap', axis_index_groups=line)]
    pallas_call x4 -> x5, Pallas kernels: 34.9 us -> 27.2 us  [the longest x1 14.8 us: column_attend(): pl.pallas_call(functools.partial(column_kernel, items, each), grid=(items...]
    unnamed x62 -> x39, local copies, waits for them, and re-layouts: 10.6 us -> 13 us
    all_to_all x1, waiting for transfers between devices: 25.2 us -> 22.9 us  [per_device_fast(): lax.all_to_all(row_out, 'dap', split_axis=0, concat_axis=0, tiled=True)]
  transfers between devices with their start and end apart: 28 -> 2, of which waited for: 11 -> 2; matrix products, arithmetic and copies ran while one was open for 5% -> 1% of each run, Pallas kernels for 3% -> 2%
where the time goes in v2:
time: 170 us; the launch traced here: 169 us
  blocking collectives  64.1 us (38%)
  waiting for transfers between devices  39.9 us (23%)
  Pallas kernels  30.8 us (18%)
  local copies, waits for them, and re-layouts  14.7 us (9%)
  between operations  14.2 us (8%)
  starting transfers between devices  4.64 us (3%)
    all_to_all x3, blocking collectives, grouped_exchange(): lax.all_to_all(blocks, 'dap', split_axis=0, concat_axis=0, tiled=True, ax...  48.3 us
    all_to_all x1, waiting for transfers between devices, per_device_fast(): lax.all_to_all(row_out, 'dap', split_axis=0, concat_axis=0, tiled=True)  22.9 us
    all_gather x1, waiting for transfers between devices, per_device_fast(): bias = lax.all_gather(bias, 'dap', axis_index_groups=plane)  16.9 us
    all_gather x1, blocking collectives, per_device_fast(): bias = lax.all_gather(bias, 'dap', axis_index_groups=line)  15.8 us
    pallas_call x1, Pallas kernels, column_attend(): pl.pallas_call(functools.partial(column_kernel, items, each), grid=(items...  14.8 us
    unnamed x39, local copies, waits for them, and re-layouts  13 us
    pallas_call x1, Pallas kernels, row_attend(): pl.pallas_call(functools.partial(row_attend_kernel, step), grid=(seqs //...  7.43 us
    all_to_all x1, starting transfers between devices, per_device_fast(): lax.all_to_all(row_out, 'dap', split_axis=0, concat_axis=0, tiled=True)  4.6 us
  transfers between devices with their start and end apart: 2, of which 2 were waited for; matrix products, arithmetic and copies ran while one was open for 1% of the time, Pallas kernels for 2%

profile of v2, /device:TPU:0, one launch (start us, length us, event | category | flops | bytes accessed | tf_op | source)
XLA Modules:
  0.0 169.2 jit_solution(11923628953468652864)
XLA Ops:
  7.2 0.7 pad.4.weight_ref
  7.9 1.0 copy-done.4
  8.9 0.7 pair_bias.1
  9.7 15.8 %all-gather = bf16[256,256]{1,0:T(8,128)(2,1)} all-gather(bf16[64,256]{1,0:T(8,128)(2,1)S(1)} %pair_bias.1), channel_id=2, replica_groups={{0,8,16,24},{1,9,17,25},{2,10,18,26},{3,11,19,27},{4,12,20,28},{5,13,21..., dimensions={0}, use_global_device_ids=true | all-gather | bytes 163840 | tf_op jit(solution)/shard_map/all_gather | solution.py:498
  25.5 1.2 copy-done.2
  26.7 1.0 copy-done.11
  27.8 2.9 %row_project.1 = (bf16[8,256,256]{2,1,0:T(8,128)(2,1)S(1)}, bf16[8,256,256]{2,1,0:T(8,128)(2,1)S(1)}, bf16[8,256,256]{2,1,0:T(8,128)(2,1)S(1)}, f32[8,256,256]{2,1,0:T(8,128)S(1)}) custom-call(bf16[8,256,256]{2,1,0:T(8,128)(2,1)S(1)} %copy-done.2, bf16[4,256,256]{2,1,0:T(8,128)(2,1)S(1)} %copy-done.11), custom_call_target="tpu_custom_call" | custom-call | tf_op jit(solution)/shard_map/row_project/pallas_call | solution.py:264
  30.7 1.0 copy-done.7
  31.6 1.0 copy-done.9
  32.6 0.7 dynamic-slice_convert_fusion
  33.3 16.9 %all-gather.4.cloned.1.call-done = bf16[32,64,256]{2,1,0:T(8,128)(2,1)} async-done(((bf16[4,64,256]{2,1,0:T(8,128)(2,1)}), bf16[32,64,256]{2,1,0:T(8,128)(2,1)}) %all-gather.4.cloned.1.call-update) | async-done | bytes 1048592 | tf_op jit(solution)/shard_map/all_gather | solution.py:500
  50.2 0.3 broadcast_in_dim.4.live_ref
  50.6 1.2 copy-done.3
  51.8 1.2 copy-done.6
  53.0 1.2 copy-done.8
  54.3 1.2 copy-done.10
  55.5 0.9 copy-done.13
  56.4 7.4 %row_attend.1 = bf16[32,64,256]{2,1,0:T(8,128)(2,1)} custom-call(bf16[8,256,256]{2,1,0:T(8,128)(2,1)S(1)} %copy-done.3, bf16[8,256,256]{2,1,0:T(8,128)(2,1)S(1)} %get-tuple-element.12.q_ref, bf16[8,256,256]{2,1,0:T(8,128)(2,1)S(1)} %copy-done.8, bf16[8,256,256]{2,1,0:T(8,128)(2,1)S(1)} %copy-done.10, f32[8,256,256]{2,1,0:T(8,128)S(1)} %get-tuple-element.15.g_ref, ...), custom_call_target="tpu_custom_call" | custom-call | tf_op jit(solution)/shard_map/row_attend/pallas_call | solution.py:307
  63.8 4.6 %all-to-all-start = ((bf16[32,64,256]{2,1,0:T(8,128)(2,1)}), bf16[32,64,256]{2,1,0:T(8,128)(2,1)S(1)}, u32[]{:S(2)}, u32[]{:S(2)}) async-start(bf16[32,64,256]{2,1,0:T(8,128)(2,1)} %row_attend.1), calls=%async_computation | async-start | bytes 2097152 | tf_op jit(solution)/shard_map/all_to_all | solution.py:518
  68.5 0.1 copy.28
  68.6 0.4 spread_weight.1.weight_ref
  69.0 1.9 %copy-done = bf16[4096,512]{1,0:T(8,128)(2,1)} copy-done((bf16[4096,512]{1,0:T(8,128)(2,1)}, bf16[4096,512]{1,0:T(8,128)(2,1)S(1)}, u32[]{:S(2)}) %copy-start) | copy-done | bytes 4194328
  71.0 0.1 constant_dynamic-slice_fusion
  71.2 0.2 fusion.1.scale_ref
  71.4 0.3 broadcast_in_dim.5.live_ref
  71.8 22.9 %all-to-all-done.x_ref = bf16[32,64,256]{2,1,0:T(8,128)(2,1)S(1)} async-done(((bf16[32,64,256]{2,1,0:T(8,128)(2,1)}), bf16[32,64,256]{2,1,0:T(8,128)(2,1)S(1)}, u32[]{:S(2)}, u32[]{:S(2)}) %all-to-all-start) | async-done | bytes 1048608 | tf_op jit(solution)/shard_map/all_to_all | solution.py:518
  94.7 14.8 %column_attend.1 = (bf16[256,8,256]{2,1,0:T(8,128)(2,1)}, bf16[8,256,256]{2,1,0:T(8,128)(2,1)S(1)}, bf16[4,256,256]{2,1,0:T(8,128)(2,1)S(1)}) custom-call(bf16[32,64,256]{2,1,0:T(8,128)(2,1)S(1)} %all-to-all-done.x_ref, bf16[8,256,128]{2,1,0:T(8,128)(2,1)S(1)} %broadcast_in_dim.5.live_ref, f32[8,256]{1,0:T(8,128)S(1)} %get-tuple-element.22.mask_ref, ...), custom_call_target="tpu_custom_call" | custom-call | tf_op jit(solution)/shard_map/column_attend/pallas_call | solution.py:373
  109.5 17.2 %all_to_all.20.right_ref = bf16[4,256,256]{2,1,0:T(8,128)(2,1)S(1)} all-to-all(bf16[4,256,256]{2,1,0:T(8,128)(2,1)S(1)} %get-tuple-element.20), channel_id=1, replica_groups={{0,8,16,24},{1,9,17,25},{2,10,18,26},{3,11,19,27},{4,12,20,28},{5,13,21..., dimensions={0} | all-to-all | bytes 1048576 | tf_op jit(solution)/shard_map/all_to_all | solution.py:538
  126.7 18.9 %all_to_all.21.left_ref = bf16[8,256,256]{2,1,0:T(8,128)(2,1)S(1)} all-to-all(bf16[8,256,256]{2,1,0:T(8,128)(2,1)S(1)} %get-tuple-element.19), channel_id=1, replica_groups={{0,1,2,3,4,5,6,7},{8,9,10,11,12,13,14,15},{16,17,18,19,20,21,22,23},{24..., dimensions={0} | all-to-all | bytes 2097152 | tf_op jit(solution)/shard_map/all_to_all | solution.py:538
  145.6 3.4 %outer_product.1 = bf16[8,8,32,128]{3,2,1,0:T(8,128)(2,1)S(1)} custom-call(bf16[8,256,256]{2,1,0:T(8,128)(2,1)S(1)} %all_to_all.21.left_ref, bf16[4,256,256]{2,1,0:T(8,128)(2,1)S(1)} %all_to_all.20.right_ref, bf16[4096,512]{1,0:T(8,128)(2,1)S(1)} %copy-done.1), custom_call_target="tpu_custom_call" | custom-call | tf_op jit(solution)/shard_map/outer_product/pallas_call | solution.py:440
  149.0 12.2 %all_to_all.22.parts_ref = bf16[8,8,32,128]{3,2,1,0:T(8,128)(2,1)S(1)} all-to-all(bf16[8,8,32,128]{3,2,1,0:T(8,128)(2,1)S(1)} %outer_product.1), channel_id=1, replica_groups={{0,1,2,3,4,5,6,7},{8,9,10,11,12,13,14,15},{16,17,18,19,20,21,22,23},{24..., dimensions={0} | all-to-all | bytes 1048576 | tf_op jit(solution)/shard_map/all_to_all | solution.py:538
  161.2 1.2 finish.1
  (33 shorter events, 0.3 us)
Async XLA Ops:
  7.2 43.1 %all-gather.4.cloned.1.call-start = ((), (), s32[]{:S(2)}) async-start(), calls=%async_computation.4 | async-start | bytes 1179648 | tf_op jit(solution)/shard_map/all_gather | solution.py:500
  7.9 1.0 copy-start.4
  25.5 1.2 copy-start.2
  26.7 1.0 copy-start.11
  30.6 1.0 copy-start.7
  31.6 1.0 copy-start.9
  50.6 1.2 copy-start.3
  51.8 1.2 copy-start.6
  53.0 1.2 copy-start.8
  54.3 1.2 copy-start.10
  55.5 0.9 copy-start.13
  56.4 12.1 %copy-start.16 = (bf16[1024,128]{1,0:T(8,128)(2,1)S(1)}, bf16[1024,128]{1,0:T(8,128)(2,1)}, u32[]{:S(2)}) copy-start(bf16[1024,128]{1,0:T(8,128)(2,1)} %param.21) | copy-start | bytes 786436
  63.8 7.1 %copy-start.18 = (s32[256]{0:T(256)S(1)}, s32[256]{0:T(256)}, u32[]{:S(2)}) copy-start(s32[256]{0:T(256)} %param.14) | copy-start | bytes 3076
  63.8 7.2 %copy-start.17 = (s32[256,256]{1,0:T(8,128)S(1)}, s32[256,256]{1,0:T(8,128)}, u32[]{:S(2)}) copy-start(s32[256,256]{1,0:T(8,128)} %param.13) | copy-start | bytes 786436
  63.8 30.9 %copy-start.12 = (bf16[4,256,256]{2,1,0:T(8,128)(2,1)S(1)}, bf16[4,256,256]{2,1,0:T(8,128)(2,1)}, u32[]{:S(2)}) copy-start(bf16[4,256,256]{2,1,0:T(8,128)(2,1)} %weight_ref.3) | copy-start | bytes 1572868
  63.8 30.9 %copy-start.14 = (bf16[256,256]{1,0:T(8,128)(2,1)S(1)}, bf16[256,256]{1,0:T(8,128)(2,1)}, u32[]{:S(2)}) copy-start(bf16[256,256]{1,0:T(8,128)(2,1)} %out_w_ref.3) | copy-start | bytes 393220
  63.8 30.9 %copy-start.15 = (bf16[256,64]{0,1:T(8,128)(2,1)S(1)}, bf16[256,64]{0,1:T(8,128)(2,1)}, u32[]{:S(2)}) copy-start(bf16[256,64]{0,1:T(8,128)(2,1)} %param.20) | copy-start | bytes 98308
  63.8 30.8 %all-to-all-start = ((bf16[32,64,256]{2,1,0:T(8,128)(2,1)}), bf16[32,64,256]{2,1,0:T(8,128)(2,1)S(1)}, u32[]{:S(2)}, u32[]{:S(2)}) async-start(bf16[32,64,256]{2,1,0:T(8,128)(2,1)} %row_attend.1), calls=%async_computation | async-start | bytes 2097152 | tf_op jit(solution)/shard_map/all_to_all | solution.py:518
  69.0 1.9 %copy-start = (bf16[4096,512]{1,0:T(8,128)(2,1)}, bf16[4096,512]{1,0:T(8,128)(2,1)S(1)}, u32[]{:S(2)}) copy-start(bf16[4096,512]{1,0:T(8,128)(2,1)S(1)} %spread_weight.1.weight_ref) | copy-start | bytes 12582916
  94.7 50.9 %copy-start.1 = (bf16[4096,512]{1,0:T(8,128)(2,1)S(1)}, bf16[4096,512]{1,0:T(8,128)(2,1)}, u32[]{:S(2)}) copy-start(bf16[4096,512]{1,0:T(8,128)(2,1)} %copy-done) | copy-start | bytes 12582916
  126.7 34.5 %copy-start.5 = (bf16[8,256,128]{2,1,0:T(8,128)(2,1)S(1)}, bf16[8,256,128]{2,1,0:T(8,128)(2,1)}, u32[]{:S(2)}) copy-start(bf16[8,256,128]{2,1,0:T(8,128)(2,1)} %pair_ref.3) | copy-start | bytes 1572868
Sparse Core Ops, SparseCore 0:
  25.6 24.5 all-gather.3

commit v3 on v1

--- a/solution.py
+++ b/solution.py
@@ -193,19 +193,21 @@
 def attend_block(query, key, value, live, lanes, bias_of):
     pieces = []
     per_tile = LANES // HEAD_CHANNELS
+    rows = query.shape[0]
     for tile in range(query.shape[1] // LANES):
         cut = slice(tile * LANES, (tile + 1) * LANES)
         query_t, key_t = query[:, cut], key[:, cut]
         value_t = value[:, cut] * live
-        total = None
+        stacked = jnp.concatenate([query_t * lanes[t][:rows] for t in range(per_tile)], axis=0)
+        stacked = nt_dot(stacked, key_t)
+        raised, sides = [], []
         for t in range(per_tile):
-            scores = nt_dot(query_t * lanes[t], key_t)
+            scores = stacked[t * rows : (t + 1) * rows]
             if bias_of is not None:
                 scores = scores + bias_of(tile * per_tile + t)
-            raised = jnp.exp2(scores).astype(BF16)
-            side = jnp.concatenate([value_t * lanes[t], live * lanes[t]], axis=1)
-            part = nn_dot(raised, side)
-            total = part if total is None else total + part
+            raised.append(jnp.exp2(scores).astype(BF16))
+            sides.append(jnp.concatenate([value_t * lanes[t], live * lanes[t]], axis=1))
+        total = nn_dot(jnp.concatenate(raised, axis=1), jnp.concatenate(sides, axis=0))
         pieces.append(total[:, :LANES] / total[:, LANES:])
     return jnp.concatenate(pieces, axis=1)
 
@@ -219,171 +221,228 @@
     return query, key, value, gate
 
 
-def bias_kernel(pair_ref, weight_ref, out_ref, held):
+def regrouped(held, values, parts):
+    items = values.shape[0] // parts
+    for t in range(held.shape[0]):
+        held[t] = values[:, t * LANES : (t + 1) * LANES]
+    return jnp.concatenate([load_strided(held, r, items, parts) for r in range(items)], axis=0)
+
+
+def bias_kernel(parts, pair_ref, weight_ref, out_ref, held, column):
     rows, cols, width = pair_ref.shape
-    normed = layer_normalize(pair_ref[...].astype(F32)).astype(BF16).reshape(rows * cols, width)
-    bias = nt_dot(weight_ref[...], normed)[:ATTN_HEAD_COUNT] * LOG2E
+    normed = layer_normalize(pair_ref[...].astype(F32))
+    ordered = [regrouped(column.at[i], normed[i], parts) for i in range(rows)]
+    normed = jnp.concatenate(ordered, axis=0).astype(BF16)
+    bias = nt_dot(weight_ref[...], normed) * LOG2E
     for i in range(rows):
         store_strided(held, i, rows, bias[:, i * cols : (i + 1) * cols])
     out_ref[...] = joined_tiles(held).astype(BF16)
 
 
-def pair_bias_block(pair_rep, bias_weight):
+def pair_bias_block(pair_rep, bias_weight, parts):
     rows, cols, width = pair_rep.shape
-    weight = jnp.pad(bias_weight.T, ((0, 16 - ATTN_HEAD_COUNT), (0, 0)))
     out = jax.ShapeDtypeStruct((ATTN_HEAD_COUNT * rows, cols), BF16)
     return pl.pallas_call(
-        bias_kernel,
+        functools.partial(bias_kernel, parts),
         out_shape=out,
-        scratch_shapes=[tiled_scratch(*out.shape)],
-        compiler_params=params(32),
+        scratch_shapes=[tiled_scratch(*out.shape), pltpu.VMEM((rows, 1, cols, width), F32)],
+        compiler_params=params(16),
         name="pair_bias",
-    )(pair_rep, weight)
-
-
-def row_project_kernel(x_ref, weight_ref, q_ref, k_ref, v_ref, g_ref):
+    )(pair_rep, bias_weight.T)
+
+
+def row_project_kernel(parts, x_ref, weight_ref, x_out, q_ref, k_ref, v_ref, g_ref, held):
     for s in range(x_ref.shape[0]):
-        normed = layer_normalize(x_ref[s].astype(F32)).astype(BF16)
+        ordered = regrouped(held.at[s], x_ref[s].astype(F32), parts)
+        x_out[s] = ordered.astype(BF16)
+        normed = layer_normalize(ordered).astype(BF16)
         q_ref[s], k_ref[s], v_ref[s], g_ref[s] = project(normed, weight_ref)
 
 
-def row_project(alignment, weight):
+def row_project(alignment, weight, parts):
     seqs, length, width = alignment.shape
     step = 2
     block = pl.BlockSpec((step, length, width), lambda i: (i, 0, 0))
     small = jax.ShapeDtypeStruct(alignment.shape, BF16)
     return pl.pallas_call(
-        row_project_kernel,
+        functools.partial(row_project_kernel, parts),
         grid=(seqs // step,),
         in_specs=[block, full_spec(weight.shape)],
-        out_specs=[block] * 4,
-        out_shape=[small, small, small, jax.ShapeDtypeStruct(alignment.shape, F32)],
-        compiler_params=params(48),
+        out_specs=[block] * 5,
+        out_shape=[small] * 4 + [jax.ShapeDtypeStruct(alignment.shape, F32)],
+        scratch_shapes=[pltpu.VMEM((step, width // LANES, length, LANES), F32)],
+        compiler_params=params(24),
         name="row_project",
     )(alignment, weight)
 
 
-def row_attend_kernel(group, step, me_ref, x_ref, q_ref, k_ref, v_ref, g_ref, live_ref, out_w_ref, *rest):
-    bias_refs, out_ref, bias_all = rest[:group], rest[group], rest[group + 1]
-    heads, length, _ = bias_all.shape
-    outer = bias_refs[0].shape[0]
-
-    @pl.when(pl.program_id(0) == 0)
+def row_attend_kernel(
+    plan, step, half, me_ref, x_ref, q_ref, k_ref, v_ref, g_ref, live_ref, out_w_ref, *rest
+):
+    bias_refs, out_ref, bias_all, held = rest[: len(plan)], rest[-3], rest[-2], rest[-1]
+    heads, rows, length = ATTN_HEAD_COUNT, q_ref.shape[1], k_ref.shape[1]
+    parts, block_rows = out_ref.shape[0], out_ref.shape[1]
+    items = rows // parts
+    at = pl.program_id(0)
+
+    @pl.when(at == 0)
     def _():
-        here = me_ref[0]
-        for k in range(group):
-            for z in range(outer):
-                rows = bias_refs[k].shape[1] // heads
-                owner = here ^ (z * group + k)
-                at = pl.ds(pl.multiple_of(owner * rows, rows), rows)
-                block = bias_refs[k][z].astype(F32).reshape(heads, rows, length)
-                bias_all[:, at, :] = block
+        for bias_ref, offsets in zip(bias_refs, plan):
+            for z, offset in enumerate(offsets):
+                owner = me_ref[0] ^ offset
+                block = bias_ref[z].astype(F32).reshape(heads, -1, length)
+                own = block.shape[1]
+                for h in range(heads):
+                    for t in range(bias_all.shape[0]):
+                        to = pl.ds(h * length + owner, own, stride=parts)
+                        bias_all[t, to, :] = block[h, :, t * LANES : (t + 1) * LANES]
+
+    def bias_of(h):
+        start = h * length + half * rows
+        return jnp.concatenate(
+            [bias_all[t, start : start + rows, :] for t in range(bias_all.shape[0])], axis=1
+        )
 
     lanes = head_lanes(length)
-    results = []
     for s in range(step):
-        heads_out = attend_block(
-            q_ref[s], k_ref[s], v_ref[s], live_ref[s], lanes, lambda h: bias_all[h]
-        )
+        heads_out = attend_block(q_ref[s], k_ref[s], v_ref[s], live_ref[s], lanes, bias_of)
         heads_out = (heads_out * g_ref[s]).astype(BF16)
         total = x_ref[s].astype(F32) + nn_dot(heads_out, out_w_ref[...])
-        parts, rows = out_ref.shape[0], out_ref.shape[1]
-        results.append(total.reshape(parts, 1, rows // step, total.shape[1]))
-    joined = jnp.concatenate(results, axis=1)
-    out_ref[...] = joined.reshape(out_ref.shape).astype(BF16)
-
-
-def row_attend(me, alignment, projected, live, out_weight, bias_parts, dap_count):
-    seqs, length, width = alignment.shape
-    rows = length // dap_count
+        for r in range(items):
+            first = (at * step + s) * items + r
+            store_strided(held, first, block_rows, total[r * parts : (r + 1) * parts])
+
+    @pl.when(at == pl.num_programs(0) - 1)
+    def _():
+        out_ref[...] = joined_tiles(held).reshape(out_ref.shape).astype(BF16)
+
+
+def row_attend(me, projected, live, out_weight, bias_parts, plan, dap_count, half, halves):
+    x_rows, query, key, value, gate = projected
+    seqs, length, width = x_rows.shape
+    rows = length // halves
     step = 2
     block = pl.BlockSpec((step, length, width), lambda i: (i, 0, 0))
+    part = pl.BlockSpec((step, rows, width), lambda i: (i, half, 0))
+    out = (dap_count, seqs * rows // dap_count, width)
     return pl.pallas_call(
-        functools.partial(row_attend_kernel, len(bias_parts), step),
+        functools.partial(row_attend_kernel, plan, step, half),
         grid=(seqs // step,),
-        in_specs=[pl.BlockSpec(memory_space=pltpu.SMEM)]
-        + [block] * 5
+        in_specs=[pl.BlockSpec(memory_space=pltpu.SMEM), part, part, block, block, part]
         + [pl.BlockSpec((step, length, LANES), lambda i: (i, 0, 0)), full_spec(out_weight.shape)]
         + [full_spec(b.shape) for b in bias_parts],
-        out_specs=pl.BlockSpec((dap_count, step * rows, width), lambda i: (0, i, 0)),
-        out_shape=jax.ShapeDtypeStruct((dap_count, seqs * rows, width), BF16),
-        scratch_shapes=[pltpu.VMEM((ATTN_HEAD_COUNT, length, length), F32)],
-        compiler_params=params(56),
+        out_specs=full_spec(out),
+        out_shape=jax.ShapeDtypeStruct(out, BF16),
+        scratch_shapes=[
+            tiled_scratch(ATTN_HEAD_COUNT * length, length),
+            tiled_scratch(seqs * rows, width),
+        ],
+        compiler_params=params(28),
         name="row_attend",
-    )(me, alignment, *projected, live, out_weight, *bias_parts)
+    )(me, x_rows, query, key, value, gate, live, out_weight, *bias_parts)
 
 
 def column_kernel(
-    items, x_ref, live_ref, mask_ref, weight_ref, out_w_ref, factor_ref,
-    out_ref, left_ref, right_ref, held, right_held,
+    first, items, each, x_ref, live_ref, mask_ref, weight_ref, out_w_ref, factor_ref, *rest
 ):
+    before, rest = rest[:-7], rest[-7:]
+    out_ref, left_ref, right_ref, x_held, held, left_held, right_held = rest
     step = pl.program_id(0)
-    total_rows = held.shape[1]
-    length = total_rows // items
+    length = out_ref.shape[0]
+    here = x_held.shape[1] // length
 
     @pl.when(step == 0)
     def _():
         for t in range(held.shape[0]):
-            part = x_ref[:, :, t * LANES : (t + 1) * LANES].astype(F32)
-            held[t] = part.reshape(total_rows, LANES)
+            cut = slice(t * LANES, (t + 1) * LANES)
+            x_held[t] = x_ref[:, :, cut].astype(F32).reshape(x_held.shape[1:])
+            if before:
+                held[t] = before[0][:, :, cut].astype(F32).reshape(held.shape[1:])
+                right_held[t] = before[2][:, cut].astype(F32)
+        if before:
+            left_held[...] = before[1][...]
 
     lanes = head_lanes(length)
-    current = load_strided(held, step, items, length)
-    normed = layer_normalize(current).astype(BF16)
-    query, key, value, gate = project(normed, weight_ref)
-    heads_out = attend_block(query, key, value, live_ref[0], lanes, None)
-    heads_out = (heads_out * gate).astype(BF16)
-    updated = (current + nn_dot(heads_out, out_w_ref[...])).astype(BF16).astype(F32)
-    store_strided(held, step, items, updated)
-    normed = layer_normalize(updated).astype(BF16)
-    factors = nt_dot(factor_ref[...], normed) * mask_ref[pl.ds(step, 1), :]
-    left_at = pl.ds(pl.multiple_of(step * FACTOR_CHANNELS, FACTOR_CHANNELS), FACTOR_CHANNELS)
-    left_ref[left_at, :] = factors[:FACTOR_CHANNELS].astype(BF16)
-    store_strided(right_held, step, items, factors[FACTOR_CHANNELS:])
-
-    @pl.when(step == items - 1)
+    for n in range(each):
+        inner = step * each + n
+        item = inner + first
+        current = load_strided(x_held, inner, here, length)
+        normed = layer_normalize(current).astype(BF16)
+        query, key, value, gate = project(normed, weight_ref)
+        heads_out = attend_block(query, key, value, live_ref[n], lanes, None)
+        heads_out = (heads_out * gate).astype(BF16)
+        updated = (current + nn_dot(heads_out, out_w_ref[...])).astype(BF16).astype(F32)
+        store_strided(held, item, items, updated)
+        normed = layer_normalize(updated).astype(BF16)
+        factors = nt_dot(factor_ref[...], normed) * mask_ref[pl.ds(item, 1), :]
+        left_at = pl.ds(pl.multiple_of(item * FACTOR_CHANNELS, FACTOR_CHANNELS), FACTOR_CHANNELS)
+        left_held[left_at, :] = factors[:FACTOR_CHANNELS].astype(BF16)
+        store_strided(right_held, item, items, factors[FACTOR_CHANNELS:])
+
+    @pl.when(step == pl.num_programs(0) - 1)
     def _():
         for t in range(held.shape[0]):
             part = held[t].reshape(out_ref.shape[:2] + (LANES,))
             out_ref[:, :, t * LANES : (t + 1) * LANES] = part.astype(BF16)
         right_ref[...] = joined_tiles(right_held).astype(BF16)
-
-
-def column_attend(moved, live, mask_rows, weight, out_weight, factor_weight, items):
+        left_ref[...] = left_held[...]
+
+
+def column_attend(moved, live, mask_rows, weight, out_weight, factor_t, half, halves, before):
     width = moved.shape[2]
-    total_rows = moved.shape[0] * moved.shape[1]
-    length = total_rows // items
-    factor_t = factor_weight.T
-    side = jax.ShapeDtypeStruct((items * FACTOR_CHANNELS, length), BF16)
-    out = jax.ShapeDtypeStruct((length, items, width), BF16)
+    items = mask_rows.shape[0]
+    here = items // halves
+    rows = moved.shape[0] * moved.shape[1]
+    length = rows // here
+    each = 2
+    start = half * here
+    side = (items * FACTOR_CHANNELS, length)
+    outs = [jax.ShapeDtypeStruct((length, items, width), BF16)]
+    outs += [jax.ShapeDtypeStruct(side, BF16)] * 2
     return pl.pallas_call(
-        functools.partial(column_kernel, items),
-        grid=(items,),
+        functools.partial(column_kernel, start, items, each),
+        grid=(here // each,),
         in_specs=[
             full_spec(moved.shape),
-            pl.BlockSpec((1, length, LANES), lambda i: (i, 0, 0)),
+            pl.BlockSpec((each, length, LANES), lambda i: (i + start // each, 0, 0)),
             full_spec(mask_rows.shape),
             full_spec(weight.shape),
             full_spec(out_weight.shape),
             full_spec(factor_t.shape),
+        ]
+        + [full_spec(b.shape) for b in before],
+        out_specs=[full_spec(o.shape) for o in outs],
+        out_shape=outs,
+        scratch_shapes=[
+            tiled_scratch(rows, width),
+            tiled_scratch(length * items, width),
+            pltpu.VMEM(side, BF16),
+            tiled_scratch(*side),
         ],
-        out_specs=[full_spec(out.shape), full_spec(side.shape), full_spec(side.shape)],
-        out_shape=[out, side, side],
-        scratch_shapes=[tiled_scratch(total_rows, width), tiled_scratch(*side.shape)],
-        compiler_params=params(56),
+        compiler_params=params(28),
         name="column_attend",
-    )(moved, live, mask_rows, weight, out_weight, factor_t)
+    )(moved, live, mask_rows, weight, out_weight, factor_t, *before)
 
 
 def outer_kernel(group, outer, items, *refs):
     lefts, rights = refs[:group], refs[group : group + outer]
     weight_ref = refs[group + outer]
-    outs = refs[group + outer + 1 : 2 * group + outer + 1]
-    held = refs[-1]
+    outs = refs[group + outer + 1 : -3]
+    weight_rows, weight, held = refs[-3:]
     feat = FACTOR_CHANNELS
     quad = LANES // feat
     tiles = items * feat // LANES
     cols = outer * items
+    width = weight_ref.shape[1]
+
+    weight_rows[...] = weight_ref[...].astype(F32)
+    weight[...] = jnp.zeros_like(weight)
+    for e in range(feat):
+        block = weight_rows[pl.ds(e, feat, stride=feat), :].astype(BF16)
+        for i in range(quad):
+            start = e * LANES + i * feat
+            weight[start : start + feat, i * width : (i + 1) * width] = block
+
     right = jnp.concatenate([r[...] for r in rights], axis=0)
     for k in range(group):
         sums = nt_dot(right, lefts[k][...])
@@ -393,8 +452,7 @@
             at = slice((k * tiles + t) * cols, (k * tiles + t + 1) * cols)
             for e in range(feat):
                 held[at, e * LANES : (e + 1) * LANES] = sums[e, :, t * LANES : (t + 1) * LANES]
-    update = nn_dot(held[...], weight_ref[...])
-    width = update.shape[1] // quad
+    update = nn_dot(held[...], weight[...])
     for k in range(group):
         for t in range(tiles):
             rows = update[(k * tiles + t) * cols : (k * tiles + t + 1) * cols]
@@ -405,54 +463,58 @@
 def outer_product(lefts, rights, weight, items):
     group, outer = len(lefts), len(rights)
     cols = outer * items
-    width = weight.shape[1] * FACTOR_CHANNELS // LANES
-    out = jax.ShapeDtypeStruct((items, cols, width), BF16)
     tiles = items * FACTOR_CHANNELS // LANES
+    depth = FACTOR_CHANNELS * LANES
+    width = weight.shape[1]
     return pl.pallas_call(
         functools.partial(outer_kernel, group, outer, items),
-        out_shape=[out] * group,
-        scratch_shapes=[pltpu.VMEM((group * tiles * cols, weight.shape[0]), BF16)],
-        compiler_params=params(56),
+        out_shape=[jax.ShapeDtypeStruct((items, cols, width), BF16)] * group,
+        scratch_shapes=[
+            pltpu.VMEM(weight.shape, F32),
+            pltpu.VMEM((depth, LANES // FACTOR_CHANNELS * width), BF16),
+            pltpu.VMEM((group * tiles * cols, depth), BF16),
+        ],
+        compiler_params=params(28),
         name="outer_product",
     )(*lefts, *rights, weight)
 
 
-def finish_kernel(group, outer, items, me_ref, pair_ref, scale_ref, *refs):
-    parts, out_ref = refs[:group], refs[group]
+def finish_kernel(offsets, line, me_ref, pair_ref, scale_ref, *refs):
+    parts, out_ref = refs[:-1], refs[-1]
     here = me_ref[0]
+    items, cols, width = parts[0].shape
+    outer = cols // items
     odd = (here & 1) == 1
-    for pairing in range(group // 2):
+    for k, offset in enumerate(offsets):
         for i in range(items):
-            first = parts[2 * pairing][i].astype(F32)
-            second = parts[2 * pairing + 1][i].astype(F32)
-            low = jnp.where(odd, second, first)
-            high = jnp.where(odd, first, second)
-            for z in range(outer):
-                owner = here ^ (z * group + 2 * pairing)
+            both = parts[k][i].astype(F32).reshape(outer // 2, 2, items, width)
+            low, high = both[:, 0:1], both[:, 1:2]
+            both = jnp.concatenate([jnp.where(odd, high, low), jnp.where(odd, low, high)], axis=1)
+            both = both.reshape(outer // 2, 2 * items, width)
+            for z in range(outer // 2):
+                owner = here ^ (offset | line[z])
                 start = pl.multiple_of((owner >> 1) * (2 * items), 2 * items)
                 at = pl.ds(start, 2 * items)
-                cut = slice(z * items, (z + 1) * items)
-                update = jnp.concatenate([low[cut], high[cut]], axis=0)
-                update = update * scale_ref[at, i : i + 1]
+                update = both[z] * scale_ref[at, i : i + 1]
                 out_ref[i, at, :] = (pair_ref[i, at, :].astype(F32) + update).astype(BF16)
 
 
-def finish(me, pair_rep, scale, parts, outer):
-    items = pair_rep.shape[0]
+def finish(me, pair_rep, scale, parts, offsets, line):
+    vmem = pl.BlockSpec(memory_space=pltpu.VMEM)
     return pl.pallas_call(
-        functools.partial(finish_kernel, len(parts), outer, items),
-        in_specs=[pl.BlockSpec(memory_space=pltpu.SMEM), full_spec(pair_rep.shape), full_spec(scale.shape)]
-        + [full_spec(p.shape) for p in parts],
-        out_specs=full_spec(pair_rep.shape),
+        functools.partial(finish_kernel, offsets, line),
+        in_specs=[pl.BlockSpec(memory_space=pltpu.SMEM)] + [vmem] * (2 + len(parts)),
+        out_specs=vmem,
         out_shape=jax.ShapeDtypeStruct(pair_rep.shape, BF16),
-        compiler_params=params(48),
+        compiler_params=params(16),
         name="finish",
     )(me, pair_rep, scale, *parts)
 
 
 def exchange(block, count, offset):
-    pairs = [(i, i ^ offset) for i in range(count)]
-    return lax.ppermute(block, "dap", pairs)
+    if offset == 0:
+        return block
+    return lax.ppermute(block, "dap", [(i, i ^ offset) for i in range(count)])
 
 
 def per_device_fast(
@@ -468,63 +530,72 @@
     outer_factor_weight,
     outer_out,
 ):
-    dap_count = lax.axis_size("dap")
-    group = inner_size(dap_count)
-    outer = dap_count // group
+    count = lax.axis_size("dap")
     dap_index = lax.axis_index("dap")
     me = jnp.reshape(dap_index, (1,)).astype(jnp.int32)
+    plane, line = offset_groups(count)
     seq_dev = alignment.shape[0]
     items = pair_rep.shape[0]
-    width = alignment.shape[2]
     total_seqs, total_res = align_mask.shape
-
-    bias = pair_bias_block(pair_rep, bias_weight)
-    column = [bias] + [exchange(bias, dap_count, z * group) for z in range(1, outer)]
-    projected = row_project(alignment, row_proj_weight)
-    column = jnp.stack(column)
-    bias_parts = [column] + [exchange(column, dap_count, k) for k in range(1, group)]
-
-    mask = align_mask.astype(F32)
+    halves = 2
+
+    bias = pair_bias_block(pair_rep, bias_weight, count)
+    bias = jnp.stack([exchange(bias, count, z) for z in line])
+    bias_parts = [exchange(bias, count, k) for k in plane]
+    plan = [[k | z for z in line] for k in plane]
+    bias_parts += [exchange(part, count, 1) for part in bias_parts]
+    plan += [[offset | 1 for offset in offsets] for offsets in plan]
+    projected = row_project(alignment, row_proj_weight, count)
+
     own_seqs = lax.dynamic_slice_in_dim(align_mask, dap_index * seq_dev, seq_dev, 0)
+    own_seqs = own_seqs.astype(BF16).reshape(seq_dev, count, items).swapaxes(1, 2)
     own_res = lax.dynamic_slice_in_dim(align_mask, dap_index * items, items, 1)
-    row_live = jnp.broadcast_to(own_seqs.astype(BF16)[:, :, None], (seq_dev, total_res, LANES))
+    row_live = own_seqs.reshape(seq_dev, total_res)[:, :, None]
+    row_live = jnp.broadcast_to(row_live, (seq_dev, total_res, LANES))
     col_live = jnp.broadcast_to(own_res.T.astype(BF16)[:, :, None], (items, total_seqs, LANES))
     counts = jnp.einsum(
-        "si,sj->ji", own_res.astype(BF16), mask.astype(BF16), preferred_element_type=F32
+        "si,sj->ji", own_res.astype(BF16), align_mask.astype(BF16), preferred_element_type=F32
     )
     res_float = residue_mask.astype(F32)
     live_rows = lax.dynamic_slice_in_dim(res_float, dap_index * items, items, 0)
     scale = live_rows[None, :] * res_float[:, None] / (counts + count_eps)
-
-    quad = LANES // FACTOR_CHANNELS
-    weight = outer_out.reshape(FACTOR_CHANNELS, FACTOR_CHANNELS, -1).swapaxes(0, 1)
-    spread = jnp.eye(quad, dtype=BF16)[None, :, None, :, None] * weight[:, None, :, None, :]
-    spread = spread.reshape(FACTOR_CHANNELS * LANES, quad * weight.shape[2])
-
-    row_out = row_attend(me, alignment, projected, row_live, row_out_weight, bias_parts, dap_count)
-    moved = lax.all_to_all(row_out, "dap", split_axis=0, concat_axis=0, tiled=True)
-    updated, left, right = column_attend(
-        moved,
-        col_live,
-        own_res.T.astype(F32),
-        column_proj_weight,
-        column_out_weight,
-        outer_factor_weight,
-        items,
-    )
-    rights = [right] + [exchange(right, dap_count, z * group) for z in range(1, outer)]
-    lefts = [left] + [exchange(left, dap_count, k) for k in range(1, group)]
-    parts = outer_product(lefts, rights, spread, items)
-    parts = [parts[0]] + [exchange(parts[k], dap_count, k) for k in range(1, group)]
-    pair_out = finish(me, pair_rep, scale, parts, outer)
+    mask_rows = own_res.T.astype(F32)
+
+    moved = []
+    for half in range(halves):
+        rows = row_attend(
+            me, projected, row_live, row_out_weight, bias_parts, plan, count, half, halves
+        )
+        moved.append(lax.all_to_all(rows, "dap", split_axis=0, concat_axis=0, tiled=True))
+    done = ()
+    for half in range(halves):
+        done = column_attend(
+            moved[half],
+            col_live,
+            mask_rows,
+            column_proj_weight,
+            column_out_weight,
+            outer_factor_weight.T,
+            half,
+            halves,
+            done,
+        )
+    updated, left, right = done
+    rights = [exchange(right, count, z) for z in line]
+    rights = [part for own in rights for part in (own, exchange(own, count, 1))]
+    lefts = [exchange(left, count, k) for k in plane]
+    parts = outer_product(lefts, rights, outer_out, items)
+    parts = [exchange(part, count, k) for part, k in zip(parts, plane)]
+    pair_out = finish(me, pair_rep, scale, parts, plane, line)
     return updated, pair_out
 
 
-def inner_size(count):
-    size = 1
-    while 2 * size * size < count * 2 and count % (2 * size) == 0:
-        size *= 2
-    return size
+def offset_groups(count):
+    bits = count.bit_length() - 1
+    near = (bits - 1) // 2
+    plane = [k << 1 for k in range(1 << near)]
+    line = [z << (1 + near) for z in range(1 << (bits - 1 - near))]
+    return plane, line
 
 
 def solution(mesh):

time: 135 us -> 130 us (0.963)
  waiting for transfers between devices: 44.6 us -> 27.9 us
  local copies, waits for them, and re-layouts: 13.8 us -> 29.1 us
  starting transfers between devices: 32.9 us -> 30.6 us
  other arithmetic: 2.99 us -> 0.73 us
    all_to_all x1 -> x2, waiting for transfers between devices: 25.2 us -> 4.68 us  [per_device_fast(): lax.all_to_all(rows, 'dap', split_axis=0, concat_axis=0, tiled=True)]
    unnamed x62 -> x81, local copies, waits for them, and re-layouts: 10.6 us -> 27 us
    ppermute x27 -> x23, starting transfers between devices: 30 us -> 21.3 us  [exchange(): return lax.ppermute(block, 'dap', [(i, i ^ offset) for i in range(count)])]
    all_to_all x1 -> x2, starting transfers between devices: 2.97 us -> 9.33 us  [per_device_fast(): lax.all_to_all(rows, 'dap', split_axis=0, concat_axis=0, tiled=True)]
    ppermute x27 -> x23, waiting for transfers between devices: 19.3 us -> 23.2 us  [exchange(): return lax.ppermute(block, 'dap', [(i, i ^ offset) for i in range(count)])]
    pallas_call x1, Pallas kernels: 6.92 us -> 3.69 us  [outer_product(): pl.pallas_call(functools.partial(outer_kernel, group, outer, items), out_...]
    pallas_call x5 -> x7, Pallas kernels: 32.5 us -> 35.6 us  [the longest x2 16.9 us: row_attend(): pl.pallas_call(functools.partial(row_attend_kernel, plan, step, half), gr...]
    mul x1 -> x0, other arithmetic: 1.65 us -> none  [per_device_fast(): jnp.eye(quad, dtype=BF16)[None, :, None, :, None]]
  transfers between devices with their start and end apart: 28 -> 25, of which waited for: 11 -> 12; matrix products, arithmetic and copies ran while one was open for 5% -> 2% of each run, Pallas kernels for 3% -> 14%
where the time goes in v3:
time: 130 us; the launch traced here: 129 us
  Pallas kernels  39.3 us (30%)
  starting transfers between devices  30.6 us (24%)
  local copies, waits for them, and re-layouts  29.1 us (22%)
  waiting for transfers between devices  27.9 us (21%)
    unnamed x81, local copies, waits for them, and re-layouts  27 us
    ppermute x23, waiting for transfers between devices, exchange(): return lax.ppermute(block, 'dap', [(i, i ^ offset) for i in range(count)])  23.2 us
    ppermute x23, starting transfers between devices, exchange(): return lax.ppermute(block, 'dap', [(i, i ^ offset) for i in range(count)])  21.3 us
    pallas_call x2, Pallas kernels, row_attend(): pl.pallas_call(functools.partial(row_attend_kernel, plan, step, half), gr...  16.9 us
    pallas_call x2, Pallas kernels, column_attend(): pl.pallas_call(functools.partial(column_kernel, start, items, each), grid...  13.6 us
    all_to_all x2, starting transfers between devices, per_device_fast(): lax.all_to_all(rows, 'dap', split_axis=0, concat_axis=0, tiled=True)  9.33 us
    all_to_all x2, waiting for transfers between devices, per_device_fast(): lax.all_to_all(rows, 'dap', split_axis=0, concat_axis=0, tiled=True)  4.68 us
    pallas_call x1, Pallas kernels, outer_product(): pl.pallas_call(functools.partial(outer_kernel, group, outer, items), out_...  3.69 us
  transfers between devices with their start and end apart: 25, of which 12 were waited for; matrix products, arithmetic and copies ran while one was open for 2% of the time, Pallas kernels for 14%

profile of v3, /device:TPU:0, one launch (start us, length us, event | category | flops | bytes accessed | tf_op | source)
XLA Modules:
  0.0 128.8 jit_solution(6485130083288228213)
XLA Ops:
  3.2 5.1 %collective-permute-start.2 = (bf16[64,256]{1,0:T(8,128)(2,1)S(1)}, bf16[64,256]{1,0:T(8,128)(2,1)S(1)}, u32[]{:S(2)}, u32[]{:S(2)}) collective-permute-start(bf16[64,256]{1,0:T(8,128)(2,1)S(1)} %pair_bias.1), channel_id=1, source_target_pairs={{0,24},{1,25},{2,26},{3,27},{4,28},{5,29},{6,30},{7,31},{8,16},{9,... | collective-permute-start | bytes 98312 | tf_op jit(solution)/shard_map/ppermute | solution.py:517
  8.9 1.3 collective-permute-done.2
  10.2 2.9 %collective-permute-done.1 = bf16[64,256]{1,0:T(8,128)(2,1)S(1)} collective-permute-done((bf16[64,256]{1,0:T(8,128)(2,1)S(1)}, bf16[64,256]{1,0:T(8,128)(2,1)S(1)}, u32[]{:S(2)}, u32[]{:S(2)}) %collective-permute-start.1) | collective-permute-done | bytes 32800 | tf_op jit(solution)/shard_map/ppermute | solution.py:517
  13.1 1.6 %collective-permute-start.3 = (bf16[4,64,256]{2,1,0:T(8,128)(2,1)S(1)}, bf16[4,64,256]{2,1,0:T(8,128)(2,1)S(1)}, u32[]{:S(2)}, u32[]{:S(2)}) collective-permute-start(bf16[4,64,256]{2,1,0:T(8,128)(2,1)S(1)} %pad_maximum_fusion.rest_0_), channel_id=1, source_target_pairs={{0,2},{1,3},{2,0},{3,1},{4,6},{5,7},{6,4},{7,5},{8,10},{9,11},{10,... | collective-permute-start | bytes 393224 | tf_op jit(solution)/shard_map/ppermute | solution.py:517
  14.7 1.5 %collective-permute-start.4 = (bf16[4,64,256]{2,1,0:T(8,128)(2,1)S(1)}, bf16[4,64,256]{2,1,0:T(8,128)(2,1)S(1)}, u32[]{:S(2)}, u32[]{:S(2)}) collective-permute-start(bf16[4,64,256]{2,1,0:T(8,128)(2,1)S(1)} %pad_maximum_fusion.rest_0_), channel_id=1, source_target_pairs={{0,4},{1,5},{2,6},{3,7},{4,0},{5,1},{6,2},{7,3},{8,12},{9,13},{10,... | collective-permute-start | bytes 393224 | tf_op jit(solution)/shard_map/ppermute | solution.py:517
  16.7 2.7 %collective-permute-done.3.rest_1_ = bf16[4,64,256]{2,1,0:T(8,128)(2,1)S(1)} collective-permute-done((bf16[4,64,256]{2,1,0:T(8,128)(2,1)S(1)}, bf16[4,64,256]{2,1,0:T(8,128)(2,1)S(1)}, u32[]{:S(2)}, u32[]{:S(2)}) %collective-permute-start.3) | collective-permute-done | bytes 131104 | tf_op jit(solution)/shard_map/ppermute | solution.py:517
  19.4 1.2 collective-permute-done.4.rest_2_
  20.6 1.4 %collective-permute-done.5.rest_3_ = bf16[4,64,256]{2,1,0:T(8,128)(2,1)S(1)} collective-permute-done((bf16[4,64,256]{2,1,0:T(8,128)(2,1)S(1)}, bf16[4,64,256]{2,1,0:T(8,128)(2,1)S(1)}, u32[]{:S(2)}, u32[]{:S(2)}) %collective-permute-start.5) | collective-permute-done | bytes 131104 | tf_op jit(solution)/shard_map/ppermute | solution.py:517
  23.1 1.2 copy-done.11
  25.4 3.0 %row_project.1 = (bf16[8,256,256]{2,1,0:T(8,128)(2,1)S(1)}, bf16[8,256,256]{2,1,0:T(8,128)(2,1)S(1)}, bf16[8,256,256]{2,1,0:T(8,128)(2,1)S(1)}, bf16[8,256,256]{2,1,0:T(8,128)(2,1)S(1)}, f32[8,256,256]{2,1,0:T(8,128)S(1)}) custom-call(bf16[8,256,256]{2,1,0:T(8,128)(2,1)S(1)} %copy-done.11, bf16[4,256,256]{2,1,0:T(8,128)(2,1)S(1)} %copy-done.27), custom_call_target="tpu_custom_call" | custom-call | tf_op jit(solution)/shard_map/row_project/pallas_call | solution.py:267
  32.0 8.4 %row_attend.3 = bf16[32,32,256]{2,1,0:T(8,128)(2,1)} custom-call(s32[1]{0:T(128)} %bitcast.me_ref, bf16[8,256,256]{2,1,0:T(8,128)(2,1)S(1)} %get-tuple-element.17.x_ref, bf16[8,256,256]{2,1,0:T(8,128)(2,1)S(1)} %get-tuple-element.18.q_ref, bf16[8,256,256]{2,1,0:T(8,128)(2,1)S(1)} %get-tuple-element.19.k_ref, ...), custom_call_target="tpu_custom_call" | custom-call | tf_op jit(solution)/shard_map/row_attend/pallas_call | solution.py:328
  44.4 3.3 %all-to-all-start.1 = ((bf16[32,32,256]{2,1,0:T(8,128)(2,1)}), bf16[32,32,256]{2,1,0:T(8,128)(2,1)S(1)}, u32[]{:S(2)}, u32[]{:S(2)}) async-start(bf16[32,32,256]{2,1,0:T(8,128)(2,1)} %row_attend.3), calls=%async_computation.1 | async-start | bytes 1048576 | tf_op jit(solution)/shard_map/all_to_all | solution.py:569
  47.7 1.2 copy-done.1
  49.0 1.2 copy-done.3
  50.2 1.2 copy-done.5
  51.4 1.2 copy-done.7
  58.1 8.4 %row_attend.2 = bf16[32,32,256]{2,1,0:T(8,128)(2,1)} custom-call(s32[1]{0:T(128)} %bitcast.me_ref, bf16[8,256,256]{2,1,0:T(8,128)(2,1)S(1)} %copy-done.1, bf16[8,256,256]{2,1,0:T(8,128)(2,1)S(1)} %copy-done.3, bf16[8,256,256]{2,1,0:T(8,128)(2,1)S(1)} %copy-done.5, bf16[8,256,256]{2,1,0:T(8,128)(2,1)S(1)} %copy-done.7, ...), custom_call_target="tpu_custom_call" | custom-call | tf_op jit(solution)/shard_map/row_attend/pallas_call | solution.py:328
  66.5 6.0 %all-to-all-start = ((bf16[32,32,256]{2,1,0:T(8,128)(2,1)}), bf16[32,32,256]{2,1,0:T(8,128)(2,1)S(1)}, u32[]{:S(2)}, u32[]{:S(2)}) async-start(bf16[32,32,256]{2,1,0:T(8,128)(2,1)} %row_attend.2), calls=%async_computation | async-start | bytes 1048576 | tf_op jit(solution)/shard_map/all_to_all | solution.py:569
  75.6 6.3 %column_attend.2 = (bf16[256,8,256]{2,1,0:T(8,128)(2,1)S(1)}, bf16[256,256]{1,0:T(8,128)(2,1)S(1)}, bf16[256,256]{1,0:T(8,128)(2,1)S(1)}) custom-call(bf16[32,32,256]{2,1,0:T(8,128)(2,1)S(1)} %all-to-all-done.1.x_ref, bf16[8,256,128]{2,1,0:T(8,128)(2,1)S(1)} %broadcast_in_dim.8.live_ref, f32[8,256]{1,0:T(8,128)S(1)} %get-tuple-element.32.mask_ref, ...), custom_call_target="tpu_custom_call" | custom-call | tf_op jit(solution)/shard_map/column_attend/pallas_call | solution.py:402
  83.2 4.7 %all-to-all-done.x_ref = bf16[32,32,256]{2,1,0:T(8,128)(2,1)S(1)} async-done(((bf16[32,32,256]{2,1,0:T(8,128)(2,1)}), bf16[32,32,256]{2,1,0:T(8,128)(2,1)S(1)}, u32[]{:S(2)}, u32[]{:S(2)}) %all-to-all-start) | async-done | bytes 524320 | tf_op jit(solution)/shard_map/all_to_all | solution.py:569
  90.5 7.4 %column_attend.3 = (bf16[256,8,256]{2,1,0:T(8,128)(2,1)}, bf16[256,256]{1,0:T(8,128)(2,1)S(1)}, bf16[256,256]{1,0:T(8,128)(2,1)S(1)}) custom-call(bf16[32,32,256]{2,1,0:T(8,128)(2,1)S(1)} %all-to-all-done.x_ref, bf16[8,256,128]{2,1,0:T(8,128)(2,1)S(1)} %broadcast_in_dim.8.live_ref, f32[8,256]{1,0:T(8,128)S(1)} %get-tuple-element.32.mask_ref, ...), custom_call_target="tpu_custom_call" | custom-call | tf_op jit(solution)/shard_map/column_attend/pallas_call | solution.py:402
  98.8 1.5 %collective-permute-start.11 = (bf16[256,256]{1,0:T(8,128)(2,1)S(1)}, bf16[256,256]{1,0:T(8,128)(2,1)S(1)}, u32[]{:S(2)}, u32[]{:S(2)}) collective-permute-start(bf16[256,256]{1,0:T(8,128)(2,1)S(1)} %get-tuple-element.26.refs_0_), channel_id=1, source_target_pairs={{0,4},{1,5},{2,6},{3,7},{4,0},{5,1},{6,2},{7,3},{8,12},{9,13},{10,... | collective-permute-start | bytes 393224 | tf_op jit(solution)/shard_map/ppermute | solution.py:517
  100.5 1.8 %collective-permute-start.16 = (bf16[256,256]{1,0:T(8,128)(2,1)S(1)}, bf16[256,256]{1,0:T(8,128)(2,1)S(1)}, u32[]{:S(2)}, u32[]{:S(2)}) collective-permute-start(bf16[256,256]{1,0:T(8,128)(2,1)S(1)} %get-tuple-element.27.refs_4_), channel_id=1, source_target_pairs={{0,16},{1,17},{2,18},{3,19},{4,20},{5,21},{6,22},{7,23},{8,24},{9,... | collective-permute-start | bytes 393224 | tf_op jit(solution)/shard_map/ppermute | solution.py:517
  102.2 2.4 %collective-permute-start.18 = (bf16[256,256]{1,0:T(8,128)(2,1)S(1)}, bf16[256,256]{1,0:T(8,128)(2,1)S(1)}, u32[]{:S(2)}, u32[]{:S(2)}) collective-permute-start(bf16[256,256]{1,0:T(8,128)(2,1)S(1)} %get-tuple-element.27.refs_4_), channel_id=1, source_target_pairs={{0,24},{1,25},{2,26},{3,27},{4,28},{5,29},{6,30},{7,31},{8,16},{9,... | collective-permute-start | bytes 393224 | tf_op jit(solution)/shard_map/ppermute | solution.py:517
  104.6 1.1 collective-permute-start.12
  106.5 6.2 %collective-permute-done.16.refs_8_ = bf16[256,256]{1,0:T(8,128)(2,1)S(1)} collective-permute-done((bf16[256,256]{1,0:T(8,128)(2,1)S(1)}, bf16[256,256]{1,0:T(8,128)(2,1)S(1)}, u32[]{:S(2)}, u32[]{:S(2)}) %collective-permute-start.16) | collective-permute-done | bytes 131104 | tf_op jit(solution)/shard_map/ppermute | solution.py:517
  114.3 3.7 %outer_product.1 = (bf16[8,64,128]{2,1,0:T(8,128)(2,1)S(1)}, bf16[8,64,128]{2,1,0:T(8,128)(2,1)S(1)}, bf16[8,64,128]{2,1,0:T(8,128)(2,1)S(1)}, bf16[8,64,128]{2,1,0:T(8,128)(2,1)S(1)}) custom-call(bf16[256,256]{1,0:T(8,128)(2,1)S(1)} %get-tuple-element.26.refs_0_, bf16[256,256]{1,0:T(8,128)(2,1)S(1)} %collective-permute-done.10.refs_1_, ...), custom_call_target="tpu_custom_call" | custom-call | tf_op jit(solution)/shard_map/outer_product/pallas_call | solution.py:469
  118.0 1.3 %collective-permute-start.20 = (bf16[8,64,128]{2,1,0:T(8,128)(2,1)S(1)}, bf16[8,64,128]{2,1,0:T(8,128)(2,1)S(1)}, u32[]{:S(2)}, u32[]{:S(2)}) collective-permute-start(bf16[8,64,128]{2,1,0:T(8,128)(2,1)S(1)} %get-tuple-element.29), channel_id=1, source_target_pairs={{0,2},{1,3},{2,0},{3,1},{4,6},{5,7},{6,4},{7,5},{8,10},{9,11},{10,... | collective-permute-start | bytes 393224 | tf_op jit(solution)/shard_map/ppermute | solution.py:517
  120.3 1.2 collective-permute-start.22
  121.7 2.6 %collective-permute-done.20.refs_1_ = bf16[8,64,128]{2,1,0:T(8,128)(2,1)S(1)} collective-permute-done((bf16[8,64,128]{2,1,0:T(8,128)(2,1)S(1)}, bf16[8,64,128]{2,1,0:T(8,128)(2,1)S(1)}, u32[]{:S(2)}, u32[]{:S(2)}) %collective-permute-start.20) | collective-permute-done | bytes 131104 | tf_op jit(solution)/shard_map/ppermute | solution.py:517
  124.3 3.2 %collective-permute-done.21.refs_2_ = bf16[8,64,128]{2,1,0:T(8,128)(2,1)S(1)} collective-permute-done((bf16[8,64,128]{2,1,0:T(8,128)(2,1)S(1)}, bf16[8,64,128]{2,1,0:T(8,128)(2,1)S(1)}, u32[]{:S(2)}, u32[]{:S(2)}) %collective-permute-start.21) | collective-permute-done | bytes 131104 | tf_op jit(solution)/shard_map/ppermute | solution.py:517
  127.5 1.3 finish.1
  (119 shorter events, 30.3 us)
Async XLA Ops:
  2.4 27.8 %copy-start.12 = (bf16[256,256]{1,0:T(8,128)(2,1)S(1)}, bf16[256,256]{1,0:T(8,128)(2,1)}, u32[]{:S(2)}) copy-start(bf16[256,256]{1,0:T(8,128)(2,1)} %out_w_ref.5) | copy-start | bytes 393220
  3.2 7.0 %collective-permute-start.2 = (bf16[64,256]{1,0:T(8,128)(2,1)S(1)}, bf16[64,256]{1,0:T(8,128)(2,1)S(1)}, u32[]{:S(2)}, u32[]{:S(2)}) collective-permute-start(bf16[64,256]{1,0:T(8,128)(2,1)S(1)} %pair_bias.1), channel_id=1, source_target_pairs={{0,24},{1,25},{2,26},{3,27},{4,28},{5,29},{6,30},{7,31},{8,16},{9,... | collective-permute-start | bytes 98312 | tf_op jit(solution)/shard_map/ppermute | solution.py:517
  8.3 4.8 %collective-permute-start.1 = (bf16[64,256]{1,0:T(8,128)(2,1)S(1)}, bf16[64,256]{1,0:T(8,128)(2,1)S(1)}, u32[]{:S(2)}, u32[]{:S(2)}) collective-permute-start(bf16[64,256]{1,0:T(8,128)(2,1)S(1)} %pair_bias.1), channel_id=1, source_target_pairs={{0,16},{1,17},{2,18},{3,19},{4,20},{5,21},{6,22},{7,23},{8,24},{9,... | collective-permute-start | bytes 98312 | tf_op jit(solution)/shard_map/ppermute | solution.py:517
  8.3 4.8 %collective-permute-start = (bf16[64,256]{1,0:T(8,128)(2,1)S(1)}, bf16[64,256]{1,0:T(8,128)(2,1)S(1)}, u32[]{:S(2)}, u32[]{:S(2)}) collective-permute-start(bf16[64,256]{1,0:T(8,128)(2,1)S(1)} %pair_bias.1), channel_id=1, source_target_pairs={{0,8},{1,9},{2,10},{3,11},{4,12},{5,13},{6,14},{7,15},{8,0},{9,1},... | collective-permute-start | bytes 98312 | tf_op jit(solution)/shard_map/ppermute | solution.py:517
  13.1 6.3 %collective-permute-start.3 = (bf16[4,64,256]{2,1,0:T(8,128)(2,1)S(1)}, bf16[4,64,256]{2,1,0:T(8,128)(2,1)S(1)}, u32[]{:S(2)}, u32[]{:S(2)}) collective-permute-start(bf16[4,64,256]{2,1,0:T(8,128)(2,1)S(1)} %pad_maximum_fusion.rest_0_), channel_id=1, source_target_pairs={{0,2},{1,3},{2,0},{3,1},{4,6},{5,7},{6,4},{7,5},{8,10},{9,11},{10,... | collective-permute-start | bytes 393224 | tf_op jit(solution)/shard_map/ppermute | solution.py:517
  14.7 5.9 %collective-permute-start.4 = (bf16[4,64,256]{2,1,0:T(8,128)(2,1)S(1)}, bf16[4,64,256]{2,1,0:T(8,128)(2,1)S(1)}, u32[]{:S(2)}, u32[]{:S(2)}) collective-permute-start(bf16[4,64,256]{2,1,0:T(8,128)(2,1)S(1)} %pad_maximum_fusion.rest_0_), channel_id=1, source_target_pairs={{0,4},{1,5},{2,6},{3,7},{4,0},{5,1},{6,2},{7,3},{8,12},{9,13},{10,... | collective-permute-start | bytes 393224 | tf_op jit(solution)/shard_map/ppermute | solution.py:517
  16.2 5.9 %collective-permute-start.5 = (bf16[4,64,256]{2,1,0:T(8,128)(2,1)S(1)}, bf16[4,64,256]{2,1,0:T(8,128)(2,1)S(1)}, u32[]{:S(2)}, u32[]{:S(2)}) collective-permute-start(bf16[4,64,256]{2,1,0:T(8,128)(2,1)S(1)} %pad_maximum_fusion.rest_0_), channel_id=1, source_target_pairs={{0,6},{1,7},{2,4},{3,5},{4,2},{5,3},{6,0},{7,1},{8,14},{9,15},{10,... | collective-permute-start | bytes 393224 | tf_op jit(solution)/shard_map/ppermute | solution.py:517
  16.7 11.7 %collective-permute-start.6 = (bf16[4,64,256]{2,1,0:T(8,128)(2,1)S(1)}, bf16[4,64,256]{2,1,0:T(8,128)(2,1)S(1)}, u32[]{:S(2)}, u32[]{:S(2)}) collective-permute-start(bf16[4,64,256]{2,1,0:T(8,128)(2,1)S(1)} %pad_maximum_fusion.rest_0_), channel_id=1, source_target_pairs={{0,1},{1,0},{2,3},{3,2},{4,5},{5,4},{6,7},{7,6},{8,9},{9,8},{10,11... | collective-permute-start | bytes 393224 | tf_op jit(solution)/shard_map/ppermute | solution.py:517
  19.4 9.0 %collective-permute-start.7 = (bf16[4,64,256]{2,1,0:T(8,128)(2,1)S(1)}, bf16[4,64,256]{2,1,0:T(8,128)(2,1)S(1)}, u32[]{:S(2)}, u32[]{:S(2)}) collective-permute-start(bf16[4,64,256]{2,1,0:T(8,128)(2,1)S(1)} %collective-permute-done.3.rest_1_), channel_id=1, source_target_pairs={{0,1},{1,0},{2,3},{3,2},{4,5},{5,4},{6,7},{7,6},{8,9},{9,8},{10,11... | collective-permute-start | bytes 393224 | tf_op jit(solution)/shard_map/ppermute | solution.py:517
  20.6 19.8 %copy-start.13 = (bf16[4,64,256]{2,1,0:T(8,128)(2,1)}, bf16[4,64,256]{2,1,0:T(8,128)(2,1)S(1)}, u32[]{:S(2)}) copy-start(bf16[4,64,256]{2,1,0:T(8,128)(2,1)S(1)} %collective-permute-done.4.rest_2_) | copy-start | bytes 393220
  20.6 7.8 %collective-permute-start.8 = (bf16[4,64,256]{2,1,0:T(8,128)(2,1)S(1)}, bf16[4,64,256]{2,1,0:T(8,128)(2,1)S(1)}, u32[]{:S(2)}, u32[]{:S(2)}) collective-permute-start(bf16[4,64,256]{2,1,0:T(8,128)(2,1)S(1)} %collective-permute-done.4.rest_2_), channel_id=1, source_target_pairs={{0,1},{1,0},{2,3},{3,2},{4,5},{5,4},{6,7},{7,6},{8,9},{9,8},{10,11... | collective-permute-start | bytes 393224 | tf_op jit(solution)/shard_map/ppermute | solution.py:517
  22.1 7.1 %collective-permute-start.9 = (bf16[4,64,256]{2,1,0:T(8,128)(2,1)S(1)}, bf16[4,64,256]{2,1,0:T(8,128)(2,1)S(1)}, u32[]{:S(2)}, u32[]{:S(2)}) collective-permute-start(bf16[4,64,256]{2,1,0:T(8,128)(2,1)S(1)} %collective-permute-done.5.rest_3_), channel_id=1, source_target_pairs={{0,1},{1,0},{2,3},{3,2},{4,5},{5,4},{6,7},{7,6},{8,9},{9,8},{10,11... | collective-permute-start | bytes 393224 | tf_op jit(solution)/shard_map/ppermute | solution.py:517
  44.4 22.1 %all-to-all-start.1 = ((bf16[32,32,256]{2,1,0:T(8,128)(2,1)}), bf16[32,32,256]{2,1,0:T(8,128)(2,1)S(1)}, u32[]{:S(2)}, u32[]{:S(2)}) async-start(bf16[32,32,256]{2,1,0:T(8,128)(2,1)} %row_attend.3), calls=%async_computation.1 | async-start | bytes 1048576 | tf_op jit(solution)/shard_map/all_to_all | solution.py:569
  66.5 21.4 %copy-start.29 = (bf16[256,256]{1,0:T(8,128)(2,1)S(1)}, bf16[256,256]{1,0:T(8,128)(2,1)}, u32[]{:S(2)}) copy-start(bf16[256,256]{1,0:T(8,128)(2,1)} %out_w_ref.7) | copy-start | bytes 393220
  66.5 21.4 %all-to-all-start = ((bf16[32,32,256]{2,1,0:T(8,128)(2,1)}), bf16[32,32,256]{2,1,0:T(8,128)(2,1)S(1)}, u32[]{:S(2)}, u32[]{:S(2)}) async-start(bf16[32,32,256]{2,1,0:T(8,128)(2,1)} %row_attend.2), calls=%async_computation | async-start | bytes 1048576 | tf_op jit(solution)/shard_map/all_to_all | solution.py:569
  75.6 38.6 %copy-start.30 = (bf16[1024,128]{1,0:T(8,128)(2,1)S(1)}, bf16[1024,128]{1,0:T(8,128)(2,1)}, u32[]{:S(2)}) copy-start(bf16[1024,128]{1,0:T(8,128)(2,1)} %refs_12_.1) | copy-start | bytes 786436
  83.2 30.0 %copy-start.39 = (s32[256]{0:T(256)S(1)}, s32[256]{0:T(256)}, u32[]{:S(2)}) copy-start(s32[256]{0:T(256)} %param.14) | copy-start | bytes 3076
  90.5 31.0 %copy-start.38 = (s32[256,256]{1,0:T(8,128)S(1)}, s32[256,256]{1,0:T(8,128)}, u32[]{:S(2)}) copy-start(s32[256,256]{1,0:T(8,128)} %param.13) | copy-start | bytes 786436
  90.5 37.0 %copy-start.9 = (bf16[8,256,128]{2,1,0:T(8,128)(2,1)S(1)}, bf16[8,256,128]{2,1,0:T(8,128)(2,1)}, u32[]{:S(2)}) copy-start(bf16[8,256,128]{2,1,0:T(8,128)(2,1)} %pair_ref.3) | copy-start | bytes 1572868
  97.8 6.8 %collective-permute-start.10 = (bf16[256,256]{1,0:T(8,128)(2,1)S(1)}, bf16[256,256]{1,0:T(8,128)(2,1)S(1)}, u32[]{:S(2)}, u32[]{:S(2)}) collective-permute-start(bf16[256,256]{1,0:T(8,128)(2,1)S(1)} %get-tuple-element.26.refs_0_), channel_id=1, source_target_pairs={{0,2},{1,3},{2,0},{3,1},{4,6},{5,7},{6,4},{7,5},{8,10},{9,11},{10,... | collective-permute-start | bytes 393224 | tf_op jit(solution)/shard_map/ppermute | solution.py:517
  98.8 7.0 %collective-permute-start.11 = (bf16[256,256]{1,0:T(8,128)(2,1)S(1)}, bf16[256,256]{1,0:T(8,128)(2,1)S(1)}, u32[]{:S(2)}, u32[]{:S(2)}) collective-permute-start(bf16[256,256]{1,0:T(8,128)(2,1)S(1)} %get-tuple-element.26.refs_0_), channel_id=1, source_target_pairs={{0,4},{1,5},{2,6},{3,7},{4,0},{5,1},{6,2},{7,3},{8,12},{9,13},{10,... | collective-permute-start | bytes 393224 | tf_op jit(solution)/shard_map/ppermute | solution.py:517
  100.3 6.3 %collective-permute-start.14 = (bf16[256,256]{1,0:T(8,128)(2,1)S(1)}, bf16[256,256]{1,0:T(8,128)(2,1)S(1)}, u32[]{:S(2)}, u32[]{:S(2)}) collective-permute-start(bf16[256,256]{1,0:T(8,128)(2,1)S(1)} %get-tuple-element.27.refs_4_), channel_id=1, source_target_pairs={{0,8},{1,9},{2,10},{3,11},{4,12},{5,13},{6,14},{7,15},{8,0},{9,1},... | collective-permute-start | bytes 393224 | tf_op jit(solution)/shard_map/ppermute | solution.py:517
  100.5 12.3 %collective-permute-start.16 = (bf16[256,256]{1,0:T(8,128)(2,1)S(1)}, bf16[256,256]{1,0:T(8,128)(2,1)S(1)}, u32[]{:S(2)}, u32[]{:S(2)}) collective-permute-start(bf16[256,256]{1,0:T(8,128)(2,1)S(1)} %get-tuple-element.27.refs_4_), channel_id=1, source_target_pairs={{0,16},{1,17},{2,18},{3,19},{4,20},{5,21},{6,22},{7,23},{8,24},{9,... | collective-permute-start | bytes 393224 | tf_op jit(solution)/shard_map/ppermute | solution.py:517
  102.2 10.5 %collective-permute-start.18 = (bf16[256,256]{1,0:T(8,128)(2,1)S(1)}, bf16[256,256]{1,0:T(8,128)(2,1)S(1)}, u32[]{:S(2)}, u32[]{:S(2)}) collective-permute-start(bf16[256,256]{1,0:T(8,128)(2,1)S(1)} %get-tuple-element.27.refs_4_), channel_id=1, source_target_pairs={{0,24},{1,25},{2,26},{3,27},{4,28},{5,29},{6,30},{7,31},{8,16},{9,... | collective-permute-start | bytes 393224 | tf_op jit(solution)/shard_map/ppermute | solution.py:517
  104.6 8.7 %collective-permute-start.12 = (bf16[256,256]{1,0:T(8,128)(2,1)S(1)}, bf16[256,256]{1,0:T(8,128)(2,1)S(1)}, u32[]{:S(2)}, u32[]{:S(2)}) collective-permute-start(bf16[256,256]{1,0:T(8,128)(2,1)S(1)} %get-tuple-element.26.refs_0_), channel_id=1, source_target_pairs={{0,6},{1,7},{2,4},{3,5},{4,2},{5,3},{6,0},{7,1},{8,14},{9,15},{10,... | collective-permute-start | bytes 393224 | tf_op jit(solution)/shard_map/ppermute | solution.py:517
  105.7 7.6 %collective-permute-start.13 = (bf16[256,256]{1,0:T(8,128)(2,1)S(1)}, bf16[256,256]{1,0:T(8,128)(2,1)S(1)}, u32[]{:S(2)}, u32[]{:S(2)}) collective-permute-start(bf16[256,256]{1,0:T(8,128)(2,1)S(1)} %get-tuple-element.27.refs_4_), channel_id=1, source_target_pairs={{0,1},{1,0},{2,3},{3,2},{4,5},{5,4},{6,7},{7,6},{8,9},{9,8},{10,11... | collective-permute-start | bytes 393224 | tf_op jit(solution)/shard_map/ppermute | solution.py:517
  106.5 6.8 %collective-permute-start.15 = (bf16[256,256]{1,0:T(8,128)(2,1)S(1)}, bf16[256,256]{1,0:T(8,128)(2,1)S(1)}, u32[]{:S(2)}, u32[]{:S(2)}) collective-permute-start(bf16[256,256]{1,0:T(8,128)(2,1)S(1)} %collective-permute-done.14.refs_6_), channel_id=1, source_target_pairs={{0,1},{1,0},{2,3},{3,2},{4,5},{5,4},{6,7},{7,6},{8,9},{9,8},{10,11... | collective-permute-start | bytes 393224 | tf_op jit(solution)/shard_map/ppermute | solution.py:517
  112.7 1.3 %collective-permute-start.17 = (bf16[256,256]{1,0:T(8,128)(2,1)S(1)}, bf16[256,256]{1,0:T(8,128)(2,1)S(1)}, u32[]{:S(2)}, u32[]{:S(2)}) collective-permute-start(bf16[256,256]{1,0:T(8,128)(2,1)S(1)} %collective-permute-done.16.refs_8_), channel_id=1, source_target_pairs={{0,1},{1,0},{2,3},{3,2},{4,5},{5,4},{6,7},{7,6},{8,9},{9,8},{10,11... | collective-permute-start | bytes 393224 | tf_op jit(solution)/shard_map/ppermute | solution.py:517
  112.7 1.5 %collective-permute-start.19 = (bf16[256,256]{1,0:T(8,128)(2,1)S(1)}, bf16[256,256]{1,0:T(8,128)(2,1)S(1)}, u32[]{:S(2)}, u32[]{:S(2)}) collective-permute-start(bf16[256,256]{1,0:T(8,128)(2,1)S(1)} %collective-permute-done.18.refs_10_), channel_id=1, source_target_pairs={{0,1},{1,0},{2,3},{3,2},{4,5},{5,4},{6,7},{7,6},{8,9},{9,8},{10,11... | collective-permute-start | bytes 393224 | tf_op jit(solution)/shard_map/ppermute | solution.py:517
  118.0 6.4 %collective-permute-start.20 = (bf16[8,64,128]{2,1,0:T(8,128)(2,1)S(1)}, bf16[8,64,128]{2,1,0:T(8,128)(2,1)S(1)}, u32[]{:S(2)}, u32[]{:S(2)}) collective-permute-start(bf16[8,64,128]{2,1,0:T(8,128)(2,1)S(1)} %get-tuple-element.29), channel_id=1, source_target_pairs={{0,2},{1,3},{2,0},{3,1},{4,6},{5,7},{6,4},{7,5},{8,10},{9,11},{10,... | collective-permute-start | bytes 393224 | tf_op jit(solution)/shard_map/ppermute | solution.py:517
  119.3 8.3 %collective-permute-start.21 = (bf16[8,64,128]{2,1,0:T(8,128)(2,1)S(1)}, bf16[8,64,128]{2,1,0:T(8,128)(2,1)S(1)}, u32[]{:S(2)}, u32[]{:S(2)}) collective-permute-start(bf16[8,64,128]{2,1,0:T(8,128)(2,1)S(1)} %get-tuple-element.30), channel_id=1, source_target_pairs={{0,4},{1,5},{2,6},{3,7},{4,0},{5,1},{6,2},{7,3},{8,12},{9,13},{10,... | collective-permute-start | bytes 393224 | tf_op jit(solution)/shard_map/ppermute | solution.py:517
  120.3 7.2 %collective-permute-start.22 = (bf16[8,64,128]{2,1,0:T(8,128)(2,1)S(1)}, bf16[8,64,128]{2,1,0:T(8,128)(2,1)S(1)}, u32[]{:S(2)}, u32[]{:S(2)}) collective-permute-start(bf16[8,64,128]{2,1,0:T(8,128)(2,1)S(1)} %get-tuple-element.31), channel_id=1, source_target_pairs={{0,6},{1,7},{2,4},{3,5},{4,2},{5,3},{6,0},{7,1},{8,14},{9,15},{10,... | collective-permute-start | bytes 393224 | tf_op jit(solution)/shard_map/ppermute | solution.py:517
  (33 other events, 76.8 us)

commit v4 on v3

--- a/solution.py
+++ b/solution.py
@@ -183,6 +183,10 @@
     return jnp.concatenate([held[t] for t in range(held.shape[0])], axis=1)
 
 
+def in_hbm(*arrays):
+    return [pltpu.with_memory_space_constraint(a, pltpu.HBM) for a in arrays]
+
+
 def head_lanes(length):
     lane = lax.broadcasted_iota(jnp.int32, (length, LANES), 1) // HEAD_CHANNELS
     return [
@@ -221,125 +225,132 @@
     return query, key, value, gate
 
 
-def regrouped(held, values, parts):
-    items = values.shape[0] // parts
-    for t in range(held.shape[0]):
-        held[t] = values[:, t * LANES : (t + 1) * LANES]
-    return jnp.concatenate([load_strided(held, r, items, parts) for r in range(items)], axis=0)
-
-
-def bias_kernel(parts, pair_ref, weight_ref, out_ref, held, column):
+def bias_kernel(pair_ref, weight_ref, out_ref, held):
     rows, cols, width = pair_ref.shape
-    normed = layer_normalize(pair_ref[...].astype(F32))
-    ordered = [regrouped(column.at[i], normed[i], parts) for i in range(rows)]
-    normed = jnp.concatenate(ordered, axis=0).astype(BF16)
+    total = out_ref.shape[0] // ATTN_HEAD_COUNT
+    step = pl.program_id(0)
+    normed = layer_normalize(pair_ref[...].astype(F32)).astype(BF16).reshape(rows * cols, width)
     bias = nt_dot(weight_ref[...], normed) * LOG2E
     for i in range(rows):
-        store_strided(held, i, rows, bias[:, i * cols : (i + 1) * cols])
-    out_ref[...] = joined_tiles(held).astype(BF16)
-
-
-def pair_bias_block(pair_rep, bias_weight, parts):
+        store_strided(held, step * rows + i, total, bias[:, i * cols : (i + 1) * cols])
+
+    @pl.when(step == pl.num_programs(0) - 1)
+    def _():
+        out_ref[...] = joined_tiles(held).astype(BF16)
+
+
+def pair_bias_block(pair_rep, bias_weight):
     rows, cols, width = pair_rep.shape
     out = jax.ShapeDtypeStruct((ATTN_HEAD_COUNT * rows, cols), BF16)
+    step = 2
+    weight = bias_weight.T
     return pl.pallas_call(
-        functools.partial(bias_kernel, parts),
+        bias_kernel,
+        grid=(rows // step,),
+        in_specs=[
+            pl.BlockSpec((step, cols, width), lambda i: (i, 0, 0)),
+            full_spec(weight.shape),
+        ],
+        out_specs=full_spec(out.shape),
         out_shape=out,
-        scratch_shapes=[tiled_scratch(*out.shape), pltpu.VMEM((rows, 1, cols, width), F32)],
+        scratch_shapes=[tiled_scratch(*out.shape)],
         compiler_params=params(16),
         name="pair_bias",
-    )(pair_rep, bias_weight.T)
-
-
-def row_project_kernel(parts, x_ref, weight_ref, x_out, q_ref, k_ref, v_ref, g_ref, held):
+    )(*in_hbm(pair_rep, weight))
+
+
+def order_kernel(plan, me_ref, *refs):
+    parts, out_ref = refs[:-1], refs[-1]
+    for part, offsets in zip(parts, plan):
+        for z, offset in enumerate(offsets):
+            out_ref[me_ref[0] ^ offset] = part[z]
+
+
+def order_blocks(me, parts, plan):
+    vmem = pl.BlockSpec(memory_space=pltpu.VMEM)
+    shape = (len(parts) * parts[0].shape[0],) + parts[0].shape[1:]
+    return pl.pallas_call(
+        functools.partial(order_kernel, plan),
+        grid=(1,),
+        in_specs=[pl.BlockSpec(memory_space=pltpu.SMEM)] + [vmem] * len(parts),
+        out_specs=full_spec(shape),
+        out_shape=pltpu.HBM(shape, BF16),
+        compiler_params=params(8),
+        name="order_blocks",
+    )(me, *parts)
+
+
+def row_project_kernel(x_ref, weight_ref, q_ref, k_ref, v_ref, g_ref):
     for s in range(x_ref.shape[0]):
-        ordered = regrouped(held.at[s], x_ref[s].astype(F32), parts)
-        x_out[s] = ordered.astype(BF16)
-        normed = layer_normalize(ordered).astype(BF16)
+        normed = layer_normalize(x_ref[s].astype(F32)).astype(BF16)
         q_ref[s], k_ref[s], v_ref[s], g_ref[s] = project(normed, weight_ref)
 
 
-def row_project(alignment, weight, parts):
+def row_project(alignment, weight):
     seqs, length, width = alignment.shape
     step = 2
     block = pl.BlockSpec((step, length, width), lambda i: (i, 0, 0))
-    small = jax.ShapeDtypeStruct(alignment.shape, BF16)
     return pl.pallas_call(
-        functools.partial(row_project_kernel, parts),
+        row_project_kernel,
         grid=(seqs // step,),
         in_specs=[block, full_spec(weight.shape)],
-        out_specs=[block] * 5,
-        out_shape=[small] * 4 + [jax.ShapeDtypeStruct(alignment.shape, F32)],
-        scratch_shapes=[pltpu.VMEM((step, width // LANES, length, LANES), F32)],
+        out_specs=[block] * 4,
+        out_shape=[pltpu.HBM(alignment.shape, BF16)] * 3 + [pltpu.HBM(alignment.shape, F32)],
         compiler_params=params(24),
         name="row_project",
-    )(alignment, weight)
+    )(*in_hbm(alignment, weight))
 
 
 def row_attend_kernel(
-    plan, step, half, me_ref, x_ref, q_ref, k_ref, v_ref, g_ref, live_ref, out_w_ref, *rest
+    halves, x_ref, q_ref, k_ref, v_ref, g_ref, live_ref, out_w_ref, bias_ref, *rest
 ):
-    bias_refs, out_ref, bias_all, held = rest[: len(plan)], rest[-3], rest[-2], rest[-1]
-    heads, rows, length = ATTN_HEAD_COUNT, q_ref.shape[1], k_ref.shape[1]
-    parts, block_rows = out_ref.shape[0], out_ref.shape[1]
-    items = rows // parts
-    at = pl.program_id(0)
-
-    @pl.when(at == 0)
+    outs, bias_all = rest[:-1], rest[-1]
+    heads, length, _ = bias_all.shape
+    parts = bias_ref.shape[0]
+
+    @pl.when(pl.program_id(0) == 0)
     def _():
-        for bias_ref, offsets in zip(bias_refs, plan):
-            for z, offset in enumerate(offsets):
-                owner = me_ref[0] ^ offset
-                block = bias_ref[z].astype(F32).reshape(heads, -1, length)
-                own = block.shape[1]
-                for h in range(heads):
-                    for t in range(bias_all.shape[0]):
-                        to = pl.ds(h * length + owner, own, stride=parts)
-                        bias_all[t, to, :] = block[h, :, t * LANES : (t + 1) * LANES]
-
-    def bias_of(h):
-        start = h * length + half * rows
-        return jnp.concatenate(
-            [bias_all[t, start : start + rows, :] for t in range(bias_all.shape[0])], axis=1
+        for owner in range(parts):
+            block = bias_ref[owner].astype(F32).reshape(heads, -1, length)
+            rows = block.shape[1]
+            bias_all[:, owner * rows : (owner + 1) * rows, :] = block
+
+    lanes = head_lanes(length)
+    results = []
+    for s in range(halves):
+        heads_out = attend_block(
+            q_ref[s], k_ref[s], v_ref[s], live_ref[s], lanes, lambda h: bias_all[h]
         )
-
-    lanes = head_lanes(length)
-    for s in range(step):
-        heads_out = attend_block(q_ref[s], k_ref[s], v_ref[s], live_ref[s], lanes, bias_of)
         heads_out = (heads_out * g_ref[s]).astype(BF16)
-        total = x_ref[s].astype(F32) + nn_dot(heads_out, out_w_ref[...])
-        for r in range(items):
-            first = (at * step + s) * items + r
-            store_strided(held, first, block_rows, total[r * parts : (r + 1) * parts])
-
-    @pl.when(at == pl.num_programs(0) - 1)
-    def _():
-        out_ref[...] = joined_tiles(held).reshape(out_ref.shape).astype(BF16)
-
-
-def row_attend(me, projected, live, out_weight, bias_parts, plan, dap_count, half, halves):
-    x_rows, query, key, value, gate = projected
-    seqs, length, width = x_rows.shape
-    rows = length // halves
-    step = 2
+        results.append(x_ref[s].astype(F32) + nn_dot(heads_out, out_w_ref[...]))
+    items = length // parts
+    first, second = (r.reshape(parts, items, -1) for r in results)
+    rolled_first = pltpu.roll(first, items // 2, 1)
+    rolled_second = pltpu.roll(second, items // 2, 1)
+    low = lax.broadcasted_iota(jnp.int32, first.shape, 1) < items // 2
+    outs[0][:, 0] = jnp.where(low, first, rolled_second).astype(BF16)
+    outs[1][:, 0] = jnp.where(low, rolled_first, second).astype(BF16)
+
+
+def row_attend(alignment, projected, live, out_weight, bias, halves):
+    seqs, length, width = alignment.shape
+    parts = bias.shape[0]
+    items = length // parts
+    step = halves
     block = pl.BlockSpec((step, length, width), lambda i: (i, 0, 0))
-    part = pl.BlockSpec((step, rows, width), lambda i: (i, half, 0))
-    out = (dap_count, seqs * rows // dap_count, width)
+    out = (parts, seqs // step, items, width)
     return pl.pallas_call(
-        functools.partial(row_attend_kernel, plan, step, half),
+        functools.partial(row_attend_kernel, halves),
         grid=(seqs // step,),
-        in_specs=[pl.BlockSpec(memory_space=pltpu.SMEM), part, part, block, block, part]
+        in_specs=[block] * 5
         + [pl.BlockSpec((step, length, LANES), lambda i: (i, 0, 0)), full_spec(out_weight.shape)]
-        + [full_spec(b.shape) for b in bias_parts],
-        out_specs=full_spec(out),
-        out_shape=jax.ShapeDtypeStruct(out, BF16),
-        scratch_shapes=[
-            tiled_scratch(ATTN_HEAD_COUNT * length, length),
-            tiled_scratch(seqs * rows, width),
-        ],
+        + [full_spec(bias.shape)],
+        out_specs=[pl.BlockSpec((parts, 1, items, width), lambda i: (0, i, 0, 0))] * halves,
+        out_shape=[pltpu.HBM(out, BF16)] * halves,
+        scratch_shapes=[pltpu.VMEM((ATTN_HEAD_COUNT, length, length), F32)],
         compiler_params=params(28),
         name="row_attend",
-    )(me, x_rows, query, key, value, gate, live, out_weight, *bias_parts)
+    )(*in_hbm(alignment, *projected, live, out_weight, bias))
 
 
 def column_kernel(
@@ -355,7 +366,7 @@
     def _():
         for t in range(held.shape[0]):
             cut = slice(t * LANES, (t + 1) * LANES)
-            x_held[t] = x_ref[:, :, cut].astype(F32).reshape(x_held.shape[1:])
+            x_held[t] = x_ref[:, :, :, cut].astype(F32).reshape(x_held.shape[1:])
             if before:
                 held[t] = before[0][:, :, cut].astype(F32).reshape(held.shape[1:])
                 right_held[t] = before[2][:, cut].astype(F32)
@@ -389,16 +400,17 @@
 
 
 def column_attend(moved, live, mask_rows, weight, out_weight, factor_t, half, halves, before):
-    width = moved.shape[2]
+    width = moved.shape[-1]
     items = mask_rows.shape[0]
     here = items // halves
-    rows = moved.shape[0] * moved.shape[1]
+    rows = math.prod(moved.shape[:-1])
     length = rows // here
     each = 2
     start = half * here
     side = (items * FACTOR_CHANNELS, length)
-    outs = [jax.ShapeDtypeStruct((length, items, width), BF16)]
-    outs += [jax.ShapeDtypeStruct(side, BF16)] * 2
+    last = half == halves - 1
+    outs = [pltpu.HBM((length, items, width), BF16)]
+    outs += [jax.ShapeDtypeStruct(side, BF16) if last else pltpu.HBM(side, BF16)] * 2
     return pl.pallas_call(
         functools.partial(column_kernel, start, items, each),
         grid=(here // each,),
@@ -421,7 +433,7 @@
         ],
         compiler_params=params(28),
         name="column_attend",
-    )(moved, live, mask_rows, weight, out_weight, factor_t, *before)
+    )(moved, *in_hbm(live, mask_rows, weight, out_weight, factor_t, *before))
 
 
 def outer_kernel(group, outer, items, *refs):
@@ -539,19 +551,20 @@
     total_seqs, total_res = align_mask.shape
     halves = 2
 
-    bias = pair_bias_block(pair_rep, bias_weight, count)
-    bias = jnp.stack([exchange(bias, count, z) for z in line])
-    bias_parts = [exchange(bias, count, k) for k in plane]
+    projected = list(row_project(alignment, row_proj_weight))
+    bias = pair_bias_block(pair_rep, bias_weight)
+    column = jnp.stack([exchange(bias, count, z) for z in line])
+    bias_parts = [exchange(column, count, k) for k in plane]
+    *bias_parts, query = lax.optimization_barrier((*bias_parts, projected[0]))
+    projected = [query] + projected[1:]
     plan = [[k | z for z in line] for k in plane]
     bias_parts += [exchange(part, count, 1) for part in bias_parts]
     plan += [[offset | 1 for offset in offsets] for offsets in plan]
-    projected = row_project(alignment, row_proj_weight, count)
+    bias = order_blocks(me, bias_parts, plan)
 
     own_seqs = lax.dynamic_slice_in_dim(align_mask, dap_index * seq_dev, seq_dev, 0)
-    own_seqs = own_seqs.astype(BF16).reshape(seq_dev, count, items).swapaxes(1, 2)
     own_res = lax.dynamic_slice_in_dim(align_mask, dap_index * items, items, 1)
-    row_live = own_seqs.reshape(seq_dev, total_res)[:, :, None]
-    row_live = jnp.broadcast_to(row_live, (seq_dev, total_res, LANES))
+    row_live = jnp.broadcast_to(own_seqs.astype(BF16)[:, :, None], (seq_dev, total_res, LANES))
     col_live = jnp.broadcast_to(own_res.T.astype(BF16)[:, :, None], (items, total_seqs, LANES))
     counts = jnp.einsum(
         "si,sj->ji", own_res.astype(BF16), align_mask.astype(BF16), preferred_element_type=F32
@@ -561,12 +574,8 @@
     scale = live_rows[None, :] * res_float[:, None] / (counts + count_eps)
     mask_rows = own_res.T.astype(F32)
 
-    moved = []
-    for half in range(halves):
-        rows = row_attend(
-            me, projected, row_live, row_out_weight, bias_parts, plan, count, half, halves
-        )
-        moved.append(lax.all_to_all(rows, "dap", split_axis=0, concat_axis=0, tiled=True))
+    rows = row_attend(alignment, projected, row_live, row_out_weight, bias, halves)
+    moved = [lax.all_to_all(r, "dap", split_axis=0, concat_axis=0, tiled=True) for r in rows]
     done = ()
     for half in range(halves):
         done = column_attend(

time: 130 us -> 114 us (0.88)
  local copies, waits for them, and re-layouts: 29.1 us -> 2.51 us
  blocking collectives: 0 us -> 18.4 us
  waiting for transfers between devices: 27.9 us -> 23.1 us
  starting transfers between devices: 30.6 us -> 26.6 us
  Pallas kernels: 39.3 us -> 41.7 us
    unnamed x81 -> x9, local copies, waits for them, and re-layouts: 27 us -> 0.07 us
    all_to_all x0 -> x1, blocking collectives: none -> 18.4 us  [per_device_fast(): lax.all_to_all(r, 'dap', split_axis=0, concat_axis=0, tiled=True)]
    all_to_all x2 -> x1, starting transfers between devices: 9.33 us -> 3.26 us  [per_device_fast(): lax.all_to_all(r, 'dap', split_axis=0, concat_axis=0, tiled=True)]
    ppermute x23, waiting for transfers between devices: 23.2 us -> 18.2 us  [exchange(): return lax.ppermute(block, 'dap', [(i, i ^ offset) for i in range(count)])]
    pallas_call x2, Pallas kernels: 13.6 us -> 17.6 us  [column_attend(): pl.pallas_call(functools.partial(column_kernel, start, items, each), grid...]
    ppermute x23, starting transfers between devices: 21.3 us -> 23.3 us  [exchange(): return lax.ppermute(block, 'dap', [(i, i ^ offset) for i in range(count)])]
    pallas_call x4, Pallas kernels: 20.7 us -> 19.2 us  [the longest x1 9.56 us: row_attend(): pl.pallas_call(functools.partial(row_attend_kernel, halves), grid=(seqs /...]
    all_to_all x2 -> x1, waiting for transfers between devices: 4.68 us -> 4.91 us  [per_device_fast(): lax.all_to_all(r, 'dap', split_axis=0, concat_axis=0, tiled=True)]
  transfers between devices with their start and end apart: 25 -> 24, of which waited for: 12 -> 15; matrix products, arithmetic and copies ran while one was open for 2% -> 2% of each run, Pallas kernels for 14% -> 12%
where the time goes in v4:
time: 114 us
  Pallas kernels  41.7 us (37%)
  starting transfers between devices  26.6 us (23%)
  waiting for transfers between devices  23.1 us (20%)
  blocking collectives  18.4 us (16%)
  local copies, waits for them, and re-layouts  2.51 us (2%)
    ppermute x23, starting transfers between devices, exchange(): return lax.ppermute(block, 'dap', [(i, i ^ offset) for i in range(count)])  23.3 us
    all_to_all x1, blocking collectives, per_device_fast(): lax.all_to_all(r, 'dap', split_axis=0, concat_axis=0, tiled=True)  18.4 us
    ppermute x23, waiting for transfers between devices, exchange(): return lax.ppermute(block, 'dap', [(i, i ^ offset) for i in range(count)])  18.2 us
    pallas_call x2, Pallas kernels, column_attend(): pl.pallas_call(functools.partial(column_kernel, start, items, each), grid...  17.6 us
    pallas_call x1, Pallas kernels, row_attend(): pl.pallas_call(functools.partial(row_attend_kernel, halves), grid=(seqs /...  9.56 us
    pallas_call x1, Pallas kernels, row_project(): pl.pallas_call(row_project_kernel, grid=(seqs // step,), in_specs=[block,...  5.58 us
    all_to_all x1, waiting for transfers between devices, per_device_fast(): lax.all_to_all(r, 'dap', split_axis=0, concat_axis=0, tiled=True)  4.91 us
    pallas_call x1, Pallas kernels, outer_product(): pl.pallas_call(functools.partial(outer_kernel, group, outer, items), out_...  3.69 us
  transfers between devices with their start and end apart: 24, of which 15 were waited for; matrix products, arithmetic and copies ran while one was open for 2% of the time, Pallas kernels for 12%

profile of v4, /device:TPU:0, one launch (start us, length us, event | category | flops | bytes accessed | tf_op | source)
XLA Modules:
  0.0 113.9 jit_solution(7841453526620028348)
XLA Ops:
  0.6 3.0 %pair_bias.1 = bf16[64,256]{1,0:T(8,128)(2,1)S(1)} custom-call(bf16[8,256,128]{2,1,0:T(8,128)(2,1)} %pair_ref.3, bf16[8,128]{1,0:T(8,128)(2,1)} %bitcast.21), custom_call_target="tpu_custom_call" | custom-call | tf_op jit(solution)/shard_map/pair_bias/pallas_call | solution.py:247
  3.6 3.1 %collective-permute-start = (bf16[64,256]{1,0:T(8,128)(2,1)S(1)}, bf16[64,256]{1,0:T(8,128)(2,1)S(1)}, u32[]{:S(2)}, u32[]{:S(2)}) collective-permute-start(bf16[64,256]{1,0:T(8,128)(2,1)S(1)} %pair_bias.1), channel_id=1, source_target_pairs={{0,8},{1,9},{2,10},{3,11},{4,12},{5,13},{6,14},{7,15},{8,0},{9,1},... | collective-permute-start | bytes 98312 | tf_op jit(solution)/shard_map/ppermute | solution.py:529
  6.7 2.6 %collective-permute-start.1 = (bf16[64,256]{1,0:T(8,128)(2,1)S(1)}, bf16[64,256]{1,0:T(8,128)(2,1)S(1)}, u32[]{:S(2)}, u32[]{:S(2)}) collective-permute-start(bf16[64,256]{1,0:T(8,128)(2,1)S(1)} %pair_bias.1), channel_id=1, source_target_pairs={{0,16},{1,17},{2,18},{3,19},{4,20},{5,21},{6,22},{7,23},{8,24},{9,... | collective-permute-start | bytes 98312 | tf_op jit(solution)/shard_map/ppermute | solution.py:529
  9.3 2.8 %collective-permute-done.1 = bf16[64,256]{1,0:T(8,128)(2,1)S(1)} collective-permute-done((bf16[64,256]{1,0:T(8,128)(2,1)S(1)}, bf16[64,256]{1,0:T(8,128)(2,1)S(1)}, u32[]{:S(2)}, u32[]{:S(2)}) %collective-permute-start.1) | collective-permute-done | bytes 32800 | tf_op jit(solution)/shard_map/ppermute | solution.py:529
  12.1 2.9 %collective-permute-done.2 = bf16[64,256]{1,0:T(8,128)(2,1)S(1)} collective-permute-done((bf16[64,256]{1,0:T(8,128)(2,1)S(1)}, bf16[64,256]{1,0:T(8,128)(2,1)S(1)}, u32[]{:S(2)}, u32[]{:S(2)}) %collective-permute-start.2) | collective-permute-done | bytes 32800 | tf_op jit(solution)/shard_map/ppermute | solution.py:529
  15.0 1.6 %collective-permute-start.3 = (bf16[4,64,256]{2,1,0:T(8,128)(2,1)S(1)}, bf16[4,64,256]{2,1,0:T(8,128)(2,1)S(1)}, u32[]{:S(2)}, u32[]{:S(2)}) collective-permute-start(bf16[4,64,256]{2,1,0:T(8,128)(2,1)S(1)} %pad_maximum_fusion.refs_0_), channel_id=1, source_target_pairs={{0,2},{1,3},{2,0},{3,1},{4,6},{5,7},{6,4},{7,5},{8,10},{9,11},{10,... | collective-permute-start | bytes 393224 | tf_op jit(solution)/shard_map/ppermute | solution.py:529
  16.6 1.5 %collective-permute-start.4 = (bf16[4,64,256]{2,1,0:T(8,128)(2,1)S(1)}, bf16[4,64,256]{2,1,0:T(8,128)(2,1)S(1)}, u32[]{:S(2)}, u32[]{:S(2)}) collective-permute-start(bf16[4,64,256]{2,1,0:T(8,128)(2,1)S(1)} %pad_maximum_fusion.refs_0_), channel_id=1, source_target_pairs={{0,4},{1,5},{2,6},{3,7},{4,0},{5,1},{6,2},{7,3},{8,12},{9,13},{10,... | collective-permute-start | bytes 393224 | tf_op jit(solution)/shard_map/ppermute | solution.py:529
  18.6 5.6 %row_project.1 = (bf16[8,256,256]{2,1,0:T(8,128)(2,1)}, bf16[8,256,256]{2,1,0:T(8,128)(2,1)}, bf16[8,256,256]{2,1,0:T(8,128)(2,1)}, f32[8,256,256]{2,1,0:T(8,128)}) custom-call(bf16[8,256,256]{2,1,0:T(8,128)(2,1)} %x_ref.3, bf16[4,256,256]{2,1,0:T(8,128)(2,1)} %weight_ref.3), custom_call_target="tpu_custom_call" | custom-call | tf_op jit(solution)/shard_map/row_project/pallas_call | solution.py:293
  26.3 1.1 order_blocks.1.bias_ref
  27.4 1.1 broadcast_in_dim.4.live_ref
  28.5 9.6 %row_attend.1 = (bf16[32,4,8,256]{3,2,1,0:T(8,128)(2,1)}, bf16[32,4,8,256]{3,2,1,0:T(8,128)(2,1)}) custom-call(bf16[8,256,256]{2,1,0:T(8,128)(2,1)} %x_ref.3, bf16[8,256,256]{2,1,0:T(8,128)(2,1)} %get-tuple-element.24.q_ref, bf16[8,256,256]{2,1,0:T(8,128)(2,1)} %get-tuple-element.25.k_ref, bf16[8,256,256]{2,1,0:T(8,128)(2,1)} %get-tuple-element.26.v_ref, ...), custom_call_target="tpu_custom_call" | custom-call | tf_op jit(solution)/shard_map/row_attend/pallas_call | solution.py:342
  38.1 18.4 %all_to_all.10.x_ref = bf16[32,4,8,256]{3,2,1,0:T(8,128)(2,1)S(1)} all-to-all(bf16[32,4,8,256]{3,2,1,0:T(8,128)(2,1)} %get-tuple-element.33), channel_id=1, replica_groups=mesh['branch'=1,'dap'=32] {'dap'}, dimensions={0} | all-to-all | bytes 1048576 | tf_op jit(solution)/shard_map/all_to_all | solution.py:578
  56.4 3.3 %all-to-all-start = ((bf16[32,4,8,256]{3,2,1,0:T(8,128)(2,1)}), bf16[32,4,8,256]{3,2,1,0:T(8,128)(2,1)S(1)}, u32[]{:S(2)}, u32[]{:S(2)}) async-start(bf16[32,4,8,256]{3,2,1,0:T(8,128)(2,1)} %get-tuple-element.32), calls=%async_computation | async-start | bytes 1048576 | tf_op jit(solution)/shard_map/all_to_all | solution.py:578
  59.9 0.6 convert_bitcast_fusion
  60.5 1.1 broadcast_in_dim.5.live_ref
  61.6 8.5 %column_attend.2 = (bf16[256,8,256]{2,1,0:T(8,128)(2,1)}, bf16[256,256]{1,0:T(8,128)(2,1)}, bf16[256,256]{1,0:T(8,128)(2,1)}) custom-call(bf16[32,4,8,256]{3,2,1,0:T(8,128)(2,1)S(1)} %all_to_all.10.x_ref, bf16[8,256,128]{2,1,0:T(8,128)(2,1)} %broadcast_in_dim.5.live_ref, f32[8,256]{1,0:T(8,128)} %get-tuple-element.44.mask_ref, ...), custom_call_target="tpu_custom_call" | custom-call | tf_op jit(solution)/shard_map/column_attend/pallas_call | solution.py:414
  70.2 4.9 %all-to-all-done.x_ref = bf16[32,4,8,256]{3,2,1,0:T(8,128)(2,1)S(1)} async-done(((bf16[32,4,8,256]{3,2,1,0:T(8,128)(2,1)}), bf16[32,4,8,256]{3,2,1,0:T(8,128)(2,1)S(1)}, u32[]{:S(2)}, u32[]{:S(2)}) %all-to-all-start) | async-done | bytes 524320 | tf_op jit(solution)/shard_map/all_to_all | solution.py:578
  75.1 9.0 %column_attend.3 = (bf16[256,8,256]{2,1,0:T(8,128)(2,1)}, bf16[256,256]{1,0:T(8,128)(2,1)S(1)}, bf16[256,256]{1,0:T(8,128)(2,1)S(1)}) custom-call(bf16[32,4,8,256]{3,2,1,0:T(8,128)(2,1)S(1)} %all-to-all-done.x_ref, bf16[8,256,128]{2,1,0:T(8,128)(2,1)} %broadcast_in_dim.5.live_ref, f32[8,256]{1,0:T(8,128)} %get-tuple-element.44.mask_ref, ...), custom_call_target="tpu_custom_call" | custom-call | tf_op jit(solution)/shard_map/column_attend/pallas_call | solution.py:414
  84.1 1.3 %collective-permute-start.14 = (bf16[256,256]{1,0:T(8,128)(2,1)S(1)}, bf16[256,256]{1,0:T(8,128)(2,1)S(1)}, u32[]{:S(2)}, u32[]{:S(2)}) collective-permute-start(bf16[256,256]{1,0:T(8,128)(2,1)S(1)} %get-tuple-element.39.refs_4_), channel_id=1, source_target_pairs={{0,8},{1,9},{2,10},{3,11},{4,12},{5,13},{6,14},{7,15},{8,0},{9,1},... | collective-permute-start | bytes 393224 | tf_op jit(solution)/shard_map/ppermute | solution.py:529
  85.8 2.7 %collective-permute-start.18 = (bf16[256,256]{1,0:T(8,128)(2,1)S(1)}, bf16[256,256]{1,0:T(8,128)(2,1)S(1)}, u32[]{:S(2)}, u32[]{:S(2)}) collective-permute-start(bf16[256,256]{1,0:T(8,128)(2,1)S(1)} %get-tuple-element.39.refs_4_), channel_id=1, source_target_pairs={{0,24},{1,25},{2,26},{3,27},{4,28},{5,29},{6,30},{7,31},{8,16},{9,... | collective-permute-start | bytes 393224 | tf_op jit(solution)/shard_map/ppermute | solution.py:529
  88.5 0.9 collective-permute-start.10
  89.4 1.5 %collective-permute-start.11 = (bf16[256,256]{1,0:T(8,128)(2,1)S(1)}, bf16[256,256]{1,0:T(8,128)(2,1)S(1)}, u32[]{:S(2)}, u32[]{:S(2)}) collective-permute-start(bf16[256,256]{1,0:T(8,128)(2,1)S(1)} %get-tuple-element.38.refs_0_), channel_id=1, source_target_pairs={{0,4},{1,5},{2,6},{3,7},{4,0},{5,1},{6,2},{7,3},{8,12},{9,13},{10,... | collective-permute-start | bytes 393224 | tf_op jit(solution)/shard_map/ppermute | solution.py:529
  91.0 1.6 %collective-permute-start.12 = (bf16[256,256]{1,0:T(8,128)(2,1)S(1)}, bf16[256,256]{1,0:T(8,128)(2,1)S(1)}, u32[]{:S(2)}, u32[]{:S(2)}) collective-permute-start(bf16[256,256]{1,0:T(8,128)(2,1)S(1)} %get-tuple-element.38.refs_0_), channel_id=1, source_target_pairs={{0,6},{1,7},{2,4},{3,5},{4,2},{5,3},{6,0},{7,1},{8,14},{9,15},{10,... | collective-permute-start | bytes 393224 | tf_op jit(solution)/shard_map/ppermute | solution.py:529
  92.7 5.1 %collective-permute-done.16.refs_8_ = bf16[256,256]{1,0:T(8,128)(2,1)S(1)} collective-permute-done((bf16[256,256]{1,0:T(8,128)(2,1)S(1)}, bf16[256,256]{1,0:T(8,128)(2,1)S(1)}, u32[]{:S(2)}, u32[]{:S(2)}) %collective-permute-start.16) | collective-permute-done | bytes 131104 | tf_op jit(solution)/shard_map/ppermute | solution.py:529
  97.8 0.5 collective-permute-start.15
  99.8 3.7 %outer_product.1 = (bf16[8,64,128]{2,1,0:T(8,128)(2,1)S(1)}, bf16[8,64,128]{2,1,0:T(8,128)(2,1)S(1)}, bf16[8,64,128]{2,1,0:T(8,128)(2,1)S(1)}, bf16[8,64,128]{2,1,0:T(8,128)(2,1)S(1)}) custom-call(bf16[256,256]{1,0:T(8,128)(2,1)S(1)} %get-tuple-element.38.refs_0_, bf16[256,256]{1,0:T(8,128)(2,1)S(1)} %collective-permute-done.10.refs_1_, ...), custom_call_target="tpu_custom_call" | custom-call | tf_op jit(solution)/shard_map/outer_product/pallas_call | solution.py:481
  103.5 0.8 collective-permute-start.20
  104.3 1.0 collective-permute-start.21
  105.3 1.8 %collective-permute-start.22 = (bf16[8,64,128]{2,1,0:T(8,128)(2,1)S(1)}, bf16[8,64,128]{2,1,0:T(8,128)(2,1)S(1)}, u32[]{:S(2)}, u32[]{:S(2)}) collective-permute-start(bf16[8,64,128]{2,1,0:T(8,128)(2,1)S(1)} %get-tuple-element.43), channel_id=1, source_target_pairs={{0,6},{1,7},{2,4},{3,5},{4,2},{5,3},{6,0},{7,1},{8,14},{9,15},{10,... | collective-permute-start | bytes 393224 | tf_op jit(solution)/shard_map/ppermute | solution.py:529
  107.3 2.6 %collective-permute-done.20.refs_1_ = bf16[8,64,128]{2,1,0:T(8,128)(2,1)S(1)} collective-permute-done((bf16[8,64,128]{2,1,0:T(8,128)(2,1)S(1)}, bf16[8,64,128]{2,1,0:T(8,128)(2,1)S(1)}, u32[]{:S(2)}, u32[]{:S(2)}) %collective-permute-start.20) | collective-permute-done | bytes 131104 | tf_op jit(solution)/shard_map/ppermute | solution.py:529
  109.9 2.7 %collective-permute-done.21.refs_2_ = bf16[8,64,128]{2,1,0:T(8,128)(2,1)S(1)} collective-permute-done((bf16[8,64,128]{2,1,0:T(8,128)(2,1)S(1)}, bf16[8,64,128]{2,1,0:T(8,128)(2,1)S(1)}, u32[]{:S(2)}, u32[]{:S(2)}) %collective-permute-start.21) | collective-permute-done | bytes 131104 | tf_op jit(solution)/shard_map/ppermute | solution.py:529
  112.6 1.2 %finish.1 = bf16[8,256,128]{2,1,0:T(8,128)(2,1)} custom-call(s32[1]{0:T(128)} %bitcast.5.me_ref, bf16[8,256,128]{2,1,0:T(8,128)(2,1)S(1)} %copy-done, f32[256,8]{1,0:T(8,128)S(1)} %fusion.1.scale_ref, bf16[8,64,128]{2,1,0:T(8,128)(2,1)S(1)} %get-tuple-element.40.refs_0_, bf16[8,64,128]{2,1,0:T(8,128)(2,1)S(1)} %collective-permute-done.20.refs_1_, ...), custom_call_target="tpu_custom_call" | custom-call | tf_op jit(solution)/shard_map/finish/pallas_call | solution.py:516
  (43 shorter events, 5.1 us)
Async XLA Ops:
  0.6 24.6 %copy-start.2 = (s32[256,256]{1,0:T(8,128)S(1)}, s32[256,256]{1,0:T(8,128)}, u32[]{:S(2)}) copy-start(s32[256,256]{1,0:T(8,128)} %param.13) | copy-start | bytes 786436
  3.6 5.7 %collective-permute-start = (bf16[64,256]{1,0:T(8,128)(2,1)S(1)}, bf16[64,256]{1,0:T(8,128)(2,1)S(1)}, u32[]{:S(2)}, u32[]{:S(2)}) collective-permute-start(bf16[64,256]{1,0:T(8,128)(2,1)S(1)} %pair_bias.1), channel_id=1, source_target_pairs={{0,8},{1,9},{2,10},{3,11},{4,12},{5,13},{6,14},{7,15},{8,0},{9,1},... | collective-permute-start | bytes 98312 | tf_op jit(solution)/shard_map/ppermute | solution.py:529
  6.7 5.4 %collective-permute-start.1 = (bf16[64,256]{1,0:T(8,128)(2,1)S(1)}, bf16[64,256]{1,0:T(8,128)(2,1)S(1)}, u32[]{:S(2)}, u32[]{:S(2)}) collective-permute-start(bf16[64,256]{1,0:T(8,128)(2,1)S(1)} %pair_bias.1), channel_id=1, source_target_pairs={{0,16},{1,17},{2,18},{3,19},{4,20},{5,21},{6,22},{7,23},{8,24},{9,... | collective-permute-start | bytes 98312 | tf_op jit(solution)/shard_map/ppermute | solution.py:529
  9.3 5.7 %collective-permute-start.2 = (bf16[64,256]{1,0:T(8,128)(2,1)S(1)}, bf16[64,256]{1,0:T(8,128)(2,1)S(1)}, u32[]{:S(2)}, u32[]{:S(2)}) collective-permute-start(bf16[64,256]{1,0:T(8,128)(2,1)S(1)} %pair_bias.1), channel_id=1, source_target_pairs={{0,24},{1,25},{2,26},{3,27},{4,28},{5,29},{6,30},{7,31},{8,16},{9,... | collective-permute-start | bytes 98312 | tf_op jit(solution)/shard_map/ppermute | solution.py:529
  15.0 9.1 %collective-permute-start.3 = (bf16[4,64,256]{2,1,0:T(8,128)(2,1)S(1)}, bf16[4,64,256]{2,1,0:T(8,128)(2,1)S(1)}, u32[]{:S(2)}, u32[]{:S(2)}) collective-permute-start(bf16[4,64,256]{2,1,0:T(8,128)(2,1)S(1)} %pad_maximum_fusion.refs_0_), channel_id=1, source_target_pairs={{0,2},{1,3},{2,0},{3,1},{4,6},{5,7},{6,4},{7,5},{8,10},{9,11},{10,... | collective-permute-start | bytes 393224 | tf_op jit(solution)/shard_map/ppermute | solution.py:529
  16.6 7.6 %collective-permute-start.4 = (bf16[4,64,256]{2,1,0:T(8,128)(2,1)S(1)}, bf16[4,64,256]{2,1,0:T(8,128)(2,1)S(1)}, u32[]{:S(2)}, u32[]{:S(2)}) collective-permute-start(bf16[4,64,256]{2,1,0:T(8,128)(2,1)S(1)} %pad_maximum_fusion.refs_0_), channel_id=1, source_target_pairs={{0,4},{1,5},{2,6},{3,7},{4,0},{5,1},{6,2},{7,3},{8,12},{9,13},{10,... | collective-permute-start | bytes 393224 | tf_op jit(solution)/shard_map/ppermute | solution.py:529
  18.1 6.1 %collective-permute-start.5 = (bf16[4,64,256]{2,1,0:T(8,128)(2,1)S(1)}, bf16[4,64,256]{2,1,0:T(8,128)(2,1)S(1)}, u32[]{:S(2)}, u32[]{:S(2)}) collective-permute-start(bf16[4,64,256]{2,1,0:T(8,128)(2,1)S(1)} %pad_maximum_fusion.refs_0_), channel_id=1, source_target_pairs={{0,6},{1,7},{2,4},{3,5},{4,2},{5,3},{6,0},{7,1},{8,14},{9,15},{10,... | collective-permute-start | bytes 393224 | tf_op jit(solution)/shard_map/ppermute | solution.py:529
  24.2 1.4 %collective-permute-start.6 = (bf16[4,64,256]{2,1,0:T(8,128)(2,1)S(1)}, bf16[4,64,256]{2,1,0:T(8,128)(2,1)S(1)}, u32[]{:S(2)}, u32[]{:S(2)}) collective-permute-start(bf16[4,64,256]{2,1,0:T(8,128)(2,1)S(1)} %pad_maximum_fusion.refs_0_), channel_id=1, source_target_pairs={{0,1},{1,0},{2,3},{3,2},{4,5},{5,4},{6,7},{7,6},{8,9},{9,8},{10,11... | collective-permute-start | bytes 393224 | tf_op jit(solution)/shard_map/ppermute | solution.py:529
  24.2 1.5 %collective-permute-start.7 = (bf16[4,64,256]{2,1,0:T(8,128)(2,1)S(1)}, bf16[4,64,256]{2,1,0:T(8,128)(2,1)S(1)}, u32[]{:S(2)}, u32[]{:S(2)}) collective-permute-start(bf16[4,64,256]{2,1,0:T(8,128)(2,1)S(1)} %collective-permute-done.3.refs_1_), channel_id=1, source_target_pairs={{0,1},{1,0},{2,3},{3,2},{4,5},{5,4},{6,7},{7,6},{8,9},{9,8},{10,11... | collective-permute-start | bytes 393224 | tf_op jit(solution)/shard_map/ppermute | solution.py:529
  24.7 1.3 %collective-permute-start.8 = (bf16[4,64,256]{2,1,0:T(8,128)(2,1)S(1)}, bf16[4,64,256]{2,1,0:T(8,128)(2,1)S(1)}, u32[]{:S(2)}, u32[]{:S(2)}) collective-permute-start(bf16[4,64,256]{2,1,0:T(8,128)(2,1)S(1)} %collective-permute-done.4.refs_2_), channel_id=1, source_target_pairs={{0,1},{1,0},{2,3},{3,2},{4,5},{5,4},{6,7},{7,6},{8,9},{9,8},{10,11... | collective-permute-start | bytes 393224 | tf_op jit(solution)/shard_map/ppermute | solution.py:529
  24.8 1.5 %collective-permute-start.9 = (bf16[4,64,256]{2,1,0:T(8,128)(2,1)S(1)}, bf16[4,64,256]{2,1,0:T(8,128)(2,1)S(1)}, u32[]{:S(2)}, u32[]{:S(2)}) collective-permute-start(bf16[4,64,256]{2,1,0:T(8,128)(2,1)S(1)} %collective-permute-done.5.refs_3_), channel_id=1, source_target_pairs={{0,1},{1,0},{2,3},{3,2},{4,5},{5,4},{6,7},{7,6},{8,9},{9,8},{10,11... | collective-permute-start | bytes 393224 | tf_op jit(solution)/shard_map/ppermute | solution.py:529
  56.4 18.6 %all-to-all-start = ((bf16[32,4,8,256]{3,2,1,0:T(8,128)(2,1)}), bf16[32,4,8,256]{3,2,1,0:T(8,128)(2,1)S(1)}, u32[]{:S(2)}, u32[]{:S(2)}) async-start(bf16[32,4,8,256]{3,2,1,0:T(8,128)(2,1)} %get-tuple-element.32), calls=%async_computation | async-start | bytes 1048576 | tf_op jit(solution)/shard_map/all_to_all | solution.py:578
  61.6 37.2 %copy-start.3 = (s32[256]{0:T(256)S(1)}, s32[256]{0:T(256)}, u32[]{:S(2)}) copy-start(s32[256]{0:T(256)} %param.14) | copy-start | bytes 3076
  61.6 38.2 %copy-start.1 = (bf16[1024,128]{1,0:T(8,128)(2,1)S(1)}, bf16[1024,128]{1,0:T(8,128)(2,1)}, u32[]{:S(2)}) copy-start(bf16[1024,128]{1,0:T(8,128)(2,1)} %refs_12_.1) | copy-start | bytes 786436
  75.1 37.5 %copy-start = (bf16[8,256,128]{2,1,0:T(8,128)(2,1)S(1)}, bf16[8,256,128]{2,1,0:T(8,128)(2,1)}, u32[]{:S(2)}) copy-start(bf16[8,256,128]{2,1,0:T(8,128)(2,1)} %pair_ref.3) | copy-start | bytes 1572868
  84.1 6.9 %collective-permute-start.14 = (bf16[256,256]{1,0:T(8,128)(2,1)S(1)}, bf16[256,256]{1,0:T(8,128)(2,1)S(1)}, u32[]{:S(2)}, u32[]{:S(2)}) collective-permute-start(bf16[256,256]{1,0:T(8,128)(2,1)S(1)} %get-tuple-element.39.refs_4_), channel_id=1, source_target_pairs={{0,8},{1,9},{2,10},{3,11},{4,12},{5,13},{6,14},{7,15},{8,0},{9,1},... | collective-permute-start | bytes 393224 | tf_op jit(solution)/shard_map/ppermute | solution.py:529
  85.4 12.4 %collective-permute-start.16 = (bf16[256,256]{1,0:T(8,128)(2,1)S(1)}, bf16[256,256]{1,0:T(8,128)(2,1)S(1)}, u32[]{:S(2)}, u32[]{:S(2)}) collective-permute-start(bf16[256,256]{1,0:T(8,128)(2,1)S(1)} %get-tuple-element.39.refs_4_), channel_id=1, source_target_pairs={{0,16},{1,17},{2,18},{3,19},{4,20},{5,21},{6,22},{7,23},{8,24},{9,... | collective-permute-start | bytes 393224 | tf_op jit(solution)/shard_map/ppermute | solution.py:529
  85.8 12.0 %collective-permute-start.18 = (bf16[256,256]{1,0:T(8,128)(2,1)S(1)}, bf16[256,256]{1,0:T(8,128)(2,1)S(1)}, u32[]{:S(2)}, u32[]{:S(2)}) collective-permute-start(bf16[256,256]{1,0:T(8,128)(2,1)S(1)} %get-tuple-element.39.refs_4_), channel_id=1, source_target_pairs={{0,24},{1,25},{2,26},{3,27},{4,28},{5,29},{6,30},{7,31},{8,16},{9,... | collective-permute-start | bytes 393224 | tf_op jit(solution)/shard_map/ppermute | solution.py:529
  88.5 9.8 %collective-permute-start.10 = (bf16[256,256]{1,0:T(8,128)(2,1)S(1)}, bf16[256,256]{1,0:T(8,128)(2,1)S(1)}, u32[]{:S(2)}, u32[]{:S(2)}) collective-permute-start(bf16[256,256]{1,0:T(8,128)(2,1)S(1)} %get-tuple-element.38.refs_0_), channel_id=1, source_target_pairs={{0,2},{1,3},{2,0},{3,1},{4,6},{5,7},{6,4},{7,5},{8,10},{9,11},{10,... | collective-permute-start | bytes 393224 | tf_op jit(solution)/shard_map/ppermute | solution.py:529
  89.4 8.9 %collective-permute-start.11 = (bf16[256,256]{1,0:T(8,128)(2,1)S(1)}, bf16[256,256]{1,0:T(8,128)(2,1)S(1)}, u32[]{:S(2)}, u32[]{:S(2)}) collective-permute-start(bf16[256,256]{1,0:T(8,128)(2,1)S(1)} %get-tuple-element.38.refs_0_), channel_id=1, source_target_pairs={{0,4},{1,5},{2,6},{3,7},{4,0},{5,1},{6,2},{7,3},{8,12},{9,13},{10,... | collective-permute-start | bytes 393224 | tf_op jit(solution)/shard_map/ppermute | solution.py:529
  91.0 7.8 %collective-permute-start.12 = (bf16[256,256]{1,0:T(8,128)(2,1)S(1)}, bf16[256,256]{1,0:T(8,128)(2,1)S(1)}, u32[]{:S(2)}, u32[]{:S(2)}) collective-permute-start(bf16[256,256]{1,0:T(8,128)(2,1)S(1)} %get-tuple-element.38.refs_0_), channel_id=1, source_target_pairs={{0,6},{1,7},{2,4},{3,5},{4,2},{5,3},{6,0},{7,1},{8,14},{9,15},{10,... | collective-permute-start | bytes 393224 | tf_op jit(solution)/shard_map/ppermute | solution.py:529
  97.8 1.3 %collective-permute-start.13 = (bf16[256,256]{1,0:T(8,128)(2,1)S(1)}, bf16[256,256]{1,0:T(8,128)(2,1)S(1)}, u32[]{:S(2)}, u32[]{:S(2)}) collective-permute-start(bf16[256,256]{1,0:T(8,128)(2,1)S(1)} %get-tuple-element.39.refs_4_), channel_id=1, source_target_pairs={{0,1},{1,0},{2,3},{3,2},{4,5},{5,4},{6,7},{7,6},{8,9},{9,8},{10,11... | collective-permute-start | bytes 393224 | tf_op jit(solution)/shard_map/ppermute | solution.py:529
  97.8 1.5 %collective-permute-start.15 = (bf16[256,256]{1,0:T(8,128)(2,1)S(1)}, bf16[256,256]{1,0:T(8,128)(2,1)S(1)}, u32[]{:S(2)}, u32[]{:S(2)}) collective-permute-start(bf16[256,256]{1,0:T(8,128)(2,1)S(1)} %collective-permute-done.14.refs_6_), channel_id=1, source_target_pairs={{0,1},{1,0},{2,3},{3,2},{4,5},{5,4},{6,7},{7,6},{8,9},{9,8},{10,11... | collective-permute-start | bytes 393224 | tf_op jit(solution)/shard_map/ppermute | solution.py:529
  98.3 1.3 %collective-permute-start.17 = (bf16[256,256]{1,0:T(8,128)(2,1)S(1)}, bf16[256,256]{1,0:T(8,128)(2,1)S(1)}, u32[]{:S(2)}, u32[]{:S(2)}) collective-permute-start(bf16[256,256]{1,0:T(8,128)(2,1)S(1)} %collective-permute-done.16.refs_8_), channel_id=1, source_target_pairs={{0,1},{1,0},{2,3},{3,2},{4,5},{5,4},{6,7},{7,6},{8,9},{9,8},{10,11... | collective-permute-start | bytes 393224 | tf_op jit(solution)/shard_map/ppermute | solution.py:529
  98.4 1.5 %collective-permute-start.19 = (bf16[256,256]{1,0:T(8,128)(2,1)S(1)}, bf16[256,256]{1,0:T(8,128)(2,1)S(1)}, u32[]{:S(2)}, u32[]{:S(2)}) collective-permute-start(bf16[256,256]{1,0:T(8,128)(2,1)S(1)} %collective-permute-done.18.refs_10_), channel_id=1, source_target_pairs={{0,1},{1,0},{2,3},{3,2},{4,5},{5,4},{6,7},{7,6},{8,9},{9,8},{10,11... | collective-permute-start | bytes 393224 | tf_op jit(solution)/shard_map/ppermute | solution.py:529
  103.5 6.4 %collective-permute-start.20 = (bf16[8,64,128]{2,1,0:T(8,128)(2,1)S(1)}, bf16[8,64,128]{2,1,0:T(8,128)(2,1)S(1)}, u32[]{:S(2)}, u32[]{:S(2)}) collective-permute-start(bf16[8,64,128]{2,1,0:T(8,128)(2,1)S(1)} %get-tuple-element.41), channel_id=1, source_target_pairs={{0,2},{1,3},{2,0},{3,1},{4,6},{5,7},{6,4},{7,5},{8,10},{9,11},{10,... | collective-permute-start | bytes 393224 | tf_op jit(solution)/shard_map/ppermute | solution.py:529
  104.3 8.3 %collective-permute-start.21 = (bf16[8,64,128]{2,1,0:T(8,128)(2,1)S(1)}, bf16[8,64,128]{2,1,0:T(8,128)(2,1)S(1)}, u32[]{:S(2)}, u32[]{:S(2)}) collective-permute-start(bf16[8,64,128]{2,1,0:T(8,128)(2,1)S(1)} %get-tuple-element.42), channel_id=1, source_target_pairs={{0,4},{1,5},{2,6},{3,7},{4,0},{5,1},{6,2},{7,3},{8,12},{9,13},{10,... | collective-permute-start | bytes 393224 | tf_op jit(solution)/shard_map/ppermute | solution.py:529
  105.3 7.3 %collective-permute-start.22 = (bf16[8,64,128]{2,1,0:T(8,128)(2,1)S(1)}, bf16[8,64,128]{2,1,0:T(8,128)(2,1)S(1)}, u32[]{:S(2)}, u32[]{:S(2)}) collective-permute-start(bf16[8,64,128]{2,1,0:T(8,128)(2,1)S(1)} %get-tuple-element.43), channel_id=1, source_target_pairs={{0,6},{1,7},{2,4},{3,5},{4,2},{5,3},{6,0},{7,1},{8,14},{9,15},{10,... | collective-permute-start | bytes 393224 | tf_op jit(solution)/shard_map/ppermute | solution.py:529

commit v5 on v4

--- a/solution.py
+++ b/solution.py
@@ -183,8 +183,8 @@
     return jnp.concatenate([held[t] for t in range(held.shape[0])], axis=1)
 
 
-def in_hbm(*arrays):
-    return [pltpu.with_memory_space_constraint(a, pltpu.HBM) for a in arrays]
+def in_vmem(*arrays):
+    return [pltpu.with_memory_space_constraint(a, pltpu.VMEM) for a in arrays]
 
 
 def head_lanes(length):
@@ -227,63 +227,37 @@
 
 def bias_kernel(pair_ref, weight_ref, out_ref, held):
     rows, cols, width = pair_ref.shape
-    total = out_ref.shape[0] // ATTN_HEAD_COUNT
-    step = pl.program_id(0)
     normed = layer_normalize(pair_ref[...].astype(F32)).astype(BF16).reshape(rows * cols, width)
     bias = nt_dot(weight_ref[...], normed) * LOG2E
     for i in range(rows):
-        store_strided(held, step * rows + i, total, bias[:, i * cols : (i + 1) * cols])
-
-    @pl.when(step == pl.num_programs(0) - 1)
-    def _():
-        out_ref[...] = joined_tiles(held).astype(BF16)
+        store_strided(held, i, rows, bias[:, i * cols : (i + 1) * cols])
+    out_ref[...] = joined_tiles(held).astype(BF16)
 
 
 def pair_bias_block(pair_rep, bias_weight):
     rows, cols, width = pair_rep.shape
     out = jax.ShapeDtypeStruct((ATTN_HEAD_COUNT * rows, cols), BF16)
-    step = 2
     weight = bias_weight.T
+    pinned = [pltpu.with_memory_space_constraint(a, pltpu.HBM) for a in (pair_rep, weight)]
     return pl.pallas_call(
         bias_kernel,
-        grid=(rows // step,),
-        in_specs=[
-            pl.BlockSpec((step, cols, width), lambda i: (i, 0, 0)),
-            full_spec(weight.shape),
-        ],
-        out_specs=full_spec(out.shape),
+        grid=(1,),
+        in_specs=[full_spec(pair_rep.shape), full_spec(weight.shape)],
+        out_specs=pl.BlockSpec(memory_space=pltpu.VMEM),
         out_shape=out,
         scratch_shapes=[tiled_scratch(*out.shape)],
         compiler_params=params(16),
         name="pair_bias",
-    )(*in_hbm(pair_rep, weight))
-
-
-def order_kernel(plan, me_ref, *refs):
-    parts, out_ref = refs[:-1], refs[-1]
-    for part, offsets in zip(parts, plan):
-        for z, offset in enumerate(offsets):
-            out_ref[me_ref[0] ^ offset] = part[z]
-
-
-def order_blocks(me, parts, plan):
-    vmem = pl.BlockSpec(memory_space=pltpu.VMEM)
-    shape = (len(parts) * parts[0].shape[0],) + parts[0].shape[1:]
-    return pl.pallas_call(
-        functools.partial(order_kernel, plan),
-        grid=(1,),
-        in_specs=[pl.BlockSpec(memory_space=pltpu.SMEM)] + [vmem] * len(parts),
-        out_specs=full_spec(shape),
-        out_shape=pltpu.HBM(shape, BF16),
-        compiler_params=params(8),
-        name="order_blocks",
-    )(me, *parts)
-
-
-def row_project_kernel(x_ref, weight_ref, q_ref, k_ref, v_ref, g_ref):
-    for s in range(x_ref.shape[0]):
+    )(*pinned)
+
+
+def row_project_kernel(x_ref, weight_ref, x_out, q_ref, k_ref, v_ref, g_ref):
+    step = x_ref.shape[0]
+    for s in range(step):
+        at = pl.program_id(0) * step + s
+        x_out[at] = x_ref[s]
         normed = layer_normalize(x_ref[s].astype(F32)).astype(BF16)
-        q_ref[s], k_ref[s], v_ref[s], g_ref[s] = project(normed, weight_ref)
+        q_ref[at], k_ref[at], v_ref[at], g_ref[at] = project(normed, weight_ref)
 
 
 def row_project(alignment, weight):
@@ -294,90 +268,79 @@
         row_project_kernel,
         grid=(seqs // step,),
         in_specs=[block, full_spec(weight.shape)],
-        out_specs=[block] * 4,
-        out_shape=[pltpu.HBM(alignment.shape, BF16)] * 3 + [pltpu.HBM(alignment.shape, F32)],
+        out_specs=[pl.BlockSpec(memory_space=pltpu.VMEM)] * 5,
+        out_shape=[pltpu.VMEM(alignment.shape, BF16)] * 4 + [pltpu.VMEM(alignment.shape, F32)],
         compiler_params=params(24),
         name="row_project",
-    )(*in_hbm(alignment, weight))
+    )(*[pltpu.with_memory_space_constraint(a, pltpu.HBM) for a in (alignment, weight)])
 
 
 def row_attend_kernel(
-    halves, x_ref, q_ref, k_ref, v_ref, g_ref, live_ref, out_w_ref, bias_ref, *rest
+    plan, step, me_ref, x_ref, q_ref, k_ref, v_ref, g_ref, live_ref, out_w_ref, *rest
 ):
-    outs, bias_all = rest[:-1], rest[-1]
+    bias_refs, out_ref, bias_all = rest[: len(plan)], rest[-2], rest[-1]
     heads, length, _ = bias_all.shape
-    parts = bias_ref.shape[0]
 
     @pl.when(pl.program_id(0) == 0)
     def _():
-        for owner in range(parts):
-            block = bias_ref[owner].astype(F32).reshape(heads, -1, length)
-            rows = block.shape[1]
-            bias_all[:, owner * rows : (owner + 1) * rows, :] = block
+        for bias_ref, offsets in zip(bias_refs, plan):
+            for z, offset in enumerate(offsets):
+                block = bias_ref[z].astype(F32).reshape(heads, -1, length)
+                rows = block.shape[1]
+                owner = me_ref[0] ^ offset
+                bias_all[:, pl.ds(pl.multiple_of(owner * rows, rows), rows), :] = block
 
     lanes = head_lanes(length)
     results = []
-    for s in range(halves):
+    parts, rows = out_ref.shape[0], out_ref.shape[1]
+    for s in range(step):
+        at = pl.program_id(0) * step + s
         heads_out = attend_block(
-            q_ref[s], k_ref[s], v_ref[s], live_ref[s], lanes, lambda h: bias_all[h]
+            q_ref[at], k_ref[at], v_ref[at], live_ref[at], lanes, lambda h: bias_all[h]
         )
-        heads_out = (heads_out * g_ref[s]).astype(BF16)
-        results.append(x_ref[s].astype(F32) + nn_dot(heads_out, out_w_ref[...]))
-    items = length // parts
-    first, second = (r.reshape(parts, items, -1) for r in results)
-    rolled_first = pltpu.roll(first, items // 2, 1)
-    rolled_second = pltpu.roll(second, items // 2, 1)
-    low = lax.broadcasted_iota(jnp.int32, first.shape, 1) < items // 2
-    outs[0][:, 0] = jnp.where(low, first, rolled_second).astype(BF16)
-    outs[1][:, 0] = jnp.where(low, rolled_first, second).astype(BF16)
-
-
-def row_attend(alignment, projected, live, out_weight, bias, halves):
-    seqs, length, width = alignment.shape
-    parts = bias.shape[0]
-    items = length // parts
-    step = halves
-    block = pl.BlockSpec((step, length, width), lambda i: (i, 0, 0))
-    out = (parts, seqs // step, items, width)
+        heads_out = (heads_out * g_ref[at]).astype(BF16)
+        total = x_ref[at].astype(F32) + nn_dot(heads_out, out_w_ref[...])
+        results.append(total.reshape(parts, 1, rows // step, total.shape[1]))
+    joined = jnp.concatenate(results, axis=1)
+    out_ref[...] = joined.reshape(out_ref.shape).astype(BF16)
+
+
+def row_attend(me, projected, live, out_weight, bias_parts, plan, parts):
+    seqs, length, width = projected[0].shape
+    rows = length // parts
+    step = 2
+    vmem = pl.BlockSpec(memory_space=pltpu.VMEM)
+    operands = in_vmem(*projected, live, out_weight, *bias_parts)
     return pl.pallas_call(
-        functools.partial(row_attend_kernel, halves),
+        functools.partial(row_attend_kernel, plan, step),
         grid=(seqs // step,),
-        in_specs=[block] * 5
-        + [pl.BlockSpec((step, length, LANES), lambda i: (i, 0, 0)), full_spec(out_weight.shape)]
-        + [full_spec(bias.shape)],
-        out_specs=[pl.BlockSpec((parts, 1, items, width), lambda i: (0, i, 0, 0))] * halves,
-        out_shape=[pltpu.HBM(out, BF16)] * halves,
+        in_specs=[pl.BlockSpec(memory_space=pltpu.SMEM)] + [vmem] * len(operands),
+        out_specs=pl.BlockSpec((parts, step * rows, width), lambda i: (0, i, 0)),
+        out_shape=jax.ShapeDtypeStruct((parts, seqs * rows, width), BF16),
         scratch_shapes=[pltpu.VMEM((ATTN_HEAD_COUNT, length, length), F32)],
-        compiler_params=params(28),
+        compiler_params=params(24),
         name="row_attend",
-    )(*in_hbm(alignment, *projected, live, out_weight, bias))
+    )(me, *operands)
 
 
 def column_kernel(
-    first, items, each, x_ref, live_ref, mask_ref, weight_ref, out_w_ref, factor_ref, *rest
+    items, each, x_ref, live_ref, mask_ref, weight_ref, out_w_ref, factor_ref,
+    out_ref, left_ref, right_ref, held, right_held,
 ):
-    before, rest = rest[:-7], rest[-7:]
-    out_ref, left_ref, right_ref, x_held, held, left_held, right_held = rest
     step = pl.program_id(0)
-    length = out_ref.shape[0]
-    here = x_held.shape[1] // length
+    total_rows = held.shape[1]
+    length = total_rows // items
 
     @pl.when(step == 0)
     def _():
         for t in range(held.shape[0]):
-            cut = slice(t * LANES, (t + 1) * LANES)
-            x_held[t] = x_ref[:, :, :, cut].astype(F32).reshape(x_held.shape[1:])
-            if before:
-                held[t] = before[0][:, :, cut].astype(F32).reshape(held.shape[1:])
-                right_held[t] = before[2][:, cut].astype(F32)
-        if before:
-            left_held[...] = before[1][...]
+            part = x_ref[:, :, t * LANES : (t + 1) * LANES].astype(F32)
+            held[t] = part.reshape(total_rows, LANES)
 
     lanes = head_lanes(length)
     for n in range(each):
-        inner = step * each + n
-        item = inner + first
-        current = load_strided(x_held, inner, here, length)
+        item = step * each + n
+        current = load_strided(held, item, items, length)
         normed = layer_normalize(current).astype(BF16)
         query, key, value, gate = project(normed, weight_ref)
         heads_out = attend_block(query, key, value, live_ref[n], lanes, None)
@@ -387,53 +350,43 @@
         normed = layer_normalize(updated).astype(BF16)
         factors = nt_dot(factor_ref[...], normed) * mask_ref[pl.ds(item, 1), :]
         left_at = pl.ds(pl.multiple_of(item * FACTOR_CHANNELS, FACTOR_CHANNELS), FACTOR_CHANNELS)
-        left_held[left_at, :] = factors[:FACTOR_CHANNELS].astype(BF16)
+        left_ref[left_at, :] = factors[:FACTOR_CHANNELS].astype(BF16)
         store_strided(right_held, item, items, factors[FACTOR_CHANNELS:])
 
-    @pl.when(step == pl.num_programs(0) - 1)
+    @pl.when(step == items // each - 1)
     def _():
         for t in range(held.shape[0]):
             part = held[t].reshape(out_ref.shape[:2] + (LANES,))
             out_ref[:, :, t * LANES : (t + 1) * LANES] = part.astype(BF16)
         right_ref[...] = joined_tiles(right_held).astype(BF16)
-        left_ref[...] = left_held[...]
-
-
-def column_attend(moved, live, mask_rows, weight, out_weight, factor_t, half, halves, before):
-    width = moved.shape[-1]
-    items = mask_rows.shape[0]
-    here = items // halves
-    rows = math.prod(moved.shape[:-1])
-    length = rows // here
-    each = 2
-    start = half * here
+
+
+def column_attend(moved, live, mask_rows, weight, out_weight, factor_weight, items):
+    width = moved.shape[2]
+    total_rows = moved.shape[0] * moved.shape[1]
+    length = total_rows // items
+    factor_t = factor_weight.T
+    each = 4
     side = (items * FACTOR_CHANNELS, length)
-    last = half == halves - 1
-    outs = [pltpu.HBM((length, items, width), BF16)]
-    outs += [jax.ShapeDtypeStruct(side, BF16) if last else pltpu.HBM(side, BF16)] * 2
+    left = right = jax.ShapeDtypeStruct(side, BF16)
+    out = jax.ShapeDtypeStruct((length, items, width), BF16)
     return pl.pallas_call(
-        functools.partial(column_kernel, start, items, each),
-        grid=(here // each,),
+        functools.partial(column_kernel, items, each),
+        grid=(items // each,),
         in_specs=[
             full_spec(moved.shape),
-            pl.BlockSpec((each, length, LANES), lambda i: (i + start // each, 0, 0)),
+            pl.BlockSpec((each, length, LANES), lambda i: (i, 0, 0)),
             full_spec(mask_rows.shape),
             full_spec(weight.shape),
             full_spec(out_weight.shape),
             full_spec(factor_t.shape),
-        ]
-        + [full_spec(b.shape) for b in before],
-        out_specs=[full_spec(o.shape) for o in outs],
-        out_shape=outs,
-        scratch_shapes=[
-            tiled_scratch(rows, width),
-            tiled_scratch(length * items, width),
-            pltpu.VMEM(side, BF16),
-            tiled_scratch(*side),
         ],
+        out_specs=[full_spec(out.shape)] + [pl.BlockSpec(memory_space=pltpu.VMEM)] * 2,
+        out_shape=[out, left, right],
+        scratch_shapes=[tiled_scratch(total_rows, width), tiled_scratch(*side)],
         compiler_params=params(28),
         name="column_attend",
-    )(moved, *in_hbm(live, mask_rows, weight, out_weight, factor_t, *before))
+    )(moved, live, mask_rows, weight, out_weight, factor_t)
 
 
 def outer_kernel(group, outer, items, *refs):
@@ -549,23 +502,23 @@
     seq_dev = alignment.shape[0]
     items = pair_rep.shape[0]
     total_seqs, total_res = align_mask.shape
-    halves = 2
-
-    projected = list(row_project(alignment, row_proj_weight))
-    bias = pair_bias_block(pair_rep, bias_weight)
-    column = jnp.stack([exchange(bias, count, z) for z in line])
-    bias_parts = [exchange(column, count, k) for k in plane]
-    *bias_parts, query = lax.optimization_barrier((*bias_parts, projected[0]))
-    projected = [query] + projected[1:]
-    plan = [[k | z for z in line] for k in plane]
-    bias_parts += [exchange(part, count, 1) for part in bias_parts]
-    plan += [[offset | 1 for offset in offsets] for offsets in plan]
-    bias = order_blocks(me, bias_parts, plan)
 
     own_seqs = lax.dynamic_slice_in_dim(align_mask, dap_index * seq_dev, seq_dev, 0)
     own_res = lax.dynamic_slice_in_dim(align_mask, dap_index * items, items, 1)
     row_live = jnp.broadcast_to(own_seqs.astype(BF16)[:, :, None], (seq_dev, total_res, LANES))
     col_live = jnp.broadcast_to(own_res.T.astype(BF16)[:, :, None], (items, total_seqs, LANES))
+
+    bias = pair_bias_block(pair_rep, bias_weight)
+    projected = list(row_project(alignment, row_proj_weight))
+    column = [exchange(bias, count, z) for z in line]
+    *column, projected[0] = lax.optimization_barrier((*column, projected[0]))
+    column = jnp.stack(column)
+    bias_parts = [exchange(column, count, k) for k in plane]
+    *bias_parts, row_live = lax.optimization_barrier((*bias_parts, row_live))
+    plan = [[k | z for z in line] for k in plane]
+    bias_parts += [exchange(part, count, 1) for part in bias_parts]
+    plan += [[offset | 1 for offset in offsets] for offsets in plan]
+
     counts = jnp.einsum(
         "si,sj->ji", own_res.astype(BF16), align_mask.astype(BF16), preferred_element_type=F32
     )
@@ -574,22 +527,17 @@
     scale = live_rows[None, :] * res_float[:, None] / (counts + count_eps)
     mask_rows = own_res.T.astype(F32)
 
-    rows = row_attend(alignment, projected, row_live, row_out_weight, bias, halves)
-    moved = [lax.all_to_all(r, "dap", split_axis=0, concat_axis=0, tiled=True) for r in rows]
-    done = ()
-    for half in range(halves):
-        done = column_attend(
-            moved[half],
-            col_live,
-            mask_rows,
-            column_proj_weight,
-            column_out_weight,
-            outer_factor_weight.T,
-            half,
-            halves,
-            done,
-        )
-    updated, left, right = done
+    rows = row_attend(me, projected, row_live, row_out_weight, bias_parts, plan, count)
+    moved = lax.all_to_all(rows, "dap", split_axis=0, concat_axis=0, tiled=True)
+    updated, left, right = column_attend(
+        moved,
+        col_live,
+        mask_rows,
+        column_proj_weight,
+        column_out_weight,
+        outer_factor_weight,
+        items,
+    )
     rights = [exchange(right, count, z) for z in line]
     rights = [part for own in rights for part in (own, exchange(own, count, 1))]
     lefts = [exchange(left, count, k) for k in plane]

time: 114 us -> 114 us (level)
  waiting for transfers between devices: 23.1 us -> 43.4 us
  blocking collectives: 18.4 us -> 0 us
  Pallas kernels: 41.7 us -> 32.1 us
  local copies, waits for them, and re-layouts: 2.51 us -> 7.55 us
  starting transfers between devices: 26.6 us -> 28.4 us
    all_to_all x1, waiting for transfers between devices: 4.91 us -> 25.8 us  [per_device_fast(): moved = lax.all_to_all(rows, 'dap', split_axis=0, concat_axis=0, tiled=True)]
    all_to_all x1 -> x0, blocking collectives: 18.4 us -> none  [per_device_fast(): lax.all_to_all(r, 'dap', split_axis=0, concat_axis=0, tiled=True)]
    pallas_call x5 -> x3, Pallas kernels: 31.2 us -> 22.9 us  [the longest x1 12.7 us: column_attend(): pl.pallas_call(functools.partial(column_kernel, items, each), grid=(items...]
    unnamed x9 -> x31, local copies, waits for them, and re-layouts: 0.07 us -> 6.7 us
    pallas_call x1, Pallas kernels: 5.58 us -> 4.27 us  [row_project(): pl.pallas_call(row_project_kernel, grid=(seqs // step,), in_specs=[block,...]
    all_to_all x1, starting transfers between devices: 3.26 us -> 4.55 us  [per_device_fast(): moved = lax.all_to_all(rows, 'dap', split_axis=0, concat_axis=0, tiled=True)]
  transfers between devices with their start and end apart: 24 -> 24, of which waited for: 15 -> 14; matrix products, arithmetic and copies ran while one was open for 2% -> 1% of each run, Pallas kernels for 12% -> 4%
where the time goes in v5:
time: 114 us; the launch traced here: 113 us
  waiting for transfers between devices  43.4 us (38%)
  Pallas kernels  32.1 us (28%)
  starting transfers between devices  28.4 us (25%)
  local copies, waits for them, and re-layouts  7.55 us (7%)
    all_to_all x1, waiting for transfers between devices, per_device_fast(): moved = lax.all_to_all(rows, 'dap', split_axis=0, concat_axis=0, tiled=True)  25.8 us
    ppermute x23, starting transfers between devices, exchange(): return lax.ppermute(block, 'dap', [(i, i ^ offset) for i in range(count)])  23.9 us
    ppermute x23, waiting for transfers between devices, exchange(): return lax.ppermute(block, 'dap', [(i, i ^ offset) for i in range(count)])  17.5 us
    pallas_call x1, Pallas kernels, column_attend(): pl.pallas_call(functools.partial(column_kernel, items, each), grid=(items...  12.7 us
    pallas_call x1, Pallas kernels, row_attend(): pl.pallas_call(functools.partial(row_attend_kernel, plan, step), grid=(se...  8.42 us
    unnamed x31, local copies, waits for them, and re-layouts  6.7 us
    all_to_all x1, starting transfers between devices, per_device_fast(): moved = lax.all_to_all(rows, 'dap', split_axis=0, concat_axis=0, tiled=True)  4.55 us
    pallas_call x1, Pallas kernels, row_project(): pl.pallas_call(row_project_kernel, grid=(seqs // step,), in_specs=[block,...  4.27 us
  transfers between devices with their start and end apart: 24, of which 14 were waited for; matrix products, arithmetic and copies ran while one was open for 1% of the time, Pallas kernels for 4%

profile of v5, /device:TPU:0, one launch (start us, length us, event | category | flops | bytes accessed | tf_op | source)
XLA Modules:
  0.0 113.3 jit_solution(13767584964734370403)
XLA Ops:
  0.6 1.8 %pair_bias.1 = bf16[64,256]{1,0:T(8,128)(2,1)S(1)} custom-call(bf16[8,256,128]{2,1,0:T(8,128)(2,1)} %pair_ref.3, bf16[8,128]{1,0:T(8,128)(2,1)} %bitcast.20), custom_call_target="tpu_custom_call" | custom-call | tf_op jit(solution)/shard_map/pair_bias/pallas_call | solution.py:242
  2.5 3.1 %collective-permute-start = (bf16[64,256]{1,0:T(8,128)(2,1)S(1)}, bf16[64,256]{1,0:T(8,128)(2,1)S(1)}, u32[]{:S(2)}, u32[]{:S(2)}) collective-permute-start(bf16[64,256]{1,0:T(8,128)(2,1)S(1)} %pair_bias.1), channel_id=1, source_target_pairs={{0,8},{1,9},{2,10},{3,11},{4,12},{5,13},{6,14},{7,15},{8,0},{9,1},... | collective-permute-start | bytes 98312 | tf_op jit(solution)/shard_map/ppermute | solution.py:482
  5.6 2.6 %collective-permute-start.1 = (bf16[64,256]{1,0:T(8,128)(2,1)S(1)}, bf16[64,256]{1,0:T(8,128)(2,1)S(1)}, u32[]{:S(2)}, u32[]{:S(2)}) collective-permute-start(bf16[64,256]{1,0:T(8,128)(2,1)S(1)} %pair_bias.1), channel_id=1, source_target_pairs={{0,16},{1,17},{2,18},{3,19},{4,20},{5,21},{6,22},{7,23},{8,24},{9,... | collective-permute-start | bytes 98312 | tf_op jit(solution)/shard_map/ppermute | solution.py:482
  8.2 4.3 %row_project.1 = (bf16[8,256,256]{2,1,0:T(8,128)(2,1)S(1)}, bf16[8,256,256]{2,1,0:T(8,128)(2,1)S(1)}, bf16[8,256,256]{2,1,0:T(8,128)(2,1)S(1)}, bf16[8,256,256]{2,1,0:T(8,128)(2,1)S(1)}, f32[8,256,256]{2,1,0:T(8,128)S(1)}) custom-call(bf16[8,256,256]{2,1,0:T(8,128)(2,1)} %x_ref.1, bf16[4,256,256]{2,1,0:T(8,128)(2,1)} %weight_ref.2), custom_call_target="tpu_custom_call" | custom-call | tf_op jit(solution)/shard_map/row_project/pallas_call | solution.py:267
  12.4 1.0 copy-done.1
  13.4 1.0 copy-done.3
  14.4 1.0 copy-done.5
  15.4 1.8 %collective-permute-start.3 = (bf16[4,64,256]{2,1,0:T(8,128)(2,1)S(1)}, bf16[4,64,256]{2,1,0:T(8,128)(2,1)S(1)}, u32[]{:S(2)}, u32[]{:S(2)}) collective-permute-start(bf16[4,64,256]{2,1,0:T(8,128)(2,1)S(1)} %pad_maximum_fusion.rest_0_), channel_id=1, source_target_pairs={{0,2},{1,3},{2,0},{3,1},{4,6},{5,7},{6,4},{7,5},{8,10},{9,11},{10,... | collective-permute-start | bytes 393224 | tf_op jit(solution)/shard_map/ppermute | solution.py:482
  17.2 1.5 %collective-permute-start.4 = (bf16[4,64,256]{2,1,0:T(8,128)(2,1)S(1)}, bf16[4,64,256]{2,1,0:T(8,128)(2,1)}, u32[]{:S(2)}, u32[]{:S(2)}) collective-permute-start(bf16[4,64,256]{2,1,0:T(8,128)(2,1)S(1)} %pad_maximum_fusion.rest_0_), channel_id=1, source_target_pairs={{0,4},{1,5},{2,6},{3,7},{4,0},{5,1},{6,2},{7,3},{8,12},{9,13},{10,... | collective-permute-start | bytes 393224 | tf_op jit(solution)/shard_map/ppermute | solution.py:482
  19.7 1.5 %collective-permute-done.3.rest_1_ = bf16[4,64,256]{2,1,0:T(8,128)(2,1)S(1)} collective-permute-done((bf16[4,64,256]{2,1,0:T(8,128)(2,1)S(1)}, bf16[4,64,256]{2,1,0:T(8,128)(2,1)S(1)}, u32[]{:S(2)}, u32[]{:S(2)}) %collective-permute-start.3) | collective-permute-done | bytes 131104 | tf_op jit(solution)/shard_map/ppermute | solution.py:482
  21.2 3.8 %collective-permute-done.4.rest_2_ = bf16[4,64,256]{2,1,0:T(8,128)(2,1)} collective-permute-done((bf16[4,64,256]{2,1,0:T(8,128)(2,1)S(1)}, bf16[4,64,256]{2,1,0:T(8,128)(2,1)}, u32[]{:S(2)}, u32[]{:S(2)}) %collective-permute-start.4) | collective-permute-done | bytes 131104 | tf_op jit(solution)/shard_map/ppermute | solution.py:482
  27.7 1.2 %copy-done.2 = bf16[8,256,256]{2,1,0:T(8,128)(2,1)S(1)} copy-done((bf16[8,256,256]{2,1,0:T(8,128)(2,1)S(1)}, bf16[8,256,256]{2,1,0:T(8,128)(2,1)}, u32[]{:S(2)}) %copy-start.2) | copy-done | bytes 1048600
  28.9 1.2 %copy-done.4 = bf16[8,256,256]{2,1,0:T(8,128)(2,1)S(1)} copy-done((bf16[8,256,256]{2,1,0:T(8,128)(2,1)S(1)}, bf16[8,256,256]{2,1,0:T(8,128)(2,1)}, u32[]{:S(2)}) %copy-start.4) | copy-done | bytes 1048600
  30.1 1.2 %copy-done.6 = bf16[8,256,256]{2,1,0:T(8,128)(2,1)S(1)} copy-done((bf16[8,256,256]{2,1,0:T(8,128)(2,1)S(1)}, bf16[8,256,256]{2,1,0:T(8,128)(2,1)}, u32[]{:S(2)}) %copy-start.6) | copy-done | bytes 1048600
  31.4 8.4 %row_attend.1 = bf16[32,64,256]{2,1,0:T(8,128)(2,1)} custom-call(s32[1]{0:T(128)} %bitcast.me_ref, bf16[8,256,256]{2,1,0:T(8,128)(2,1)S(1)} %get-tuple-element.25.x_ref, bf16[8,256,256]{2,1,0:T(8,128)(2,1)S(1)} %copy-done.2, bf16[8,256,256]{2,1,0:T(8,128)(2,1)S(1)} %copy-done.4, bf16[8,256,256]{2,1,0:T(8,128)(2,1)S(1)} %copy-done.6, ...), custom_call_target="tpu_custom_call" | custom-call | tf_op jit(solution)/shard_map/row_attend/pallas_call | solution.py:314
  39.8 4.5 %all-to-all-start = ((bf16[32,64,256]{2,1,0:T(8,128)(2,1)}), bf16[32,64,256]{2,1,0:T(8,128)(2,1)S(1)}, u32[]{:S(2)}, u32[]{:S(2)}) async-start(bf16[32,64,256]{2,1,0:T(8,128)(2,1)} %row_attend.1), calls=%async_computation | async-start | bytes 2097152 | tf_op jit(solution)/shard_map/all_to_all | solution.py:531
  44.6 25.8 %all-to-all-done.x_ref = bf16[32,64,256]{2,1,0:T(8,128)(2,1)S(1)} async-done(((bf16[32,64,256]{2,1,0:T(8,128)(2,1)}), bf16[32,64,256]{2,1,0:T(8,128)(2,1)S(1)}, u32[]{:S(2)}, u32[]{:S(2)}) %all-to-all-start) | async-done | bytes 1048608 | tf_op jit(solution)/shard_map/all_to_all | solution.py:531
  70.8 12.7 %column_attend.1 = (bf16[256,8,256]{2,1,0:T(8,128)(2,1)}, bf16[256,256]{1,0:T(8,128)(2,1)S(1)}, bf16[256,256]{1,0:T(8,128)(2,1)S(1)}) custom-call(bf16[32,64,256]{2,1,0:T(8,128)(2,1)S(1)} %all-to-all-done.x_ref, bf16[8,256,128]{2,1,0:T(8,128)(2,1)S(1)} %broadcast_in_dim.5.live_ref, f32[8,256]{1,0:T(8,128)S(1)} %get-tuple-element.46.mask_ref, ...), custom_call_target="tpu_custom_call" | custom-call | tf_op jit(solution)/shard_map/column_attend/pallas_call | solution.py:373
  83.5 0.8 collective-permute-start.14
  84.2 1.1 collective-permute-start.16
  85.3 2.5 %collective-permute-start.18 = (bf16[256,256]{1,0:T(8,128)(2,1)S(1)}, bf16[256,256]{1,0:T(8,128)(2,1)S(1)}, u32[]{:S(2)}, u32[]{:S(2)}) collective-permute-start(bf16[256,256]{1,0:T(8,128)(2,1)S(1)} %get-tuple-element.41.refs_4_), channel_id=1, source_target_pairs={{0,24},{1,25},{2,26},{3,27},{4,28},{5,29},{6,30},{7,31},{8,16},{9,... | collective-permute-start | bytes 393224 | tf_op jit(solution)/shard_map/ppermute | solution.py:482
  87.9 1.4 %collective-permute-start.10 = (bf16[256,256]{1,0:T(8,128)(2,1)S(1)}, bf16[256,256]{1,0:T(8,128)(2,1)S(1)}, u32[]{:S(2)}, u32[]{:S(2)}) collective-permute-start(bf16[256,256]{1,0:T(8,128)(2,1)S(1)} %get-tuple-element.40.refs_0_), channel_id=1, source_target_pairs={{0,2},{1,3},{2,0},{3,1},{4,6},{5,7},{6,4},{7,5},{8,10},{9,11},{10,... | collective-permute-start | bytes 393224 | tf_op jit(solution)/shard_map/ppermute | solution.py:482
  89.3 1.5 %collective-permute-start.11 = (bf16[256,256]{1,0:T(8,128)(2,1)S(1)}, bf16[256,256]{1,0:T(8,128)(2,1)S(1)}, u32[]{:S(2)}, u32[]{:S(2)}) collective-permute-start(bf16[256,256]{1,0:T(8,128)(2,1)S(1)} %get-tuple-element.40.refs_0_), channel_id=1, source_target_pairs={{0,4},{1,5},{2,6},{3,7},{4,0},{5,1},{6,2},{7,3},{8,12},{9,13},{10,... | collective-permute-start | bytes 393224 | tf_op jit(solution)/shard_map/ppermute | solution.py:482
  90.8 1.6 %collective-permute-start.12 = (bf16[256,256]{1,0:T(8,128)(2,1)S(1)}, bf16[256,256]{1,0:T(8,128)(2,1)S(1)}, u32[]{:S(2)}, u32[]{:S(2)}) collective-permute-start(bf16[256,256]{1,0:T(8,128)(2,1)S(1)} %get-tuple-element.40.refs_0_), channel_id=1, source_target_pairs={{0,6},{1,7},{2,4},{3,5},{4,2},{5,3},{6,0},{7,1},{8,14},{9,15},{10,... | collective-permute-start | bytes 393224 | tf_op jit(solution)/shard_map/ppermute | solution.py:482
  92.5 4.7 %collective-permute-done.16.refs_8_ = bf16[256,256]{1,0:T(8,128)(2,1)S(1)} collective-permute-done((bf16[256,256]{1,0:T(8,128)(2,1)S(1)}, bf16[256,256]{1,0:T(8,128)(2,1)S(1)}, u32[]{:S(2)}, u32[]{:S(2)}) %collective-permute-start.16) | collective-permute-done | bytes 131104 | tf_op jit(solution)/shard_map/ppermute | solution.py:482
  99.2 3.7 %outer_product.1 = (bf16[8,64,128]{2,1,0:T(8,128)(2,1)S(1)}, bf16[8,64,128]{2,1,0:T(8,128)(2,1)S(1)}, bf16[8,64,128]{2,1,0:T(8,128)(2,1)S(1)}, bf16[8,64,128]{2,1,0:T(8,128)(2,1)S(1)}) custom-call(bf16[256,256]{1,0:T(8,128)(2,1)S(1)} %get-tuple-element.40.refs_0_, bf16[256,256]{1,0:T(8,128)(2,1)S(1)} %collective-permute-done.10.refs_1_, ...), custom_call_target="tpu_custom_call" | custom-call | tf_op jit(solution)/shard_map/outer_product/pallas_call | solution.py:434
  102.9 0.9 collective-permute-start.20
  103.7 1.3 %collective-permute-start.21 = (bf16[8,64,128]{2,1,0:T(8,128)(2,1)S(1)}, bf16[8,64,128]{2,1,0:T(8,128)(2,1)S(1)}, u32[]{:S(2)}, u32[]{:S(2)}) collective-permute-start(bf16[8,64,128]{2,1,0:T(8,128)(2,1)S(1)} %get-tuple-element.44), channel_id=1, source_target_pairs={{0,4},{1,5},{2,6},{3,7},{4,0},{5,1},{6,2},{7,3},{8,12},{9,13},{10,... | collective-permute-start | bytes 393224 | tf_op jit(solution)/shard_map/ppermute | solution.py:482
  105.1 1.4 %collective-permute-start.22 = (bf16[8,64,128]{2,1,0:T(8,128)(2,1)S(1)}, bf16[8,64,128]{2,1,0:T(8,128)(2,1)S(1)}, u32[]{:S(2)}, u32[]{:S(2)}) collective-permute-start(bf16[8,64,128]{2,1,0:T(8,128)(2,1)S(1)} %get-tuple-element.45), channel_id=1, source_target_pairs={{0,6},{1,7},{2,4},{3,5},{4,2},{5,3},{6,0},{7,1},{8,14},{9,15},{10,... | collective-permute-start | bytes 393224 | tf_op jit(solution)/shard_map/ppermute | solution.py:482
  106.7 2.6 %collective-permute-done.20.refs_1_ = bf16[8,64,128]{2,1,0:T(8,128)(2,1)S(1)} collective-permute-done((bf16[8,64,128]{2,1,0:T(8,128)(2,1)S(1)}, bf16[8,64,128]{2,1,0:T(8,128)(2,1)S(1)}, u32[]{:S(2)}, u32[]{:S(2)}) %collective-permute-start.20) | collective-permute-done | bytes 131104 | tf_op jit(solution)/shard_map/ppermute | solution.py:482
  109.3 2.7 %collective-permute-done.21.refs_2_ = bf16[8,64,128]{2,1,0:T(8,128)(2,1)S(1)} collective-permute-done((bf16[8,64,128]{2,1,0:T(8,128)(2,1)S(1)}, bf16[8,64,128]{2,1,0:T(8,128)(2,1)S(1)}, u32[]{:S(2)}, u32[]{:S(2)}) %collective-permute-start.21) | collective-permute-done | bytes 131104 | tf_op jit(solution)/shard_map/ppermute | solution.py:482
  112.0 1.2 %finish.1 = bf16[8,256,128]{2,1,0:T(8,128)(2,1)} custom-call(s32[1]{0:T(128)} %bitcast.me_ref, bf16[8,256,128]{2,1,0:T(8,128)(2,1)S(1)} %copy-done, f32[256,8]{1,0:T(8,128)S(1)} %fusion.1.scale_ref, bf16[8,64,128]{2,1,0:T(8,128)(2,1)S(1)} %get-tuple-element.42.refs_0_, bf16[8,64,128]{2,1,0:T(8,128)(2,1)S(1)} %collective-permute-done.20.refs_1_, ...), custom_call_target="tpu_custom_call" | custom-call | tf_op jit(solution)/shard_map/finish/pallas_call | solution.py:469
  (62 shorter events, 6.5 us)
Async XLA Ops:
  0.6 27.1 %copy-start.9 = (bf16[256,256]{1,0:T(8,128)(2,1)S(1)}, bf16[256,256]{1,0:T(8,128)(2,1)}, u32[]{:S(2)}) copy-start(bf16[256,256]{1,0:T(8,128)(2,1)} %out_w_ref.2) | copy-start | bytes 393220
  2.5 12.9 %collective-permute-start = (bf16[64,256]{1,0:T(8,128)(2,1)S(1)}, bf16[64,256]{1,0:T(8,128)(2,1)S(1)}, u32[]{:S(2)}, u32[]{:S(2)}) collective-permute-start(bf16[64,256]{1,0:T(8,128)(2,1)S(1)} %pair_bias.1), channel_id=1, source_target_pairs={{0,8},{1,9},{2,10},{3,11},{4,12},{5,13},{6,14},{7,15},{8,0},{9,1},... | collective-permute-start | bytes 98312 | tf_op jit(solution)/shard_map/ppermute | solution.py:482
  5.6 9.8 %collective-permute-start.1 = (bf16[64,256]{1,0:T(8,128)(2,1)S(1)}, bf16[64,256]{1,0:T(8,128)(2,1)S(1)}, u32[]{:S(2)}, u32[]{:S(2)}) collective-permute-start(bf16[64,256]{1,0:T(8,128)(2,1)S(1)} %pair_bias.1), channel_id=1, source_target_pairs={{0,16},{1,17},{2,18},{3,19},{4,20},{5,21},{6,22},{7,23},{8,24},{9,... | collective-permute-start | bytes 98312 | tf_op jit(solution)/shard_map/ppermute | solution.py:482
  8.2 7.2 %collective-permute-start.2 = (bf16[64,256]{1,0:T(8,128)(2,1)S(1)}, bf16[64,256]{1,0:T(8,128)(2,1)S(1)}, u32[]{:S(2)}, u32[]{:S(2)}) collective-permute-start(bf16[64,256]{1,0:T(8,128)(2,1)S(1)} %pair_bias.1), channel_id=1, source_target_pairs={{0,24},{1,25},{2,26},{3,27},{4,28},{5,29},{6,30},{7,31},{8,16},{9,... | collective-permute-start | bytes 98312 | tf_op jit(solution)/shard_map/ppermute | solution.py:482
  15.4 5.8 %collective-permute-start.3 = (bf16[4,64,256]{2,1,0:T(8,128)(2,1)S(1)}, bf16[4,64,256]{2,1,0:T(8,128)(2,1)S(1)}, u32[]{:S(2)}, u32[]{:S(2)}) collective-permute-start(bf16[4,64,256]{2,1,0:T(8,128)(2,1)S(1)} %pad_maximum_fusion.rest_0_), channel_id=1, source_target_pairs={{0,2},{1,3},{2,0},{3,1},{4,6},{5,7},{6,4},{7,5},{8,10},{9,11},{10,... | collective-permute-start | bytes 393224 | tf_op jit(solution)/shard_map/ppermute | solution.py:482
  17.2 7.8 %collective-permute-start.4 = (bf16[4,64,256]{2,1,0:T(8,128)(2,1)S(1)}, bf16[4,64,256]{2,1,0:T(8,128)(2,1)}, u32[]{:S(2)}, u32[]{:S(2)}) collective-permute-start(bf16[4,64,256]{2,1,0:T(8,128)(2,1)S(1)} %pad_maximum_fusion.rest_0_), channel_id=1, source_target_pairs={{0,4},{1,5},{2,6},{3,7},{4,0},{5,1},{6,2},{7,3},{8,12},{9,13},{10,... | collective-permute-start | bytes 393224 | tf_op jit(solution)/shard_map/ppermute | solution.py:482
  18.7 6.3 %collective-permute-start.5 = (bf16[4,64,256]{2,1,0:T(8,128)(2,1)S(1)}, bf16[4,64,256]{2,1,0:T(8,128)(2,1)}, u32[]{:S(2)}, u32[]{:S(2)}) collective-permute-start(bf16[4,64,256]{2,1,0:T(8,128)(2,1)S(1)} %pad_maximum_fusion.rest_0_), channel_id=1, source_target_pairs={{0,6},{1,7},{2,4},{3,5},{4,2},{5,3},{6,0},{7,1},{8,14},{9,15},{10,... | collective-permute-start | bytes 393224 | tf_op jit(solution)/shard_map/ppermute | solution.py:482
  25.4 1.4 %collective-permute-start.6 = (bf16[4,64,256]{2,1,0:T(8,128)(2,1)S(1)}, bf16[4,64,256]{2,1,0:T(8,128)(2,1)S(1)}, u32[]{:S(2)}, u32[]{:S(2)}) collective-permute-start(bf16[4,64,256]{2,1,0:T(8,128)(2,1)S(1)} %pad_maximum_fusion.rest_0_), channel_id=1, source_target_pairs={{0,1},{1,0},{2,3},{3,2},{4,5},{5,4},{6,7},{7,6},{8,9},{9,8},{10,11... | collective-permute-start | bytes 393224 | tf_op jit(solution)/shard_map/ppermute | solution.py:482
  25.4 1.5 %collective-permute-start.7 = (bf16[4,64,256]{2,1,0:T(8,128)(2,1)S(1)}, bf16[4,64,256]{2,1,0:T(8,128)(2,1)S(1)}, u32[]{:S(2)}, u32[]{:S(2)}) collective-permute-start(bf16[4,64,256]{2,1,0:T(8,128)(2,1)S(1)} %collective-permute-done.3.rest_1_), channel_id=1, source_target_pairs={{0,1},{1,0},{2,3},{3,2},{4,5},{5,4},{6,7},{7,6},{8,9},{9,8},{10,11... | collective-permute-start | bytes 393224 | tf_op jit(solution)/shard_map/ppermute | solution.py:482
  25.9 1.6 %collective-permute-start.8 = (bf16[4,64,256]{2,1,0:T(8,128)(2,1)}, bf16[4,64,256]{2,1,0:T(8,128)(2,1)S(1)}, u32[]{:S(2)}, u32[]{:S(2)}) collective-permute-start(bf16[4,64,256]{2,1,0:T(8,128)(2,1)} %collective-permute-done.4.rest_2_), channel_id=1, source_target_pairs={{0,1},{1,0},{2,3},{3,2},{4,5},{5,4},{6,7},{7,6},{8,9},{9,8},{10,11... | collective-permute-start | bytes 393224 | tf_op jit(solution)/shard_map/ppermute | solution.py:482
  26.0 1.7 %collective-permute-start.9 = (bf16[4,64,256]{2,1,0:T(8,128)(2,1)}, bf16[4,64,256]{2,1,0:T(8,128)(2,1)S(1)}, u32[]{:S(2)}, u32[]{:S(2)}) collective-permute-start(bf16[4,64,256]{2,1,0:T(8,128)(2,1)} %collective-permute-done.5.rest_3_), channel_id=1, source_target_pairs={{0,1},{1,0},{2,3},{3,2},{4,5},{5,4},{6,7},{7,6},{8,9},{9,8},{10,11... | collective-permute-start | bytes 393224 | tf_op jit(solution)/shard_map/ppermute | solution.py:482
  39.8 31.0 %copy-start.7 = (bf16[4,256,256]{2,1,0:T(8,128)(2,1)S(1)}, bf16[4,256,256]{2,1,0:T(8,128)(2,1)}, u32[]{:S(2)}) copy-start(bf16[4,256,256]{2,1,0:T(8,128)(2,1)} %weight_ref.3) | copy-start | bytes 1572868
  39.8 31.0 %copy-start.10 = (bf16[256,256]{1,0:T(8,128)(2,1)S(1)}, bf16[256,256]{1,0:T(8,128)(2,1)}, u32[]{:S(2)}) copy-start(bf16[256,256]{1,0:T(8,128)(2,1)} %out_w_ref.3) | copy-start | bytes 393220
  39.8 31.0 %copy-start.11 = (bf16[256,64]{0,1:T(8,128)(2,1)S(1)}, bf16[256,64]{0,1:T(8,128)(2,1)}, u32[]{:S(2)}) copy-start(bf16[256,64]{0,1:T(8,128)(2,1)} %param.20) | copy-start | bytes 98308
  39.8 30.6 %all-to-all-start = ((bf16[32,64,256]{2,1,0:T(8,128)(2,1)}), bf16[32,64,256]{2,1,0:T(8,128)(2,1)S(1)}, u32[]{:S(2)}, u32[]{:S(2)}) async-start(bf16[32,64,256]{2,1,0:T(8,128)(2,1)} %row_attend.1), calls=%async_computation | async-start | bytes 2097152 | tf_op jit(solution)/shard_map/all_to_all | solution.py:531
  44.4 53.8 %copy-start.14 = (s32[256]{0:T(256)S(1)}, s32[256]{0:T(256)}, u32[]{:S(2)}) copy-start(s32[256]{0:T(256)} %param.14) | copy-start | bytes 3076
  44.4 54.8 %copy-start.8 = (bf16[1024,128]{1,0:T(8,128)(2,1)S(1)}, bf16[1024,128]{1,0:T(8,128)(2,1)}, u32[]{:S(2)}) copy-start(bf16[1024,128]{1,0:T(8,128)(2,1)} %refs_12_.1) | copy-start | bytes 786436
  70.8 35.7 %copy-start.13 = (s32[256,256]{1,0:T(8,128)S(1)}, s32[256,256]{1,0:T(8,128)}, u32[]{:S(2)}) copy-start(s32[256,256]{1,0:T(8,128)} %param.13) | copy-start | bytes 786436
  70.8 41.2 %copy-start = (bf16[8,256,128]{2,1,0:T(8,128)(2,1)S(1)}, bf16[8,256,128]{2,1,0:T(8,128)(2,1)}, u32[]{:S(2)}) copy-start(bf16[8,256,128]{2,1,0:T(8,128)(2,1)} %pair_ref.3) | copy-start | bytes 1572868
  83.5 7.3 %collective-permute-start.14 = (bf16[256,256]{1,0:T(8,128)(2,1)S(1)}, bf16[256,256]{1,0:T(8,128)(2,1)S(1)}, u32[]{:S(2)}, u32[]{:S(2)}) collective-permute-start(bf16[256,256]{1,0:T(8,128)(2,1)S(1)} %get-tuple-element.41.refs_4_), channel_id=1, source_target_pairs={{0,8},{1,9},{2,10},{3,11},{4,12},{5,13},{6,14},{7,15},{8,0},{9,1},... | collective-permute-start | bytes 393224 | tf_op jit(solution)/shard_map/ppermute | solution.py:482
  84.2 12.9 %collective-permute-start.16 = (bf16[256,256]{1,0:T(8,128)(2,1)S(1)}, bf16[256,256]{1,0:T(8,128)(2,1)S(1)}, u32[]{:S(2)}, u32[]{:S(2)}) collective-permute-start(bf16[256,256]{1,0:T(8,128)(2,1)S(1)} %get-tuple-element.41.refs_4_), channel_id=1, source_target_pairs={{0,16},{1,17},{2,18},{3,19},{4,20},{5,21},{6,22},{7,23},{8,24},{9,... | collective-permute-start | bytes 393224 | tf_op jit(solution)/shard_map/ppermute | solution.py:482
  85.3 11.8 %collective-permute-start.18 = (bf16[256,256]{1,0:T(8,128)(2,1)S(1)}, bf16[256,256]{1,0:T(8,128)(2,1)S(1)}, u32[]{:S(2)}, u32[]{:S(2)}) collective-permute-start(bf16[256,256]{1,0:T(8,128)(2,1)S(1)} %get-tuple-element.41.refs_4_), channel_id=1, source_target_pairs={{0,24},{1,25},{2,26},{3,27},{4,28},{5,29},{6,30},{7,31},{8,16},{9,... | collective-permute-start | bytes 393224 | tf_op jit(solution)/shard_map/ppermute | solution.py:482
  87.9 9.8 %collective-permute-start.10 = (bf16[256,256]{1,0:T(8,128)(2,1)S(1)}, bf16[256,256]{1,0:T(8,128)(2,1)S(1)}, u32[]{:S(2)}, u32[]{:S(2)}) collective-permute-start(bf16[256,256]{1,0:T(8,128)(2,1)S(1)} %get-tuple-element.40.refs_0_), channel_id=1, source_target_pairs={{0,2},{1,3},{2,0},{3,1},{4,6},{5,7},{6,4},{7,5},{8,10},{9,11},{10,... | collective-permute-start | bytes 393224 | tf_op jit(solution)/shard_map/ppermute | solution.py:482
  89.3 8.4 %collective-permute-start.11 = (bf16[256,256]{1,0:T(8,128)(2,1)S(1)}, bf16[256,256]{1,0:T(8,128)(2,1)S(1)}, u32[]{:S(2)}, u32[]{:S(2)}) collective-permute-start(bf16[256,256]{1,0:T(8,128)(2,1)S(1)} %get-tuple-element.40.refs_0_), channel_id=1, source_target_pairs={{0,4},{1,5},{2,6},{3,7},{4,0},{5,1},{6,2},{7,3},{8,12},{9,13},{10,... | collective-permute-start | bytes 393224 | tf_op jit(solution)/shard_map/ppermute | solution.py:482
  90.8 7.4 %collective-permute-start.12 = (bf16[256,256]{1,0:T(8,128)(2,1)S(1)}, bf16[256,256]{1,0:T(8,128)(2,1)S(1)}, u32[]{:S(2)}, u32[]{:S(2)}) collective-permute-start(bf16[256,256]{1,0:T(8,128)(2,1)S(1)} %get-tuple-element.40.refs_0_), channel_id=1, source_target_pairs={{0,6},{1,7},{2,4},{3,5},{4,2},{5,3},{6,0},{7,1},{8,14},{9,15},{10,... | collective-permute-start | bytes 393224 | tf_op jit(solution)/shard_map/ppermute | solution.py:482
  97.1 1.3 %collective-permute-start.13 = (bf16[256,256]{1,0:T(8,128)(2,1)S(1)}, bf16[256,256]{1,0:T(8,128)(2,1)S(1)}, u32[]{:S(2)}, u32[]{:S(2)}) collective-permute-start(bf16[256,256]{1,0:T(8,128)(2,1)S(1)} %get-tuple-element.41.refs_4_), channel_id=1, source_target_pairs={{0,1},{1,0},{2,3},{3,2},{4,5},{5,4},{6,7},{7,6},{8,9},{9,8},{10,11... | collective-permute-start | bytes 393224 | tf_op jit(solution)/shard_map/ppermute | solution.py:482
  97.1 1.5 %collective-permute-start.15 = (bf16[256,256]{1,0:T(8,128)(2,1)S(1)}, bf16[256,256]{1,0:T(8,128)(2,1)S(1)}, u32[]{:S(2)}, u32[]{:S(2)}) collective-permute-start(bf16[256,256]{1,0:T(8,128)(2,1)S(1)} %collective-permute-done.14.refs_6_), channel_id=1, source_target_pairs={{0,1},{1,0},{2,3},{3,2},{4,5},{5,4},{6,7},{7,6},{8,9},{9,8},{10,11... | collective-permute-start | bytes 393224 | tf_op jit(solution)/shard_map/ppermute | solution.py:482
  97.6 1.3 %collective-permute-start.17 = (bf16[256,256]{1,0:T(8,128)(2,1)S(1)}, bf16[256,256]{1,0:T(8,128)(2,1)S(1)}, u32[]{:S(2)}, u32[]{:S(2)}) collective-permute-start(bf16[256,256]{1,0:T(8,128)(2,1)S(1)} %collective-permute-done.16.refs_8_), channel_id=1, source_target_pairs={{0,1},{1,0},{2,3},{3,2},{4,5},{5,4},{6,7},{7,6},{8,9},{9,8},{10,11... | collective-permute-start | bytes 393224 | tf_op jit(solution)/shard_map/ppermute | solution.py:482
  97.7 1.5 %collective-permute-start.19 = (bf16[256,256]{1,0:T(8,128)(2,1)S(1)}, bf16[256,256]{1,0:T(8,128)(2,1)S(1)}, u32[]{:S(2)}, u32[]{:S(2)}) collective-permute-start(bf16[256,256]{1,0:T(8,128)(2,1)S(1)} %collective-permute-done.18.refs_10_), channel_id=1, source_target_pairs={{0,1},{1,0},{2,3},{3,2},{4,5},{5,4},{6,7},{7,6},{8,9},{9,8},{10,11... | collective-permute-start | bytes 393224 | tf_op jit(solution)/shard_map/ppermute | solution.py:482
  102.9 6.4 %collective-permute-start.20 = (bf16[8,64,128]{2,1,0:T(8,128)(2,1)S(1)}, bf16[8,64,128]{2,1,0:T(8,128)(2,1)S(1)}, u32[]{:S(2)}, u32[]{:S(2)}) collective-permute-start(bf16[8,64,128]{2,1,0:T(8,128)(2,1)S(1)} %get-tuple-element.43), channel_id=1, source_target_pairs={{0,2},{1,3},{2,0},{3,1},{4,6},{5,7},{6,4},{7,5},{8,10},{9,11},{10,... | collective-permute-start | bytes 393224 | tf_op jit(solution)/shard_map/ppermute | solution.py:482
  103.7 8.3 %collective-permute-start.21 = (bf16[8,64,128]{2,1,0:T(8,128)(2,1)S(1)}, bf16[8,64,128]{2,1,0:T(8,128)(2,1)S(1)}, u32[]{:S(2)}, u32[]{:S(2)}) collective-permute-start(bf16[8,64,128]{2,1,0:T(8,128)(2,1)S(1)} %get-tuple-element.44), channel_id=1, source_target_pairs={{0,4},{1,5},{2,6},{3,7},{4,0},{5,1},{6,2},{7,3},{8,12},{9,13},{10,... | collective-permute-start | bytes 393224 | tf_op jit(solution)/shard_map/ppermute | solution.py:482
  105.1 6.9 %collective-permute-start.22 = (bf16[8,64,128]{2,1,0:T(8,128)(2,1)S(1)}, bf16[8,64,128]{2,1,0:T(8,128)(2,1)S(1)}, u32[]{:S(2)}, u32[]{:S(2)}) collective-permute-start(bf16[8,64,128]{2,1,0:T(8,128)(2,1)S(1)} %get-tuple-element.45), channel_id=1, source_target_pairs={{0,6},{1,7},{2,4},{3,5},{4,2},{5,3},{6,0},{7,1},{8,14},{9,15},{10,... | collective-permute-start | bytes 393224 | tf_op jit(solution)/shard_map/ppermute | solution.py:482
  (7 other events, 11.2 us)

commit v6 on v5

--- a/solution.py
+++ b/solution.py
@@ -141,7 +141,7 @@
 
 LANES = 128
 LOG2E = math.log2(math.e)
-VALUE_SCALE = 1.0 / 128.0
+LIVE_SCALE = 1.0 / 128.0
 BF16 = jnp.bfloat16
 F32 = jnp.float32
 MIB = 1024 * 1024
@@ -181,6 +181,10 @@
 
 def joined_tiles(held):
     return jnp.concatenate([held[t] for t in range(held.shape[0])], axis=1)
+
+
+def in_hbm(*arrays):
+    return [pltpu.with_memory_space_constraint(a, pltpu.HBM) for a in arrays]
 
 
 def in_vmem(*arrays):
@@ -192,6 +196,11 @@
     return [
         jnp.where(lane == t, 1.0, 0.0).astype(BF16) for t in range(LANES // HEAD_CHANNELS)
     ]
+
+
+def quotient(top, below):
+    guess = pl.reciprocal(below, approx=True)
+    return top * (guess * (2.0 - below * guess))
 
 
 def attend_block(query, key, value, live, lanes, bias_of):
@@ -212,7 +221,7 @@
             raised.append(jnp.exp2(scores).astype(BF16))
             sides.append(jnp.concatenate([value_t * lanes[t], live * lanes[t]], axis=1))
         total = nn_dot(jnp.concatenate(raised, axis=1), jnp.concatenate(sides, axis=0))
-        pieces.append(total[:, :LANES] / total[:, LANES:])
+        pieces.append(quotient(total[:, :LANES], total[:, LANES:]))
     return jnp.concatenate(pieces, axis=1)
 
 
@@ -220,8 +229,8 @@
     scale = LOG2E / math.sqrt(HEAD_CHANNELS)
     query = (nn_dot(normed, weight_ref[0]) * scale).astype(BF16)
     key = nn_dot(normed, weight_ref[1]).astype(BF16)
-    value = (nn_dot(normed, weight_ref[2]) * VALUE_SCALE).astype(BF16)
-    gate = jax.nn.sigmoid(nn_dot(normed, weight_ref[3])) * (1.0 / VALUE_SCALE)
+    value = nn_dot(normed, weight_ref[2]).astype(BF16)
+    gate = 0.5 * jnp.tanh(0.5 * nn_dot(normed, weight_ref[3])) + 0.5
     return query, key, value, gate
 
 
@@ -238,7 +247,6 @@
     rows, cols, width = pair_rep.shape
     out = jax.ShapeDtypeStruct((ATTN_HEAD_COUNT * rows, cols), BF16)
     weight = bias_weight.T
-    pinned = [pltpu.with_memory_space_constraint(a, pltpu.HBM) for a in (pair_rep, weight)]
     return pl.pallas_call(
         bias_kernel,
         grid=(1,),
@@ -248,16 +256,13 @@
         scratch_shapes=[tiled_scratch(*out.shape)],
         compiler_params=params(16),
         name="pair_bias",
-    )(*pinned)
-
-
-def row_project_kernel(x_ref, weight_ref, x_out, q_ref, k_ref, v_ref, g_ref):
-    step = x_ref.shape[0]
-    for s in range(step):
-        at = pl.program_id(0) * step + s
-        x_out[at] = x_ref[s]
+    )(*in_hbm(pair_rep, weight))
+
+
+def row_project_kernel(x_ref, weight_ref, q_ref, k_ref, v_ref, g_ref):
+    for s in range(x_ref.shape[0]):
         normed = layer_normalize(x_ref[s].astype(F32)).astype(BF16)
-        q_ref[at], k_ref[at], v_ref[at], g_ref[at] = project(normed, weight_ref)
+        q_ref[s], k_ref[s], v_ref[s], g_ref[s] = project(normed, weight_ref)
 
 
 def row_project(alignment, weight):
@@ -268,11 +273,11 @@
         row_project_kernel,
         grid=(seqs // step,),
         in_specs=[block, full_spec(weight.shape)],
-        out_specs=[pl.BlockSpec(memory_space=pltpu.VMEM)] * 5,
-        out_shape=[pltpu.VMEM(alignment.shape, BF16)] * 4 + [pltpu.VMEM(alignment.shape, F32)],
+        out_specs=[block] * 4,
+        out_shape=[pltpu.HBM(alignment.shape, BF16)] * 3 + [pltpu.HBM(alignment.shape, F32)],
         compiler_params=params(24),
         name="row_project",
-    )(*[pltpu.with_memory_space_constraint(a, pltpu.HBM) for a in (alignment, weight)])
+    )(*in_hbm(alignment, weight))
 
 
 def row_attend_kernel(
@@ -294,33 +299,36 @@
     results = []
     parts, rows = out_ref.shape[0], out_ref.shape[1]
     for s in range(step):
-        at = pl.program_id(0) * step + s
         heads_out = attend_block(
-            q_ref[at], k_ref[at], v_ref[at], live_ref[at], lanes, lambda h: bias_all[h]
+            q_ref[s], k_ref[s], v_ref[s], live_ref[s], lanes, lambda h: bias_all[h]
         )
-        heads_out = (heads_out * g_ref[at]).astype(BF16)
-        total = x_ref[at].astype(F32) + nn_dot(heads_out, out_w_ref[...])
+        heads_out = (heads_out * g_ref[s]).astype(BF16)
+        total = x_ref[s].astype(F32) + nn_dot(heads_out, out_w_ref[...])
         results.append(total.reshape(parts, 1, rows // step, total.shape[1]))
     joined = jnp.concatenate(results, axis=1)
     out_ref[...] = joined.reshape(out_ref.shape).astype(BF16)
 
 
-def row_attend(me, projected, live, out_weight, bias_parts, plan, parts):
-    seqs, length, width = projected[0].shape
+def row_attend(me, alignment, projected, live, out_weight, bias_parts, plan, parts):
+    seqs, length, width = alignment.shape
     rows = length // parts
     step = 2
     vmem = pl.BlockSpec(memory_space=pltpu.VMEM)
-    operands = in_vmem(*projected, live, out_weight, *bias_parts)
+    block = pl.BlockSpec((step, length, width), lambda i: (i, 0, 0))
+    narrow = pl.BlockSpec((step, length, LANES), lambda i: (i, 0, 0))
     return pl.pallas_call(
         functools.partial(row_attend_kernel, plan, step),
         grid=(seqs // step,),
-        in_specs=[pl.BlockSpec(memory_space=pltpu.SMEM)] + [vmem] * len(operands),
+        in_specs=[pl.BlockSpec(memory_space=pltpu.SMEM)]
+        + [block] * 5
+        + [narrow, full_spec(out_weight.shape)]
+        + [vmem] * len(bias_parts),
         out_specs=pl.BlockSpec((parts, step * rows, width), lambda i: (0, i, 0)),
         out_shape=jax.ShapeDtypeStruct((parts, seqs * rows, width), BF16),
         scratch_shapes=[pltpu.VMEM((ATTN_HEAD_COUNT, length, length), F32)],
         compiler_params=params(24),
         name="row_attend",
-    )(me, *operands)
+    )(me, *in_hbm(alignment, *projected, live, out_weight), *in_vmem(*bias_parts))
 
 
 def column_kernel(
@@ -343,7 +351,12 @@
         current = load_strided(held, item, items, length)
         normed = layer_normalize(current).astype(BF16)
         query, key, value, gate = project(normed, weight_ref)
-        heads_out = attend_block(query, key, value, live_ref[n], lanes, None)
+        live = live_ref[:, n : n + 1]
+        for later in range(1, items // each):
+            at = later * each + n
+            live = jnp.where(step == later, live_ref[:, at : at + 1], live)
+        live = jnp.broadcast_to(live * LIVE_SCALE, (length, LANES)).astype(BF16)
+        heads_out = attend_block(query, key, value, live, lanes, None)
         heads_out = (heads_out * gate).astype(BF16)
         updated = (current + nn_dot(heads_out, out_w_ref[...])).astype(BF16).astype(F32)
         store_strided(held, item, items, updated)
@@ -375,7 +388,7 @@
         grid=(items // each,),
         in_specs=[
             full_spec(moved.shape),
-            pl.BlockSpec((each, length, LANES), lambda i: (i, 0, 0)),
+            full_spec(live.shape),
             full_spec(mask_rows.shape),
             full_spec(weight.shape),
             full_spec(out_weight.shape),
@@ -505,8 +518,9 @@
 
     own_seqs = lax.dynamic_slice_in_dim(align_mask, dap_index * seq_dev, seq_dev, 0)
     own_res = lax.dynamic_slice_in_dim(align_mask, dap_index * items, items, 1)
-    row_live = jnp.broadcast_to(own_seqs.astype(BF16)[:, :, None], (seq_dev, total_res, LANES))
-    col_live = jnp.broadcast_to(own_res.T.astype(BF16)[:, :, None], (items, total_seqs, LANES))
+    row_live = (own_seqs.astype(F32) * LIVE_SCALE).astype(BF16)[:, :, None]
+    row_live = jnp.broadcast_to(row_live, (seq_dev, total_res, LANES))
+    col_live = own_res.astype(F32)
 
     bias = pair_bias_block(pair_rep, bias_weight)
     projected = list(row_project(alignment, row_proj_weight))
@@ -527,7 +541,9 @@
     scale = live_rows[None, :] * res_float[:, None] / (counts + count_eps)
     mask_rows = own_res.T.astype(F32)
 
-    rows = row_attend(me, projected, row_live, row_out_weight, bias_parts, plan, count)
+    rows = row_attend(
+        me, alignment, projected, row_live, row_out_weight, bias_parts, plan, count
+    )
     moved = lax.all_to_all(rows, "dap", split_axis=0, concat_axis=0, tiled=True)
     updated, left, right = column_attend(
         moved,
@@ -541,8 +557,10 @@
     rights = [exchange(right, count, z) for z in line]
     rights = [part for own in rights for part in (own, exchange(own, count, 1))]
     lefts = [exchange(left, count, k) for k in plane]
-    parts = outer_product(lefts, rights, outer_out, items)
-    parts = [exchange(part, count, k) for part, k in zip(parts, plane)]
+    sent = outer_product(lefts[1:], rights, outer_out, items)
+    parts = [exchange(part, count, k) for part, k in zip(sent, plane[1:])]
+    own = outer_product([left], rights, outer_out, items)
+    parts = list(own) + parts
     pair_out = finish(me, pair_rep, scale, parts, plane, line)
     return updated, pair_out
 

time: 114 us -> 111 us (0.974)
  local copies, waits for them, and re-layouts: 7.55 us -> 1.54 us
  Pallas kernels: 32.1 us -> 35.4 us
  waiting for transfers between devices: 43.4 us -> 45.5 us
    unnamed x31 -> x15, local copies, waits for them, and re-layouts: 6.7 us -> 0.09 us
    ppermute x23, waiting for transfers between devices: 17.5 us -> 19.8 us  [exchange(): return lax.ppermute(block, 'dap', [(i, i ^ offset) for i in range(count)])]
    pallas_call x1, Pallas kernels: 4.27 us -> 5.6 us  [row_project(): pl.pallas_call(row_project_kernel, grid=(seqs // step,), in_specs=[block,...]
    pallas_call x1 -> x2, Pallas kernels: 3.69 us -> 4.78 us  [outer_product(): pl.pallas_call(functools.partial(outer_kernel, group, outer, items), out_...]
  transfers between devices with their start and end apart: 24 -> 24, of which waited for: 14 -> 13; matrix products, arithmetic and copies ran while one was open for 1% -> 1% of each run, Pallas kernels for 4% -> 7%
where the time goes in v6:
time: 111 us
  waiting for transfers between devices  45.5 us (41%)
  Pallas kernels  35.4 us (32%)
  starting transfers between devices  27.3 us (25%)
  local copies, waits for them, and re-layouts  1.54 us (1%)
    all_to_all x1, waiting for transfers between devices, per_device_fast(): moved = lax.all_to_all(rows, 'dap', split_axis=0, concat_axis=0, tiled=True)  25.7 us
    ppermute x23, starting transfers between devices, exchange(): return lax.ppermute(block, 'dap', [(i, i ^ offset) for i in range(count)])  22.8 us
    ppermute x23, waiting for transfers between devices, exchange(): return lax.ppermute(block, 'dap', [(i, i ^ offset) for i in range(count)])  19.8 us
    pallas_call x1, Pallas kernels, column_attend(): pl.pallas_call(functools.partial(column_kernel, items, each), grid=(items...  12.8 us
    pallas_call x1, Pallas kernels, row_attend(): pl.pallas_call(functools.partial(row_attend_kernel, plan, step), grid=(se...  9.22 us
    pallas_call x1, Pallas kernels, row_project(): pl.pallas_call(row_project_kernel, grid=(seqs // step,), in_specs=[block,...  5.6 us
    pallas_call x2, Pallas kernels, outer_product(): pl.pallas_call(functools.partial(outer_kernel, group, outer, items), out_...  4.78 us
    all_to_all x1, starting transfers between devices, per_device_fast(): moved = lax.all_to_all(rows, 'dap', split_axis=0, concat_axis=0, tiled=True)  4.56 us
  transfers between devices with their start and end apart: 24, of which 13 were waited for; matrix products, arithmetic and copies ran while one was open for 1% of the time, Pallas kernels for 7%

profile of v6, /device:TPU:0, one launch (start us, length us, event | category | flops | bytes accessed | tf_op | source)
XLA Modules:
  0.0 110.9 jit_solution(6238535111441608603)
XLA Ops:
  0.6 1.8 %pair_bias.1 = bf16[64,256]{1,0:T(8,128)(2,1)S(1)} custom-call(bf16[8,256,128]{2,1,0:T(8,128)(2,1)} %pair_ref.3, bf16[8,128]{1,0:T(8,128)(2,1)} %bitcast.18), custom_call_target="tpu_custom_call" | custom-call | tf_op jit(solution)/shard_map/pair_bias/pallas_call | solution.py:250
  2.5 3.1 %collective-permute-start = (bf16[64,256]{1,0:T(8,128)(2,1)S(1)}, bf16[64,256]{1,0:T(8,128)(2,1)S(1)}, u32[]{:S(2)}, u32[]{:S(2)}) collective-permute-start(bf16[64,256]{1,0:T(8,128)(2,1)S(1)} %pair_bias.1), channel_id=1, source_target_pairs={{0,8},{1,9},{2,10},{3,11},{4,12},{5,13},{6,14},{7,15},{8,0},{9,1},... | collective-permute-start | bytes 98312 | tf_op jit(solution)/shard_map/ppermute | solution.py:495
  5.6 2.6 %collective-permute-start.1 = (bf16[64,256]{1,0:T(8,128)(2,1)S(1)}, bf16[64,256]{1,0:T(8,128)(2,1)S(1)}, u32[]{:S(2)}, u32[]{:S(2)}) collective-permute-start(bf16[64,256]{1,0:T(8,128)(2,1)S(1)} %pair_bias.1), channel_id=1, source_target_pairs={{0,16},{1,17},{2,18},{3,19},{4,20},{5,21},{6,22},{7,23},{8,24},{9,... | collective-permute-start | bytes 98312 | tf_op jit(solution)/shard_map/ppermute | solution.py:495
  8.2 5.6 %row_project.1 = (bf16[8,256,256]{2,1,0:T(8,128)(2,1)}, bf16[8,256,256]{2,1,0:T(8,128)(2,1)}, bf16[8,256,256]{2,1,0:T(8,128)(2,1)}, f32[8,256,256]{2,1,0:T(8,128)}) custom-call(bf16[8,256,256]{2,1,0:T(8,128)(2,1)} %x_ref.3, bf16[4,256,256]{2,1,0:T(8,128)(2,1)} %weight_ref.2), custom_call_target="tpu_custom_call" | custom-call | tf_op jit(solution)/shard_map/row_project/pallas_call | solution.py:272
  13.9 1.7 %collective-permute-start.3 = (bf16[4,64,256]{2,1,0:T(8,128)(2,1)S(1)}, bf16[4,64,256]{2,1,0:T(8,128)(2,1)S(1)}, u32[]{:S(2)}, u32[]{:S(2)}) collective-permute-start(bf16[4,64,256]{2,1,0:T(8,128)(2,1)S(1)} %pad_maximum_fusion.rest_0_), channel_id=1, source_target_pairs={{0,2},{1,3},{2,0},{3,1},{4,6},{5,7},{6,4},{7,5},{8,10},{9,11},{10,... | collective-permute-start | bytes 393224 | tf_op jit(solution)/shard_map/ppermute | solution.py:495
  15.6 1.5 %collective-permute-start.4 = (bf16[4,64,256]{2,1,0:T(8,128)(2,1)S(1)}, bf16[4,64,256]{2,1,0:T(8,128)(2,1)S(1)}, u32[]{:S(2)}, u32[]{:S(2)}) collective-permute-start(bf16[4,64,256]{2,1,0:T(8,128)(2,1)S(1)} %pad_maximum_fusion.rest_0_), channel_id=1, source_target_pairs={{0,4},{1,5},{2,6},{3,7},{4,0},{5,1},{6,2},{7,3},{8,12},{9,13},{10,... | collective-permute-start | bytes 393224 | tf_op jit(solution)/shard_map/ppermute | solution.py:495
  17.5 2.3 %collective-permute-done.3.rest_1_ = bf16[4,64,256]{2,1,0:T(8,128)(2,1)S(1)} collective-permute-done((bf16[4,64,256]{2,1,0:T(8,128)(2,1)S(1)}, bf16[4,64,256]{2,1,0:T(8,128)(2,1)S(1)}, u32[]{:S(2)}, u32[]{:S(2)}) %collective-permute-start.3) | collective-permute-done | bytes 131104 | tf_op jit(solution)/shard_map/ppermute | solution.py:495
  19.8 3.5 %collective-permute-done.4.rest_2_ = bf16[4,64,256]{2,1,0:T(8,128)(2,1)S(1)} collective-permute-done((bf16[4,64,256]{2,1,0:T(8,128)(2,1)S(1)}, bf16[4,64,256]{2,1,0:T(8,128)(2,1)S(1)}, u32[]{:S(2)}, u32[]{:S(2)}) %collective-permute-start.4) | collective-permute-done | bytes 131104 | tf_op jit(solution)/shard_map/ppermute | solution.py:495
  23.3 1.1 %broadcast_in_dim.2.live_ref = bf16[8,256,128]{2,1,0:T(8,128)(2,1)} broadcast(bf16[8,256]{1,0:T(8,128)(2,1)S(1)} %multiply_convert_fusion), dimensions={0,1} | broadcast | bytes 528384 | tf_op jit(solution)/shard_map/broadcast_in_dim | solution.py:522
  24.4 0.5 collective-permute-start.7
  24.9 0.5 collective-permute-start.9
  26.5 9.2 %row_attend.1 = bf16[32,64,256]{2,1,0:T(8,128)(2,1)} custom-call(s32[1]{0:T(128)} %bitcast.me_ref, bf16[8,256,256]{2,1,0:T(8,128)(2,1)} %x_ref.3, bf16[8,256,256]{2,1,0:T(8,128)(2,1)} %get-tuple-element.23.q_ref, bf16[8,256,256]{2,1,0:T(8,128)(2,1)} %get-tuple-element.24.k_ref, bf16[8,256,256]{2,1,0:T(8,128)(2,1)} %get-tuple-element.25.v_ref, ...), custom_call_target="tpu_custom_call" | custom-call | tf_op jit(solution)/shard_map/row_attend/pallas_call | solution.py:319
  35.8 4.6 %all-to-all-start = ((bf16[32,64,256]{2,1,0:T(8,128)(2,1)}), bf16[32,64,256]{2,1,0:T(8,128)(2,1)S(1)}, u32[]{:S(2)}, u32[]{:S(2)}) async-start(bf16[32,64,256]{2,1,0:T(8,128)(2,1)} %row_attend.1), calls=%async_computation | async-start | bytes 2097152 | tf_op jit(solution)/shard_map/all_to_all | solution.py:547
  40.6 25.7 %all-to-all-done.x_ref = bf16[32,64,256]{2,1,0:T(8,128)(2,1)S(1)} async-done(((bf16[32,64,256]{2,1,0:T(8,128)(2,1)}), bf16[32,64,256]{2,1,0:T(8,128)(2,1)S(1)}, u32[]{:S(2)}, u32[]{:S(2)}) %all-to-all-start) | async-done | bytes 1048608 | tf_op jit(solution)/shard_map/all_to_all | solution.py:547
  66.4 12.8 %column_attend.1 = (bf16[256,8,256]{2,1,0:T(8,128)(2,1)}, bf16[256,256]{1,0:T(8,128)(2,1)S(1)}, bf16[256,256]{1,0:T(8,128)(2,1)S(1)}) custom-call(bf16[32,64,256]{2,1,0:T(8,128)(2,1)S(1)} %all-to-all-done.x_ref, f32[256,8]{1,0:T(8,128)S(1)} %copy.17.live_ref, f32[8,256]{1,0:T(8,128)S(1)} %get-tuple-element.42.mask_ref, bf16[4,256,256]{2,1,0:T(8,128)(2,1)S(1)} %copy-done.2, ...), custom_call_target="tpu_custom_call" | custom-call | tf_op jit(solution)/shard_map/column_attend/pallas_call | solution.py:386
  79.2 0.8 collective-permute-start.11
  79.9 1.1 collective-permute-start.13
  81.0 2.5 %collective-permute-start.15 = (bf16[256,256]{1,0:T(8,128)(2,1)S(1)}, bf16[256,256]{1,0:T(8,128)(2,1)S(1)}, u32[]{:S(2)}, u32[]{:S(2)}) collective-permute-start(bf16[256,256]{1,0:T(8,128)(2,1)S(1)} %get-tuple-element.38.refs_1_.refs_3_), channel_id=1, source_target_pairs={{0,24},{1,25},{2,26},{3,27},{4,28},{5,29},{6,30},{7,31},{8,16},{9,... | collective-permute-start | bytes 393224 | tf_op jit(solution)/shard_map/ppermute | solution.py:495
  83.5 1.5 %collective-permute-start.17 = (bf16[256,256]{1,0:T(8,128)(2,1)S(1)}, bf16[256,256]{1,0:T(8,128)(2,1)S(1)}, u32[]{:S(2)}, u32[]{:S(2)}) collective-permute-start(bf16[256,256]{1,0:T(8,128)(2,1)S(1)} %get-tuple-element.37.refs_0_), channel_id=1, source_target_pairs={{0,2},{1,3},{2,0},{3,1},{4,6},{5,7},{6,4},{7,5},{8,10},{9,11},{10,... | collective-permute-start | bytes 393224 | tf_op jit(solution)/shard_map/ppermute | solution.py:495
  85.0 1.1 %collective-permute-done.11.refs_3_.refs_5_ = bf16[256,256]{1,0:T(8,128)(2,1)S(1)} collective-permute-done((bf16[256,256]{1,0:T(8,128)(2,1)S(1)}, bf16[256,256]{1,0:T(8,128)(2,1)S(1)}, u32[]{:S(2)}, u32[]{:S(2)}) %collective-permute-start.11) | collective-permute-done | bytes 131104 | tf_op jit(solution)/shard_map/ppermute | solution.py:495
  86.1 1.0 collective-permute-start.18
  87.1 5.7 %collective-permute-done.13.refs_5_.refs_7_ = bf16[256,256]{1,0:T(8,128)(2,1)S(1)} collective-permute-done((bf16[256,256]{1,0:T(8,128)(2,1)S(1)}, bf16[256,256]{1,0:T(8,128)(2,1)S(1)}, u32[]{:S(2)}, u32[]{:S(2)}) %collective-permute-start.13) | collective-permute-done | bytes 131104 | tf_op jit(solution)/shard_map/ppermute | solution.py:495
  92.8 1.6 %collective-permute-start.19 = (bf16[256,256]{1,0:T(8,128)(2,1)S(1)}, bf16[256,256]{1,0:T(8,128)(2,1)S(1)}, u32[]{:S(2)}, u32[]{:S(2)}) collective-permute-start(bf16[256,256]{1,0:T(8,128)(2,1)S(1)} %get-tuple-element.37.refs_0_), channel_id=1, source_target_pairs={{0,6},{1,7},{2,4},{3,5},{4,2},{5,3},{6,0},{7,1},{8,14},{9,15},{10,... | collective-permute-start | bytes 393224 | tf_op jit(solution)/shard_map/ppermute | solution.py:495
  94.4 0.5 collective-permute-start.14
  95.0 3.6 %collective-permute-done.19.refs_2_ = bf16[256,256]{1,0:T(8,128)(2,1)S(1)} collective-permute-done((bf16[256,256]{1,0:T(8,128)(2,1)S(1)}, bf16[256,256]{1,0:T(8,128)(2,1)S(1)}, u32[]{:S(2)}, u32[]{:S(2)}) %collective-permute-start.19) | collective-permute-done | bytes 131104 | tf_op jit(solution)/shard_map/ppermute | solution.py:495
  98.7 2.9 %outer_product.3 = (bf16[8,64,128]{2,1,0:T(8,128)(2,1)S(1)}, bf16[8,64,128]{2,1,0:T(8,128)(2,1)S(1)}, bf16[8,64,128]{2,1,0:T(8,128)(2,1)S(1)}) custom-call(bf16[256,256]{1,0:T(8,128)(2,1)S(1)} %collective-permute-done.17.refs_0_, bf16[256,256]{1,0:T(8,128)(2,1)S(1)} %collective-permute-done.18.refs_1_, bf16[256,256]{1,0:T(8,128)(2,1)S(1)} %collective-permute-done.19.refs_2_, ...), custom_call_target="tpu_custom_call" | custom-call | tf_op jit(solution)/shard_map/outer_product/pallas_call | solution.py:447
  101.6 0.9 collective-permute-start.20
  102.4 1.3 %collective-permute-start.21 = (bf16[8,64,128]{2,1,0:T(8,128)(2,1)S(1)}, bf16[8,64,128]{2,1,0:T(8,128)(2,1)S(1)}, u32[]{:S(2)}, u32[]{:S(2)}) collective-permute-start(bf16[8,64,128]{2,1,0:T(8,128)(2,1)S(1)} %get-tuple-element.40), channel_id=1, source_target_pairs={{0,4},{1,5},{2,6},{3,7},{4,0},{5,1},{6,2},{7,3},{8,12},{9,13},{10,... | collective-permute-start | bytes 393224 | tf_op jit(solution)/shard_map/ppermute | solution.py:495
  103.8 1.4 %collective-permute-start.22 = (bf16[8,64,128]{2,1,0:T(8,128)(2,1)S(1)}, bf16[8,64,128]{2,1,0:T(8,128)(2,1)S(1)}, u32[]{:S(2)}, u32[]{:S(2)}) collective-permute-start(bf16[8,64,128]{2,1,0:T(8,128)(2,1)S(1)} %get-tuple-element.41), channel_id=1, source_target_pairs={{0,6},{1,7},{2,4},{3,5},{4,2},{5,3},{6,0},{7,1},{8,14},{9,15},{10,... | collective-permute-start | bytes 393224 | tf_op jit(solution)/shard_map/ppermute | solution.py:495
  105.4 1.9 %outer_product.2.refs_0_ = bf16[8,64,128]{2,1,0:T(8,128)(2,1)S(1)} custom-call(bf16[256,256]{1,0:T(8,128)(2,1)S(1)} %get-tuple-element.37.refs_0_, bf16[256,256]{1,0:T(8,128)(2,1)S(1)} %get-tuple-element.38.refs_1_.refs_3_, bf16[256,256]{1,0:T(8,128)(2,1)S(1)} %collective-permute-done.10.refs_2_.refs_4_, ...), custom_call_target="tpu_custom_call" | custom-call | tf_op jit(solution)/shard_map/outer_product/pallas_call | solution.py:447
  107.4 2.2 %collective-permute-done.22.refs_3_ = bf16[8,64,128]{2,1,0:T(8,128)(2,1)S(1)} collective-permute-done((bf16[8,64,128]{2,1,0:T(8,128)(2,1)S(1)}, bf16[8,64,128]{2,1,0:T(8,128)(2,1)S(1)}, u32[]{:S(2)}, u32[]{:S(2)}) %collective-permute-start.22) | collective-permute-done | bytes 131104 | tf_op jit(solution)/shard_map/ppermute | solution.py:495
  109.6 1.2 %finish.1 = bf16[8,256,128]{2,1,0:T(8,128)(2,1)} custom-call(s32[1]{0:T(128)} %bitcast.me_ref, bf16[8,256,128]{2,1,0:T(8,128)(2,1)S(1)} %copy-done, f32[256,8]{1,0:T(8,128)S(1)} %fusion.1.scale_ref, bf16[8,64,128]{2,1,0:T(8,128)(2,1)S(1)} %outer_product.2.refs_0_, bf16[8,64,128]{2,1,0:T(8,128)(2,1)S(1)} %collective-permute-done.20.refs_1_, ...), custom_call_target="tpu_custom_call" | custom-call | tf_op jit(solution)/shard_map/finish/pallas_call | solution.py:482
  (47 shorter events, 2.4 us)
Async XLA Ops:
  0.6 16.8 %copy-start.5 = (s32[256,256]{1,0:T(8,128)S(1)}, s32[256,256]{1,0:T(8,128)}, u32[]{:S(2)}) copy-start(s32[256,256]{1,0:T(8,128)} %param.13) | copy-start | bytes 786436
  2.5 11.3 %collective-permute-start = (bf16[64,256]{1,0:T(8,128)(2,1)S(1)}, bf16[64,256]{1,0:T(8,128)(2,1)S(1)}, u32[]{:S(2)}, u32[]{:S(2)}) collective-permute-start(bf16[64,256]{1,0:T(8,128)(2,1)S(1)} %pair_bias.1), channel_id=1, source_target_pairs={{0,8},{1,9},{2,10},{3,11},{4,12},{5,13},{6,14},{7,15},{8,0},{9,1},... | collective-permute-start | bytes 98312 | tf_op jit(solution)/shard_map/ppermute | solution.py:495
  5.6 8.2 %collective-permute-start.1 = (bf16[64,256]{1,0:T(8,128)(2,1)S(1)}, bf16[64,256]{1,0:T(8,128)(2,1)S(1)}, u32[]{:S(2)}, u32[]{:S(2)}) collective-permute-start(bf16[64,256]{1,0:T(8,128)(2,1)S(1)} %pair_bias.1), channel_id=1, source_target_pairs={{0,16},{1,17},{2,18},{3,19},{4,20},{5,21},{6,22},{7,23},{8,24},{9,... | collective-permute-start | bytes 98312 | tf_op jit(solution)/shard_map/ppermute | solution.py:495
  8.2 5.7 %collective-permute-start.2 = (bf16[64,256]{1,0:T(8,128)(2,1)S(1)}, bf16[64,256]{1,0:T(8,128)(2,1)S(1)}, u32[]{:S(2)}, u32[]{:S(2)}) collective-permute-start(bf16[64,256]{1,0:T(8,128)(2,1)S(1)} %pair_bias.1), channel_id=1, source_target_pairs={{0,24},{1,25},{2,26},{3,27},{4,28},{5,29},{6,30},{7,31},{8,16},{9,... | collective-permute-start | bytes 98312 | tf_op jit(solution)/shard_map/ppermute | solution.py:495
  13.9 5.9 %collective-permute-start.3 = (bf16[4,64,256]{2,1,0:T(8,128)(2,1)S(1)}, bf16[4,64,256]{2,1,0:T(8,128)(2,1)S(1)}, u32[]{:S(2)}, u32[]{:S(2)}) collective-permute-start(bf16[4,64,256]{2,1,0:T(8,128)(2,1)S(1)} %pad_maximum_fusion.rest_0_), channel_id=1, source_target_pairs={{0,2},{1,3},{2,0},{3,1},{4,6},{5,7},{6,4},{7,5},{8,10},{9,11},{10,... | collective-permute-start | bytes 393224 | tf_op jit(solution)/shard_map/ppermute | solution.py:495
  15.6 7.7 %collective-permute-start.4 = (bf16[4,64,256]{2,1,0:T(8,128)(2,1)S(1)}, bf16[4,64,256]{2,1,0:T(8,128)(2,1)S(1)}, u32[]{:S(2)}, u32[]{:S(2)}) collective-permute-start(bf16[4,64,256]{2,1,0:T(8,128)(2,1)S(1)} %pad_maximum_fusion.rest_0_), channel_id=1, source_target_pairs={{0,4},{1,5},{2,6},{3,7},{4,0},{5,1},{6,2},{7,3},{8,12},{9,13},{10,... | collective-permute-start | bytes 393224 | tf_op jit(solution)/shard_map/ppermute | solution.py:495
  17.1 6.2 %collective-permute-start.5 = (bf16[4,64,256]{2,1,0:T(8,128)(2,1)S(1)}, bf16[4,64,256]{2,1,0:T(8,128)(2,1)S(1)}, u32[]{:S(2)}, u32[]{:S(2)}) collective-permute-start(bf16[4,64,256]{2,1,0:T(8,128)(2,1)S(1)} %pad_maximum_fusion.rest_0_), channel_id=1, source_target_pairs={{0,6},{1,7},{2,4},{3,5},{4,2},{5,3},{6,0},{7,1},{8,14},{9,15},{10,... | collective-permute-start | bytes 393224 | tf_op jit(solution)/shard_map/ppermute | solution.py:495
  24.4 1.3 %collective-permute-start.6 = (bf16[4,64,256]{2,1,0:T(8,128)(2,1)S(1)}, bf16[4,64,256]{2,1,0:T(8,128)(2,1)S(1)}, u32[]{:S(2)}, u32[]{:S(2)}) collective-permute-start(bf16[4,64,256]{2,1,0:T(8,128)(2,1)S(1)} %pad_maximum_fusion.rest_0_), channel_id=1, source_target_pairs={{0,1},{1,0},{2,3},{3,2},{4,5},{5,4},{6,7},{7,6},{8,9},{9,8},{10,11... | collective-permute-start | bytes 393224 | tf_op jit(solution)/shard_map/ppermute | solution.py:495
  24.4 1.5 %collective-permute-start.7 = (bf16[4,64,256]{2,1,0:T(8,128)(2,1)S(1)}, bf16[4,64,256]{2,1,0:T(8,128)(2,1)S(1)}, u32[]{:S(2)}, u32[]{:S(2)}) collective-permute-start(bf16[4,64,256]{2,1,0:T(8,128)(2,1)S(1)} %collective-permute-done.3.rest_1_), channel_id=1, source_target_pairs={{0,1},{1,0},{2,3},{3,2},{4,5},{5,4},{6,7},{7,6},{8,9},{9,8},{10,11... | collective-permute-start | bytes 393224 | tf_op jit(solution)/shard_map/ppermute | solution.py:495
  24.9 1.3 %collective-permute-start.8 = (bf16[4,64,256]{2,1,0:T(8,128)(2,1)S(1)}, bf16[4,64,256]{2,1,0:T(8,128)(2,1)S(1)}, u32[]{:S(2)}, u32[]{:S(2)}) collective-permute-start(bf16[4,64,256]{2,1,0:T(8,128)(2,1)S(1)} %collective-permute-done.4.rest_2_), channel_id=1, source_target_pairs={{0,1},{1,0},{2,3},{3,2},{4,5},{5,4},{6,7},{7,6},{8,9},{9,8},{10,11... | collective-permute-start | bytes 393224 | tf_op jit(solution)/shard_map/ppermute | solution.py:495
  24.9 1.5 %collective-permute-start.9 = (bf16[4,64,256]{2,1,0:T(8,128)(2,1)S(1)}, bf16[4,64,256]{2,1,0:T(8,128)(2,1)S(1)}, u32[]{:S(2)}, u32[]{:S(2)}) collective-permute-start(bf16[4,64,256]{2,1,0:T(8,128)(2,1)S(1)} %collective-permute-done.5.rest_3_), channel_id=1, source_target_pairs={{0,1},{1,0},{2,3},{3,2},{4,5},{5,4},{6,7},{7,6},{8,9},{9,8},{10,11... | collective-permute-start | bytes 393224 | tf_op jit(solution)/shard_map/ppermute | solution.py:495
  35.7 30.7 %copy-start.2 = (bf16[4,256,256]{2,1,0:T(8,128)(2,1)S(1)}, bf16[4,256,256]{2,1,0:T(8,128)(2,1)}, u32[]{:S(2)}) copy-start(bf16[4,256,256]{2,1,0:T(8,128)(2,1)} %weight_ref.3) | copy-start | bytes 1572868
  35.7 30.7 %copy-start.3 = (bf16[256,256]{1,0:T(8,128)(2,1)S(1)}, bf16[256,256]{1,0:T(8,128)(2,1)}, u32[]{:S(2)}) copy-start(bf16[256,256]{1,0:T(8,128)(2,1)} %out_w_ref.3) | copy-start | bytes 393220
  35.7 30.7 %copy-start.4 = (bf16[256,64]{0,1:T(8,128)(2,1)S(1)}, bf16[256,64]{0,1:T(8,128)(2,1)}, u32[]{:S(2)}) copy-start(bf16[256,64]{0,1:T(8,128)(2,1)} %param.20) | copy-start | bytes 98308
  35.7 59.2 %copy-start.6 = (s32[256]{0:T(256)S(1)}, s32[256]{0:T(256)}, u32[]{:S(2)}) copy-start(s32[256]{0:T(256)} %param.14) | copy-start | bytes 3076
  35.7 62.9 %copy-start.1 = (bf16[1024,128]{1,0:T(8,128)(2,1)S(1)}, bf16[1024,128]{1,0:T(8,128)(2,1)}, u32[]{:S(2)}) copy-start(bf16[1024,128]{1,0:T(8,128)(2,1)} %refs_11_.1) | copy-start | bytes 786436
  35.8 30.6 %all-to-all-start = ((bf16[32,64,256]{2,1,0:T(8,128)(2,1)}), bf16[32,64,256]{2,1,0:T(8,128)(2,1)S(1)}, u32[]{:S(2)}, u32[]{:S(2)}) async-start(bf16[32,64,256]{2,1,0:T(8,128)(2,1)} %row_attend.1), calls=%async_computation | async-start | bytes 2097152 | tf_op jit(solution)/shard_map/all_to_all | solution.py:547
  79.1 30.5 %copy-start = (bf16[8,256,128]{2,1,0:T(8,128)(2,1)S(1)}, bf16[8,256,128]{2,1,0:T(8,128)(2,1)}, u32[]{:S(2)}) copy-start(bf16[8,256,128]{2,1,0:T(8,128)(2,1)} %pair_ref.3) | copy-start | bytes 1572868
  79.2 7.0 %collective-permute-start.11 = (bf16[256,256]{1,0:T(8,128)(2,1)S(1)}, bf16[256,256]{1,0:T(8,128)(2,1)S(1)}, u32[]{:S(2)}, u32[]{:S(2)}) collective-permute-start(bf16[256,256]{1,0:T(8,128)(2,1)S(1)} %get-tuple-element.38.refs_1_.refs_3_), channel_id=1, source_target_pairs={{0,8},{1,9},{2,10},{3,11},{4,12},{5,13},{6,14},{7,15},{8,0},{9,1},... | collective-permute-start | bytes 393224 | tf_op jit(solution)/shard_map/ppermute | solution.py:495
  79.9 12.9 %collective-permute-start.13 = (bf16[256,256]{1,0:T(8,128)(2,1)S(1)}, bf16[256,256]{1,0:T(8,128)(2,1)S(1)}, u32[]{:S(2)}, u32[]{:S(2)}) collective-permute-start(bf16[256,256]{1,0:T(8,128)(2,1)S(1)} %get-tuple-element.38.refs_1_.refs_3_), channel_id=1, source_target_pairs={{0,16},{1,17},{2,18},{3,19},{4,20},{5,21},{6,22},{7,23},{8,24},{9,... | collective-permute-start | bytes 393224 | tf_op jit(solution)/shard_map/ppermute | solution.py:495
  81.0 13.4 %collective-permute-start.15 = (bf16[256,256]{1,0:T(8,128)(2,1)S(1)}, bf16[256,256]{1,0:T(8,128)(2,1)S(1)}, u32[]{:S(2)}, u32[]{:S(2)}) collective-permute-start(bf16[256,256]{1,0:T(8,128)(2,1)S(1)} %get-tuple-element.38.refs_1_.refs_3_), channel_id=1, source_target_pairs={{0,24},{1,25},{2,26},{3,27},{4,28},{5,29},{6,30},{7,31},{8,16},{9,... | collective-permute-start | bytes 393224 | tf_op jit(solution)/shard_map/ppermute | solution.py:495
  83.5 10.8 %collective-permute-start.10 = (bf16[256,256]{1,0:T(8,128)(2,1)S(1)}, bf16[256,256]{1,0:T(8,128)(2,1)S(1)}, u32[]{:S(2)}, u32[]{:S(2)}) collective-permute-start(bf16[256,256]{1,0:T(8,128)(2,1)S(1)} %get-tuple-element.38.refs_1_.refs_3_), channel_id=1, source_target_pairs={{0,1},{1,0},{2,3},{3,2},{4,5},{5,4},{6,7},{7,6},{8,9},{9,8},{10,11... | collective-permute-start | bytes 393224 | tf_op jit(solution)/shard_map/ppermute | solution.py:495
  83.5 11.3 %collective-permute-start.17 = (bf16[256,256]{1,0:T(8,128)(2,1)S(1)}, bf16[256,256]{1,0:T(8,128)(2,1)S(1)}, u32[]{:S(2)}, u32[]{:S(2)}) collective-permute-start(bf16[256,256]{1,0:T(8,128)(2,1)S(1)} %get-tuple-element.37.refs_0_), channel_id=1, source_target_pairs={{0,2},{1,3},{2,0},{3,1},{4,6},{5,7},{6,4},{7,5},{8,10},{9,11},{10,... | collective-permute-start | bytes 393224 | tf_op jit(solution)/shard_map/ppermute | solution.py:495
  86.1 8.9 %collective-permute-start.18 = (bf16[256,256]{1,0:T(8,128)(2,1)S(1)}, bf16[256,256]{1,0:T(8,128)(2,1)S(1)}, u32[]{:S(2)}, u32[]{:S(2)}) collective-permute-start(bf16[256,256]{1,0:T(8,128)(2,1)S(1)} %get-tuple-element.37.refs_0_), channel_id=1, source_target_pairs={{0,4},{1,5},{2,6},{3,7},{4,0},{5,1},{6,2},{7,3},{8,12},{9,13},{10,... | collective-permute-start | bytes 393224 | tf_op jit(solution)/shard_map/ppermute | solution.py:495
  92.8 5.9 %collective-permute-start.19 = (bf16[256,256]{1,0:T(8,128)(2,1)S(1)}, bf16[256,256]{1,0:T(8,128)(2,1)S(1)}, u32[]{:S(2)}, u32[]{:S(2)}) collective-permute-start(bf16[256,256]{1,0:T(8,128)(2,1)S(1)} %get-tuple-element.37.refs_0_), channel_id=1, source_target_pairs={{0,6},{1,7},{2,4},{3,5},{4,2},{5,3},{6,0},{7,1},{8,14},{9,15},{10,... | collective-permute-start | bytes 393224 | tf_op jit(solution)/shard_map/ppermute | solution.py:495
  94.4 4.3 %collective-permute-start.12 = (bf16[256,256]{1,0:T(8,128)(2,1)S(1)}, bf16[256,256]{1,0:T(8,128)(2,1)S(1)}, u32[]{:S(2)}, u32[]{:S(2)}) collective-permute-start(bf16[256,256]{1,0:T(8,128)(2,1)S(1)} %collective-permute-done.11.refs_3_.refs_5_), channel_id=1, source_target_pairs={{0,1},{1,0},{2,3},{3,2},{4,5},{5,4},{6,7},{7,6},{8,9},{9,8},{10,11... | collective-permute-start | bytes 393224 | tf_op jit(solution)/shard_map/ppermute | solution.py:495
  94.4 4.3 %collective-permute-start.14 = (bf16[256,256]{1,0:T(8,128)(2,1)S(1)}, bf16[256,256]{1,0:T(8,128)(2,1)S(1)}, u32[]{:S(2)}, u32[]{:S(2)}) collective-permute-start(bf16[256,256]{1,0:T(8,128)(2,1)S(1)} %collective-permute-done.13.refs_5_.refs_7_), channel_id=1, source_target_pairs={{0,1},{1,0},{2,3},{3,2},{4,5},{5,4},{6,7},{7,6},{8,9},{9,8},{10,11... | collective-permute-start | bytes 393224 | tf_op jit(solution)/shard_map/ppermute | solution.py:495
  94.9 3.8 %collective-permute-start.16 = (bf16[256,256]{1,0:T(8,128)(2,1)S(1)}, bf16[256,256]{1,0:T(8,128)(2,1)S(1)}, u32[]{:S(2)}, u32[]{:S(2)}) collective-permute-start(bf16[256,256]{1,0:T(8,128)(2,1)S(1)} %collective-permute-done.15.refs_7_.refs_9_), channel_id=1, source_target_pairs={{0,1},{1,0},{2,3},{3,2},{4,5},{5,4},{6,7},{7,6},{8,9},{9,8},{10,11... | collective-permute-start | bytes 393224 | tf_op jit(solution)/shard_map/ppermute | solution.py:495
  101.6 5.7 %collective-permute-start.20 = (bf16[8,64,128]{2,1,0:T(8,128)(2,1)S(1)}, bf16[8,64,128]{2,1,0:T(8,128)(2,1)S(1)}, u32[]{:S(2)}, u32[]{:S(2)}) collective-permute-start(bf16[8,64,128]{2,1,0:T(8,128)(2,1)S(1)} %get-tuple-element.39), channel_id=1, source_target_pairs={{0,2},{1,3},{2,0},{3,1},{4,6},{5,7},{6,4},{7,5},{8,10},{9,11},{10,... | collective-permute-start | bytes 393224 | tf_op jit(solution)/shard_map/ppermute | solution.py:495
  102.4 5.0 %collective-permute-start.21 = (bf16[8,64,128]{2,1,0:T(8,128)(2,1)S(1)}, bf16[8,64,128]{2,1,0:T(8,128)(2,1)S(1)}, u32[]{:S(2)}, u32[]{:S(2)}) collective-permute-start(bf16[8,64,128]{2,1,0:T(8,128)(2,1)S(1)} %get-tuple-element.40), channel_id=1, source_target_pairs={{0,4},{1,5},{2,6},{3,7},{4,0},{5,1},{6,2},{7,3},{8,12},{9,13},{10,... | collective-permute-start | bytes 393224 | tf_op jit(solution)/shard_map/ppermute | solution.py:495
  103.8 5.9 %collective-permute-start.22 = (bf16[8,64,128]{2,1,0:T(8,128)(2,1)S(1)}, bf16[8,64,128]{2,1,0:T(8,128)(2,1)S(1)}, u32[]{:S(2)}, u32[]{:S(2)}) collective-permute-start(bf16[8,64,128]{2,1,0:T(8,128)(2,1)S(1)} %get-tuple-element.41), channel_id=1, source_target_pairs={{0,6},{1,7},{2,4},{3,5},{4,2},{5,3},{6,0},{7,1},{8,14},{9,15},{10,... | collective-permute-start | bytes 393224 | tf_op jit(solution)/shard_map/ppermute | solution.py:495

commit v7 on v6

--- a/solution.py
+++ b/solution.py
@@ -198,6 +198,19 @@
     ]
 
 
+def live_lanes(live_ref, step):
+    length, items = live_ref.shape
+    at = pl.program_id(0)
+    lives = []
+    for n in range(step):
+        live = live_ref[:, n : n + 1]
+        for later in range(1, items // step):
+            column = later * step + n
+            live = jnp.where(at == later, live_ref[:, column : column + 1], live)
+        lives.append(jnp.broadcast_to(live * LIVE_SCALE, (length, LANES)).astype(BF16))
+    return lives
+
+
 def quotient(top, below):
     guess = pl.reciprocal(below, approx=True)
     return top * (guess * (2.0 - below * guess))
@@ -298,9 +311,10 @@
     lanes = head_lanes(length)
     results = []
     parts, rows = out_ref.shape[0], out_ref.shape[1]
+    lives = live_lanes(live_ref, step)
     for s in range(step):
         heads_out = attend_block(
-            q_ref[s], k_ref[s], v_ref[s], live_ref[s], lanes, lambda h: bias_all[h]
+            q_ref[s], k_ref[s], v_ref[s], lives[s], lanes, lambda h: bias_all[h]
         )
         heads_out = (heads_out * g_ref[s]).astype(BF16)
         total = x_ref[s].astype(F32) + nn_dot(heads_out, out_w_ref[...])
@@ -315,13 +329,12 @@
     step = 2
     vmem = pl.BlockSpec(memory_space=pltpu.VMEM)
     block = pl.BlockSpec((step, length, width), lambda i: (i, 0, 0))
-    narrow = pl.BlockSpec((step, length, LANES), lambda i: (i, 0, 0))
     return pl.pallas_call(
         functools.partial(row_attend_kernel, plan, step),
         grid=(seqs // step,),
         in_specs=[pl.BlockSpec(memory_space=pltpu.SMEM)]
         + [block] * 5
-        + [narrow, full_spec(out_weight.shape)]
+        + [full_spec(live.shape), full_spec(out_weight.shape)]
         + [vmem] * len(bias_parts),
         out_specs=pl.BlockSpec((parts, step * rows, width), lambda i: (0, i, 0)),
         out_shape=jax.ShapeDtypeStruct((parts, seqs * rows, width), BF16),
@@ -346,31 +359,27 @@
             held[t] = part.reshape(total_rows, LANES)
 
     lanes = head_lanes(length)
+    lives = live_lanes(live_ref, each)
+    rows = [load_strided(held, step * each + n, items, length) for n in range(each)]
+    results = []
     for n in range(each):
+        normed = layer_normalize(rows[n]).astype(BF16)
+        query, key, value, gate = project(normed, weight_ref)
+        heads_out = attend_block(query, key, value, lives[n], lanes, None)
+        heads_out = (heads_out * gate).astype(BF16)
+        updated = (rows[n] + nn_dot(heads_out, out_w_ref[...])).astype(BF16)
+        normed = layer_normalize(updated.astype(F32)).astype(BF16)
+        factors = nt_dot(factor_ref[...], normed) * mask_ref[pl.ds(step * each + n, 1), :]
+        results.append((updated, factors))
+    feat = FACTOR_CHANNELS
+    for n, (updated, factors) in enumerate(results):
         item = step * each + n
-        current = load_strided(held, item, items, length)
-        normed = layer_normalize(current).astype(BF16)
-        query, key, value, gate = project(normed, weight_ref)
-        live = live_ref[:, n : n + 1]
-        for later in range(1, items // each):
-            at = later * each + n
-            live = jnp.where(step == later, live_ref[:, at : at + 1], live)
-        live = jnp.broadcast_to(live * LIVE_SCALE, (length, LANES)).astype(BF16)
-        heads_out = attend_block(query, key, value, live, lanes, None)
-        heads_out = (heads_out * gate).astype(BF16)
-        updated = (current + nn_dot(heads_out, out_w_ref[...])).astype(BF16).astype(F32)
-        store_strided(held, item, items, updated)
-        normed = layer_normalize(updated).astype(BF16)
-        factors = nt_dot(factor_ref[...], normed) * mask_ref[pl.ds(item, 1), :]
-        left_at = pl.ds(pl.multiple_of(item * FACTOR_CHANNELS, FACTOR_CHANNELS), FACTOR_CHANNELS)
-        left_ref[left_at, :] = factors[:FACTOR_CHANNELS].astype(BF16)
-        store_strided(right_held, item, items, factors[FACTOR_CHANNELS:])
+        out_ref[n] = updated
+        left_ref[pl.ds(pl.multiple_of(item * feat, feat), feat), :] = factors[:feat].astype(BF16)
+        store_strided(right_held, item, items, factors[feat:])
 
     @pl.when(step == items // each - 1)
     def _():
-        for t in range(held.shape[0]):
-            part = held[t].reshape(out_ref.shape[:2] + (LANES,))
-            out_ref[:, :, t * LANES : (t + 1) * LANES] = part.astype(BF16)
         right_ref[...] = joined_tiles(right_held).astype(BF16)
 
 
@@ -378,28 +387,43 @@
     width = moved.shape[2]
     total_rows = moved.shape[0] * moved.shape[1]
     length = total_rows // items
-    factor_t = factor_weight.T
     each = 4
     side = (items * FACTOR_CHANNELS, length)
     left = right = jax.ShapeDtypeStruct(side, BF16)
-    out = jax.ShapeDtypeStruct((length, items, width), BF16)
+    vmem = pl.BlockSpec(memory_space=pltpu.VMEM)
+    operands = in_vmem(moved, live, mask_rows, weight, out_weight, factor_weight.T)
     return pl.pallas_call(
         functools.partial(column_kernel, items, each),
         grid=(items // each,),
-        in_specs=[
-            full_spec(moved.shape),
-            full_spec(live.shape),
-            full_spec(mask_rows.shape),
-            full_spec(weight.shape),
-            full_spec(out_weight.shape),
-            full_spec(factor_t.shape),
-        ],
-        out_specs=[full_spec(out.shape)] + [pl.BlockSpec(memory_space=pltpu.VMEM)] * 2,
-        out_shape=[out, left, right],
+        in_specs=[vmem] * len(operands),
+        out_specs=[pl.BlockSpec((each, length, width), lambda i: (i, 0, 0)), vmem, vmem],
+        out_shape=[pltpu.HBM((items, length, width), BF16), left, right],
         scratch_shapes=[tiled_scratch(total_rows, width), tiled_scratch(*side)],
         compiler_params=params(28),
         name="column_attend",
-    )(moved, live, mask_rows, weight, out_weight, factor_t)
+    )(*operands)
+
+
+def interleave_kernel(rows_ref, out_ref, held):
+    items = rows_ref.shape[0]
+    for item in range(items):
+        store_strided(held, item, items, rows_ref[item].astype(F32))
+    out_ref[...] = joined_tiles(held).reshape(out_ref.shape).astype(BF16)
+
+
+def interleave(rows):
+    items, length, width = rows.shape
+    step = length // 4
+    return pl.pallas_call(
+        interleave_kernel,
+        grid=(length // step,),
+        in_specs=[pl.BlockSpec((items, step, width), lambda i: (0, i, 0))],
+        out_specs=pl.BlockSpec((step, items, width), lambda i: (i, 0, 0)),
+        out_shape=pltpu.HBM((length, items, width), BF16),
+        scratch_shapes=[tiled_scratch(items * step, width)],
+        compiler_params=params(16),
+        name="interleave",
+    )(*in_hbm(rows))
 
 
 def outer_kernel(group, outer, items, *refs):
@@ -518,8 +542,7 @@
 
     own_seqs = lax.dynamic_slice_in_dim(align_mask, dap_index * seq_dev, seq_dev, 0)
     own_res = lax.dynamic_slice_in_dim(align_mask, dap_index * items, items, 1)
-    row_live = (own_seqs.astype(F32) * LIVE_SCALE).astype(BF16)[:, :, None]
-    row_live = jnp.broadcast_to(row_live, (seq_dev, total_res, LANES))
+    row_live = own_seqs.astype(F32).T
     col_live = own_res.astype(F32)
 
     bias = pair_bias_block(pair_rep, bias_weight)
@@ -528,7 +551,7 @@
     *column, projected[0] = lax.optimization_barrier((*column, projected[0]))
     column = jnp.stack(column)
     bias_parts = [exchange(column, count, k) for k in plane]
-    *bias_parts, row_live = lax.optimization_barrier((*bias_parts, row_live))
+    *bias_parts, row_live, col_live = lax.optimization_barrier((*bias_parts, row_live, col_live))
     plan = [[k | z for z in line] for k in plane]
     bias_parts += [exchange(part, count, 1) for part in bias_parts]
     plan += [[offset | 1 for offset in offsets] for offsets in plan]
@@ -555,6 +578,8 @@
         items,
     )
     rights = [exchange(right, count, z) for z in line]
+    updated = interleave(updated)
+    *rights, updated = lax.optimization_barrier((*rights, updated))
     rights = [part for own in rights for part in (own, exchange(own, count, 1))]
     lefts = [exchange(left, count, k) for k in plane]
     sent = outer_product(lefts[1:], rights, outer_out, items)

time: 111 us -> 111 us (level)
  waiting for transfers between devices: 45.5 us -> 39.8 us
  Pallas kernels: 35.4 us -> 39.5 us
    ppermute x23, waiting for transfers between devices: 19.8 us -> 13.9 us  [exchange(): return lax.ppermute(block, 'dap', [(i, i ^ offset) for i in range(count)])]
    pallas_call x0 -> x1, Pallas kernels: none -> 3.64 us  [interleave(): pl.pallas_call(interleave_kernel, grid=(length // step,), in_specs=[pl.Bl...]
    broadcast_in_dim x1 -> x0, local copies, waits for them, and re-layouts: 1.13 us -> none  [per_device_fast(): row_live = jnp.broadcast_to(row_live, (seq_dev, total_res, LANES))]
  transfers between devices with their start and end apart: 24 -> 24, of which waited for: 13 -> 11; matrix products, arithmetic and copies ran while one was open for 1% -> 3% of each run, Pallas kernels for 7% -> 10%
where the time goes in v7:
time: 111 us; the launch traced here: 110 us
  waiting for transfers between devices  39.8 us (36%)
  Pallas kernels  39.5 us (36%)
  starting transfers between devices  27.3 us (25%)
  local copies, waits for them, and re-layouts  2.11 us (2%)
    all_to_all x1, waiting for transfers between devices, per_device_fast(): moved = lax.all_to_all(rows, 'dap', split_axis=0, concat_axis=0, tiled=True)  25.9 us
    ppermute x23, starting transfers between devices, exchange(): return lax.ppermute(block, 'dap', [(i, i ^ offset) for i in range(count)])  22.7 us
    ppermute x23, waiting for transfers between devices, exchange(): return lax.ppermute(block, 'dap', [(i, i ^ offset) for i in range(count)])  13.9 us
    pallas_call x1, Pallas kernels, column_attend(): pl.pallas_call(functools.partial(column_kernel, items, each), grid=(items...  12.5 us
    pallas_call x1, Pallas kernels, row_attend(): pl.pallas_call(functools.partial(row_attend_kernel, plan, step), grid=(se...  9.89 us
    pallas_call x1, Pallas kernels, row_project(): pl.pallas_call(row_project_kernel, grid=(seqs // step,), in_specs=[block,...  5.61 us
    pallas_call x2, Pallas kernels, outer_product(): pl.pallas_call(functools.partial(outer_kernel, group, outer, items), out_...  4.8 us
    all_to_all x1, starting transfers between devices, per_device_fast(): moved = lax.all_to_all(rows, 'dap', split_axis=0, concat_axis=0, tiled=True)  4.57 us
  transfers between devices with their start and end apart: 24, of which 11 were waited for; matrix products, arithmetic and copies ran while one was open for 3% of the time, Pallas kernels for 10%

profile of v7, /device:TPU:0, one launch (start us, length us, event | category | flops | bytes accessed | tf_op | source)
XLA Modules:
  0.0 110.4 jit_solution(11933043523018219245)
XLA Ops:
  0.6 1.8 %pair_bias.1 = bf16[64,256]{1,0:T(8,128)(2,1)S(1)} custom-call(bf16[8,256,128]{2,1,0:T(8,128)(2,1)} %pair_ref.3, bf16[8,128]{1,0:T(8,128)(2,1)} %bitcast.20), custom_call_target="tpu_custom_call" | custom-call | tf_op jit(solution)/shard_map/pair_bias/pallas_call | solution.py:263
  2.4 3.1 %collective-permute-start = (bf16[64,256]{1,0:T(8,128)(2,1)S(1)}, bf16[64,256]{1,0:T(8,128)(2,1)S(1)}, u32[]{:S(2)}, u32[]{:S(2)}) collective-permute-start(bf16[64,256]{1,0:T(8,128)(2,1)S(1)} %pair_bias.1), channel_id=1, source_target_pairs={{0,8},{1,9},{2,10},{3,11},{4,12},{5,13},{6,14},{7,15},{8,0},{9,1},... | collective-permute-start | bytes 98312 | tf_op jit(solution)/shard_map/ppermute | solution.py:519
  5.5 2.6 %collective-permute-start.1 = (bf16[64,256]{1,0:T(8,128)(2,1)S(1)}, bf16[64,256]{1,0:T(8,128)(2,1)S(1)}, u32[]{:S(2)}, u32[]{:S(2)}) collective-permute-start(bf16[64,256]{1,0:T(8,128)(2,1)S(1)} %pair_bias.1), channel_id=1, source_target_pairs={{0,16},{1,17},{2,18},{3,19},{4,20},{5,21},{6,22},{7,23},{8,24},{9,... | collective-permute-start | bytes 98312 | tf_op jit(solution)/shard_map/ppermute | solution.py:519
  8.1 0.7 constant_dynamic-slice_fusion.1
  8.9 0.7 convert_bitcast_fusion.live_ref
  9.6 1.0 constant_dynamic-slice_fusion
  10.7 5.6 %row_project.1 = (bf16[8,256,256]{2,1,0:T(8,128)(2,1)}, bf16[8,256,256]{2,1,0:T(8,128)(2,1)}, bf16[8,256,256]{2,1,0:T(8,128)(2,1)}, f32[8,256,256]{2,1,0:T(8,128)}) custom-call(bf16[8,256,256]{2,1,0:T(8,128)(2,1)} %x_ref.3, bf16[4,256,256]{2,1,0:T(8,128)(2,1)} %weight_ref.2), custom_call_target="tpu_custom_call" | custom-call | tf_op jit(solution)/shard_map/row_project/pallas_call | solution.py:285
  16.3 1.8 %collective-permute-start.3 = (bf16[4,64,256]{2,1,0:T(8,128)(2,1)S(1)}, bf16[4,64,256]{2,1,0:T(8,128)(2,1)S(1)}, u32[]{:S(2)}, u32[]{:S(2)}) collective-permute-start(bf16[4,64,256]{2,1,0:T(8,128)(2,1)S(1)} %pad_maximum_fusion.rest_0_), channel_id=1, source_target_pairs={{0,2},{1,3},{2,0},{3,1},{4,6},{5,7},{6,4},{7,5},{8,10},{9,11},{10,... | collective-permute-start | bytes 393224 | tf_op jit(solution)/shard_map/ppermute | solution.py:519
  18.1 1.5 %collective-permute-start.4 = (bf16[4,64,256]{2,1,0:T(8,128)(2,1)S(1)}, bf16[4,64,256]{2,1,0:T(8,128)(2,1)S(1)}, u32[]{:S(2)}, u32[]{:S(2)}) collective-permute-start(bf16[4,64,256]{2,1,0:T(8,128)(2,1)S(1)} %pad_maximum_fusion.rest_0_), channel_id=1, source_target_pairs={{0,4},{1,5},{2,6},{3,7},{4,0},{5,1},{6,2},{7,3},{8,12},{9,13},{10,... | collective-permute-start | bytes 393224 | tf_op jit(solution)/shard_map/ppermute | solution.py:519
  19.9 2.2 %collective-permute-done.3.rest_1_ = bf16[4,64,256]{2,1,0:T(8,128)(2,1)S(1)} collective-permute-done((bf16[4,64,256]{2,1,0:T(8,128)(2,1)S(1)}, bf16[4,64,256]{2,1,0:T(8,128)(2,1)S(1)}, u32[]{:S(2)}, u32[]{:S(2)}) %collective-permute-start.3) | collective-permute-done | bytes 131104 | tf_op jit(solution)/shard_map/ppermute | solution.py:519
  22.1 3.7 %collective-permute-done.4.rest_2_ = bf16[4,64,256]{2,1,0:T(8,128)(2,1)S(1)} collective-permute-done((bf16[4,64,256]{2,1,0:T(8,128)(2,1)S(1)}, bf16[4,64,256]{2,1,0:T(8,128)(2,1)S(1)}, u32[]{:S(2)}, u32[]{:S(2)}) %collective-permute-start.4) | collective-permute-done | bytes 131104 | tf_op jit(solution)/shard_map/ppermute | solution.py:519
  27.9 9.9 %row_attend.1 = bf16[32,64,256]{2,1,0:T(8,128)(2,1)} custom-call(s32[1]{0:T(128)} %bitcast.me_ref, bf16[8,256,256]{2,1,0:T(8,128)(2,1)} %x_ref.3, bf16[8,256,256]{2,1,0:T(8,128)(2,1)} %get-tuple-element.29.q_ref, bf16[8,256,256]{2,1,0:T(8,128)(2,1)} %get-tuple-element.30.k_ref, bf16[8,256,256]{2,1,0:T(8,128)(2,1)} %get-tuple-element.31.v_ref, ...), custom_call_target="tpu_custom_call" | custom-call | tf_op jit(solution)/shard_map/row_attend/pallas_call | solution.py:332
  37.8 4.6 %all-to-all-start = ((bf16[32,64,256]{2,1,0:T(8,128)(2,1)}), bf16[32,64,256]{2,1,0:T(8,128)(2,1)S(1)}, u32[]{:S(2)}, u32[]{:S(2)}) async-start(bf16[32,64,256]{2,1,0:T(8,128)(2,1)} %row_attend.1), calls=%async_computation | async-start | bytes 2097152 | tf_op jit(solution)/shard_map/all_to_all | solution.py:570
  42.5 25.9 %all-to-all-done.x_ref = bf16[32,64,256]{2,1,0:T(8,128)(2,1)S(1)} async-done(((bf16[32,64,256]{2,1,0:T(8,128)(2,1)}), bf16[32,64,256]{2,1,0:T(8,128)(2,1)S(1)}, u32[]{:S(2)}, u32[]{:S(2)}) %all-to-all-start) | async-done | bytes 1048608 | tf_op jit(solution)/shard_map/all_to_all | solution.py:570
  68.4 12.5 %column_attend.1 = (bf16[8,256,256]{2,1,0:T(8,128)(2,1)}, bf16[256,256]{1,0:T(8,128)(2,1)S(1)}, bf16[256,256]{1,0:T(8,128)(2,1)S(1)}) custom-call(bf16[32,64,256]{2,1,0:T(8,128)(2,1)S(1)} %all-to-all-done.x_ref, f32[256,8]{1,0:T(8,128)S(1)} %copy.19.live_ref, f32[8,256]{1,0:T(8,128)S(1)} %get-tuple-element.54.mask_ref, bf16[4,256,256]{2,1,0:T(8,128)(2,1)S(1)} %copy-done.2, ...), custom_call_target="tpu_custom_call" | custom-call | tf_op jit(solution)/shard_map/column_attend/pallas_call | solution.py:395
  80.9 0.8 collective-permute-start.10
  81.7 1.1 collective-permute-start.11
  82.8 2.5 %collective-permute-start.12 = (bf16[256,256]{1,0:T(8,128)(2,1)S(1)}, bf16[256,256]{1,0:T(8,128)(2,1)S(1)}, u32[]{:S(2)}, u32[]{:S(2)}) collective-permute-start(bf16[256,256]{1,0:T(8,128)(2,1)S(1)} %get-tuple-element.47.refs_1_.refs_3_), channel_id=1, source_target_pairs={{0,24},{1,25},{2,26},{3,27},{4,28},{5,29},{6,30},{7,31},{8,16},{9,... | collective-permute-start | bytes 393224 | tf_op jit(solution)/shard_map/ppermute | solution.py:519
  85.3 1.5 %collective-permute-start.17 = (bf16[256,256]{1,0:T(8,128)(2,1)S(1)}, bf16[256,256]{1,0:T(8,128)(2,1)S(1)}, u32[]{:S(2)}, u32[]{:S(2)}) collective-permute-start(bf16[256,256]{1,0:T(8,128)(2,1)S(1)} %get-tuple-element.46.refs_0_), channel_id=1, source_target_pairs={{0,2},{1,3},{2,0},{3,1},{4,6},{5,7},{6,4},{7,5},{8,10},{9,11},{10,... | collective-permute-start | bytes 393224 | tf_op jit(solution)/shard_map/ppermute | solution.py:519
  86.8 1.5 %collective-permute-start.18 = (bf16[256,256]{1,0:T(8,128)(2,1)S(1)}, bf16[256,256]{1,0:T(8,128)(2,1)S(1)}, u32[]{:S(2)}, u32[]{:S(2)}) collective-permute-start(bf16[256,256]{1,0:T(8,128)(2,1)S(1)} %get-tuple-element.46.refs_0_), channel_id=1, source_target_pairs={{0,4},{1,5},{2,6},{3,7},{4,0},{5,1},{6,2},{7,3},{8,12},{9,13},{10,... | collective-permute-start | bytes 393224 | tf_op jit(solution)/shard_map/ppermute | solution.py:519
  88.3 3.6 %interleave.1 = bf16[256,8,256]{2,1,0:T(8,128)(2,1)} custom-call(bf16[8,256,256]{2,1,0:T(8,128)(2,1)} %get-tuple-element.44.rows_ref), custom_call_target="tpu_custom_call" | custom-call | tf_op jit(solution)/shard_map/interleave/pallas_call | solution.py:417
  91.9 0.5 collective-permute-start.19
  92.4 2.1 %collective-permute-done.11.refs_5_.refs_7_ = bf16[256,256]{1,0:T(8,128)(2,1)S(1)} collective-permute-done((bf16[256,256]{1,0:T(8,128)(2,1)S(1)}, bf16[256,256]{1,0:T(8,128)(2,1)S(1)}, u32[]{:S(2)}, u32[]{:S(2)}) %collective-permute-start.11) | collective-permute-done | bytes 131104 | tf_op jit(solution)/shard_map/ppermute | solution.py:519
  95.7 2.1 %collective-permute-done.19.refs_2_ = bf16[256,256]{1,0:T(8,128)(2,1)S(1)} collective-permute-done((bf16[256,256]{1,0:T(8,128)(2,1)S(1)}, bf16[256,256]{1,0:T(8,128)(2,1)S(1)}, u32[]{:S(2)}, u32[]{:S(2)}) %collective-permute-start.19) | collective-permute-done | bytes 131104 | tf_op jit(solution)/shard_map/ppermute | solution.py:519
  97.8 2.9 %outer_product.3 = (bf16[8,64,128]{2,1,0:T(8,128)(2,1)S(1)}, bf16[8,64,128]{2,1,0:T(8,128)(2,1)S(1)}, bf16[8,64,128]{2,1,0:T(8,128)(2,1)S(1)}) custom-call(bf16[256,256]{1,0:T(8,128)(2,1)S(1)} %collective-permute-done.17.refs_0_, bf16[256,256]{1,0:T(8,128)(2,1)S(1)} %collective-permute-done.18.refs_1_, bf16[256,256]{1,0:T(8,128)(2,1)S(1)} %collective-permute-done.19.refs_2_, ...), custom_call_target="tpu_custom_call" | custom-call | tf_op jit(solution)/shard_map/outer_product/pallas_call | solution.py:471
  100.7 0.6 collective-permute-start.20
  101.3 0.5 collective-permute-start.21
  101.9 2.4 %collective-permute-start.22 = (bf16[8,64,128]{2,1,0:T(8,128)(2,1)S(1)}, bf16[8,64,128]{2,1,0:T(8,128)(2,1)S(1)}, u32[]{:S(2)}, u32[]{:S(2)}) collective-permute-start(bf16[8,64,128]{2,1,0:T(8,128)(2,1)S(1)} %get-tuple-element.53), channel_id=1, source_target_pairs={{0,6},{1,7},{2,4},{3,5},{4,2},{5,3},{6,0},{7,1},{8,14},{9,15},{10,... | collective-permute-start | bytes 393224 | tf_op jit(solution)/shard_map/ppermute | solution.py:519
  104.5 1.9 %outer_product.2.refs_0_ = bf16[8,64,128]{2,1,0:T(8,128)(2,1)S(1)} custom-call(bf16[256,256]{1,0:T(8,128)(2,1)S(1)} %get-tuple-element.46.refs_0_, bf16[256,256]{1,0:T(8,128)(2,1)S(1)} %get-tuple-element.47.refs_1_.refs_3_, bf16[256,256]{1,0:T(8,128)(2,1)S(1)} %collective-permute-done.13.refs_2_.refs_4_, ...), custom_call_target="tpu_custom_call" | custom-call | tf_op jit(solution)/shard_map/outer_product/pallas_call | solution.py:471
  106.4 0.6 collective-permute-done.20.refs_1_
  107.0 2.1 %collective-permute-done.21.refs_2_ = bf16[8,64,128]{2,1,0:T(8,128)(2,1)S(1)} collective-permute-done((bf16[8,64,128]{2,1,0:T(8,128)(2,1)S(1)}, bf16[8,64,128]{2,1,0:T(8,128)(2,1)S(1)}, u32[]{:S(2)}, u32[]{:S(2)}) %collective-permute-start.21) | collective-permute-done | bytes 131104 | tf_op jit(solution)/shard_map/ppermute | solution.py:519
  109.1 1.2 %finish.1 = bf16[8,256,128]{2,1,0:T(8,128)(2,1)} custom-call(s32[1]{0:T(128)} %bitcast.me_ref, bf16[8,256,128]{2,1,0:T(8,128)(2,1)S(1)} %copy-done, f32[256,8]{1,0:T(8,128)S(1)} %fusion.1.scale_ref, bf16[8,64,128]{2,1,0:T(8,128)(2,1)S(1)} %outer_product.2.refs_0_, bf16[8,64,128]{2,1,0:T(8,128)(2,1)S(1)} %collective-permute-done.20.refs_1_, ...), custom_call_target="tpu_custom_call" | custom-call | tf_op jit(solution)/shard_map/finish/pallas_call | solution.py:506
  (49 shorter events, 4.1 us)
Async XLA Ops:
  2.4 13.9 %collective-permute-start = (bf16[64,256]{1,0:T(8,128)(2,1)S(1)}, bf16[64,256]{1,0:T(8,128)(2,1)S(1)}, u32[]{:S(2)}, u32[]{:S(2)}) collective-permute-start(bf16[64,256]{1,0:T(8,128)(2,1)S(1)} %pair_bias.1), channel_id=1, source_target_pairs={{0,8},{1,9},{2,10},{3,11},{4,12},{5,13},{6,14},{7,15},{8,0},{9,1},... | collective-permute-start | bytes 98312 | tf_op jit(solution)/shard_map/ppermute | solution.py:519
  5.5 10.8 %collective-permute-start.1 = (bf16[64,256]{1,0:T(8,128)(2,1)S(1)}, bf16[64,256]{1,0:T(8,128)(2,1)S(1)}, u32[]{:S(2)}, u32[]{:S(2)}) collective-permute-start(bf16[64,256]{1,0:T(8,128)(2,1)S(1)} %pair_bias.1), channel_id=1, source_target_pairs={{0,16},{1,17},{2,18},{3,19},{4,20},{5,21},{6,22},{7,23},{8,24},{9,... | collective-permute-start | bytes 98312 | tf_op jit(solution)/shard_map/ppermute | solution.py:519
  8.1 8.2 %collective-permute-start.2 = (bf16[64,256]{1,0:T(8,128)(2,1)S(1)}, bf16[64,256]{1,0:T(8,128)(2,1)S(1)}, u32[]{:S(2)}, u32[]{:S(2)}) collective-permute-start(bf16[64,256]{1,0:T(8,128)(2,1)S(1)} %pair_bias.1), channel_id=1, source_target_pairs={{0,24},{1,25},{2,26},{3,27},{4,28},{5,29},{6,30},{7,31},{8,16},{9,... | collective-permute-start | bytes 98312 | tf_op jit(solution)/shard_map/ppermute | solution.py:519
  16.3 5.8 %collective-permute-start.3 = (bf16[4,64,256]{2,1,0:T(8,128)(2,1)S(1)}, bf16[4,64,256]{2,1,0:T(8,128)(2,1)S(1)}, u32[]{:S(2)}, u32[]{:S(2)}) collective-permute-start(bf16[4,64,256]{2,1,0:T(8,128)(2,1)S(1)} %pad_maximum_fusion.rest_0_), channel_id=1, source_target_pairs={{0,2},{1,3},{2,0},{3,1},{4,6},{5,7},{6,4},{7,5},{8,10},{9,11},{10,... | collective-permute-start | bytes 393224 | tf_op jit(solution)/shard_map/ppermute | solution.py:519
  18.1 7.7 %collective-permute-start.4 = (bf16[4,64,256]{2,1,0:T(8,128)(2,1)S(1)}, bf16[4,64,256]{2,1,0:T(8,128)(2,1)S(1)}, u32[]{:S(2)}, u32[]{:S(2)}) collective-permute-start(bf16[4,64,256]{2,1,0:T(8,128)(2,1)S(1)} %pad_maximum_fusion.rest_0_), channel_id=1, source_target_pairs={{0,4},{1,5},{2,6},{3,7},{4,0},{5,1},{6,2},{7,3},{8,12},{9,13},{10,... | collective-permute-start | bytes 393224 | tf_op jit(solution)/shard_map/ppermute | solution.py:519
  19.6 6.2 %collective-permute-start.5 = (bf16[4,64,256]{2,1,0:T(8,128)(2,1)S(1)}, bf16[4,64,256]{2,1,0:T(8,128)(2,1)S(1)}, u32[]{:S(2)}, u32[]{:S(2)}) collective-permute-start(bf16[4,64,256]{2,1,0:T(8,128)(2,1)S(1)} %pad_maximum_fusion.rest_0_), channel_id=1, source_target_pairs={{0,6},{1,7},{2,4},{3,5},{4,2},{5,3},{6,0},{7,1},{8,14},{9,15},{10,... | collective-permute-start | bytes 393224 | tf_op jit(solution)/shard_map/ppermute | solution.py:519
  25.8 1.3 %collective-permute-start.6 = (bf16[4,64,256]{2,1,0:T(8,128)(2,1)S(1)}, bf16[4,64,256]{2,1,0:T(8,128)(2,1)S(1)}, u32[]{:S(2)}, u32[]{:S(2)}) collective-permute-start(bf16[4,64,256]{2,1,0:T(8,128)(2,1)S(1)} %pad_maximum_fusion.rest_0_), channel_id=1, source_target_pairs={{0,1},{1,0},{2,3},{3,2},{4,5},{5,4},{6,7},{7,6},{8,9},{9,8},{10,11... | collective-permute-start | bytes 393224 | tf_op jit(solution)/shard_map/ppermute | solution.py:519
  25.8 1.5 %collective-permute-start.7 = (bf16[4,64,256]{2,1,0:T(8,128)(2,1)S(1)}, bf16[4,64,256]{2,1,0:T(8,128)(2,1)S(1)}, u32[]{:S(2)}, u32[]{:S(2)}) collective-permute-start(bf16[4,64,256]{2,1,0:T(8,128)(2,1)S(1)} %collective-permute-done.3.rest_1_), channel_id=1, source_target_pairs={{0,1},{1,0},{2,3},{3,2},{4,5},{5,4},{6,7},{7,6},{8,9},{9,8},{10,11... | collective-permute-start | bytes 393224 | tf_op jit(solution)/shard_map/ppermute | solution.py:519
  26.3 1.3 %collective-permute-start.8 = (bf16[4,64,256]{2,1,0:T(8,128)(2,1)S(1)}, bf16[4,64,256]{2,1,0:T(8,128)(2,1)S(1)}, u32[]{:S(2)}, u32[]{:S(2)}) collective-permute-start(bf16[4,64,256]{2,1,0:T(8,128)(2,1)S(1)} %collective-permute-done.4.rest_2_), channel_id=1, source_target_pairs={{0,1},{1,0},{2,3},{3,2},{4,5},{5,4},{6,7},{7,6},{8,9},{9,8},{10,11... | collective-permute-start | bytes 393224 | tf_op jit(solution)/shard_map/ppermute | solution.py:519
  26.3 1.5 %collective-permute-start.9 = (bf16[4,64,256]{2,1,0:T(8,128)(2,1)S(1)}, bf16[4,64,256]{2,1,0:T(8,128)(2,1)S(1)}, u32[]{:S(2)}, u32[]{:S(2)}) collective-permute-start(bf16[4,64,256]{2,1,0:T(8,128)(2,1)S(1)} %collective-permute-done.5.rest_3_), channel_id=1, source_target_pairs={{0,1},{1,0},{2,3},{3,2},{4,5},{5,4},{6,7},{7,6},{8,9},{9,8},{10,11... | collective-permute-start | bytes 393224 | tf_op jit(solution)/shard_map/ppermute | solution.py:519
  37.8 30.7 %copy-start.2 = (bf16[4,256,256]{2,1,0:T(8,128)(2,1)S(1)}, bf16[4,256,256]{2,1,0:T(8,128)(2,1)}, u32[]{:S(2)}) copy-start(bf16[4,256,256]{2,1,0:T(8,128)(2,1)} %weight_ref.3) | copy-start | bytes 1572868
  37.8 30.7 %copy-start.3 = (bf16[256,256]{1,0:T(8,128)(2,1)S(1)}, bf16[256,256]{1,0:T(8,128)(2,1)}, u32[]{:S(2)}) copy-start(bf16[256,256]{1,0:T(8,128)(2,1)} %out_w_ref.3) | copy-start | bytes 393220
  37.8 30.6 %copy-start.4 = (bf16[256,64]{0,1:T(8,128)(2,1)S(1)}, bf16[256,64]{0,1:T(8,128)(2,1)}, u32[]{:S(2)}) copy-start(bf16[256,64]{0,1:T(8,128)(2,1)} %param.20) | copy-start | bytes 98308
  37.8 30.6 %all-to-all-start = ((bf16[32,64,256]{2,1,0:T(8,128)(2,1)}), bf16[32,64,256]{2,1,0:T(8,128)(2,1)S(1)}, u32[]{:S(2)}, u32[]{:S(2)}) async-start(bf16[32,64,256]{2,1,0:T(8,128)(2,1)} %row_attend.1), calls=%async_computation | async-start | bytes 2097152 | tf_op jit(solution)/shard_map/all_to_all | solution.py:570
  42.3 53.3 %copy-start.6 = (s32[256]{0:T(256)S(1)}, s32[256]{0:T(256)}, u32[]{:S(2)}) copy-start(s32[256]{0:T(256)} %param.14) | copy-start | bytes 3076
  42.4 55.4 %copy-start.1 = (bf16[1024,128]{1,0:T(8,128)(2,1)S(1)}, bf16[1024,128]{1,0:T(8,128)(2,1)}, u32[]{:S(2)}) copy-start(bf16[1024,128]{1,0:T(8,128)(2,1)} %refs_11_.1) | copy-start | bytes 786436
  80.9 23.3 %copy-start.5 = (s32[256,256]{1,0:T(8,128)S(1)}, s32[256,256]{1,0:T(8,128)}, u32[]{:S(2)}) copy-start(s32[256,256]{1,0:T(8,128)} %param.13) | copy-start | bytes 786436
  80.9 11.0 %collective-permute-start.10 = (bf16[256,256]{1,0:T(8,128)(2,1)S(1)}, bf16[256,256]{1,0:T(8,128)(2,1)S(1)}, u32[]{:S(2)}, u32[]{:S(2)}) collective-permute-start(bf16[256,256]{1,0:T(8,128)(2,1)S(1)} %get-tuple-element.47.refs_1_.refs_3_), channel_id=1, source_target_pairs={{0,8},{1,9},{2,10},{3,11},{4,12},{5,13},{6,14},{7,15},{8,0},{9,1},... | collective-permute-start | bytes 393224 | tf_op jit(solution)/shard_map/ppermute | solution.py:519
  81.7 12.9 %collective-permute-start.11 = (bf16[256,256]{1,0:T(8,128)(2,1)S(1)}, bf16[256,256]{1,0:T(8,128)(2,1)S(1)}, u32[]{:S(2)}, u32[]{:S(2)}) collective-permute-start(bf16[256,256]{1,0:T(8,128)(2,1)S(1)} %get-tuple-element.47.refs_1_.refs_3_), channel_id=1, source_target_pairs={{0,16},{1,17},{2,18},{3,19},{4,20},{5,21},{6,22},{7,23},{8,24},{9,... | collective-permute-start | bytes 393224 | tf_op jit(solution)/shard_map/ppermute | solution.py:519
  82.8 11.8 %collective-permute-start.12 = (bf16[256,256]{1,0:T(8,128)(2,1)S(1)}, bf16[256,256]{1,0:T(8,128)(2,1)S(1)}, u32[]{:S(2)}, u32[]{:S(2)}) collective-permute-start(bf16[256,256]{1,0:T(8,128)(2,1)S(1)} %get-tuple-element.47.refs_1_.refs_3_), channel_id=1, source_target_pairs={{0,24},{1,25},{2,26},{3,27},{4,28},{5,29},{6,30},{7,31},{8,16},{9,... | collective-permute-start | bytes 393224 | tf_op jit(solution)/shard_map/ppermute | solution.py:519
  85.3 9.8 %collective-permute-start.17 = (bf16[256,256]{1,0:T(8,128)(2,1)S(1)}, bf16[256,256]{1,0:T(8,128)(2,1)S(1)}, u32[]{:S(2)}, u32[]{:S(2)}) collective-permute-start(bf16[256,256]{1,0:T(8,128)(2,1)S(1)} %get-tuple-element.46.refs_0_), channel_id=1, source_target_pairs={{0,2},{1,3},{2,0},{3,1},{4,6},{5,7},{6,4},{7,5},{8,10},{9,11},{10,... | collective-permute-start | bytes 393224 | tf_op jit(solution)/shard_map/ppermute | solution.py:519
  86.8 8.3 %collective-permute-start.18 = (bf16[256,256]{1,0:T(8,128)(2,1)S(1)}, bf16[256,256]{1,0:T(8,128)(2,1)S(1)}, u32[]{:S(2)}, u32[]{:S(2)}) collective-permute-start(bf16[256,256]{1,0:T(8,128)(2,1)S(1)} %get-tuple-element.46.refs_0_), channel_id=1, source_target_pairs={{0,4},{1,5},{2,6},{3,7},{4,0},{5,1},{6,2},{7,3},{8,12},{9,13},{10,... | collective-permute-start | bytes 393224 | tf_op jit(solution)/shard_map/ppermute | solution.py:519
  91.9 17.2 %copy-start = (bf16[8,256,128]{2,1,0:T(8,128)(2,1)S(1)}, bf16[8,256,128]{2,1,0:T(8,128)(2,1)}, u32[]{:S(2)}) copy-start(bf16[8,256,128]{2,1,0:T(8,128)(2,1)} %pair_ref.3) | copy-start | bytes 1572868
  91.9 5.9 %collective-permute-start.19 = (bf16[256,256]{1,0:T(8,128)(2,1)S(1)}, bf16[256,256]{1,0:T(8,128)(2,1)S(1)}, u32[]{:S(2)}, u32[]{:S(2)}) collective-permute-start(bf16[256,256]{1,0:T(8,128)(2,1)S(1)} %get-tuple-element.46.refs_0_), channel_id=1, source_target_pairs={{0,6},{1,7},{2,4},{3,5},{4,2},{5,3},{6,0},{7,1},{8,14},{9,15},{10,... | collective-permute-start | bytes 393224 | tf_op jit(solution)/shard_map/ppermute | solution.py:519
  94.6 3.2 %collective-permute-start.13 = (bf16[256,256]{1,0:T(8,128)(2,1)S(1)}, bf16[256,256]{1,0:T(8,128)(2,1)S(1)}, u32[]{:S(2)}, u32[]{:S(2)}) collective-permute-start(bf16[256,256]{1,0:T(8,128)(2,1)S(1)} %get-tuple-element.47.refs_1_.refs_3_), channel_id=1, source_target_pairs={{0,1},{1,0},{2,3},{3,2},{4,5},{5,4},{6,7},{7,6},{8,9},{9,8},{10,11... | collective-permute-start | bytes 393224 | tf_op jit(solution)/shard_map/ppermute | solution.py:519
  94.6 3.2 %collective-permute-start.14 = (bf16[256,256]{1,0:T(8,128)(2,1)S(1)}, bf16[256,256]{1,0:T(8,128)(2,1)S(1)}, u32[]{:S(2)}, u32[]{:S(2)}) collective-permute-start(bf16[256,256]{1,0:T(8,128)(2,1)S(1)} %collective-permute-done.10.refs_3_.refs_5_), channel_id=1, source_target_pairs={{0,1},{1,0},{2,3},{3,2},{4,5},{5,4},{6,7},{7,6},{8,9},{9,8},{10,11... | collective-permute-start | bytes 393224 | tf_op jit(solution)/shard_map/ppermute | solution.py:519
  95.1 2.7 %collective-permute-start.15 = (bf16[256,256]{1,0:T(8,128)(2,1)S(1)}, bf16[256,256]{1,0:T(8,128)(2,1)S(1)}, u32[]{:S(2)}, u32[]{:S(2)}) collective-permute-start(bf16[256,256]{1,0:T(8,128)(2,1)S(1)} %collective-permute-done.11.refs_5_.refs_7_), channel_id=1, source_target_pairs={{0,1},{1,0},{2,3},{3,2},{4,5},{5,4},{6,7},{7,6},{8,9},{9,8},{10,11... | collective-permute-start | bytes 393224 | tf_op jit(solution)/shard_map/ppermute | solution.py:519
  95.1 2.7 %collective-permute-start.16 = (bf16[256,256]{1,0:T(8,128)(2,1)S(1)}, bf16[256,256]{1,0:T(8,128)(2,1)S(1)}, u32[]{:S(2)}, u32[]{:S(2)}) collective-permute-start(bf16[256,256]{1,0:T(8,128)(2,1)S(1)} %collective-permute-done.12.refs_7_.refs_9_), channel_id=1, source_target_pairs={{0,1},{1,0},{2,3},{3,2},{4,5},{5,4},{6,7},{7,6},{8,9},{9,8},{10,11... | collective-permute-start | bytes 393224 | tf_op jit(solution)/shard_map/ppermute | solution.py:519
  100.7 6.3 %collective-permute-start.20 = (bf16[8,64,128]{2,1,0:T(8,128)(2,1)S(1)}, bf16[8,64,128]{2,1,0:T(8,128)(2,1)S(1)}, u32[]{:S(2)}, u32[]{:S(2)}) collective-permute-start(bf16[8,64,128]{2,1,0:T(8,128)(2,1)S(1)} %get-tuple-element.51), channel_id=1, source_target_pairs={{0,2},{1,3},{2,0},{3,1},{4,6},{5,7},{6,4},{7,5},{8,10},{9,11},{10,... | collective-permute-start | bytes 393224 | tf_op jit(solution)/shard_map/ppermute | solution.py:519
  101.3 7.8 %collective-permute-start.21 = (bf16[8,64,128]{2,1,0:T(8,128)(2,1)S(1)}, bf16[8,64,128]{2,1,0:T(8,128)(2,1)S(1)}, u32[]{:S(2)}, u32[]{:S(2)}) collective-permute-start(bf16[8,64,128]{2,1,0:T(8,128)(2,1)S(1)} %get-tuple-element.52), channel_id=1, source_target_pairs={{0,4},{1,5},{2,6},{3,7},{4,0},{5,1},{6,2},{7,3},{8,12},{9,13},{10,... | collective-permute-start | bytes 393224 | tf_op jit(solution)/shard_map/ppermute | solution.py:519
  101.9 7.2 %collective-permute-start.22 = (bf16[8,64,128]{2,1,0:T(8,128)(2,1)S(1)}, bf16[8,64,128]{2,1,0:T(8,128)(2,1)S(1)}, u32[]{:S(2)}, u32[]{:S(2)}) collective-permute-start(bf16[8,64,128]{2,1,0:T(8,128)(2,1)S(1)} %get-tuple-element.53), channel_id=1, source_target_pairs={{0,6},{1,7},{2,4},{3,5},{4,2},{5,3},{6,0},{7,1},{8,14},{9,15},{10,... | collective-permute-start | bytes 393224 | tf_op jit(solution)/shard_map/ppermute | solution.py:519

commit v8 on v7

--- a/solution.py
+++ b/solution.py
@@ -198,17 +198,9 @@
     ]
 
 
-def live_lanes(live_ref, step):
-    length, items = live_ref.shape
-    at = pl.program_id(0)
-    lives = []
-    for n in range(step):
-        live = live_ref[:, n : n + 1]
-        for later in range(1, items // step):
-            column = later * step + n
-            live = jnp.where(at == later, live_ref[:, column : column + 1], live)
-        lives.append(jnp.broadcast_to(live * LIVE_SCALE, (length, LANES)).astype(BF16))
-    return lives
+def one_hot(shape, dim, place, value=1.0):
+    hit = lax.broadcasted_iota(jnp.int32, shape, dim) == place
+    return jnp.where(hit, value, 0.0).astype(BF16)
 
 
 def quotient(top, below):
@@ -216,26 +208,49 @@
     return top * (guess * (2.0 - below * guess))
 
 
-def attend_block(query, key, value, live, lanes, bias_of):
-    pieces = []
+def attend_all(items, lanes, bias_of):
     per_tile = LANES // HEAD_CHANNELS
-    rows = query.shape[0]
-    for tile in range(query.shape[1] // LANES):
+    rows, width = items[0][0].shape
+    tasks = [(n, tile) for n in range(len(items)) for tile in range(width // LANES)]
+    scores, raised, pieces = {}, {}, [[] for _ in items]
+
+    def score(at):
+        n, tile = tasks[at]
         cut = slice(tile * LANES, (tile + 1) * LANES)
-        query_t, key_t = query[:, cut], key[:, cut]
-        value_t = value[:, cut] * live
-        stacked = jnp.concatenate([query_t * lanes[t][:rows] for t in range(per_tile)], axis=0)
-        stacked = nt_dot(stacked, key_t)
-        raised, sides = [], []
+        query, key = items[n][0][:, cut], items[n][1][:, cut]
+        stacked = jnp.concatenate([query * lanes[t] for t in range(per_tile)], axis=0)
+        scores[at] = nt_dot(stacked, key)
+
+    def raise_scores(at):
+        n, tile = tasks[at]
+        stacked = scores.pop(at)
+        parts = []
         for t in range(per_tile):
-            scores = stacked[t * rows : (t + 1) * rows]
+            part = stacked[t * rows : (t + 1) * rows]
             if bias_of is not None:
-                scores = scores + bias_of(tile * per_tile + t)
-            raised.append(jnp.exp2(scores).astype(BF16))
-            sides.append(jnp.concatenate([value_t * lanes[t], live * lanes[t]], axis=1))
-        total = nn_dot(jnp.concatenate(raised, axis=1), jnp.concatenate(sides, axis=0))
-        pieces.append(quotient(total[:, :LANES], total[:, LANES:]))
-    return jnp.concatenate(pieces, axis=1)
+                part = part + bias_of(tile * per_tile + t)
+            parts.append(jnp.exp2(part).astype(BF16))
+        raised[at] = jnp.concatenate(parts, axis=1)
+
+    def gather(at):
+        n, tile = tasks[at]
+        cut = slice(tile * LANES, (tile + 1) * LANES)
+        live = items[n][3]
+        value = items[n][2][:, cut] * live
+        sides = [
+            jnp.concatenate([value * lanes[t], live * lanes[t]], axis=1) for t in range(per_tile)
+        ]
+        total = nn_dot(raised.pop(at), jnp.concatenate(sides, axis=0))
+        pieces[n].append(quotient(total[:, :LANES], total[:, LANES:]))
+
+    for at in range(len(tasks) + 2):
+        if at < len(tasks):
+            score(at)
+        if 0 <= at - 2:
+            gather(at - 2)
+        if 0 <= at - 1 < len(tasks):
+            raise_scores(at - 1)
+    return [jnp.concatenate(p, axis=1) for p in pieces]
 
 
 def project(normed, weight_ref):
@@ -294,7 +309,7 @@
 
 
 def row_attend_kernel(
-    plan, step, me_ref, x_ref, q_ref, k_ref, v_ref, g_ref, live_ref, out_w_ref, *rest
+    plan, step, seqs, me_ref, x_ref, q_ref, k_ref, v_ref, g_ref, mask_ref, out_w_ref, *rest
 ):
     bias_refs, out_ref, bias_all = rest[: len(plan)], rest[-2], rest[-1]
     heads, length, _ = bias_all.shape
@@ -309,13 +324,19 @@
                 bias_all[:, pl.ds(pl.multiple_of(owner * rows, rows), rows), :] = block
 
     lanes = head_lanes(length)
+    parts, rows = out_ref.shape[0], out_ref.shape[1]
+    own = mask_ref[pl.ds(pl.multiple_of(me_ref[0] * seqs, seqs), seqs), :]
+    own = own.astype(F32).astype(BF16)
+    items = []
+    for s in range(step):
+        place = pl.program_id(0) * step + s
+        spot = one_hot((seqs, LANES), 0, place, LIVE_SCALE)
+        live = lax.dot_general(
+            own, spot, (((0,), (0,)), ((), ())), preferred_element_type=F32
+        ).astype(BF16)
+        items.append((q_ref[s], k_ref[s], v_ref[s], live))
     results = []
-    parts, rows = out_ref.shape[0], out_ref.shape[1]
-    lives = live_lanes(live_ref, step)
-    for s in range(step):
-        heads_out = attend_block(
-            q_ref[s], k_ref[s], v_ref[s], lives[s], lanes, lambda h: bias_all[h]
-        )
+    for s, heads_out in enumerate(attend_all(items, lanes, lambda h: bias_all[h])):
         heads_out = (heads_out * g_ref[s]).astype(BF16)
         total = x_ref[s].astype(F32) + nn_dot(heads_out, out_w_ref[...])
         results.append(total.reshape(parts, 1, rows // step, total.shape[1]))
@@ -323,29 +344,29 @@
     out_ref[...] = joined.reshape(out_ref.shape).astype(BF16)
 
 
-def row_attend(me, alignment, projected, live, out_weight, bias_parts, plan, parts):
+def row_attend(me, alignment, projected, mask, out_weight, bias_parts, plan, parts):
     seqs, length, width = alignment.shape
     rows = length // parts
     step = 2
     vmem = pl.BlockSpec(memory_space=pltpu.VMEM)
     block = pl.BlockSpec((step, length, width), lambda i: (i, 0, 0))
     return pl.pallas_call(
-        functools.partial(row_attend_kernel, plan, step),
+        functools.partial(row_attend_kernel, plan, step, seqs),
         grid=(seqs // step,),
         in_specs=[pl.BlockSpec(memory_space=pltpu.SMEM)]
         + [block] * 5
-        + [full_spec(live.shape), full_spec(out_weight.shape)]
+        + [full_spec(mask.shape), full_spec(out_weight.shape)]
         + [vmem] * len(bias_parts),
         out_specs=pl.BlockSpec((parts, step * rows, width), lambda i: (0, i, 0)),
         out_shape=jax.ShapeDtypeStruct((parts, seqs * rows, width), BF16),
         scratch_shapes=[pltpu.VMEM((ATTN_HEAD_COUNT, length, length), F32)],
         compiler_params=params(24),
         name="row_attend",
-    )(me, *in_hbm(alignment, *projected, live, out_weight), *in_vmem(*bias_parts))
+    )(me, *in_hbm(alignment, *projected, mask, out_weight), *in_vmem(*bias_parts))
 
 
 def column_kernel(
-    items, each, x_ref, live_ref, mask_ref, weight_ref, out_w_ref, factor_ref,
+    items, each, me_ref, x_ref, mask_ref, weight_ref, out_w_ref, factor_ref,
     out_ref, left_ref, right_ref, held, right_held,
 ):
     step = pl.program_id(0)
@@ -359,18 +380,24 @@
             held[t] = part.reshape(total_rows, LANES)
 
     lanes = head_lanes(length)
-    lives = live_lanes(live_ref, each)
+    mask = mask_ref[...].astype(F32).astype(BF16)
+    residues = mask.shape[1]
+    place = me_ref[0] * items + step * each
     rows = [load_strided(held, step * each + n, items, length) for n in range(each)]
-    results = []
+    inputs, gates = [], []
     for n in range(each):
         normed = layer_normalize(rows[n]).astype(BF16)
         query, key, value, gate = project(normed, weight_ref)
-        heads_out = attend_block(query, key, value, lives[n], lanes, None)
-        heads_out = (heads_out * gate).astype(BF16)
+        live = nn_dot(mask, one_hot((residues, LANES), 0, place + n, LIVE_SCALE)).astype(BF16)
+        inputs.append((query, key, value, live))
+        gates.append(gate)
+    results = []
+    for n, heads_out in enumerate(attend_all(inputs, lanes, None)):
+        heads_out = (heads_out * gates[n]).astype(BF16)
         updated = (rows[n] + nn_dot(heads_out, out_w_ref[...])).astype(BF16)
         normed = layer_normalize(updated.astype(F32)).astype(BF16)
-        factors = nt_dot(factor_ref[...], normed) * mask_ref[pl.ds(step * each + n, 1), :]
-        results.append((updated, factors))
+        live_row = nt_dot(one_hot((8, residues), 1, place + n), mask)[:1]
+        results.append((updated, nt_dot(factor_ref[...], normed) * live_row))
     feat = FACTOR_CHANNELS
     for n, (updated, factors) in enumerate(results):
         item = step * each + n
@@ -383,7 +410,7 @@
         right_ref[...] = joined_tiles(right_held).astype(BF16)
 
 
-def column_attend(moved, live, mask_rows, weight, out_weight, factor_weight, items):
+def column_attend(me, moved, mask, weight, out_weight, factor_weight, items):
     width = moved.shape[2]
     total_rows = moved.shape[0] * moved.shape[1]
     length = total_rows // items
@@ -391,17 +418,17 @@
     side = (items * FACTOR_CHANNELS, length)
     left = right = jax.ShapeDtypeStruct(side, BF16)
     vmem = pl.BlockSpec(memory_space=pltpu.VMEM)
-    operands = in_vmem(moved, live, mask_rows, weight, out_weight, factor_weight.T)
+    operands = in_vmem(moved, mask, weight, out_weight, factor_weight.T)
     return pl.pallas_call(
         functools.partial(column_kernel, items, each),
         grid=(items // each,),
-        in_specs=[vmem] * len(operands),
+        in_specs=[pl.BlockSpec(memory_space=pltpu.SMEM)] + [vmem] * len(operands),
         out_specs=[pl.BlockSpec((each, length, width), lambda i: (i, 0, 0)), vmem, vmem],
         out_shape=[pltpu.HBM((items, length, width), BF16), left, right],
         scratch_shapes=[tiled_scratch(total_rows, width), tiled_scratch(*side)],
         compiler_params=params(28),
         name="column_attend",
-    )(*operands)
+    )(me, *operands)
 
 
 def interleave_kernel(rows_ref, out_ref, held):
@@ -536,14 +563,7 @@
     dap_index = lax.axis_index("dap")
     me = jnp.reshape(dap_index, (1,)).astype(jnp.int32)
     plane, line = offset_groups(count)
-    seq_dev = alignment.shape[0]
     items = pair_rep.shape[0]
-    total_seqs, total_res = align_mask.shape
-
-    own_seqs = lax.dynamic_slice_in_dim(align_mask, dap_index * seq_dev, seq_dev, 0)
-    own_res = lax.dynamic_slice_in_dim(align_mask, dap_index * items, items, 1)
-    row_live = own_seqs.astype(F32).T
-    col_live = own_res.astype(F32)
 
     bias = pair_bias_block(pair_rep, bias_weight)
     projected = list(row_project(alignment, row_proj_weight))
@@ -551,33 +571,33 @@
     *column, projected[0] = lax.optimization_barrier((*column, projected[0]))
     column = jnp.stack(column)
     bias_parts = [exchange(column, count, k) for k in plane]
-    *bias_parts, row_live, col_live = lax.optimization_barrier((*bias_parts, row_live, col_live))
     plan = [[k | z for z in line] for k in plane]
     bias_parts += [exchange(part, count, 1) for part in bias_parts]
     plan += [[offset | 1 for offset in offsets] for offsets in plan]
 
+    rows = row_attend(
+        me, alignment, projected, align_mask, row_out_weight, bias_parts, plan, count
+    )
+    rows, late_mask = lax.optimization_barrier((rows, align_mask))
+    moved = lax.all_to_all(rows, "dap", split_axis=0, concat_axis=0, tiled=True)
+    own_res = lax.dynamic_slice_in_dim(late_mask, dap_index * items, items, 1)
     counts = jnp.einsum(
-        "si,sj->ji", own_res.astype(BF16), align_mask.astype(BF16), preferred_element_type=F32
+        "si,sj->ji", own_res.astype(BF16), late_mask.astype(BF16), preferred_element_type=F32
     )
     res_float = residue_mask.astype(F32)
     live_rows = lax.dynamic_slice_in_dim(res_float, dap_index * items, items, 0)
     scale = live_rows[None, :] * res_float[:, None] / (counts + count_eps)
-    mask_rows = own_res.T.astype(F32)
-
-    rows = row_attend(
-        me, alignment, projected, row_live, row_out_weight, bias_parts, plan, count
-    )
-    moved = lax.all_to_all(rows, "dap", split_axis=0, concat_axis=0, tiled=True)
     updated, left, right = column_attend(
+        me,
         moved,
-        col_live,
-        mask_rows,
+        align_mask,
         column_proj_weight,
         column_out_weight,
         outer_factor_weight,
         items,
     )
     rights = [exchange(right, count, z) for z in line]
+    rights[1], updated = lax.optimization_barrier((rights[1], updated))
     updated = interleave(updated)
     *rights, updated = lax.optimization_barrier((*rights, updated))
     rights = [part for own in rights for part in (own, exchange(own, count, 1))]

time: 111 us -> 102 us (0.919)
  blocking collectives: 0 us -> 30.4 us
  waiting for transfers between devices: 39.8 us -> 12.3 us
  Pallas kernels: 39.5 us -> 34.8 us
  starting transfers between devices: 27.3 us -> 23.3 us
  local copies, waits for them, and re-layouts: 2.11 us -> 0.11 us
    all_to_all x0 -> x1, blocking collectives: none -> 30.4 us  [per_device_fast(): moved = lax.all_to_all(rows, 'dap', split_axis=0, concat_axis=0, tiled=True)]
    all_to_all x1 -> x0, waiting for transfers between devices: 25.9 us -> none  [per_device_fast(): moved = lax.all_to_all(rows, 'dap', split_axis=0, concat_axis=0, tiled=True)]
    all_to_all x1 -> x0, starting transfers between devices: 4.57 us -> none  [per_device_fast(): moved = lax.all_to_all(rows, 'dap', split_axis=0, concat_axis=0, tiled=True)]
    pallas_call x1, Pallas kernels: 12.5 us -> 9.87 us  [column_attend(): pl.pallas_call(functools.partial(column_kernel, items, each), grid=(items...]
    pallas_call x1, Pallas kernels: 9.89 us -> 7.84 us  [row_attend(): pl.pallas_call(functools.partial(row_attend_kernel, plan, step, seqs), gr...]
    dynamic_slice x2 -> x0, local copies, waits for them, and re-layouts: 1.69 us -> none  [the longest x1 0.99 us: per_device_fast(): own_res = lax.dynamic_slice_in_dim(align_mask, dap_index * items, items, 1)]
    ppermute x23, waiting for transfers between devices: 13.9 us -> 12.3 us  [exchange(): return lax.ppermute(block, 'dap', [(i, i ^ offset) for i in range(count)])]
  transfers between devices with their start and end apart: 24 -> 23, of which waited for: 11 -> 12; matrix products, arithmetic and copies ran while one was open for 3% -> 0% of each run, Pallas kernels for 10% -> 11%
where the time goes in v8:
time: 102 us
  Pallas kernels  34.8 us (34%)
  blocking collectives  30.4 us (30%)
  starting transfers between devices  23.3 us (23%)
  waiting for transfers between devices  12.3 us (12%)
    all_to_all x1, blocking collectives, per_device_fast(): moved = lax.all_to_all(rows, 'dap', split_axis=0, concat_axis=0, tiled=True)  30.4 us
    ppermute x23, starting transfers between devices, exchange(): return lax.ppermute(block, 'dap', [(i, i ^ offset) for i in range(count)])  23.3 us
    ppermute x23, waiting for transfers between devices, exchange(): return lax.ppermute(block, 'dap', [(i, i ^ offset) for i in range(count)])  12.3 us
    pallas_call x1, Pallas kernels, column_attend(): pl.pallas_call(functools.partial(column_kernel, items, each), grid=(items...  9.87 us
    pallas_call x1, Pallas kernels, row_attend(): pl.pallas_call(functools.partial(row_attend_kernel, plan, step, seqs), gr...  7.84 us
    pallas_call x1, Pallas kernels, row_project(): pl.pallas_call(row_project_kernel, grid=(seqs // step,), in_specs=[block,...  5.58 us
    pallas_call x2, Pallas kernels, outer_product(): pl.pallas_call(functools.partial(outer_kernel, group, outer, items), out_...  4.79 us
    pallas_call x1, Pallas kernels, interleave(): pl.pallas_call(interleave_kernel, grid=(length // step,), in_specs=[pl.Bl...  3.64 us
  transfers between devices with their start and end apart: 23, of which 12 were waited for; matrix products, arithmetic and copies ran while one was open for 0% of the time, Pallas kernels for 11%

profile of v8, /device:TPU:0, one launch (start us, length us, event | category | flops | bytes accessed | tf_op | source)
XLA Modules:
  0.0 102.0 jit_solution(13285560062749318327)
XLA Ops:
  0.6 1.8 %pair_bias.1 = bf16[64,256]{1,0:T(8,128)(2,1)S(1)} custom-call(bf16[8,256,128]{2,1,0:T(8,128)(2,1)} %pair_ref.3, bf16[8,128]{1,0:T(8,128)(2,1)} %bitcast.12), custom_call_target="tpu_custom_call" | custom-call | tf_op jit(solution)/shard_map/pair_bias/pallas_call | solution.py:278
  2.4 3.1 %collective-permute-start = (bf16[64,256]{1,0:T(8,128)(2,1)S(1)}, bf16[64,256]{1,0:T(8,128)(2,1)S(1)}, u32[]{:S(2)}, u32[]{:S(2)}) collective-permute-start(bf16[64,256]{1,0:T(8,128)(2,1)S(1)} %pair_bias.1), channel_id=1, source_target_pairs={{0,8},{1,9},{2,10},{3,11},{4,12},{5,13},{6,14},{7,15},{8,0},{9,1},... | collective-permute-start | bytes 98312 | tf_op jit(solution)/shard_map/ppermute | solution.py:546
  5.5 2.6 %collective-permute-start.1 = (bf16[64,256]{1,0:T(8,128)(2,1)S(1)}, bf16[64,256]{1,0:T(8,128)(2,1)S(1)}, u32[]{:S(2)}, u32[]{:S(2)}) collective-permute-start(bf16[64,256]{1,0:T(8,128)(2,1)S(1)} %pair_bias.1), channel_id=1, source_target_pairs={{0,16},{1,17},{2,18},{3,19},{4,20},{5,21},{6,22},{7,23},{8,24},{9,... | collective-permute-start | bytes 98312 | tf_op jit(solution)/shard_map/ppermute | solution.py:546
  8.1 5.6 %row_project.1 = (bf16[8,256,256]{2,1,0:T(8,128)(2,1)}, bf16[8,256,256]{2,1,0:T(8,128)(2,1)}, bf16[8,256,256]{2,1,0:T(8,128)(2,1)}, f32[8,256,256]{2,1,0:T(8,128)}) custom-call(bf16[8,256,256]{2,1,0:T(8,128)(2,1)} %x_ref.3, bf16[4,256,256]{2,1,0:T(8,128)(2,1)} %weight_ref.2), custom_call_target="tpu_custom_call" | custom-call | tf_op jit(solution)/shard_map/row_project/pallas_call | solution.py:300
  13.8 1.7 %collective-permute-start.3 = (bf16[4,64,256]{2,1,0:T(8,128)(2,1)S(1)}, bf16[4,64,256]{2,1,0:T(8,128)(2,1)S(1)}, u32[]{:S(2)}, u32[]{:S(2)}) collective-permute-start(bf16[4,64,256]{2,1,0:T(8,128)(2,1)S(1)} %pad_maximum_fusion.rest_0_), channel_id=1, source_target_pairs={{0,2},{1,3},{2,0},{3,1},{4,6},{5,7},{6,4},{7,5},{8,10},{9,11},{10,... | collective-permute-start | bytes 393224 | tf_op jit(solution)/shard_map/ppermute | solution.py:546
  15.5 1.5 %collective-permute-start.4 = (bf16[4,64,256]{2,1,0:T(8,128)(2,1)S(1)}, bf16[4,64,256]{2,1,0:T(8,128)(2,1)S(1)}, u32[]{:S(2)}, u32[]{:S(2)}) collective-permute-start(bf16[4,64,256]{2,1,0:T(8,128)(2,1)S(1)} %pad_maximum_fusion.rest_0_), channel_id=1, source_target_pairs={{0,4},{1,5},{2,6},{3,7},{4,0},{5,1},{6,2},{7,3},{8,12},{9,13},{10,... | collective-permute-start | bytes 393224 | tf_op jit(solution)/shard_map/ppermute | solution.py:546
  17.1 0.3 collective-permute-start.5
  17.4 2.3 %collective-permute-done.3.rest_1_ = bf16[4,64,256]{2,1,0:T(8,128)(2,1)S(1)} collective-permute-done((bf16[4,64,256]{2,1,0:T(8,128)(2,1)S(1)}, bf16[4,64,256]{2,1,0:T(8,128)(2,1)S(1)}, u32[]{:S(2)}, u32[]{:S(2)}) %collective-permute-start.3) | collective-permute-done | bytes 131104 | tf_op jit(solution)/shard_map/ppermute | solution.py:546
  19.7 3.5 %collective-permute-done.4.rest_2_ = bf16[4,64,256]{2,1,0:T(8,128)(2,1)S(1)} collective-permute-done((bf16[4,64,256]{2,1,0:T(8,128)(2,1)S(1)}, bf16[4,64,256]{2,1,0:T(8,128)(2,1)S(1)}, u32[]{:S(2)}, u32[]{:S(2)}) %collective-permute-start.4) | collective-permute-done | bytes 131104 | tf_op jit(solution)/shard_map/ppermute | solution.py:546
  23.3 0.5 collective-permute-start.9
  23.8 0.8 collective-permute-done.8.rest_6_
  24.8 7.8 %row_attend.1 = bf16[32,64,256]{2,1,0:T(8,128)(2,1)S(1)} custom-call(s32[1]{0:T(128)} %bitcast.me_ref, bf16[8,256,256]{2,1,0:T(8,128)(2,1)} %x_ref.3, bf16[8,256,256]{2,1,0:T(8,128)(2,1)} %get-tuple-element.27.q_ref, bf16[8,256,256]{2,1,0:T(8,128)(2,1)} %get-tuple-element.28.k_ref, bf16[8,256,256]{2,1,0:T(8,128)(2,1)} %get-tuple-element.29.v_ref, ...), custom_call_target="tpu_custom_call" | custom-call | tf_op jit(solution)/shard_map/row_attend/pallas_call | solution.py:353
  32.7 30.4 %all_to_all.5.x_ref = bf16[32,64,256]{2,1,0:T(8,128)(2,1)S(1)} all-to-all(bf16[32,64,256]{2,1,0:T(8,128)(2,1)S(1)} %row_attend.1), channel_id=1, replica_groups=mesh['branch'=1,'dap'=32] {'dap'}, dimensions={0} | all-to-all | bytes 2097152 | tf_op jit(solution)/shard_map/all_to_all | solution.py:582
  63.1 9.9 %column_attend.1 = (bf16[8,256,256]{2,1,0:T(8,128)(2,1)}, bf16[256,256]{1,0:T(8,128)(2,1)S(1)}, bf16[256,256]{1,0:T(8,128)(2,1)S(1)}) custom-call(s32[1]{0:T(128)} %bitcast.me_ref, bf16[32,64,256]{2,1,0:T(8,128)(2,1)S(1)} %all_to_all.5.x_ref, s32[256,256]{1,0:T(8,128)S(1)} %copy-done.1, bf16[4,256,256]{2,1,0:T(8,128)(2,1)S(1)} %copy-done.3, ...), custom_call_target="tpu_custom_call" | custom-call | tf_op jit(solution)/shard_map/column_attend/pallas_call | solution.py:422
  73.0 0.8 collective-permute-start.10
  73.7 1.1 %collective-permute-start.11 = (bf16[256,256]{1,0:T(8,128)(2,1)S(1)}, bf16[256,256]{1,0:T(8,128)(2,1)S(1)}, u32[]{:S(2)}, u32[]{:S(2)}) collective-permute-start(bf16[256,256]{1,0:T(8,128)(2,1)S(1)} %get-tuple-element.43.refs_1_.refs_3_), channel_id=1, source_target_pairs={{0,16},{1,17},{2,18},{3,19},{4,20},{5,21},{6,22},{7,23},{8,24},{9,... | collective-permute-start | bytes 393224 | tf_op jit(solution)/shard_map/ppermute | solution.py:546
  74.8 2.5 %collective-permute-start.12 = (bf16[256,256]{1,0:T(8,128)(2,1)S(1)}, bf16[256,256]{1,0:T(8,128)(2,1)S(1)}, u32[]{:S(2)}, u32[]{:S(2)}) collective-permute-start(bf16[256,256]{1,0:T(8,128)(2,1)S(1)} %get-tuple-element.43.refs_1_.refs_3_), channel_id=1, source_target_pairs={{0,24},{1,25},{2,26},{3,27},{4,28},{5,29},{6,30},{7,31},{8,16},{9,... | collective-permute-start | bytes 393224 | tf_op jit(solution)/shard_map/ppermute | solution.py:546
  77.4 1.5 %collective-permute-start.17 = (bf16[256,256]{1,0:T(8,128)(2,1)S(1)}, bf16[256,256]{1,0:T(8,128)(2,1)S(1)}, u32[]{:S(2)}, u32[]{:S(2)}) collective-permute-start(bf16[256,256]{1,0:T(8,128)(2,1)S(1)} %get-tuple-element.42.refs_0_), channel_id=1, source_target_pairs={{0,2},{1,3},{2,0},{3,1},{4,6},{5,7},{6,4},{7,5},{8,10},{9,11},{10,... | collective-permute-start | bytes 393224 | tf_op jit(solution)/shard_map/ppermute | solution.py:546
  78.8 1.5 %collective-permute-start.18 = (bf16[256,256]{1,0:T(8,128)(2,1)S(1)}, bf16[256,256]{1,0:T(8,128)(2,1)S(1)}, u32[]{:S(2)}, u32[]{:S(2)}) collective-permute-start(bf16[256,256]{1,0:T(8,128)(2,1)S(1)} %get-tuple-element.42.refs_0_), channel_id=1, source_target_pairs={{0,4},{1,5},{2,6},{3,7},{4,0},{5,1},{6,2},{7,3},{8,12},{9,13},{10,... | collective-permute-start | bytes 393224 | tf_op jit(solution)/shard_map/ppermute | solution.py:546
  80.3 1.7 %collective-permute-start.19 = (bf16[256,256]{1,0:T(8,128)(2,1)S(1)}, bf16[256,256]{1,0:T(8,128)(2,1)S(1)}, u32[]{:S(2)}, u32[]{:S(2)}) collective-permute-start(bf16[256,256]{1,0:T(8,128)(2,1)S(1)} %get-tuple-element.42.refs_0_), channel_id=1, source_target_pairs={{0,6},{1,7},{2,4},{3,5},{4,2},{5,3},{6,0},{7,1},{8,14},{9,15},{10,... | collective-permute-start | bytes 393224 | tf_op jit(solution)/shard_map/ppermute | solution.py:546
  82.0 3.6 %interleave.1 = bf16[256,8,256]{2,1,0:T(8,128)(2,1)} custom-call(bf16[8,256,256]{2,1,0:T(8,128)(2,1)} %get-tuple-element.39.rows_ref), custom_call_target="tpu_custom_call" | custom-call | tf_op jit(solution)/shard_map/interleave/pallas_call | solution.py:444
  85.6 1.0 collective-permute-done.11.refs_5_.refs_7_
  86.6 0.5 collective-permute-start.14
  87.2 0.5 collective-permute-start.16
  88.7 2.9 %outer_product.3 = (bf16[8,64,128]{2,1,0:T(8,128)(2,1)S(1)}, bf16[8,64,128]{2,1,0:T(8,128)(2,1)S(1)}, bf16[8,64,128]{2,1,0:T(8,128)(2,1)S(1)}) custom-call(bf16[256,256]{1,0:T(8,128)(2,1)S(1)} %collective-permute-done.17.refs_0_, bf16[256,256]{1,0:T(8,128)(2,1)S(1)} %collective-permute-done.18.refs_1_, bf16[256,256]{1,0:T(8,128)(2,1)S(1)} %collective-permute-done.19.refs_2_, ...), custom_call_target="tpu_custom_call" | custom-call | tf_op jit(solution)/shard_map/outer_product/pallas_call | solution.py:498
  91.6 0.9 collective-permute-start.20
  92.4 1.3 %collective-permute-start.21 = (bf16[8,64,128]{2,1,0:T(8,128)(2,1)S(1)}, bf16[8,64,128]{2,1,0:T(8,128)(2,1)S(1)}, u32[]{:S(2)}, u32[]{:S(2)}) collective-permute-start(bf16[8,64,128]{2,1,0:T(8,128)(2,1)S(1)} %get-tuple-element.48), channel_id=1, source_target_pairs={{0,4},{1,5},{2,6},{3,7},{4,0},{5,1},{6,2},{7,3},{8,12},{9,13},{10,... | collective-permute-start | bytes 393224 | tf_op jit(solution)/shard_map/ppermute | solution.py:546
  93.8 1.4 %collective-permute-start.22 = (bf16[8,64,128]{2,1,0:T(8,128)(2,1)S(1)}, bf16[8,64,128]{2,1,0:T(8,128)(2,1)S(1)}, u32[]{:S(2)}, u32[]{:S(2)}) collective-permute-start(bf16[8,64,128]{2,1,0:T(8,128)(2,1)S(1)} %get-tuple-element.49), channel_id=1, source_target_pairs={{0,6},{1,7},{2,4},{3,5},{4,2},{5,3},{6,0},{7,1},{8,14},{9,15},{10,... | collective-permute-start | bytes 393224 | tf_op jit(solution)/shard_map/ppermute | solution.py:546
  95.4 1.9 %outer_product.2.refs_0_ = bf16[8,64,128]{2,1,0:T(8,128)(2,1)S(1)} custom-call(bf16[256,256]{1,0:T(8,128)(2,1)S(1)} %get-tuple-element.42.refs_0_, bf16[256,256]{1,0:T(8,128)(2,1)S(1)} %get-tuple-element.43.refs_1_.refs_3_, bf16[256,256]{1,0:T(8,128)(2,1)S(1)} %collective-permute-done.13.refs_2_.refs_4_, ...), custom_call_target="tpu_custom_call" | custom-call | tf_op jit(solution)/shard_map/outer_product/pallas_call | solution.py:498
  97.3 0.6 collective-permute-done.20.refs_1_
  98.0 2.7 %collective-permute-done.21.refs_2_ = bf16[8,64,128]{2,1,0:T(8,128)(2,1)S(1)} collective-permute-done((bf16[8,64,128]{2,1,0:T(8,128)(2,1)S(1)}, bf16[8,64,128]{2,1,0:T(8,128)(2,1)S(1)}, u32[]{:S(2)}, u32[]{:S(2)}) %collective-permute-start.21) | collective-permute-done | bytes 131104 | tf_op jit(solution)/shard_map/ppermute | solution.py:546
  100.7 1.3 %finish.1 = bf16[8,256,128]{2,1,0:T(8,128)(2,1)} custom-call(s32[1]{0:T(128)} %bitcast.me_ref, bf16[8,256,128]{2,1,0:T(8,128)(2,1)S(1)} %copy-done, f32[256,8]{1,0:T(8,128)S(1)} %fusion.scale_ref, bf16[8,64,128]{2,1,0:T(8,128)(2,1)S(1)} %outer_product.2.refs_0_, bf16[8,64,128]{2,1,0:T(8,128)(2,1)S(1)} %collective-permute-done.20.refs_1_, ...), custom_call_target="tpu_custom_call" | custom-call | tf_op jit(solution)/shard_map/finish/pallas_call | solution.py:533
  (41 shorter events, 1.7 us)
Async XLA Ops:
  2.4 11.3 %collective-permute-start = (bf16[64,256]{1,0:T(8,128)(2,1)S(1)}, bf16[64,256]{1,0:T(8,128)(2,1)S(1)}, u32[]{:S(2)}, u32[]{:S(2)}) collective-permute-start(bf16[64,256]{1,0:T(8,128)(2,1)S(1)} %pair_bias.1), channel_id=1, source_target_pairs={{0,8},{1,9},{2,10},{3,11},{4,12},{5,13},{6,14},{7,15},{8,0},{9,1},... | collective-permute-start | bytes 98312 | tf_op jit(solution)/shard_map/ppermute | solution.py:546
  5.5 8.2 %collective-permute-start.1 = (bf16[64,256]{1,0:T(8,128)(2,1)S(1)}, bf16[64,256]{1,0:T(8,128)(2,1)S(1)}, u32[]{:S(2)}, u32[]{:S(2)}) collective-permute-start(bf16[64,256]{1,0:T(8,128)(2,1)S(1)} %pair_bias.1), channel_id=1, source_target_pairs={{0,16},{1,17},{2,18},{3,19},{4,20},{5,21},{6,22},{7,23},{8,24},{9,... | collective-permute-start | bytes 98312 | tf_op jit(solution)/shard_map/ppermute | solution.py:546
  8.1 5.7 %collective-permute-start.2 = (bf16[64,256]{1,0:T(8,128)(2,1)S(1)}, bf16[64,256]{1,0:T(8,128)(2,1)S(1)}, u32[]{:S(2)}, u32[]{:S(2)}) collective-permute-start(bf16[64,256]{1,0:T(8,128)(2,1)S(1)} %pair_bias.1), channel_id=1, source_target_pairs={{0,24},{1,25},{2,26},{3,27},{4,28},{5,29},{6,30},{7,31},{8,16},{9,... | collective-permute-start | bytes 98312 | tf_op jit(solution)/shard_map/ppermute | solution.py:546
  13.8 5.9 %collective-permute-start.3 = (bf16[4,64,256]{2,1,0:T(8,128)(2,1)S(1)}, bf16[4,64,256]{2,1,0:T(8,128)(2,1)S(1)}, u32[]{:S(2)}, u32[]{:S(2)}) collective-permute-start(bf16[4,64,256]{2,1,0:T(8,128)(2,1)S(1)} %pad_maximum_fusion.rest_0_), channel_id=1, source_target_pairs={{0,2},{1,3},{2,0},{3,1},{4,6},{5,7},{6,4},{7,5},{8,10},{9,11},{10,... | collective-permute-start | bytes 393224 | tf_op jit(solution)/shard_map/ppermute | solution.py:546
  15.5 7.7 %collective-permute-start.4 = (bf16[4,64,256]{2,1,0:T(8,128)(2,1)S(1)}, bf16[4,64,256]{2,1,0:T(8,128)(2,1)S(1)}, u32[]{:S(2)}, u32[]{:S(2)}) collective-permute-start(bf16[4,64,256]{2,1,0:T(8,128)(2,1)S(1)} %pad_maximum_fusion.rest_0_), channel_id=1, source_target_pairs={{0,4},{1,5},{2,6},{3,7},{4,0},{5,1},{6,2},{7,3},{8,12},{9,13},{10,... | collective-permute-start | bytes 393224 | tf_op jit(solution)/shard_map/ppermute | solution.py:546
  17.1 6.2 %collective-permute-start.5 = (bf16[4,64,256]{2,1,0:T(8,128)(2,1)S(1)}, bf16[4,64,256]{2,1,0:T(8,128)(2,1)S(1)}, u32[]{:S(2)}, u32[]{:S(2)}) collective-permute-start(bf16[4,64,256]{2,1,0:T(8,128)(2,1)S(1)} %pad_maximum_fusion.rest_0_), channel_id=1, source_target_pairs={{0,6},{1,7},{2,4},{3,5},{4,2},{5,3},{6,0},{7,1},{8,14},{9,15},{10,... | collective-permute-start | bytes 393224 | tf_op jit(solution)/shard_map/ppermute | solution.py:546
  17.4 6.4 %collective-permute-start.6 = (bf16[4,64,256]{2,1,0:T(8,128)(2,1)S(1)}, bf16[4,64,256]{2,1,0:T(8,128)(2,1)S(1)}, u32[]{:S(2)}, u32[]{:S(2)}) collective-permute-start(bf16[4,64,256]{2,1,0:T(8,128)(2,1)S(1)} %pad_maximum_fusion.rest_0_), channel_id=1, source_target_pairs={{0,1},{1,0},{2,3},{3,2},{4,5},{5,4},{6,7},{7,6},{8,9},{9,8},{10,11... | collective-permute-start | bytes 393224 | tf_op jit(solution)/shard_map/ppermute | solution.py:546
  19.7 4.1 %collective-permute-start.7 = (bf16[4,64,256]{2,1,0:T(8,128)(2,1)S(1)}, bf16[4,64,256]{2,1,0:T(8,128)(2,1)S(1)}, u32[]{:S(2)}, u32[]{:S(2)}) collective-permute-start(bf16[4,64,256]{2,1,0:T(8,128)(2,1)S(1)} %collective-permute-done.3.rest_1_), channel_id=1, source_target_pairs={{0,1},{1,0},{2,3},{3,2},{4,5},{5,4},{6,7},{7,6},{8,9},{9,8},{10,11... | collective-permute-start | bytes 393224 | tf_op jit(solution)/shard_map/ppermute | solution.py:546
  23.3 1.3 %collective-permute-start.8 = (bf16[4,64,256]{2,1,0:T(8,128)(2,1)S(1)}, bf16[4,64,256]{2,1,0:T(8,128)(2,1)S(1)}, u32[]{:S(2)}, u32[]{:S(2)}) collective-permute-start(bf16[4,64,256]{2,1,0:T(8,128)(2,1)S(1)} %collective-permute-done.4.rest_2_), channel_id=1, source_target_pairs={{0,1},{1,0},{2,3},{3,2},{4,5},{5,4},{6,7},{7,6},{8,9},{9,8},{10,11... | collective-permute-start | bytes 393224 | tf_op jit(solution)/shard_map/ppermute | solution.py:546
  23.3 1.5 %collective-permute-start.9 = (bf16[4,64,256]{2,1,0:T(8,128)(2,1)S(1)}, bf16[4,64,256]{2,1,0:T(8,128)(2,1)S(1)}, u32[]{:S(2)}, u32[]{:S(2)}) collective-permute-start(bf16[4,64,256]{2,1,0:T(8,128)(2,1)S(1)} %collective-permute-done.5.rest_3_), channel_id=1, source_target_pairs={{0,1},{1,0},{2,3},{3,2},{4,5},{5,4},{6,7},{7,6},{8,9},{9,8},{10,11... | collective-permute-start | bytes 393224 | tf_op jit(solution)/shard_map/ppermute | solution.py:546
  32.7 30.4 %copy-start.1 = (s32[256,256]{1,0:T(8,128)S(1)}, s32[256,256]{1,0:T(8,128)}, u32[]{:S(2)}) copy-start(s32[256,256]{1,0:T(8,128)} %mask_ref.3) | copy-start | bytes 786436
  32.7 30.4 %copy-start.3 = (bf16[4,256,256]{2,1,0:T(8,128)(2,1)S(1)}, bf16[4,256,256]{2,1,0:T(8,128)(2,1)}, u32[]{:S(2)}) copy-start(bf16[4,256,256]{2,1,0:T(8,128)(2,1)} %weight_ref.3) | copy-start | bytes 1572868
  32.7 30.4 %copy-start.4 = (bf16[256,256]{1,0:T(8,128)(2,1)S(1)}, bf16[256,256]{1,0:T(8,128)(2,1)}, u32[]{:S(2)}) copy-start(bf16[256,256]{1,0:T(8,128)(2,1)} %out_w_ref.3) | copy-start | bytes 393220
  32.7 30.4 %copy-start.5 = (bf16[256,64]{0,1:T(8,128)(2,1)S(1)}, bf16[256,64]{0,1:T(8,128)(2,1)}, u32[]{:S(2)}) copy-start(bf16[256,64]{0,1:T(8,128)(2,1)} %param.20) | copy-start | bytes 98308
  63.1 24.6 %copy-start.6 = (s32[256]{0:T(256)S(1)}, s32[256]{0:T(256)}, u32[]{:S(2)}) copy-start(s32[256]{0:T(256)} %param.14) | copy-start | bytes 3076
  63.1 25.6 %copy-start.2 = (bf16[1024,128]{1,0:T(8,128)(2,1)S(1)}, bf16[1024,128]{1,0:T(8,128)(2,1)}, u32[]{:S(2)}) copy-start(bf16[1024,128]{1,0:T(8,128)(2,1)} %refs_11_.1) | copy-start | bytes 786436
  73.0 7.3 %collective-permute-start.10 = (bf16[256,256]{1,0:T(8,128)(2,1)S(1)}, bf16[256,256]{1,0:T(8,128)(2,1)S(1)}, u32[]{:S(2)}, u32[]{:S(2)}) collective-permute-start(bf16[256,256]{1,0:T(8,128)(2,1)S(1)} %get-tuple-element.43.refs_1_.refs_3_), channel_id=1, source_target_pairs={{0,8},{1,9},{2,10},{3,11},{4,12},{5,13},{6,14},{7,15},{8,0},{9,1},... | collective-permute-start | bytes 393224 | tf_op jit(solution)/shard_map/ppermute | solution.py:546
  73.7 12.9 %collective-permute-start.11 = (bf16[256,256]{1,0:T(8,128)(2,1)S(1)}, bf16[256,256]{1,0:T(8,128)(2,1)S(1)}, u32[]{:S(2)}, u32[]{:S(2)}) collective-permute-start(bf16[256,256]{1,0:T(8,128)(2,1)S(1)} %get-tuple-element.43.refs_1_.refs_3_), channel_id=1, source_target_pairs={{0,16},{1,17},{2,18},{3,19},{4,20},{5,21},{6,22},{7,23},{8,24},{9,... | collective-permute-start | bytes 393224 | tf_op jit(solution)/shard_map/ppermute | solution.py:546
  74.8 11.8 %collective-permute-start.12 = (bf16[256,256]{1,0:T(8,128)(2,1)S(1)}, bf16[256,256]{1,0:T(8,128)(2,1)S(1)}, u32[]{:S(2)}, u32[]{:S(2)}) collective-permute-start(bf16[256,256]{1,0:T(8,128)(2,1)S(1)} %get-tuple-element.43.refs_1_.refs_3_), channel_id=1, source_target_pairs={{0,24},{1,25},{2,26},{3,27},{4,28},{5,29},{6,30},{7,31},{8,16},{9,... | collective-permute-start | bytes 393224 | tf_op jit(solution)/shard_map/ppermute | solution.py:546
  77.4 9.8 %collective-permute-start.17 = (bf16[256,256]{1,0:T(8,128)(2,1)S(1)}, bf16[256,256]{1,0:T(8,128)(2,1)S(1)}, u32[]{:S(2)}, u32[]{:S(2)}) collective-permute-start(bf16[256,256]{1,0:T(8,128)(2,1)S(1)} %get-tuple-element.42.refs_0_), channel_id=1, source_target_pairs={{0,2},{1,3},{2,0},{3,1},{4,6},{5,7},{6,4},{7,5},{8,10},{9,11},{10,... | collective-permute-start | bytes 393224 | tf_op jit(solution)/shard_map/ppermute | solution.py:546
  78.8 8.3 %collective-permute-start.18 = (bf16[256,256]{1,0:T(8,128)(2,1)S(1)}, bf16[256,256]{1,0:T(8,128)(2,1)S(1)}, u32[]{:S(2)}, u32[]{:S(2)}) collective-permute-start(bf16[256,256]{1,0:T(8,128)(2,1)S(1)} %get-tuple-element.42.refs_0_), channel_id=1, source_target_pairs={{0,4},{1,5},{2,6},{3,7},{4,0},{5,1},{6,2},{7,3},{8,12},{9,13},{10,... | collective-permute-start | bytes 393224 | tf_op jit(solution)/shard_map/ppermute | solution.py:546
  80.3 7.4 %collective-permute-start.19 = (bf16[256,256]{1,0:T(8,128)(2,1)S(1)}, bf16[256,256]{1,0:T(8,128)(2,1)S(1)}, u32[]{:S(2)}, u32[]{:S(2)}) collective-permute-start(bf16[256,256]{1,0:T(8,128)(2,1)S(1)} %get-tuple-element.42.refs_0_), channel_id=1, source_target_pairs={{0,6},{1,7},{2,4},{3,5},{4,2},{5,3},{6,0},{7,1},{8,14},{9,15},{10,... | collective-permute-start | bytes 393224 | tf_op jit(solution)/shard_map/ppermute | solution.py:546
  85.6 15.1 %copy-start = (bf16[8,256,128]{2,1,0:T(8,128)(2,1)S(1)}, bf16[8,256,128]{2,1,0:T(8,128)(2,1)}, u32[]{:S(2)}) copy-start(bf16[8,256,128]{2,1,0:T(8,128)(2,1)} %pair_ref.3) | copy-start | bytes 1572868
  86.6 1.3 %collective-permute-start.13 = (bf16[256,256]{1,0:T(8,128)(2,1)S(1)}, bf16[256,256]{1,0:T(8,128)(2,1)S(1)}, u32[]{:S(2)}, u32[]{:S(2)}) collective-permute-start(bf16[256,256]{1,0:T(8,128)(2,1)S(1)} %get-tuple-element.43.refs_1_.refs_3_), channel_id=1, source_target_pairs={{0,1},{1,0},{2,3},{3,2},{4,5},{5,4},{6,7},{7,6},{8,9},{9,8},{10,11... | collective-permute-start | bytes 393224 | tf_op jit(solution)/shard_map/ppermute | solution.py:546
  86.6 1.5 %collective-permute-start.14 = (bf16[256,256]{1,0:T(8,128)(2,1)S(1)}, bf16[256,256]{1,0:T(8,128)(2,1)S(1)}, u32[]{:S(2)}, u32[]{:S(2)}) collective-permute-start(bf16[256,256]{1,0:T(8,128)(2,1)S(1)} %collective-permute-done.10.refs_3_.refs_5_), channel_id=1, source_target_pairs={{0,1},{1,0},{2,3},{3,2},{4,5},{5,4},{6,7},{7,6},{8,9},{9,8},{10,11... | collective-permute-start | bytes 393224 | tf_op jit(solution)/shard_map/ppermute | solution.py:546
  87.1 1.3 %collective-permute-start.15 = (bf16[256,256]{1,0:T(8,128)(2,1)S(1)}, bf16[256,256]{1,0:T(8,128)(2,1)S(1)}, u32[]{:S(2)}, u32[]{:S(2)}) collective-permute-start(bf16[256,256]{1,0:T(8,128)(2,1)S(1)} %collective-permute-done.11.refs_5_.refs_7_), channel_id=1, source_target_pairs={{0,1},{1,0},{2,3},{3,2},{4,5},{5,4},{6,7},{7,6},{8,9},{9,8},{10,11... | collective-permute-start | bytes 393224 | tf_op jit(solution)/shard_map/ppermute | solution.py:546
  87.2 1.5 %collective-permute-start.16 = (bf16[256,256]{1,0:T(8,128)(2,1)S(1)}, bf16[256,256]{1,0:T(8,128)(2,1)S(1)}, u32[]{:S(2)}, u32[]{:S(2)}) collective-permute-start(bf16[256,256]{1,0:T(8,128)(2,1)S(1)} %collective-permute-done.12.refs_7_.refs_9_), channel_id=1, source_target_pairs={{0,1},{1,0},{2,3},{3,2},{4,5},{5,4},{6,7},{7,6},{8,9},{9,8},{10,11... | collective-permute-start | bytes 393224 | tf_op jit(solution)/shard_map/ppermute | solution.py:546
  91.6 6.4 %collective-permute-start.20 = (bf16[8,64,128]{2,1,0:T(8,128)(2,1)S(1)}, bf16[8,64,128]{2,1,0:T(8,128)(2,1)S(1)}, u32[]{:S(2)}, u32[]{:S(2)}) collective-permute-start(bf16[8,64,128]{2,1,0:T(8,128)(2,1)S(1)} %get-tuple-element.47), channel_id=1, source_target_pairs={{0,2},{1,3},{2,0},{3,1},{4,6},{5,7},{6,4},{7,5},{8,10},{9,11},{10,... | collective-permute-start | bytes 393224 | tf_op jit(solution)/shard_map/ppermute | solution.py:546
  92.4 8.2 %collective-permute-start.21 = (bf16[8,64,128]{2,1,0:T(8,128)(2,1)S(1)}, bf16[8,64,128]{2,1,0:T(8,128)(2,1)S(1)}, u32[]{:S(2)}, u32[]{:S(2)}) collective-permute-start(bf16[8,64,128]{2,1,0:T(8,128)(2,1)S(1)} %get-tuple-element.48), channel_id=1, source_target_pairs={{0,4},{1,5},{2,6},{3,7},{4,0},{5,1},{6,2},{7,3},{8,12},{9,13},{10,... | collective-permute-start | bytes 393224 | tf_op jit(solution)/shard_map/ppermute | solution.py:546
  93.8 6.9 %collective-permute-start.22 = (bf16[8,64,128]{2,1,0:T(8,128)(2,1)S(1)}, bf16[8,64,128]{2,1,0:T(8,128)(2,1)S(1)}, u32[]{:S(2)}, u32[]{:S(2)}) collective-permute-start(bf16[8,64,128]{2,1,0:T(8,128)(2,1)S(1)} %get-tuple-element.49), channel_id=1, source_target_pairs={{0,6},{1,7},{2,4},{3,5},{4,2},{5,3},{6,0},{7,1},{8,14},{9,15},{10,... | collective-permute-start | bytes 393224 | tf_op jit(solution)/shard_map/ppermute | solution.py:546

commit v9 on v8

--- a/solution.py
+++ b/solution.py
@@ -208,11 +208,13 @@
     return top * (guess * (2.0 - below * guess))
 
 
-def attend_all(items, lanes, bias_of):
+def attend_all(count, prepare, close, lanes, bias_of):
     per_tile = LANES // HEAD_CHANNELS
+    items = {0: prepare(0)}
     rows, width = items[0][0].shape
-    tasks = [(n, tile) for n in range(len(items)) for tile in range(width // LANES)]
-    scores, raised, pieces = {}, {}, [[] for _ in items]
+    tiles = width // LANES
+    tasks = [(n, tile) for n in range(count) for tile in range(tiles)]
+    scores, raised, pieces = {}, {}, [[] for _ in range(count)]
 
     def score(at):
         n, tile = tasks[at]
@@ -246,11 +248,16 @@
     for at in range(len(tasks) + 2):
         if at < len(tasks):
             score(at)
+            n, tile = tasks[at]
+            if tile == 0 and n + 1 < count:
+                items[n + 1] = prepare(n + 1)
         if 0 <= at - 2:
             gather(at - 2)
         if 0 <= at - 1 < len(tasks):
             raise_scores(at - 1)
-    return [jnp.concatenate(p, axis=1) for p in pieces]
+        if 0 <= at - 2 and tasks[at - 2][1] == tiles - 1:
+            n = tasks[at - 2][0]
+            close(n, jnp.concatenate(pieces[n], axis=1))
 
 
 def project(normed, weight_ref):
@@ -327,27 +334,34 @@
     parts, rows = out_ref.shape[0], out_ref.shape[1]
     own = mask_ref[pl.ds(pl.multiple_of(me_ref[0] * seqs, seqs), seqs), :]
     own = own.astype(F32).astype(BF16)
-    items = []
-    for s in range(step):
+    results = []
+
+    def prepare(s):
         place = pl.program_id(0) * step + s
         spot = one_hot((seqs, LANES), 0, place, LIVE_SCALE)
         live = lax.dot_general(
             own, spot, (((0,), (0,)), ((), ())), preferred_element_type=F32
         ).astype(BF16)
-        items.append((q_ref[s], k_ref[s], v_ref[s], live))
-    results = []
-    for s, heads_out in enumerate(attend_all(items, lanes, lambda h: bias_all[h])):
+        return q_ref[s], k_ref[s], v_ref[s], live
+
+    def close(s, heads_out):
         heads_out = (heads_out * g_ref[s]).astype(BF16)
         total = x_ref[s].astype(F32) + nn_dot(heads_out, out_w_ref[...])
         results.append(total.reshape(parts, 1, rows // step, total.shape[1]))
-    joined = jnp.concatenate(results, axis=1)
-    out_ref[...] = joined.reshape(out_ref.shape).astype(BF16)
+        if len(results) == 2:
+            joined = jnp.concatenate(results, axis=1)
+            height = 2 * rows // step
+            joined = joined.reshape(parts, height, total.shape[1]).astype(BF16)
+            out_ref[:, (s // 2) * height : (s // 2 + 1) * height, :] = joined
+            results.clear()
+
+    attend_all(step, prepare, close, lanes, lambda h: bias_all[h])
 
 
 def row_attend(me, alignment, projected, mask, out_weight, bias_parts, plan, parts):
     seqs, length, width = alignment.shape
     rows = length // parts
-    step = 2
+    step = 4
     vmem = pl.BlockSpec(memory_space=pltpu.VMEM)
     block = pl.BlockSpec((step, length, width), lambda i: (i, 0, 0))
     return pl.pallas_call(
@@ -360,7 +374,7 @@
         out_specs=pl.BlockSpec((parts, step * rows, width), lambda i: (0, i, 0)),
         out_shape=jax.ShapeDtypeStruct((parts, seqs * rows, width), BF16),
         scratch_shapes=[pltpu.VMEM((ATTN_HEAD_COUNT, length, length), F32)],
-        compiler_params=params(24),
+        compiler_params=params(40),
         name="row_attend",
     )(me, *in_hbm(alignment, *projected, mask, out_weight), *in_vmem(*bias_parts))
 
@@ -383,27 +397,28 @@
     mask = mask_ref[...].astype(F32).astype(BF16)
     residues = mask.shape[1]
     place = me_ref[0] * items + step * each
-    rows = [load_strided(held, step * each + n, items, length) for n in range(each)]
-    inputs, gates = [], []
-    for n in range(each):
+    feat = FACTOR_CHANNELS
+    rows, gates = {}, {}
+
+    def prepare(n):
+        rows[n] = load_strided(held, step * each + n, items, length)
         normed = layer_normalize(rows[n]).astype(BF16)
-        query, key, value, gate = project(normed, weight_ref)
+        query, key, value, gates[n] = project(normed, weight_ref)
         live = nn_dot(mask, one_hot((residues, LANES), 0, place + n, LIVE_SCALE)).astype(BF16)
-        inputs.append((query, key, value, live))
-        gates.append(gate)
-    results = []
-    for n, heads_out in enumerate(attend_all(inputs, lanes, None)):
+        return query, key, value, live
+
+    def close(n, heads_out):
         heads_out = (heads_out * gates[n]).astype(BF16)
         updated = (rows[n] + nn_dot(heads_out, out_w_ref[...])).astype(BF16)
+        out_ref[n] = updated
         normed = layer_normalize(updated.astype(F32)).astype(BF16)
         live_row = nt_dot(one_hot((8, residues), 1, place + n), mask)[:1]
-        results.append((updated, nt_dot(factor_ref[...], normed) * live_row))
-    feat = FACTOR_CHANNELS
-    for n, (updated, factors) in enumerate(results):
+        factors = nt_dot(factor_ref[...], normed) * live_row
         item = step * each + n
-        out_ref[n] = updated
         left_ref[pl.ds(pl.multiple_of(item * feat, feat), feat), :] = factors[:feat].astype(BF16)
         store_strided(right_held, item, items, factors[feat:])
+
+    attend_all(each, prepare, close, lanes, None)
 
     @pl.when(step == items // each - 1)
     def _():
@@ -426,7 +441,7 @@
         out_specs=[pl.BlockSpec((each, length, width), lambda i: (i, 0, 0)), vmem, vmem],
         out_shape=[pltpu.HBM((items, length, width), BF16), left, right],
         scratch_shapes=[tiled_scratch(total_rows, width), tiled_scratch(*side)],
-        compiler_params=params(28),
+        compiler_params=params(40),
         name="column_attend",
     )(me, *operands)
 

time: 102 us -> 105 us (1.029)
  Pallas kernels: 34.8 us -> 37 us
    pallas_call x1, Pallas kernels: 9.87 us -> 11.5 us  [column_attend(): pl.pallas_call(functools.partial(column_kernel, items, each), grid=(items...]
where the time goes in v9:
time: 105 us; the launch traced here: 104 us
  Pallas kernels  37 us (35%)
  blocking collectives  30.4 us (29%)
  starting transfers between devices  23.3 us (22%)
  waiting for transfers between devices  12.3 us (12%)
    all_to_all x1, blocking collectives, per_device_fast(): moved = lax.all_to_all(rows, 'dap', split_axis=0, concat_axis=0, tiled=True)  30.4 us
    ppermute x23, starting transfers between devices, exchange(): return lax.ppermute(block, 'dap', [(i, i ^ offset) for i in range(count)])  23.3 us
    ppermute x23, waiting for transfers between devices, exchange(): return lax.ppermute(block, 'dap', [(i, i ^ offset) for i in range(count)])  12.3 us
    pallas_call x1, Pallas kernels, column_attend(): pl.pallas_call(functools.partial(column_kernel, items, each), grid=(items...  11.5 us
    pallas_call x1, Pallas kernels, row_attend(): pl.pallas_call(functools.partial(row_attend_kernel, plan, step, seqs), gr...  8.5 us
    pallas_call x1, Pallas kernels, row_project(): pl.pallas_call(row_project_kernel, grid=(seqs // step,), in_specs=[block,...  5.58 us
    pallas_call x2, Pallas kernels, outer_product(): pl.pallas_call(functools.partial(outer_kernel, group, outer, items), out_...  4.79 us
    pallas_call x1, Pallas kernels, interleave(): pl.pallas_call(interleave_kernel, grid=(length // step,), in_specs=[pl.Bl...  3.64 us
  transfers between devices with their start and end apart: 23, of which 12 were waited for; matrix products, arithmetic and copies ran while one was open for 0% of the time, Pallas kernels for 11%

profile of v9, /device:TPU:0, one launch (start us, length us, event | category | flops | bytes accessed | tf_op | source)
XLA Modules:
  0.0 104.2 jit_solution(17698876026758787497)
XLA Ops:
  0.6 1.8 %pair_bias.1 = bf16[64,256]{1,0:T(8,128)(2,1)S(1)} custom-call(bf16[8,256,128]{2,1,0:T(8,128)(2,1)} %pair_ref.3, bf16[8,128]{1,0:T(8,128)(2,1)} %bitcast.12), custom_call_target="tpu_custom_call" | custom-call | tf_op jit(solution)/shard_map/pair_bias/pallas_call | solution.py:285
  2.4 3.1 %collective-permute-start = (bf16[64,256]{1,0:T(8,128)(2,1)S(1)}, bf16[64,256]{1,0:T(8,128)(2,1)S(1)}, u32[]{:S(2)}, u32[]{:S(2)}) collective-permute-start(bf16[64,256]{1,0:T(8,128)(2,1)S(1)} %pair_bias.1), channel_id=1, source_target_pairs={{0,8},{1,9},{2,10},{3,11},{4,12},{5,13},{6,14},{7,15},{8,0},{9,1},... | collective-permute-start | bytes 98312 | tf_op jit(solution)/shard_map/ppermute | solution.py:561
  5.5 2.6 %collective-permute-start.1 = (bf16[64,256]{1,0:T(8,128)(2,1)S(1)}, bf16[64,256]{1,0:T(8,128)(2,1)S(1)}, u32[]{:S(2)}, u32[]{:S(2)}) collective-permute-start(bf16[64,256]{1,0:T(8,128)(2,1)S(1)} %pair_bias.1), channel_id=1, source_target_pairs={{0,16},{1,17},{2,18},{3,19},{4,20},{5,21},{6,22},{7,23},{8,24},{9,... | collective-permute-start | bytes 98312 | tf_op jit(solution)/shard_map/ppermute | solution.py:561
  8.1 5.6 %row_project.1 = (bf16[8,256,256]{2,1,0:T(8,128)(2,1)}, bf16[8,256,256]{2,1,0:T(8,128)(2,1)}, bf16[8,256,256]{2,1,0:T(8,128)(2,1)}, f32[8,256,256]{2,1,0:T(8,128)}) custom-call(bf16[8,256,256]{2,1,0:T(8,128)(2,1)} %x_ref.3, bf16[4,256,256]{2,1,0:T(8,128)(2,1)} %weight_ref.2), custom_call_target="tpu_custom_call" | custom-call | tf_op jit(solution)/shard_map/row_project/pallas_call | solution.py:307
  13.8 1.7 %collective-permute-start.3 = (bf16[4,64,256]{2,1,0:T(8,128)(2,1)S(1)}, bf16[4,64,256]{2,1,0:T(8,128)(2,1)S(1)}, u32[]{:S(2)}, u32[]{:S(2)}) collective-permute-start(bf16[4,64,256]{2,1,0:T(8,128)(2,1)S(1)} %pad_maximum_fusion.rest_0_), channel_id=1, source_target_pairs={{0,2},{1,3},{2,0},{3,1},{4,6},{5,7},{6,4},{7,5},{8,10},{9,11},{10,... | collective-permute-start | bytes 393224 | tf_op jit(solution)/shard_map/ppermute | solution.py:561
  15.5 1.5 %collective-permute-start.4 = (bf16[4,64,256]{2,1,0:T(8,128)(2,1)S(1)}, bf16[4,64,256]{2,1,0:T(8,128)(2,1)S(1)}, u32[]{:S(2)}, u32[]{:S(2)}) collective-permute-start(bf16[4,64,256]{2,1,0:T(8,128)(2,1)S(1)} %pad_maximum_fusion.rest_0_), channel_id=1, source_target_pairs={{0,4},{1,5},{2,6},{3,7},{4,0},{5,1},{6,2},{7,3},{8,12},{9,13},{10,... | collective-permute-start | bytes 393224 | tf_op jit(solution)/shard_map/ppermute | solution.py:561
  17.1 0.3 collective-permute-start.5
  17.4 2.3 %collective-permute-done.3.rest_1_ = bf16[4,64,256]{2,1,0:T(8,128)(2,1)S(1)} collective-permute-done((bf16[4,64,256]{2,1,0:T(8,128)(2,1)S(1)}, bf16[4,64,256]{2,1,0:T(8,128)(2,1)S(1)}, u32[]{:S(2)}, u32[]{:S(2)}) %collective-permute-start.3) | collective-permute-done | bytes 131104 | tf_op jit(solution)/shard_map/ppermute | solution.py:561
  19.7 3.5 %collective-permute-done.4.rest_2_ = bf16[4,64,256]{2,1,0:T(8,128)(2,1)S(1)} collective-permute-done((bf16[4,64,256]{2,1,0:T(8,128)(2,1)S(1)}, bf16[4,64,256]{2,1,0:T(8,128)(2,1)S(1)}, u32[]{:S(2)}, u32[]{:S(2)}) %collective-permute-start.4) | collective-permute-done | bytes 131104 | tf_op jit(solution)/shard_map/ppermute | solution.py:561
  23.3 0.5 collective-permute-start.9
  23.8 0.8 collective-permute-done.8.rest_6_
  24.8 8.5 %row_attend.1 = bf16[32,64,256]{2,1,0:T(8,128)(2,1)S(1)} custom-call(s32[1]{0:T(128)} %bitcast.me_ref, bf16[8,256,256]{2,1,0:T(8,128)(2,1)} %x_ref.3, bf16[8,256,256]{2,1,0:T(8,128)(2,1)} %get-tuple-element.27.q_ref, bf16[8,256,256]{2,1,0:T(8,128)(2,1)} %get-tuple-element.28.k_ref, bf16[8,256,256]{2,1,0:T(8,128)(2,1)} %get-tuple-element.29.v_ref, ...), custom_call_target="tpu_custom_call" | custom-call | tf_op jit(solution)/shard_map/row_attend/pallas_call | solution.py:367
  33.4 30.4 %all_to_all.5.x_ref = bf16[32,64,256]{2,1,0:T(8,128)(2,1)S(1)} all-to-all(bf16[32,64,256]{2,1,0:T(8,128)(2,1)S(1)} %row_attend.1), channel_id=1, replica_groups=mesh['branch'=1,'dap'=32] {'dap'}, dimensions={0} | all-to-all | bytes 2097152 | tf_op jit(solution)/shard_map/all_to_all | solution.py:597
  63.8 11.5 %column_attend.1 = (bf16[8,256,256]{2,1,0:T(8,128)(2,1)}, bf16[256,256]{1,0:T(8,128)(2,1)S(1)}, bf16[256,256]{1,0:T(8,128)(2,1)S(1)}) custom-call(s32[1]{0:T(128)} %bitcast.me_ref, bf16[32,64,256]{2,1,0:T(8,128)(2,1)S(1)} %all_to_all.5.x_ref, s32[256,256]{1,0:T(8,128)S(1)} %copy-done.1, bf16[4,256,256]{2,1,0:T(8,128)(2,1)S(1)} %copy-done.3, ...), custom_call_target="tpu_custom_call" | custom-call | tf_op jit(solution)/shard_map/column_attend/pallas_call | solution.py:437
  75.3 0.8 collective-permute-start.10
  76.0 1.1 %collective-permute-start.11 = (bf16[256,256]{1,0:T(8,128)(2,1)S(1)}, bf16[256,256]{1,0:T(8,128)(2,1)S(1)}, u32[]{:S(2)}, u32[]{:S(2)}) collective-permute-start(bf16[256,256]{1,0:T(8,128)(2,1)S(1)} %get-tuple-element.43.refs_1_.refs_3_), channel_id=1, source_target_pairs={{0,16},{1,17},{2,18},{3,19},{4,20},{5,21},{6,22},{7,23},{8,24},{9,... | collective-permute-start | bytes 393224 | tf_op jit(solution)/shard_map/ppermute | solution.py:561
  77.1 2.5 %collective-permute-start.12 = (bf16[256,256]{1,0:T(8,128)(2,1)S(1)}, bf16[256,256]{1,0:T(8,128)(2,1)S(1)}, u32[]{:S(2)}, u32[]{:S(2)}) collective-permute-start(bf16[256,256]{1,0:T(8,128)(2,1)S(1)} %get-tuple-element.43.refs_1_.refs_3_), channel_id=1, source_target_pairs={{0,24},{1,25},{2,26},{3,27},{4,28},{5,29},{6,30},{7,31},{8,16},{9,... | collective-permute-start | bytes 393224 | tf_op jit(solution)/shard_map/ppermute | solution.py:561
  79.7 1.5 %collective-permute-start.17 = (bf16[256,256]{1,0:T(8,128)(2,1)S(1)}, bf16[256,256]{1,0:T(8,128)(2,1)S(1)}, u32[]{:S(2)}, u32[]{:S(2)}) collective-permute-start(bf16[256,256]{1,0:T(8,128)(2,1)S(1)} %get-tuple-element.42.refs_0_), channel_id=1, source_target_pairs={{0,2},{1,3},{2,0},{3,1},{4,6},{5,7},{6,4},{7,5},{8,10},{9,11},{10,... | collective-permute-start | bytes 393224 | tf_op jit(solution)/shard_map/ppermute | solution.py:561
  81.1 1.5 %collective-permute-start.18 = (bf16[256,256]{1,0:T(8,128)(2,1)S(1)}, bf16[256,256]{1,0:T(8,128)(2,1)S(1)}, u32[]{:S(2)}, u32[]{:S(2)}) collective-permute-start(bf16[256,256]{1,0:T(8,128)(2,1)S(1)} %get-tuple-element.42.refs_0_), channel_id=1, source_target_pairs={{0,4},{1,5},{2,6},{3,7},{4,0},{5,1},{6,2},{7,3},{8,12},{9,13},{10,... | collective-permute-start | bytes 393224 | tf_op jit(solution)/shard_map/ppermute | solution.py:561
  82.6 1.7 %collective-permute-start.19 = (bf16[256,256]{1,0:T(8,128)(2,1)S(1)}, bf16[256,256]{1,0:T(8,128)(2,1)S(1)}, u32[]{:S(2)}, u32[]{:S(2)}) collective-permute-start(bf16[256,256]{1,0:T(8,128)(2,1)S(1)} %get-tuple-element.42.refs_0_), channel_id=1, source_target_pairs={{0,6},{1,7},{2,4},{3,5},{4,2},{5,3},{6,0},{7,1},{8,14},{9,15},{10,... | collective-permute-start | bytes 393224 | tf_op jit(solution)/shard_map/ppermute | solution.py:561
  84.3 3.6 %interleave.1 = bf16[256,8,256]{2,1,0:T(8,128)(2,1)} custom-call(bf16[8,256,256]{2,1,0:T(8,128)(2,1)} %get-tuple-element.39.rows_ref), custom_call_target="tpu_custom_call" | custom-call | tf_op jit(solution)/shard_map/interleave/pallas_call | solution.py:459
  87.9 1.0 collective-permute-done.11.refs_5_.refs_7_
  88.9 0.5 collective-permute-start.14
  89.4 0.5 collective-permute-start.16
  91.0 2.9 %outer_product.3 = (bf16[8,64,128]{2,1,0:T(8,128)(2,1)S(1)}, bf16[8,64,128]{2,1,0:T(8,128)(2,1)S(1)}, bf16[8,64,128]{2,1,0:T(8,128)(2,1)S(1)}) custom-call(bf16[256,256]{1,0:T(8,128)(2,1)S(1)} %collective-permute-done.17.refs_0_, bf16[256,256]{1,0:T(8,128)(2,1)S(1)} %collective-permute-done.18.refs_1_, bf16[256,256]{1,0:T(8,128)(2,1)S(1)} %collective-permute-done.19.refs_2_, ...), custom_call_target="tpu_custom_call" | custom-call | tf_op jit(solution)/shard_map/outer_product/pallas_call | solution.py:513
  93.9 0.8 collective-permute-start.20
  94.7 1.3 %collective-permute-start.21 = (bf16[8,64,128]{2,1,0:T(8,128)(2,1)S(1)}, bf16[8,64,128]{2,1,0:T(8,128)(2,1)S(1)}, u32[]{:S(2)}, u32[]{:S(2)}) collective-permute-start(bf16[8,64,128]{2,1,0:T(8,128)(2,1)S(1)} %get-tuple-element.48), channel_id=1, source_target_pairs={{0,4},{1,5},{2,6},{3,7},{4,0},{5,1},{6,2},{7,3},{8,12},{9,13},{10,... | collective-permute-start | bytes 393224 | tf_op jit(solution)/shard_map/ppermute | solution.py:561
  96.1 1.4 %collective-permute-start.22 = (bf16[8,64,128]{2,1,0:T(8,128)(2,1)S(1)}, bf16[8,64,128]{2,1,0:T(8,128)(2,1)S(1)}, u32[]{:S(2)}, u32[]{:S(2)}) collective-permute-start(bf16[8,64,128]{2,1,0:T(8,128)(2,1)S(1)} %get-tuple-element.49), channel_id=1, source_target_pairs={{0,6},{1,7},{2,4},{3,5},{4,2},{5,3},{6,0},{7,1},{8,14},{9,15},{10,... | collective-permute-start | bytes 393224 | tf_op jit(solution)/shard_map/ppermute | solution.py:561
  97.7 1.9 %outer_product.2.refs_0_ = bf16[8,64,128]{2,1,0:T(8,128)(2,1)S(1)} custom-call(bf16[256,256]{1,0:T(8,128)(2,1)S(1)} %get-tuple-element.42.refs_0_, bf16[256,256]{1,0:T(8,128)(2,1)S(1)} %get-tuple-element.43.refs_1_.refs_3_, bf16[256,256]{1,0:T(8,128)(2,1)S(1)} %collective-permute-done.13.refs_2_.refs_4_, ...), custom_call_target="tpu_custom_call" | custom-call | tf_op jit(solution)/shard_map/outer_product/pallas_call | solution.py:513
  99.6 0.6 collective-permute-done.20.refs_1_
  100.2 2.7 %collective-permute-done.21.refs_2_ = bf16[8,64,128]{2,1,0:T(8,128)(2,1)S(1)} collective-permute-done((bf16[8,64,128]{2,1,0:T(8,128)(2,1)S(1)}, bf16[8,64,128]{2,1,0:T(8,128)(2,1)S(1)}, u32[]{:S(2)}, u32[]{:S(2)}) %collective-permute-start.21) | collective-permute-done | bytes 131104 | tf_op jit(solution)/shard_map/ppermute | solution.py:561
  103.0 1.3 %finish.1 = bf16[8,256,128]{2,1,0:T(8,128)(2,1)} custom-call(s32[1]{0:T(128)} %bitcast.me_ref, bf16[8,256,128]{2,1,0:T(8,128)(2,1)S(1)} %copy-done, f32[256,8]{1,0:T(8,128)S(1)} %fusion.scale_ref, bf16[8,64,128]{2,1,0:T(8,128)(2,1)S(1)} %outer_product.2.refs_0_, bf16[8,64,128]{2,1,0:T(8,128)(2,1)S(1)} %collective-permute-done.20.refs_1_, ...), custom_call_target="tpu_custom_call" | custom-call | tf_op jit(solution)/shard_map/finish/pallas_call | solution.py:548
  (41 shorter events, 1.7 us)
Async XLA Ops:
  2.4 11.3 %collective-permute-start = (bf16[64,256]{1,0:T(8,128)(2,1)S(1)}, bf16[64,256]{1,0:T(8,128)(2,1)S(1)}, u32[]{:S(2)}, u32[]{:S(2)}) collective-permute-start(bf16[64,256]{1,0:T(8,128)(2,1)S(1)} %pair_bias.1), channel_id=1, source_target_pairs={{0,8},{1,9},{2,10},{3,11},{4,12},{5,13},{6,14},{7,15},{8,0},{9,1},... | collective-permute-start | bytes 98312 | tf_op jit(solution)/shard_map/ppermute | solution.py:561
  5.5 8.2 %collective-permute-start.1 = (bf16[64,256]{1,0:T(8,128)(2,1)S(1)}, bf16[64,256]{1,0:T(8,128)(2,1)S(1)}, u32[]{:S(2)}, u32[]{:S(2)}) collective-permute-start(bf16[64,256]{1,0:T(8,128)(2,1)S(1)} %pair_bias.1), channel_id=1, source_target_pairs={{0,16},{1,17},{2,18},{3,19},{4,20},{5,21},{6,22},{7,23},{8,24},{9,... | collective-permute-start | bytes 98312 | tf_op jit(solution)/shard_map/ppermute | solution.py:561
  8.1 5.7 %collective-permute-start.2 = (bf16[64,256]{1,0:T(8,128)(2,1)S(1)}, bf16[64,256]{1,0:T(8,128)(2,1)S(1)}, u32[]{:S(2)}, u32[]{:S(2)}) collective-permute-start(bf16[64,256]{1,0:T(8,128)(2,1)S(1)} %pair_bias.1), channel_id=1, source_target_pairs={{0,24},{1,25},{2,26},{3,27},{4,28},{5,29},{6,30},{7,31},{8,16},{9,... | collective-permute-start | bytes 98312 | tf_op jit(solution)/shard_map/ppermute | solution.py:561
  13.8 5.9 %collective-permute-start.3 = (bf16[4,64,256]{2,1,0:T(8,128)(2,1)S(1)}, bf16[4,64,256]{2,1,0:T(8,128)(2,1)S(1)}, u32[]{:S(2)}, u32[]{:S(2)}) collective-permute-start(bf16[4,64,256]{2,1,0:T(8,128)(2,1)S(1)} %pad_maximum_fusion.rest_0_), channel_id=1, source_target_pairs={{0,2},{1,3},{2,0},{3,1},{4,6},{5,7},{6,4},{7,5},{8,10},{9,11},{10,... | collective-permute-start | bytes 393224 | tf_op jit(solution)/shard_map/ppermute | solution.py:561
  15.5 7.7 %collective-permute-start.4 = (bf16[4,64,256]{2,1,0:T(8,128)(2,1)S(1)}, bf16[4,64,256]{2,1,0:T(8,128)(2,1)S(1)}, u32[]{:S(2)}, u32[]{:S(2)}) collective-permute-start(bf16[4,64,256]{2,1,0:T(8,128)(2,1)S(1)} %pad_maximum_fusion.rest_0_), channel_id=1, source_target_pairs={{0,4},{1,5},{2,6},{3,7},{4,0},{5,1},{6,2},{7,3},{8,12},{9,13},{10,... | collective-permute-start | bytes 393224 | tf_op jit(solution)/shard_map/ppermute | solution.py:561
  17.1 6.2 %collective-permute-start.5 = (bf16[4,64,256]{2,1,0:T(8,128)(2,1)S(1)}, bf16[4,64,256]{2,1,0:T(8,128)(2,1)S(1)}, u32[]{:S(2)}, u32[]{:S(2)}) collective-permute-start(bf16[4,64,256]{2,1,0:T(8,128)(2,1)S(1)} %pad_maximum_fusion.rest_0_), channel_id=1, source_target_pairs={{0,6},{1,7},{2,4},{3,5},{4,2},{5,3},{6,0},{7,1},{8,14},{9,15},{10,... | collective-permute-start | bytes 393224 | tf_op jit(solution)/shard_map/ppermute | solution.py:561
  17.4 6.4 %collective-permute-start.6 = (bf16[4,64,256]{2,1,0:T(8,128)(2,1)S(1)}, bf16[4,64,256]{2,1,0:T(8,128)(2,1)S(1)}, u32[]{:S(2)}, u32[]{:S(2)}) collective-permute-start(bf16[4,64,256]{2,1,0:T(8,128)(2,1)S(1)} %pad_maximum_fusion.rest_0_), channel_id=1, source_target_pairs={{0,1},{1,0},{2,3},{3,2},{4,5},{5,4},{6,7},{7,6},{8,9},{9,8},{10,11... | collective-permute-start | bytes 393224 | tf_op jit(solution)/shard_map/ppermute | solution.py:561
  19.7 4.1 %collective-permute-start.7 = (bf16[4,64,256]{2,1,0:T(8,128)(2,1)S(1)}, bf16[4,64,256]{2,1,0:T(8,128)(2,1)S(1)}, u32[]{:S(2)}, u32[]{:S(2)}) collective-permute-start(bf16[4,64,256]{2,1,0:T(8,128)(2,1)S(1)} %collective-permute-done.3.rest_1_), channel_id=1, source_target_pairs={{0,1},{1,0},{2,3},{3,2},{4,5},{5,4},{6,7},{7,6},{8,9},{9,8},{10,11... | collective-permute-start | bytes 393224 | tf_op jit(solution)/shard_map/ppermute | solution.py:561
  23.3 1.3 %collective-permute-start.8 = (bf16[4,64,256]{2,1,0:T(8,128)(2,1)S(1)}, bf16[4,64,256]{2,1,0:T(8,128)(2,1)S(1)}, u32[]{:S(2)}, u32[]{:S(2)}) collective-permute-start(bf16[4,64,256]{2,1,0:T(8,128)(2,1)S(1)} %collective-permute-done.4.rest_2_), channel_id=1, source_target_pairs={{0,1},{1,0},{2,3},{3,2},{4,5},{5,4},{6,7},{7,6},{8,9},{9,8},{10,11... | collective-permute-start | bytes 393224 | tf_op jit(solution)/shard_map/ppermute | solution.py:561
  23.3 1.5 %collective-permute-start.9 = (bf16[4,64,256]{2,1,0:T(8,128)(2,1)S(1)}, bf16[4,64,256]{2,1,0:T(8,128)(2,1)S(1)}, u32[]{:S(2)}, u32[]{:S(2)}) collective-permute-start(bf16[4,64,256]{2,1,0:T(8,128)(2,1)S(1)} %collective-permute-done.5.rest_3_), channel_id=1, source_target_pairs={{0,1},{1,0},{2,3},{3,2},{4,5},{5,4},{6,7},{7,6},{8,9},{9,8},{10,11... | collective-permute-start | bytes 393224 | tf_op jit(solution)/shard_map/ppermute | solution.py:561
  33.3 30.4 %copy-start.1 = (s32[256,256]{1,0:T(8,128)S(1)}, s32[256,256]{1,0:T(8,128)}, u32[]{:S(2)}) copy-start(s32[256,256]{1,0:T(8,128)} %mask_ref.3) | copy-start | bytes 786436
  33.3 30.4 %copy-start.3 = (bf16[4,256,256]{2,1,0:T(8,128)(2,1)S(1)}, bf16[4,256,256]{2,1,0:T(8,128)(2,1)}, u32[]{:S(2)}) copy-start(bf16[4,256,256]{2,1,0:T(8,128)(2,1)} %weight_ref.3) | copy-start | bytes 1572868
  33.3 30.4 %copy-start.4 = (bf16[256,256]{1,0:T(8,128)(2,1)S(1)}, bf16[256,256]{1,0:T(8,128)(2,1)}, u32[]{:S(2)}) copy-start(bf16[256,256]{1,0:T(8,128)(2,1)} %out_w_ref.3) | copy-start | bytes 393220
  33.3 30.4 %copy-start.5 = (bf16[256,64]{0,1:T(8,128)(2,1)S(1)}, bf16[256,64]{0,1:T(8,128)(2,1)}, u32[]{:S(2)}) copy-start(bf16[256,64]{0,1:T(8,128)(2,1)} %param.20) | copy-start | bytes 98308
  63.7 26.2 %copy-start.6 = (s32[256]{0:T(256)S(1)}, s32[256]{0:T(256)}, u32[]{:S(2)}) copy-start(s32[256]{0:T(256)} %param.14) | copy-start | bytes 3076
  63.7 27.2 %copy-start.2 = (bf16[1024,128]{1,0:T(8,128)(2,1)S(1)}, bf16[1024,128]{1,0:T(8,128)(2,1)}, u32[]{:S(2)}) copy-start(bf16[1024,128]{1,0:T(8,128)(2,1)} %refs_11_.1) | copy-start | bytes 786436
  75.3 7.3 %collective-permute-start.10 = (bf16[256,256]{1,0:T(8,128)(2,1)S(1)}, bf16[256,256]{1,0:T(8,128)(2,1)S(1)}, u32[]{:S(2)}, u32[]{:S(2)}) collective-permute-start(bf16[256,256]{1,0:T(8,128)(2,1)S(1)} %get-tuple-element.43.refs_1_.refs_3_), channel_id=1, source_target_pairs={{0,8},{1,9},{2,10},{3,11},{4,12},{5,13},{6,14},{7,15},{8,0},{9,1},... | collective-permute-start | bytes 393224 | tf_op jit(solution)/shard_map/ppermute | solution.py:561
  76.0 12.9 %collective-permute-start.11 = (bf16[256,256]{1,0:T(8,128)(2,1)S(1)}, bf16[256,256]{1,0:T(8,128)(2,1)S(1)}, u32[]{:S(2)}, u32[]{:S(2)}) collective-permute-start(bf16[256,256]{1,0:T(8,128)(2,1)S(1)} %get-tuple-element.43.refs_1_.refs_3_), channel_id=1, source_target_pairs={{0,16},{1,17},{2,18},{3,19},{4,20},{5,21},{6,22},{7,23},{8,24},{9,... | collective-permute-start | bytes 393224 | tf_op jit(solution)/shard_map/ppermute | solution.py:561
  77.1 11.8 %collective-permute-start.12 = (bf16[256,256]{1,0:T(8,128)(2,1)S(1)}, bf16[256,256]{1,0:T(8,128)(2,1)S(1)}, u32[]{:S(2)}, u32[]{:S(2)}) collective-permute-start(bf16[256,256]{1,0:T(8,128)(2,1)S(1)} %get-tuple-element.43.refs_1_.refs_3_), channel_id=1, source_target_pairs={{0,24},{1,25},{2,26},{3,27},{4,28},{5,29},{6,30},{7,31},{8,16},{9,... | collective-permute-start | bytes 393224 | tf_op jit(solution)/shard_map/ppermute | solution.py:561
  79.7 9.8 %collective-permute-start.17 = (bf16[256,256]{1,0:T(8,128)(2,1)S(1)}, bf16[256,256]{1,0:T(8,128)(2,1)S(1)}, u32[]{:S(2)}, u32[]{:S(2)}) collective-permute-start(bf16[256,256]{1,0:T(8,128)(2,1)S(1)} %get-tuple-element.42.refs_0_), channel_id=1, source_target_pairs={{0,2},{1,3},{2,0},{3,1},{4,6},{5,7},{6,4},{7,5},{8,10},{9,11},{10,... | collective-permute-start | bytes 393224 | tf_op jit(solution)/shard_map/ppermute | solution.py:561
  81.1 8.3 %collective-permute-start.18 = (bf16[256,256]{1,0:T(8,128)(2,1)S(1)}, bf16[256,256]{1,0:T(8,128)(2,1)S(1)}, u32[]{:S(2)}, u32[]{:S(2)}) collective-permute-start(bf16[256,256]{1,0:T(8,128)(2,1)S(1)} %get-tuple-element.42.refs_0_), channel_id=1, source_target_pairs={{0,4},{1,5},{2,6},{3,7},{4,0},{5,1},{6,2},{7,3},{8,12},{9,13},{10,... | collective-permute-start | bytes 393224 | tf_op jit(solution)/shard_map/ppermute | solution.py:561
  82.6 7.4 %collective-permute-start.19 = (bf16[256,256]{1,0:T(8,128)(2,1)S(1)}, bf16[256,256]{1,0:T(8,128)(2,1)S(1)}, u32[]{:S(2)}, u32[]{:S(2)}) collective-permute-start(bf16[256,256]{1,0:T(8,128)(2,1)S(1)} %get-tuple-element.42.refs_0_), channel_id=1, source_target_pairs={{0,6},{1,7},{2,4},{3,5},{4,2},{5,3},{6,0},{7,1},{8,14},{9,15},{10,... | collective-permute-start | bytes 393224 | tf_op jit(solution)/shard_map/ppermute | solution.py:561
  87.9 15.1 %copy-start = (bf16[8,256,128]{2,1,0:T(8,128)(2,1)S(1)}, bf16[8,256,128]{2,1,0:T(8,128)(2,1)}, u32[]{:S(2)}) copy-start(bf16[8,256,128]{2,1,0:T(8,128)(2,1)} %pair_ref.3) | copy-start | bytes 1572868
  88.9 1.3 %collective-permute-start.13 = (bf16[256,256]{1,0:T(8,128)(2,1)S(1)}, bf16[256,256]{1,0:T(8,128)(2,1)S(1)}, u32[]{:S(2)}, u32[]{:S(2)}) collective-permute-start(bf16[256,256]{1,0:T(8,128)(2,1)S(1)} %get-tuple-element.43.refs_1_.refs_3_), channel_id=1, source_target_pairs={{0,1},{1,0},{2,3},{3,2},{4,5},{5,4},{6,7},{7,6},{8,9},{9,8},{10,11... | collective-permute-start | bytes 393224 | tf_op jit(solution)/shard_map/ppermute | solution.py:561
  88.9 1.5 %collective-permute-start.14 = (bf16[256,256]{1,0:T(8,128)(2,1)S(1)}, bf16[256,256]{1,0:T(8,128)(2,1)S(1)}, u32[]{:S(2)}, u32[]{:S(2)}) collective-permute-start(bf16[256,256]{1,0:T(8,128)(2,1)S(1)} %collective-permute-done.10.refs_3_.refs_5_), channel_id=1, source_target_pairs={{0,1},{1,0},{2,3},{3,2},{4,5},{5,4},{6,7},{7,6},{8,9},{9,8},{10,11... | collective-permute-start | bytes 393224 | tf_op jit(solution)/shard_map/ppermute | solution.py:561
  89.4 1.3 %collective-permute-start.15 = (bf16[256,256]{1,0:T(8,128)(2,1)S(1)}, bf16[256,256]{1,0:T(8,128)(2,1)S(1)}, u32[]{:S(2)}, u32[]{:S(2)}) collective-permute-start(bf16[256,256]{1,0:T(8,128)(2,1)S(1)} %collective-permute-done.11.refs_5_.refs_7_), channel_id=1, source_target_pairs={{0,1},{1,0},{2,3},{3,2},{4,5},{5,4},{6,7},{7,6},{8,9},{9,8},{10,11... | collective-permute-start | bytes 393224 | tf_op jit(solution)/shard_map/ppermute | solution.py:561
  89.4 1.5 %collective-permute-start.16 = (bf16[256,256]{1,0:T(8,128)(2,1)S(1)}, bf16[256,256]{1,0:T(8,128)(2,1)S(1)}, u32[]{:S(2)}, u32[]{:S(2)}) collective-permute-start(bf16[256,256]{1,0:T(8,128)(2,1)S(1)} %collective-permute-done.12.refs_7_.refs_9_), channel_id=1, source_target_pairs={{0,1},{1,0},{2,3},{3,2},{4,5},{5,4},{6,7},{7,6},{8,9},{9,8},{10,11... | collective-permute-start | bytes 393224 | tf_op jit(solution)/shard_map/ppermute | solution.py:561
  93.9 6.4 %collective-permute-start.20 = (bf16[8,64,128]{2,1,0:T(8,128)(2,1)S(1)}, bf16[8,64,128]{2,1,0:T(8,128)(2,1)S(1)}, u32[]{:S(2)}, u32[]{:S(2)}) collective-permute-start(bf16[8,64,128]{2,1,0:T(8,128)(2,1)S(1)} %get-tuple-element.47), channel_id=1, source_target_pairs={{0,2},{1,3},{2,0},{3,1},{4,6},{5,7},{6,4},{7,5},{8,10},{9,11},{10,... | collective-permute-start | bytes 393224 | tf_op jit(solution)/shard_map/ppermute | solution.py:561
  94.7 8.3 %collective-permute-start.21 = (bf16[8,64,128]{2,1,0:T(8,128)(2,1)S(1)}, bf16[8,64,128]{2,1,0:T(8,128)(2,1)S(1)}, u32[]{:S(2)}, u32[]{:S(2)}) collective-permute-start(bf16[8,64,128]{2,1,0:T(8,128)(2,1)S(1)} %get-tuple-element.48), channel_id=1, source_target_pairs={{0,4},{1,5},{2,6},{3,7},{4,0},{5,1},{6,2},{7,3},{8,12},{9,13},{10,... | collective-permute-start | bytes 393224 | tf_op jit(solution)/shard_map/ppermute | solution.py:561
  96.1 6.9 %collective-permute-start.22 = (bf16[8,64,128]{2,1,0:T(8,128)(2,1)S(1)}, bf16[8,64,128]{2,1,0:T(8,128)(2,1)S(1)}, u32[]{:S(2)}, u32[]{:S(2)}) collective-permute-start(bf16[8,64,128]{2,1,0:T(8,128)(2,1)S(1)} %get-tuple-element.49), channel_id=1, source_target_pairs={{0,6},{1,7},{2,4},{3,5},{4,2},{5,3},{6,0},{7,1},{8,14},{9,15},{10,... | collective-permute-start | bytes 393224 | tf_op jit(solution)/shard_map/ppermute | solution.py:561

commit v10 on v8

--- a/solution.py
+++ b/solution.py
@@ -253,6 +253,49 @@
     return [jnp.concatenate(p, axis=1) for p in pieces]
 
 
+def attend_heads_all(items, lanes, bias_of):
+    per_tile = LANES // HEAD_CHANNELS
+    width = items[0][0].shape[1]
+    tiles = width // LANES
+    tasks = [(n, h) for n in range(len(items)) for h in range(tiles * per_tile)]
+    scores, raised, totals, pieces = {}, {}, {}, [[] for _ in items]
+
+    def split(h):
+        tile = h // per_tile
+        return slice(tile * LANES, (tile + 1) * LANES), lanes[h % per_tile]
+
+    def score(at):
+        n, h = tasks[at]
+        cut, own = split(h)
+        scores[at] = nt_dot(items[n][0][:, cut] * own, items[n][1][:, cut])
+
+    def raise_scores(at):
+        part = scores.pop(at)
+        if bias_of is not None:
+            part = part + bias_of(tasks[at][1])
+        raised[at] = jnp.exp2(part).astype(BF16)
+
+    def gather(at):
+        n, h = tasks[at]
+        cut, own = split(h)
+        live = items[n][3]
+        side = jnp.concatenate([items[n][2][:, cut] * live * own, live * own], axis=1)
+        part = nn_dot(raised.pop(at), side)
+        totals[n] = part if h % per_tile == 0 else totals[n] + part
+        if h % per_tile == per_tile - 1:
+            total = totals.pop(n)
+            pieces[n].append(quotient(total[:, :LANES], total[:, LANES:]))
+
+    for at in range(len(tasks) + 2):
+        if at < len(tasks):
+            score(at)
+        if 0 <= at - 2:
+            gather(at - 2)
+        if 0 <= at - 1 < len(tasks):
+            raise_scores(at - 1)
+    return [jnp.concatenate(p, axis=1) for p in pieces]
+
+
 def project(normed, weight_ref):
     scale = LOG2E / math.sqrt(HEAD_CHANNELS)
     query = (nn_dot(normed, weight_ref[0]) * scale).astype(BF16)
@@ -336,7 +379,7 @@
         ).astype(BF16)
         items.append((q_ref[s], k_ref[s], v_ref[s], live))
     results = []
-    for s, heads_out in enumerate(attend_all(items, lanes, lambda h: bias_all[h])):
+    for s, heads_out in enumerate(attend_heads_all(items, lanes, lambda h: bias_all[h])):
         heads_out = (heads_out * g_ref[s]).astype(BF16)
         total = x_ref[s].astype(F32) + nn_dot(heads_out, out_w_ref[...])
         results.append(total.reshape(parts, 1, rows // step, total.shape[1]))
@@ -384,26 +427,32 @@
     residues = mask.shape[1]
     place = me_ref[0] * items + step * each
     rows = [load_strided(held, step * each + n, items, length) for n in range(each)]
-    inputs, gates = [], []
+    inputs, gates, normed = [], [], {0: layer_normalize(rows[0]).astype(BF16)}
     for n in range(each):
-        normed = layer_normalize(rows[n]).astype(BF16)
-        query, key, value, gate = project(normed, weight_ref)
+        if n + 1 < each:
+            normed[n + 1] = layer_normalize(rows[n + 1]).astype(BF16)
+        query, key, value, gate = project(normed[n], weight_ref)
         live = nn_dot(mask, one_hot((residues, LANES), 0, place + n, LIVE_SCALE)).astype(BF16)
         inputs.append((query, key, value, live))
         gates.append(gate)
-    results = []
-    for n, heads_out in enumerate(attend_all(inputs, lanes, None)):
-        heads_out = (heads_out * gates[n]).astype(BF16)
-        updated = (rows[n] + nn_dot(heads_out, out_w_ref[...])).astype(BF16)
-        normed = layer_normalize(updated.astype(F32)).astype(BF16)
-        live_row = nt_dot(one_hot((8, residues), 1, place + n), mask)[:1]
-        results.append((updated, nt_dot(factor_ref[...], normed) * live_row))
+    heads = attend_all(inputs, lanes, None)
     feat = FACTOR_CHANNELS
-    for n, (updated, factors) in enumerate(results):
-        item = step * each + n
-        out_ref[n] = updated
-        left_ref[pl.ds(pl.multiple_of(item * feat, feat), feat), :] = factors[:feat].astype(BF16)
-        store_strided(right_held, item, items, factors[feat:])
+    updated = {}
+    for at in range(each + 2):
+        if at < each:
+            heads_out = (heads[at] * gates[at]).astype(BF16)
+            updated[at] = (rows[at] + nn_dot(heads_out, out_w_ref[...])).astype(BF16)
+            out_ref[at] = updated[at]
+        if 0 <= at - 2:
+            n = at - 2
+            item = step * each + n
+            live_row = nt_dot(one_hot((8, residues), 1, place + n), mask)[:1]
+            factors = nt_dot(factor_ref[...], normed[n]) * live_row
+            left_at = pl.ds(pl.multiple_of(item * feat, feat), feat)
+            left_ref[left_at, :] = factors[:feat].astype(BF16)
+            store_strided(right_held, item, items, factors[feat:])
+        if 0 <= at - 1 < each:
+            normed[at - 1] = layer_normalize(updated[at - 1].astype(F32)).astype(BF16)
 
     @pl.when(step == items // each - 1)
     def _():

time: 102 us -> 102 us (level)
  no operation moved by 1% of the time
where the time goes in v10:
time: 102 us
  Pallas kernels  34.8 us (34%)
  blocking collectives  30.4 us (30%)
  starting transfers between devices  23.3 us (23%)
  waiting for transfers between devices  12.3 us (12%)
    all_to_all x1, blocking collectives, per_device_fast(): moved = lax.all_to_all(rows, 'dap', split_axis=0, concat_axis=0, tiled=True)  30.4 us
    ppermute x23, starting transfers between devices, exchange(): return lax.ppermute(block, 'dap', [(i, i ^ offset) for i in range(count)])  23.3 us
    ppermute x23, waiting for transfers between devices, exchange(): return lax.ppermute(block, 'dap', [(i, i ^ offset) for i in range(count)])  12.3 us
    pallas_call x1, Pallas kernels, column_attend(): pl.pallas_call(functools.partial(column_kernel, items, each), grid=(items...  9.42 us
    pallas_call x1, Pallas kernels, row_attend(): pl.pallas_call(functools.partial(row_attend_kernel, plan, step, seqs), gr...  8.35 us
    pallas_call x1, Pallas kernels, row_project(): pl.pallas_call(row_project_kernel, grid=(seqs // step,), in_specs=[block,...  5.58 us
    pallas_call x2, Pallas kernels, outer_product(): pl.pallas_call(functools.partial(outer_kernel, group, outer, items), out_...  4.8 us
    pallas_call x1, Pallas kernels, interleave(): pl.pallas_call(interleave_kernel, grid=(length // step,), in_specs=[pl.Bl...  3.64 us
  transfers between devices with their start and end apart: 23, of which 12 were waited for; matrix products, arithmetic and copies ran while one was open for 0% of the time, Pallas kernels for 11%

profile of v10, /device:TPU:0, one launch (start us, length us, event | category | flops | bytes accessed | tf_op | source)
XLA Modules:
  0.0 102.1 jit_solution(11450434182422841620)
XLA Ops:
  0.6 1.8 %pair_bias.1 = bf16[64,256]{1,0:T(8,128)(2,1)S(1)} custom-call(bf16[8,256,128]{2,1,0:T(8,128)(2,1)} %pair_ref.3, bf16[8,128]{1,0:T(8,128)(2,1)} %bitcast.12), custom_call_target="tpu_custom_call" | custom-call | tf_op jit(solution)/shard_map/pair_bias/pallas_call | solution.py:321
  2.4 3.1 %collective-permute-start = (bf16[64,256]{1,0:T(8,128)(2,1)S(1)}, bf16[64,256]{1,0:T(8,128)(2,1)S(1)}, u32[]{:S(2)}, u32[]{:S(2)}) collective-permute-start(bf16[64,256]{1,0:T(8,128)(2,1)S(1)} %pair_bias.1), channel_id=1, source_target_pairs={{0,8},{1,9},{2,10},{3,11},{4,12},{5,13},{6,14},{7,15},{8,0},{9,1},... | collective-permute-start | bytes 98312 | tf_op jit(solution)/shard_map/ppermute | solution.py:595
  5.5 2.6 %collective-permute-start.1 = (bf16[64,256]{1,0:T(8,128)(2,1)S(1)}, bf16[64,256]{1,0:T(8,128)(2,1)S(1)}, u32[]{:S(2)}, u32[]{:S(2)}) collective-permute-start(bf16[64,256]{1,0:T(8,128)(2,1)S(1)} %pair_bias.1), channel_id=1, source_target_pairs={{0,16},{1,17},{2,18},{3,19},{4,20},{5,21},{6,22},{7,23},{8,24},{9,... | collective-permute-start | bytes 98312 | tf_op jit(solution)/shard_map/ppermute | solution.py:595
  8.1 5.6 %row_project.1 = (bf16[8,256,256]{2,1,0:T(8,128)(2,1)}, bf16[8,256,256]{2,1,0:T(8,128)(2,1)}, bf16[8,256,256]{2,1,0:T(8,128)(2,1)}, f32[8,256,256]{2,1,0:T(8,128)}) custom-call(bf16[8,256,256]{2,1,0:T(8,128)(2,1)} %x_ref.3, bf16[4,256,256]{2,1,0:T(8,128)(2,1)} %weight_ref.2), custom_call_target="tpu_custom_call" | custom-call | tf_op jit(solution)/shard_map/row_project/pallas_call | solution.py:343
  13.8 1.7 %collective-permute-start.3 = (bf16[4,64,256]{2,1,0:T(8,128)(2,1)S(1)}, bf16[4,64,256]{2,1,0:T(8,128)(2,1)S(1)}, u32[]{:S(2)}, u32[]{:S(2)}) collective-permute-start(bf16[4,64,256]{2,1,0:T(8,128)(2,1)S(1)} %pad_maximum_fusion.rest_0_), channel_id=1, source_target_pairs={{0,2},{1,3},{2,0},{3,1},{4,6},{5,7},{6,4},{7,5},{8,10},{9,11},{10,... | collective-permute-start | bytes 393224 | tf_op jit(solution)/shard_map/ppermute | solution.py:595
  15.5 1.5 %collective-permute-start.4 = (bf16[4,64,256]{2,1,0:T(8,128)(2,1)S(1)}, bf16[4,64,256]{2,1,0:T(8,128)(2,1)S(1)}, u32[]{:S(2)}, u32[]{:S(2)}) collective-permute-start(bf16[4,64,256]{2,1,0:T(8,128)(2,1)S(1)} %pad_maximum_fusion.rest_0_), channel_id=1, source_target_pairs={{0,4},{1,5},{2,6},{3,7},{4,0},{5,1},{6,2},{7,3},{8,12},{9,13},{10,... | collective-permute-start | bytes 393224 | tf_op jit(solution)/shard_map/ppermute | solution.py:595
  17.1 0.3 collective-permute-start.5
  17.4 2.3 %collective-permute-done.3.rest_1_ = bf16[4,64,256]{2,1,0:T(8,128)(2,1)S(1)} collective-permute-done((bf16[4,64,256]{2,1,0:T(8,128)(2,1)S(1)}, bf16[4,64,256]{2,1,0:T(8,128)(2,1)S(1)}, u32[]{:S(2)}, u32[]{:S(2)}) %collective-permute-start.3) | collective-permute-done | bytes 131104 | tf_op jit(solution)/shard_map/ppermute | solution.py:595
  19.7 3.5 %collective-permute-done.4.rest_2_ = bf16[4,64,256]{2,1,0:T(8,128)(2,1)S(1)} collective-permute-done((bf16[4,64,256]{2,1,0:T(8,128)(2,1)S(1)}, bf16[4,64,256]{2,1,0:T(8,128)(2,1)S(1)}, u32[]{:S(2)}, u32[]{:S(2)}) %collective-permute-start.4) | collective-permute-done | bytes 131104 | tf_op jit(solution)/shard_map/ppermute | solution.py:595
  23.3 0.5 collective-permute-start.9
  23.8 0.8 collective-permute-done.8.rest_6_
  24.8 8.4 %row_attend.1 = bf16[32,64,256]{2,1,0:T(8,128)(2,1)S(1)} custom-call(s32[1]{0:T(128)} %bitcast.me_ref, bf16[8,256,256]{2,1,0:T(8,128)(2,1)} %x_ref.3, bf16[8,256,256]{2,1,0:T(8,128)(2,1)} %get-tuple-element.27.q_ref, bf16[8,256,256]{2,1,0:T(8,128)(2,1)} %get-tuple-element.28.k_ref, bf16[8,256,256]{2,1,0:T(8,128)(2,1)} %get-tuple-element.29.v_ref, ...), custom_call_target="tpu_custom_call" | custom-call | tf_op jit(solution)/shard_map/row_attend/pallas_call | solution.py:396
  33.2 30.4 %all_to_all.5.x_ref = bf16[32,64,256]{2,1,0:T(8,128)(2,1)S(1)} all-to-all(bf16[32,64,256]{2,1,0:T(8,128)(2,1)S(1)} %row_attend.1), channel_id=1, replica_groups=mesh['branch'=1,'dap'=32] {'dap'}, dimensions={0} | all-to-all | bytes 2097152 | tf_op jit(solution)/shard_map/all_to_all | solution.py:631
  63.6 9.4 %column_attend.1 = (bf16[8,256,256]{2,1,0:T(8,128)(2,1)}, bf16[256,256]{1,0:T(8,128)(2,1)S(1)}, bf16[256,256]{1,0:T(8,128)(2,1)S(1)}) custom-call(s32[1]{0:T(128)} %bitcast.me_ref, bf16[32,64,256]{2,1,0:T(8,128)(2,1)S(1)} %all_to_all.5.x_ref, s32[256,256]{1,0:T(8,128)S(1)} %copy-done.1, bf16[4,256,256]{2,1,0:T(8,128)(2,1)S(1)} %copy-done.3, ...), custom_call_target="tpu_custom_call" | custom-call | tf_op jit(solution)/shard_map/column_attend/pallas_call | solution.py:471
  73.1 0.8 collective-permute-start.10
  73.8 1.1 %collective-permute-start.11 = (bf16[256,256]{1,0:T(8,128)(2,1)S(1)}, bf16[256,256]{1,0:T(8,128)(2,1)S(1)}, u32[]{:S(2)}, u32[]{:S(2)}) collective-permute-start(bf16[256,256]{1,0:T(8,128)(2,1)S(1)} %get-tuple-element.43.refs_1_.refs_3_), channel_id=1, source_target_pairs={{0,16},{1,17},{2,18},{3,19},{4,20},{5,21},{6,22},{7,23},{8,24},{9,... | collective-permute-start | bytes 393224 | tf_op jit(solution)/shard_map/ppermute | solution.py:595
  74.9 2.5 %collective-permute-start.12 = (bf16[256,256]{1,0:T(8,128)(2,1)S(1)}, bf16[256,256]{1,0:T(8,128)(2,1)S(1)}, u32[]{:S(2)}, u32[]{:S(2)}) collective-permute-start(bf16[256,256]{1,0:T(8,128)(2,1)S(1)} %get-tuple-element.43.refs_1_.refs_3_), channel_id=1, source_target_pairs={{0,24},{1,25},{2,26},{3,27},{4,28},{5,29},{6,30},{7,31},{8,16},{9,... | collective-permute-start | bytes 393224 | tf_op jit(solution)/shard_map/ppermute | solution.py:595
  77.4 1.5 %collective-permute-start.17 = (bf16[256,256]{1,0:T(8,128)(2,1)S(1)}, bf16[256,256]{1,0:T(8,128)(2,1)S(1)}, u32[]{:S(2)}, u32[]{:S(2)}) collective-permute-start(bf16[256,256]{1,0:T(8,128)(2,1)S(1)} %get-tuple-element.42.refs_0_), channel_id=1, source_target_pairs={{0,2},{1,3},{2,0},{3,1},{4,6},{5,7},{6,4},{7,5},{8,10},{9,11},{10,... | collective-permute-start | bytes 393224 | tf_op jit(solution)/shard_map/ppermute | solution.py:595
  78.9 1.5 %collective-permute-start.18 = (bf16[256,256]{1,0:T(8,128)(2,1)S(1)}, bf16[256,256]{1,0:T(8,128)(2,1)S(1)}, u32[]{:S(2)}, u32[]{:S(2)}) collective-permute-start(bf16[256,256]{1,0:T(8,128)(2,1)S(1)} %get-tuple-element.42.refs_0_), channel_id=1, source_target_pairs={{0,4},{1,5},{2,6},{3,7},{4,0},{5,1},{6,2},{7,3},{8,12},{9,13},{10,... | collective-permute-start | bytes 393224 | tf_op jit(solution)/shard_map/ppermute | solution.py:595
  80.4 1.7 %collective-permute-start.19 = (bf16[256,256]{1,0:T(8,128)(2,1)S(1)}, bf16[256,256]{1,0:T(8,128)(2,1)S(1)}, u32[]{:S(2)}, u32[]{:S(2)}) collective-permute-start(bf16[256,256]{1,0:T(8,128)(2,1)S(1)} %get-tuple-element.42.refs_0_), channel_id=1, source_target_pairs={{0,6},{1,7},{2,4},{3,5},{4,2},{5,3},{6,0},{7,1},{8,14},{9,15},{10,... | collective-permute-start | bytes 393224 | tf_op jit(solution)/shard_map/ppermute | solution.py:595
  82.1 3.6 %interleave.1 = bf16[256,8,256]{2,1,0:T(8,128)(2,1)} custom-call(bf16[8,256,256]{2,1,0:T(8,128)(2,1)} %get-tuple-element.39.rows_ref), custom_call_target="tpu_custom_call" | custom-call | tf_op jit(solution)/shard_map/interleave/pallas_call | solution.py:493
  85.7 1.0 collective-permute-done.11.refs_5_.refs_7_
  86.7 0.5 collective-permute-start.14
  87.2 0.5 collective-permute-start.16
  88.8 2.9 %outer_product.3 = (bf16[8,64,128]{2,1,0:T(8,128)(2,1)S(1)}, bf16[8,64,128]{2,1,0:T(8,128)(2,1)S(1)}, bf16[8,64,128]{2,1,0:T(8,128)(2,1)S(1)}) custom-call(bf16[256,256]{1,0:T(8,128)(2,1)S(1)} %collective-permute-done.17.refs_0_, bf16[256,256]{1,0:T(8,128)(2,1)S(1)} %collective-permute-done.18.refs_1_, bf16[256,256]{1,0:T(8,128)(2,1)S(1)} %collective-permute-done.19.refs_2_, ...), custom_call_target="tpu_custom_call" | custom-call | tf_op jit(solution)/shard_map/outer_product/pallas_call | solution.py:547
  91.7 0.9 collective-permute-start.20
  92.5 1.3 %collective-permute-start.21 = (bf16[8,64,128]{2,1,0:T(8,128)(2,1)S(1)}, bf16[8,64,128]{2,1,0:T(8,128)(2,1)S(1)}, u32[]{:S(2)}, u32[]{:S(2)}) collective-permute-start(bf16[8,64,128]{2,1,0:T(8,128)(2,1)S(1)} %get-tuple-element.48), channel_id=1, source_target_pairs={{0,4},{1,5},{2,6},{3,7},{4,0},{5,1},{6,2},{7,3},{8,12},{9,13},{10,... | collective-permute-start | bytes 393224 | tf_op jit(solution)/shard_map/ppermute | solution.py:595
  93.8 1.4 %collective-permute-start.22 = (bf16[8,64,128]{2,1,0:T(8,128)(2,1)S(1)}, bf16[8,64,128]{2,1,0:T(8,128)(2,1)S(1)}, u32[]{:S(2)}, u32[]{:S(2)}) collective-permute-start(bf16[8,64,128]{2,1,0:T(8,128)(2,1)S(1)} %get-tuple-element.49), channel_id=1, source_target_pairs={{0,6},{1,7},{2,4},{3,5},{4,2},{5,3},{6,0},{7,1},{8,14},{9,15},{10,... | collective-permute-start | bytes 393224 | tf_op jit(solution)/shard_map/ppermute | solution.py:595
  95.5 1.9 %outer_product.2.refs_0_ = bf16[8,64,128]{2,1,0:T(8,128)(2,1)S(1)} custom-call(bf16[256,256]{1,0:T(8,128)(2,1)S(1)} %get-tuple-element.42.refs_0_, bf16[256,256]{1,0:T(8,128)(2,1)S(1)} %get-tuple-element.43.refs_1_.refs_3_, bf16[256,256]{1,0:T(8,128)(2,1)S(1)} %collective-permute-done.13.refs_2_.refs_4_, ...), custom_call_target="tpu_custom_call" | custom-call | tf_op jit(solution)/shard_map/outer_product/pallas_call | solution.py:547
  97.4 0.6 collective-permute-done.20.refs_1_
  98.0 2.7 %collective-permute-done.21.refs_2_ = bf16[8,64,128]{2,1,0:T(8,128)(2,1)S(1)} collective-permute-done((bf16[8,64,128]{2,1,0:T(8,128)(2,1)S(1)}, bf16[8,64,128]{2,1,0:T(8,128)(2,1)S(1)}, u32[]{:S(2)}, u32[]{:S(2)}) %collective-permute-start.21) | collective-permute-done | bytes 131104 | tf_op jit(solution)/shard_map/ppermute | solution.py:595
  100.8 1.3 %finish.1 = bf16[8,256,128]{2,1,0:T(8,128)(2,1)} custom-call(s32[1]{0:T(128)} %bitcast.me_ref, bf16[8,256,128]{2,1,0:T(8,128)(2,1)S(1)} %copy-done, f32[256,8]{1,0:T(8,128)S(1)} %fusion.scale_ref, bf16[8,64,128]{2,1,0:T(8,128)(2,1)S(1)} %outer_product.2.refs_0_, bf16[8,64,128]{2,1,0:T(8,128)(2,1)S(1)} %collective-permute-done.20.refs_1_, ...), custom_call_target="tpu_custom_call" | custom-call | tf_op jit(solution)/shard_map/finish/pallas_call | solution.py:582
  (41 shorter events, 1.7 us)
Async XLA Ops:
  2.4 11.3 %collective-permute-start = (bf16[64,256]{1,0:T(8,128)(2,1)S(1)}, bf16[64,256]{1,0:T(8,128)(2,1)S(1)}, u32[]{:S(2)}, u32[]{:S(2)}) collective-permute-start(bf16[64,256]{1,0:T(8,128)(2,1)S(1)} %pair_bias.1), channel_id=1, source_target_pairs={{0,8},{1,9},{2,10},{3,11},{4,12},{5,13},{6,14},{7,15},{8,0},{9,1},... | collective-permute-start | bytes 98312 | tf_op jit(solution)/shard_map/ppermute | solution.py:595
  5.5 8.2 %collective-permute-start.1 = (bf16[64,256]{1,0:T(8,128)(2,1)S(1)}, bf16[64,256]{1,0:T(8,128)(2,1)S(1)}, u32[]{:S(2)}, u32[]{:S(2)}) collective-permute-start(bf16[64,256]{1,0:T(8,128)(2,1)S(1)} %pair_bias.1), channel_id=1, source_target_pairs={{0,16},{1,17},{2,18},{3,19},{4,20},{5,21},{6,22},{7,23},{8,24},{9,... | collective-permute-start | bytes 98312 | tf_op jit(solution)/shard_map/ppermute | solution.py:595
  8.1 5.7 %collective-permute-start.2 = (bf16[64,256]{1,0:T(8,128)(2,1)S(1)}, bf16[64,256]{1,0:T(8,128)(2,1)S(1)}, u32[]{:S(2)}, u32[]{:S(2)}) collective-permute-start(bf16[64,256]{1,0:T(8,128)(2,1)S(1)} %pair_bias.1), channel_id=1, source_target_pairs={{0,24},{1,25},{2,26},{3,27},{4,28},{5,29},{6,30},{7,31},{8,16},{9,... | collective-permute-start | bytes 98312 | tf_op jit(solution)/shard_map/ppermute | solution.py:595
  13.8 5.9 %collective-permute-start.3 = (bf16[4,64,256]{2,1,0:T(8,128)(2,1)S(1)}, bf16[4,64,256]{2,1,0:T(8,128)(2,1)S(1)}, u32[]{:S(2)}, u32[]{:S(2)}) collective-permute-start(bf16[4,64,256]{2,1,0:T(8,128)(2,1)S(1)} %pad_maximum_fusion.rest_0_), channel_id=1, source_target_pairs={{0,2},{1,3},{2,0},{3,1},{4,6},{5,7},{6,4},{7,5},{8,10},{9,11},{10,... | collective-permute-start | bytes 393224 | tf_op jit(solution)/shard_map/ppermute | solution.py:595
  15.5 7.7 %collective-permute-start.4 = (bf16[4,64,256]{2,1,0:T(8,128)(2,1)S(1)}, bf16[4,64,256]{2,1,0:T(8,128)(2,1)S(1)}, u32[]{:S(2)}, u32[]{:S(2)}) collective-permute-start(bf16[4,64,256]{2,1,0:T(8,128)(2,1)S(1)} %pad_maximum_fusion.rest_0_), channel_id=1, source_target_pairs={{0,4},{1,5},{2,6},{3,7},{4,0},{5,1},{6,2},{7,3},{8,12},{9,13},{10,... | collective-permute-start | bytes 393224 | tf_op jit(solution)/shard_map/ppermute | solution.py:595
  17.1 6.2 %collective-permute-start.5 = (bf16[4,64,256]{2,1,0:T(8,128)(2,1)S(1)}, bf16[4,64,256]{2,1,0:T(8,128)(2,1)S(1)}, u32[]{:S(2)}, u32[]{:S(2)}) collective-permute-start(bf16[4,64,256]{2,1,0:T(8,128)(2,1)S(1)} %pad_maximum_fusion.rest_0_), channel_id=1, source_target_pairs={{0,6},{1,7},{2,4},{3,5},{4,2},{5,3},{6,0},{7,1},{8,14},{9,15},{10,... | collective-permute-start | bytes 393224 | tf_op jit(solution)/shard_map/ppermute | solution.py:595
  17.4 6.4 %collective-permute-start.6 = (bf16[4,64,256]{2,1,0:T(8,128)(2,1)S(1)}, bf16[4,64,256]{2,1,0:T(8,128)(2,1)S(1)}, u32[]{:S(2)}, u32[]{:S(2)}) collective-permute-start(bf16[4,64,256]{2,1,0:T(8,128)(2,1)S(1)} %pad_maximum_fusion.rest_0_), channel_id=1, source_target_pairs={{0,1},{1,0},{2,3},{3,2},{4,5},{5,4},{6,7},{7,6},{8,9},{9,8},{10,11... | collective-permute-start | bytes 393224 | tf_op jit(solution)/shard_map/ppermute | solution.py:595
  19.7 4.1 %collective-permute-start.7 = (bf16[4,64,256]{2,1,0:T(8,128)(2,1)S(1)}, bf16[4,64,256]{2,1,0:T(8,128)(2,1)S(1)}, u32[]{:S(2)}, u32[]{:S(2)}) collective-permute-start(bf16[4,64,256]{2,1,0:T(8,128)(2,1)S(1)} %collective-permute-done.3.rest_1_), channel_id=1, source_target_pairs={{0,1},{1,0},{2,3},{3,2},{4,5},{5,4},{6,7},{7,6},{8,9},{9,8},{10,11... | collective-permute-start | bytes 393224 | tf_op jit(solution)/shard_map/ppermute | solution.py:595
  23.3 1.3 %collective-permute-start.8 = (bf16[4,64,256]{2,1,0:T(8,128)(2,1)S(1)}, bf16[4,64,256]{2,1,0:T(8,128)(2,1)S(1)}, u32[]{:S(2)}, u32[]{:S(2)}) collective-permute-start(bf16[4,64,256]{2,1,0:T(8,128)(2,1)S(1)} %collective-permute-done.4.rest_2_), channel_id=1, source_target_pairs={{0,1},{1,0},{2,3},{3,2},{4,5},{5,4},{6,7},{7,6},{8,9},{9,8},{10,11... | collective-permute-start | bytes 393224 | tf_op jit(solution)/shard_map/ppermute | solution.py:595
  23.3 1.5 %collective-permute-start.9 = (bf16[4,64,256]{2,1,0:T(8,128)(2,1)S(1)}, bf16[4,64,256]{2,1,0:T(8,128)(2,1)S(1)}, u32[]{:S(2)}, u32[]{:S(2)}) collective-permute-start(bf16[4,64,256]{2,1,0:T(8,128)(2,1)S(1)} %collective-permute-done.5.rest_3_), channel_id=1, source_target_pairs={{0,1},{1,0},{2,3},{3,2},{4,5},{5,4},{6,7},{7,6},{8,9},{9,8},{10,11... | collective-permute-start | bytes 393224 | tf_op jit(solution)/shard_map/ppermute | solution.py:595
  33.2 30.5 %copy-start.1 = (s32[256,256]{1,0:T(8,128)S(1)}, s32[256,256]{1,0:T(8,128)}, u32[]{:S(2)}) copy-start(s32[256,256]{1,0:T(8,128)} %mask_ref.3) | copy-start | bytes 786436
  33.2 30.4 %copy-start.3 = (bf16[4,256,256]{2,1,0:T(8,128)(2,1)S(1)}, bf16[4,256,256]{2,1,0:T(8,128)(2,1)}, u32[]{:S(2)}) copy-start(bf16[4,256,256]{2,1,0:T(8,128)(2,1)} %weight_ref.3) | copy-start | bytes 1572868
  33.2 30.4 %copy-start.4 = (bf16[256,256]{1,0:T(8,128)(2,1)S(1)}, bf16[256,256]{1,0:T(8,128)(2,1)}, u32[]{:S(2)}) copy-start(bf16[256,256]{1,0:T(8,128)(2,1)} %out_w_ref.3) | copy-start | bytes 393220
  33.2 30.4 %copy-start.5 = (bf16[256,64]{0,1:T(8,128)(2,1)S(1)}, bf16[256,64]{0,1:T(8,128)(2,1)}, u32[]{:S(2)}) copy-start(bf16[256,64]{0,1:T(8,128)(2,1)} %param.20) | copy-start | bytes 98308
  63.6 24.1 %copy-start.6 = (s32[256]{0:T(256)S(1)}, s32[256]{0:T(256)}, u32[]{:S(2)}) copy-start(s32[256]{0:T(256)} %param.14) | copy-start | bytes 3076
  63.6 25.2 %copy-start.2 = (bf16[1024,128]{1,0:T(8,128)(2,1)S(1)}, bf16[1024,128]{1,0:T(8,128)(2,1)}, u32[]{:S(2)}) copy-start(bf16[1024,128]{1,0:T(8,128)(2,1)} %refs_11_.1) | copy-start | bytes 786436
  73.1 7.3 %collective-permute-start.10 = (bf16[256,256]{1,0:T(8,128)(2,1)S(1)}, bf16[256,256]{1,0:T(8,128)(2,1)S(1)}, u32[]{:S(2)}, u32[]{:S(2)}) collective-permute-start(bf16[256,256]{1,0:T(8,128)(2,1)S(1)} %get-tuple-element.43.refs_1_.refs_3_), channel_id=1, source_target_pairs={{0,8},{1,9},{2,10},{3,11},{4,12},{5,13},{6,14},{7,15},{8,0},{9,1},... | collective-permute-start | bytes 393224 | tf_op jit(solution)/shard_map/ppermute | solution.py:595
  73.8 12.9 %collective-permute-start.11 = (bf16[256,256]{1,0:T(8,128)(2,1)S(1)}, bf16[256,256]{1,0:T(8,128)(2,1)S(1)}, u32[]{:S(2)}, u32[]{:S(2)}) collective-permute-start(bf16[256,256]{1,0:T(8,128)(2,1)S(1)} %get-tuple-element.43.refs_1_.refs_3_), channel_id=1, source_target_pairs={{0,16},{1,17},{2,18},{3,19},{4,20},{5,21},{6,22},{7,23},{8,24},{9,... | collective-permute-start | bytes 393224 | tf_op jit(solution)/shard_map/ppermute | solution.py:595
  74.9 11.8 %collective-permute-start.12 = (bf16[256,256]{1,0:T(8,128)(2,1)S(1)}, bf16[256,256]{1,0:T(8,128)(2,1)S(1)}, u32[]{:S(2)}, u32[]{:S(2)}) collective-permute-start(bf16[256,256]{1,0:T(8,128)(2,1)S(1)} %get-tuple-element.43.refs_1_.refs_3_), channel_id=1, source_target_pairs={{0,24},{1,25},{2,26},{3,27},{4,28},{5,29},{6,30},{7,31},{8,16},{9,... | collective-permute-start | bytes 393224 | tf_op jit(solution)/shard_map/ppermute | solution.py:595
  77.4 9.8 %collective-permute-start.17 = (bf16[256,256]{1,0:T(8,128)(2,1)S(1)}, bf16[256,256]{1,0:T(8,128)(2,1)S(1)}, u32[]{:S(2)}, u32[]{:S(2)}) collective-permute-start(bf16[256,256]{1,0:T(8,128)(2,1)S(1)} %get-tuple-element.42.refs_0_), channel_id=1, source_target_pairs={{0,2},{1,3},{2,0},{3,1},{4,6},{5,7},{6,4},{7,5},{8,10},{9,11},{10,... | collective-permute-start | bytes 393224 | tf_op jit(solution)/shard_map/ppermute | solution.py:595
  78.9 8.3 %collective-permute-start.18 = (bf16[256,256]{1,0:T(8,128)(2,1)S(1)}, bf16[256,256]{1,0:T(8,128)(2,1)S(1)}, u32[]{:S(2)}, u32[]{:S(2)}) collective-permute-start(bf16[256,256]{1,0:T(8,128)(2,1)S(1)} %get-tuple-element.42.refs_0_), channel_id=1, source_target_pairs={{0,4},{1,5},{2,6},{3,7},{4,0},{5,1},{6,2},{7,3},{8,12},{9,13},{10,... | collective-permute-start | bytes 393224 | tf_op jit(solution)/shard_map/ppermute | solution.py:595
  80.4 7.4 %collective-permute-start.19 = (bf16[256,256]{1,0:T(8,128)(2,1)S(1)}, bf16[256,256]{1,0:T(8,128)(2,1)S(1)}, u32[]{:S(2)}, u32[]{:S(2)}) collective-permute-start(bf16[256,256]{1,0:T(8,128)(2,1)S(1)} %get-tuple-element.42.refs_0_), channel_id=1, source_target_pairs={{0,6},{1,7},{2,4},{3,5},{4,2},{5,3},{6,0},{7,1},{8,14},{9,15},{10,... | collective-permute-start | bytes 393224 | tf_op jit(solution)/shard_map/ppermute | solution.py:595
  85.7 15.1 %copy-start = (bf16[8,256,128]{2,1,0:T(8,128)(2,1)S(1)}, bf16[8,256,128]{2,1,0:T(8,128)(2,1)}, u32[]{:S(2)}) copy-start(bf16[8,256,128]{2,1,0:T(8,128)(2,1)} %pair_ref.3) | copy-start | bytes 1572868
  86.7 1.3 %collective-permute-start.13 = (bf16[256,256]{1,0:T(8,128)(2,1)S(1)}, bf16[256,256]{1,0:T(8,128)(2,1)S(1)}, u32[]{:S(2)}, u32[]{:S(2)}) collective-permute-start(bf16[256,256]{1,0:T(8,128)(2,1)S(1)} %get-tuple-element.43.refs_1_.refs_3_), channel_id=1, source_target_pairs={{0,1},{1,0},{2,3},{3,2},{4,5},{5,4},{6,7},{7,6},{8,9},{9,8},{10,11... | collective-permute-start | bytes 393224 | tf_op jit(solution)/shard_map/ppermute | solution.py:595
  86.7 1.5 %collective-permute-start.14 = (bf16[256,256]{1,0:T(8,128)(2,1)S(1)}, bf16[256,256]{1,0:T(8,128)(2,1)S(1)}, u32[]{:S(2)}, u32[]{:S(2)}) collective-permute-start(bf16[256,256]{1,0:T(8,128)(2,1)S(1)} %collective-permute-done.10.refs_3_.refs_5_), channel_id=1, source_target_pairs={{0,1},{1,0},{2,3},{3,2},{4,5},{5,4},{6,7},{7,6},{8,9},{9,8},{10,11... | collective-permute-start | bytes 393224 | tf_op jit(solution)/shard_map/ppermute | solution.py:595
  87.2 1.3 %collective-permute-start.15 = (bf16[256,256]{1,0:T(8,128)(2,1)S(1)}, bf16[256,256]{1,0:T(8,128)(2,1)S(1)}, u32[]{:S(2)}, u32[]{:S(2)}) collective-permute-start(bf16[256,256]{1,0:T(8,128)(2,1)S(1)} %collective-permute-done.11.refs_5_.refs_7_), channel_id=1, source_target_pairs={{0,1},{1,0},{2,3},{3,2},{4,5},{5,4},{6,7},{7,6},{8,9},{9,8},{10,11... | collective-permute-start | bytes 393224 | tf_op jit(solution)/shard_map/ppermute | solution.py:595
  87.2 1.5 %collective-permute-start.16 = (bf16[256,256]{1,0:T(8,128)(2,1)S(1)}, bf16[256,256]{1,0:T(8,128)(2,1)S(1)}, u32[]{:S(2)}, u32[]{:S(2)}) collective-permute-start(bf16[256,256]{1,0:T(8,128)(2,1)S(1)} %collective-permute-done.12.refs_7_.refs_9_), channel_id=1, source_target_pairs={{0,1},{1,0},{2,3},{3,2},{4,5},{5,4},{6,7},{7,6},{8,9},{9,8},{10,11... | collective-permute-start | bytes 393224 | tf_op jit(solution)/shard_map/ppermute | solution.py:595
  91.7 6.4 %collective-permute-start.20 = (bf16[8,64,128]{2,1,0:T(8,128)(2,1)S(1)}, bf16[8,64,128]{2,1,0:T(8,128)(2,1)S(1)}, u32[]{:S(2)}, u32[]{:S(2)}) collective-permute-start(bf16[8,64,128]{2,1,0:T(8,128)(2,1)S(1)} %get-tuple-element.47), channel_id=1, source_target_pairs={{0,2},{1,3},{2,0},{3,1},{4,6},{5,7},{6,4},{7,5},{8,10},{9,11},{10,... | collective-permute-start | bytes 393224 | tf_op jit(solution)/shard_map/ppermute | solution.py:595
  92.5 8.3 %collective-permute-start.21 = (bf16[8,64,128]{2,1,0:T(8,128)(2,1)S(1)}, bf16[8,64,128]{2,1,0:T(8,128)(2,1)S(1)}, u32[]{:S(2)}, u32[]{:S(2)}) collective-permute-start(bf16[8,64,128]{2,1,0:T(8,128)(2,1)S(1)} %get-tuple-element.48), channel_id=1, source_target_pairs={{0,4},{1,5},{2,6},{3,7},{4,0},{5,1},{6,2},{7,3},{8,12},{9,13},{10,... | collective-permute-start | bytes 393224 | tf_op jit(solution)/shard_map/ppermute | solution.py:595
  93.8 7.0 %collective-permute-start.22 = (bf16[8,64,128]{2,1,0:T(8,128)(2,1)S(1)}, bf16[8,64,128]{2,1,0:T(8,128)(2,1)S(1)}, u32[]{:S(2)}, u32[]{:S(2)}) collective-permute-start(bf16[8,64,128]{2,1,0:T(8,128)(2,1)S(1)} %get-tuple-element.49), channel_id=1, source_target_pairs={{0,6},{1,7},{2,4},{3,5},{4,2},{5,3},{6,0},{7,1},{8,14},{9,15},{10,... | collective-permute-start | bytes 393224 | tf_op jit(solution)/shard_map/ppermute | solution.py:595

commit v11 on v8

--- a/solution.py
+++ b/solution.py
@@ -366,75 +366,74 @@
 
 
 def column_kernel(
-    items, each, me_ref, x_ref, mask_ref, weight_ref, out_w_ref, factor_ref,
+    items, me_ref, x_ref, mask_ref, weight_ref, out_w_ref, factor_ref,
     out_ref, left_ref, right_ref, held, right_held,
 ):
-    step = pl.program_id(0)
     total_rows = held.shape[1]
     length = total_rows // items
-
-    @pl.when(step == 0)
-    def _():
-        for t in range(held.shape[0]):
-            part = x_ref[:, :, t * LANES : (t + 1) * LANES].astype(F32)
-            held[t] = part.reshape(total_rows, LANES)
+    for t in range(held.shape[0]):
+        part = x_ref[:, :, t * LANES : (t + 1) * LANES].astype(F32)
+        held[t] = part.reshape(total_rows, LANES)
 
     lanes = head_lanes(length)
     mask = mask_ref[...].astype(F32).astype(BF16)
     residues = mask.shape[1]
-    place = me_ref[0] * items + step * each
-    rows = [load_strided(held, step * each + n, items, length) for n in range(each)]
-    inputs, gates = [], []
-    for n in range(each):
-        normed = layer_normalize(rows[n]).astype(BF16)
-        query, key, value, gate = project(normed, weight_ref)
+    place = me_ref[0] * items
+    rows = [load_strided(held, n, items, length) for n in range(items)]
+    inputs, gates, normed = [], [], {0: layer_normalize(rows[0]).astype(BF16)}
+    for n in range(items):
+        if n + 1 < items:
+            normed[n + 1] = layer_normalize(rows[n + 1]).astype(BF16)
+        query, key, value, gate = project(normed[n], weight_ref)
         live = nn_dot(mask, one_hot((residues, LANES), 0, place + n, LIVE_SCALE)).astype(BF16)
         inputs.append((query, key, value, live))
         gates.append(gate)
-    results = []
-    for n, heads_out in enumerate(attend_all(inputs, lanes, None)):
-        heads_out = (heads_out * gates[n]).astype(BF16)
-        updated = (rows[n] + nn_dot(heads_out, out_w_ref[...])).astype(BF16)
-        normed = layer_normalize(updated.astype(F32)).astype(BF16)
-        live_row = nt_dot(one_hot((8, residues), 1, place + n), mask)[:1]
-        results.append((updated, nt_dot(factor_ref[...], normed) * live_row))
+    heads = attend_all(inputs, lanes, None)
     feat = FACTOR_CHANNELS
-    for n, (updated, factors) in enumerate(results):
-        item = step * each + n
-        out_ref[n] = updated
-        left_ref[pl.ds(pl.multiple_of(item * feat, feat), feat), :] = factors[:feat].astype(BF16)
-        store_strided(right_held, item, items, factors[feat:])
-
-    @pl.when(step == items // each - 1)
-    def _():
-        right_ref[...] = joined_tiles(right_held).astype(BF16)
+    live_rows = nt_dot(
+        one_hot((items, residues), 1, place + lax.broadcasted_iota(jnp.int32, (items, residues), 0)),
+        mask,
+    )
+    updated = {}
+    for at in range(items + 2):
+        if at < items:
+            heads_out = (heads[at] * gates[at]).astype(BF16)
+            updated[at] = (rows[at] + nn_dot(heads_out, out_w_ref[...])).astype(BF16)
+            out_ref[at] = updated[at]
+        if 0 <= at - 2:
+            n = at - 2
+            factors = nt_dot(factor_ref[...], normed[n]) * live_rows[n : n + 1]
+            left_ref[n * feat : (n + 1) * feat, :] = factors[:feat].astype(BF16)
+            store_strided(right_held, n, items, factors[feat:])
+        if 0 <= at - 1 < items:
+            normed[at - 1] = layer_normalize(updated[at - 1].astype(F32)).astype(BF16)
+    right_ref[...] = joined_tiles(right_held).astype(BF16)
 
 
 def column_attend(me, moved, mask, weight, out_weight, factor_weight, items):
     width = moved.shape[2]
     total_rows = moved.shape[0] * moved.shape[1]
     length = total_rows // items
-    each = 4
     side = (items * FACTOR_CHANNELS, length)
     left = right = jax.ShapeDtypeStruct(side, BF16)
     vmem = pl.BlockSpec(memory_space=pltpu.VMEM)
     operands = in_vmem(moved, mask, weight, out_weight, factor_weight.T)
     return pl.pallas_call(
-        functools.partial(column_kernel, items, each),
-        grid=(items // each,),
+        functools.partial(column_kernel, items),
         in_specs=[pl.BlockSpec(memory_space=pltpu.SMEM)] + [vmem] * len(operands),
-        out_specs=[pl.BlockSpec((each, length, width), lambda i: (i, 0, 0)), vmem, vmem],
-        out_shape=[pltpu.HBM((items, length, width), BF16), left, right],
+        out_specs=[vmem] * 3,
+        out_shape=[pltpu.VMEM((items, length, width), BF16), left, right],
         scratch_shapes=[tiled_scratch(total_rows, width), tiled_scratch(*side)],
-        compiler_params=params(28),
+        compiler_params=params(48),
         name="column_attend",
     )(me, *operands)
 
 
 def interleave_kernel(rows_ref, out_ref, held):
-    items = rows_ref.shape[0]
+    items, step = rows_ref.shape[0], out_ref.shape[0]
+    at = pl.ds(pl.multiple_of(pl.program_id(0) * step, step), step)
     for item in range(items):
-        store_strided(held, item, items, rows_ref[item].astype(F32))
+        store_strided(held, item, items, rows_ref[item, at, :].astype(F32))
     out_ref[...] = joined_tiles(held).reshape(out_ref.shape).astype(BF16)
 
 
@@ -444,13 +443,13 @@
     return pl.pallas_call(
         interleave_kernel,
         grid=(length // step,),
-        in_specs=[pl.BlockSpec((items, step, width), lambda i: (0, i, 0))],
+        in_specs=[pl.BlockSpec(memory_space=pltpu.VMEM)],
         out_specs=pl.BlockSpec((step, items, width), lambda i: (i, 0, 0)),
         out_shape=pltpu.HBM((length, items, width), BF16),
         scratch_shapes=[tiled_scratch(items * step, width)],
         compiler_params=params(16),
         name="interleave",
-    )(*in_hbm(rows))
+    )(*in_vmem(rows))
 
 
 def outer_kernel(group, outer, items, *refs):
@@ -459,8 +458,9 @@
     outs = refs[group + outer + 1 : -3]
     weight_rows, weight, held = refs[-3:]
     feat = FACTOR_CHANNELS
-    quad = LANES // feat
-    tiles = items * feat // LANES
+    half = LANES // 2
+    duo = half // feat
+    tiles = items * feat // half
     cols = outer * items
     width = weight_ref.shape[1]
 
@@ -468,8 +468,8 @@
     weight[...] = jnp.zeros_like(weight)
     for e in range(feat):
         block = weight_rows[pl.ds(e, feat, stride=feat), :].astype(BF16)
-        for i in range(quad):
-            start = e * LANES + i * feat
+        for i in range(duo):
+            start = (e * duo + i) * feat
             weight[start : start + feat, i * width : (i + 1) * width] = block
 
     right = jnp.concatenate([r[...] for r in rights], axis=0)
@@ -477,30 +477,33 @@
         sums = nt_dot(right, lefts[k][...])
         sums = sums.reshape(outer, feat, items, sums.shape[1])
         sums = jnp.transpose(sums, (1, 0, 2, 3)).reshape(feat, cols, sums.shape[3]).astype(BF16)
-        for t in range(tiles):
-            at = slice((k * tiles + t) * cols, (k * tiles + t + 1) * cols)
-            for e in range(feat):
-                held[at, e * LANES : (e + 1) * LANES] = sums[e, :, t * LANES : (t + 1) * LANES]
+        for e in range(0, feat, 2):
+            for t in range(tiles):
+                at = slice((k * tiles + t) * cols, (k * tiles + t + 1) * cols)
+                cut = slice(t * half, (t + 1) * half)
+                both = jnp.concatenate([sums[e, :, cut], sums[e + 1, :, cut]], axis=1)
+                held[at, e * half : (e + 2) * half] = both
     update = nn_dot(held[...], weight[...])
     for k in range(group):
         for t in range(tiles):
             rows = update[(k * tiles + t) * cols : (k * tiles + t + 1) * cols]
-            for i in range(quad):
-                outs[k][t * quad + i] = rows[:, i * width : (i + 1) * width].astype(BF16)
+            for i in range(duo):
+                outs[k][t * duo + i] = rows[:, i * width : (i + 1) * width].astype(BF16)
 
 
 def outer_product(lefts, rights, weight, items):
     group, outer = len(lefts), len(rights)
     cols = outer * items
-    tiles = items * FACTOR_CHANNELS // LANES
-    depth = FACTOR_CHANNELS * LANES
+    half = LANES // 2
+    tiles = items * FACTOR_CHANNELS // half
+    depth = FACTOR_CHANNELS * half
     width = weight.shape[1]
     return pl.pallas_call(
         functools.partial(outer_kernel, group, outer, items),
         out_shape=[jax.ShapeDtypeStruct((items, cols, width), BF16)] * group,
         scratch_shapes=[
             pltpu.VMEM(weight.shape, F32),
-            pltpu.VMEM((depth, LANES // FACTOR_CHANNELS * width), BF16),
+            pltpu.VMEM((depth, half // FACTOR_CHANNELS * width), BF16),
             pltpu.VMEM((group * tiles * cols, depth), BF16),
         ],
         compiler_params=params(28),

time: 102 us -> 101 us (level)
  Pallas kernels: 34.8 us -> 31.6 us
  waiting for transfers between devices: 12.3 us -> 14.4 us
    ppermute x23, waiting for transfers between devices: 12.3 us -> 14.4 us  [exchange(): return lax.ppermute(block, 'dap', [(i, i ^ offset) for i in range(count)])]
    pallas_call x1, Pallas kernels: 9.87 us -> 8.07 us  [column_attend(): pl.pallas_call(functools.partial(column_kernel, items), in_specs=[pl.Bloc...]
    pallas_call x1, Pallas kernels: 3.64 us -> 1.89 us  [interleave(): pl.pallas_call(interleave_kernel, grid=(length // step,), in_specs=[pl.Bl...]
  transfers between devices with their start and end apart: 23 -> 23, of which waited for: 12 -> 12; matrix products, arithmetic and copies ran while one was open for 0% -> 0% of each run, Pallas kernels for 11% -> 9%
where the time goes in v11:
time: 101 us
  Pallas kernels  31.6 us (31%)
  blocking collectives  30.4 us (30%)
  starting transfers between devices  23.3 us (23%)
  waiting for transfers between devices  14.4 us (14%)
    all_to_all x1, blocking collectives, per_device_fast(): moved = lax.all_to_all(rows, 'dap', split_axis=0, concat_axis=0, tiled=True)  30.4 us
    ppermute x23, starting transfers between devices, exchange(): return lax.ppermute(block, 'dap', [(i, i ^ offset) for i in range(count)])  23.3 us
    ppermute x23, waiting for transfers between devices, exchange(): return lax.ppermute(block, 'dap', [(i, i ^ offset) for i in range(count)])  14.4 us
    pallas_call x1, Pallas kernels, column_attend(): pl.pallas_call(functools.partial(column_kernel, items), in_specs=[pl.Bloc...  8.07 us
    pallas_call x1, Pallas kernels, row_attend(): pl.pallas_call(functools.partial(row_attend_kernel, plan, step, seqs), gr...  7.84 us
    pallas_call x1, Pallas kernels, row_project(): pl.pallas_call(row_project_kernel, grid=(seqs // step,), in_specs=[block,...  5.58 us
    pallas_call x2, Pallas kernels, outer_product(): pl.pallas_call(functools.partial(outer_kernel, group, outer, items), out_...  5.2 us
  transfers between devices with their start and end apart: 23, of which 12 were waited for; matrix products, arithmetic and copies ran while one was open for 0% of the time, Pallas kernels for 9%

profile of v11, /device:TPU:0, one launch (start us, length us, event | category | flops | bytes accessed | tf_op | source)
XLA Modules:
  0.0 101.0 jit_solution(6311224743268640207)
XLA Ops:
  0.6 1.8 %pair_bias.1 = bf16[64,256]{1,0:T(8,128)(2,1)S(1)} custom-call(bf16[8,256,128]{2,1,0:T(8,128)(2,1)} %pair_ref.3, bf16[8,128]{1,0:T(8,128)(2,1)} %bitcast.12), custom_call_target="tpu_custom_call" | custom-call | tf_op jit(solution)/shard_map/pair_bias/pallas_call | solution.py:278
  2.4 3.1 %collective-permute-start = (bf16[64,256]{1,0:T(8,128)(2,1)S(1)}, bf16[64,256]{1,0:T(8,128)(2,1)S(1)}, u32[]{:S(2)}, u32[]{:S(2)}) collective-permute-start(bf16[64,256]{1,0:T(8,128)(2,1)S(1)} %pair_bias.1), channel_id=1, source_target_pairs={{0,8},{1,9},{2,10},{3,11},{4,12},{5,13},{6,14},{7,15},{8,0},{9,1},... | collective-permute-start | bytes 98312 | tf_op jit(solution)/shard_map/ppermute | solution.py:549
  5.5 2.6 %collective-permute-start.1 = (bf16[64,256]{1,0:T(8,128)(2,1)S(1)}, bf16[64,256]{1,0:T(8,128)(2,1)S(1)}, u32[]{:S(2)}, u32[]{:S(2)}) collective-permute-start(bf16[64,256]{1,0:T(8,128)(2,1)S(1)} %pair_bias.1), channel_id=1, source_target_pairs={{0,16},{1,17},{2,18},{3,19},{4,20},{5,21},{6,22},{7,23},{8,24},{9,... | collective-permute-start | bytes 98312 | tf_op jit(solution)/shard_map/ppermute | solution.py:549
  8.1 5.6 %row_project.1 = (bf16[8,256,256]{2,1,0:T(8,128)(2,1)}, bf16[8,256,256]{2,1,0:T(8,128)(2,1)}, bf16[8,256,256]{2,1,0:T(8,128)(2,1)}, f32[8,256,256]{2,1,0:T(8,128)}) custom-call(bf16[8,256,256]{2,1,0:T(8,128)(2,1)} %x_ref.3, bf16[4,256,256]{2,1,0:T(8,128)(2,1)} %weight_ref.2), custom_call_target="tpu_custom_call" | custom-call | tf_op jit(solution)/shard_map/row_project/pallas_call | solution.py:300
  13.8 1.7 %collective-permute-start.3 = (bf16[4,64,256]{2,1,0:T(8,128)(2,1)S(1)}, bf16[4,64,256]{2,1,0:T(8,128)(2,1)S(1)}, u32[]{:S(2)}, u32[]{:S(2)}) collective-permute-start(bf16[4,64,256]{2,1,0:T(8,128)(2,1)S(1)} %pad_maximum_fusion.rest_0_), channel_id=1, source_target_pairs={{0,2},{1,3},{2,0},{3,1},{4,6},{5,7},{6,4},{7,5},{8,10},{9,11},{10,... | collective-permute-start | bytes 393224 | tf_op jit(solution)/shard_map/ppermute | solution.py:549
  15.5 1.5 %collective-permute-start.4 = (bf16[4,64,256]{2,1,0:T(8,128)(2,1)S(1)}, bf16[4,64,256]{2,1,0:T(8,128)(2,1)S(1)}, u32[]{:S(2)}, u32[]{:S(2)}) collective-permute-start(bf16[4,64,256]{2,1,0:T(8,128)(2,1)S(1)} %pad_maximum_fusion.rest_0_), channel_id=1, source_target_pairs={{0,4},{1,5},{2,6},{3,7},{4,0},{5,1},{6,2},{7,3},{8,12},{9,13},{10,... | collective-permute-start | bytes 393224 | tf_op jit(solution)/shard_map/ppermute | solution.py:549
  17.1 0.3 collective-permute-start.5
  17.4 2.3 %collective-permute-done.3.rest_1_ = bf16[4,64,256]{2,1,0:T(8,128)(2,1)S(1)} collective-permute-done((bf16[4,64,256]{2,1,0:T(8,128)(2,1)S(1)}, bf16[4,64,256]{2,1,0:T(8,128)(2,1)S(1)}, u32[]{:S(2)}, u32[]{:S(2)}) %collective-permute-start.3) | collective-permute-done | bytes 131104 | tf_op jit(solution)/shard_map/ppermute | solution.py:549
  19.7 3.5 %collective-permute-done.4.rest_2_ = bf16[4,64,256]{2,1,0:T(8,128)(2,1)S(1)} collective-permute-done((bf16[4,64,256]{2,1,0:T(8,128)(2,1)S(1)}, bf16[4,64,256]{2,1,0:T(8,128)(2,1)S(1)}, u32[]{:S(2)}, u32[]{:S(2)}) %collective-permute-start.4) | collective-permute-done | bytes 131104 | tf_op jit(solution)/shard_map/ppermute | solution.py:549
  23.3 0.5 collective-permute-start.9
  23.8 0.8 collective-permute-done.8.rest_6_
  24.8 7.8 %row_attend.1 = bf16[32,64,256]{2,1,0:T(8,128)(2,1)S(1)} custom-call(s32[1]{0:T(128)} %bitcast.me_ref, bf16[8,256,256]{2,1,0:T(8,128)(2,1)} %x_ref.3, bf16[8,256,256]{2,1,0:T(8,128)(2,1)} %get-tuple-element.27.q_ref, bf16[8,256,256]{2,1,0:T(8,128)(2,1)} %get-tuple-element.28.k_ref, bf16[8,256,256]{2,1,0:T(8,128)(2,1)} %get-tuple-element.29.v_ref, ...), custom_call_target="tpu_custom_call" | custom-call | tf_op jit(solution)/shard_map/row_attend/pallas_call | solution.py:353
  32.7 30.4 %all_to_all.5.x_ref = bf16[32,64,256]{2,1,0:T(8,128)(2,1)S(1)} all-to-all(bf16[32,64,256]{2,1,0:T(8,128)(2,1)S(1)} %row_attend.1), channel_id=1, replica_groups=mesh['branch'=1,'dap'=32] {'dap'}, dimensions={0} | all-to-all | bytes 2097152 | tf_op jit(solution)/shard_map/all_to_all | solution.py:585
  63.1 8.1 %column_attend.1 = (bf16[8,256,256]{2,1,0:T(8,128)(2,1)S(1)}, bf16[256,256]{1,0:T(8,128)(2,1)S(1)}, bf16[256,256]{1,0:T(8,128)(2,1)S(1)}) custom-call(s32[1]{0:T(128)} %bitcast.me_ref, bf16[32,64,256]{2,1,0:T(8,128)(2,1)S(1)} %all_to_all.5.x_ref, s32[256,256]{1,0:T(8,128)S(1)} %copy-done.1, bf16[4,256,256]{2,1,0:T(8,128)(2,1)S(1)} %copy-done.3, ...), custom_call_target="tpu_custom_call" | custom-call | tf_op jit(solution)/shard_map/column_attend/pallas_call | solution.py:421
  71.2 0.8 collective-permute-start.10
  72.0 1.1 %collective-permute-start.11 = (bf16[256,256]{1,0:T(8,128)(2,1)S(1)}, bf16[256,256]{1,0:T(8,128)(2,1)S(1)}, u32[]{:S(2)}, u32[]{:S(2)}) collective-permute-start(bf16[256,256]{1,0:T(8,128)(2,1)S(1)} %get-tuple-element.43.refs_1_.refs_3_), channel_id=1, source_target_pairs={{0,16},{1,17},{2,18},{3,19},{4,20},{5,21},{6,22},{7,23},{8,24},{9,... | collective-permute-start | bytes 393224 | tf_op jit(solution)/shard_map/ppermute | solution.py:549
  73.1 2.5 %collective-permute-start.12 = (bf16[256,256]{1,0:T(8,128)(2,1)S(1)}, bf16[256,256]{1,0:T(8,128)(2,1)S(1)}, u32[]{:S(2)}, u32[]{:S(2)}) collective-permute-start(bf16[256,256]{1,0:T(8,128)(2,1)S(1)} %get-tuple-element.43.refs_1_.refs_3_), channel_id=1, source_target_pairs={{0,24},{1,25},{2,26},{3,27},{4,28},{5,29},{6,30},{7,31},{8,16},{9,... | collective-permute-start | bytes 393224 | tf_op jit(solution)/shard_map/ppermute | solution.py:549
  75.7 1.5 %collective-permute-start.17 = (bf16[256,256]{1,0:T(8,128)(2,1)S(1)}, bf16[256,256]{1,0:T(8,128)(2,1)S(1)}, u32[]{:S(2)}, u32[]{:S(2)}) collective-permute-start(bf16[256,256]{1,0:T(8,128)(2,1)S(1)} %get-tuple-element.42.refs_0_), channel_id=1, source_target_pairs={{0,2},{1,3},{2,0},{3,1},{4,6},{5,7},{6,4},{7,5},{8,10},{9,11},{10,... | collective-permute-start | bytes 393224 | tf_op jit(solution)/shard_map/ppermute | solution.py:549
  77.1 1.5 %collective-permute-start.18 = (bf16[256,256]{1,0:T(8,128)(2,1)S(1)}, bf16[256,256]{1,0:T(8,128)(2,1)S(1)}, u32[]{:S(2)}, u32[]{:S(2)}) collective-permute-start(bf16[256,256]{1,0:T(8,128)(2,1)S(1)} %get-tuple-element.42.refs_0_), channel_id=1, source_target_pairs={{0,4},{1,5},{2,6},{3,7},{4,0},{5,1},{6,2},{7,3},{8,12},{9,13},{10,... | collective-permute-start | bytes 393224 | tf_op jit(solution)/shard_map/ppermute | solution.py:549
  78.6 1.6 %collective-permute-start.19 = (bf16[256,256]{1,0:T(8,128)(2,1)S(1)}, bf16[256,256]{1,0:T(8,128)(2,1)S(1)}, u32[]{:S(2)}, u32[]{:S(2)}) collective-permute-start(bf16[256,256]{1,0:T(8,128)(2,1)S(1)} %get-tuple-element.42.refs_0_), channel_id=1, source_target_pairs={{0,6},{1,7},{2,4},{3,5},{4,2},{5,3},{6,0},{7,1},{8,14},{9,15},{10,... | collective-permute-start | bytes 393224 | tf_op jit(solution)/shard_map/ppermute | solution.py:549
  80.2 1.9 %interleave.1 = bf16[256,8,256]{2,1,0:T(8,128)(2,1)} custom-call(bf16[8,256,256]{2,1,0:T(8,128)(2,1)S(1)} %get-tuple-element.39.rows_ref), custom_call_target="tpu_custom_call" | custom-call | tf_op jit(solution)/shard_map/interleave/pallas_call | solution.py:443
  82.1 2.8 %collective-permute-done.11.refs_5_.refs_7_ = bf16[256,256]{1,0:T(8,128)(2,1)S(1)} collective-permute-done((bf16[256,256]{1,0:T(8,128)(2,1)S(1)}, bf16[256,256]{1,0:T(8,128)(2,1)S(1)}, u32[]{:S(2)}, u32[]{:S(2)}) %collective-permute-start.11) | collective-permute-done | bytes 131104 | tf_op jit(solution)/shard_map/ppermute | solution.py:549
  84.9 0.5 collective-permute-start.14
  85.4 0.5 collective-permute-start.16
  87.0 3.6 %outer_product.3 = (bf16[8,64,128]{2,1,0:T(8,128)(2,1)S(1)}, bf16[8,64,128]{2,1,0:T(8,128)(2,1)S(1)}, bf16[8,64,128]{2,1,0:T(8,128)(2,1)S(1)}) custom-call(bf16[256,256]{1,0:T(8,128)(2,1)S(1)} %collective-permute-done.17.refs_0_, bf16[256,256]{1,0:T(8,128)(2,1)S(1)} %collective-permute-done.18.refs_1_, bf16[256,256]{1,0:T(8,128)(2,1)S(1)} %collective-permute-done.19.refs_2_, ...), custom_call_target="tpu_custom_call" | custom-call | tf_op jit(solution)/shard_map/outer_product/pallas_call | solution.py:501
  90.6 0.9 collective-permute-start.20
  91.5 1.4 %collective-permute-start.21 = (bf16[8,64,128]{2,1,0:T(8,128)(2,1)S(1)}, bf16[8,64,128]{2,1,0:T(8,128)(2,1)S(1)}, u32[]{:S(2)}, u32[]{:S(2)}) collective-permute-start(bf16[8,64,128]{2,1,0:T(8,128)(2,1)S(1)} %get-tuple-element.48), channel_id=1, source_target_pairs={{0,4},{1,5},{2,6},{3,7},{4,0},{5,1},{6,2},{7,3},{8,12},{9,13},{10,... | collective-permute-start | bytes 393224 | tf_op jit(solution)/shard_map/ppermute | solution.py:549
  92.9 1.3 %collective-permute-start.22 = (bf16[8,64,128]{2,1,0:T(8,128)(2,1)S(1)}, bf16[8,64,128]{2,1,0:T(8,128)(2,1)S(1)}, u32[]{:S(2)}, u32[]{:S(2)}) collective-permute-start(bf16[8,64,128]{2,1,0:T(8,128)(2,1)S(1)} %get-tuple-element.49), channel_id=1, source_target_pairs={{0,6},{1,7},{2,4},{3,5},{4,2},{5,3},{6,0},{7,1},{8,14},{9,15},{10,... | collective-permute-start | bytes 393224 | tf_op jit(solution)/shard_map/ppermute | solution.py:549
  94.5 1.6 %outer_product.2.refs_0_ = bf16[8,64,128]{2,1,0:T(8,128)(2,1)S(1)} custom-call(bf16[256,256]{1,0:T(8,128)(2,1)S(1)} %get-tuple-element.42.refs_0_, bf16[256,256]{1,0:T(8,128)(2,1)S(1)} %get-tuple-element.43.refs_1_.refs_3_, bf16[256,256]{1,0:T(8,128)(2,1)S(1)} %collective-permute-done.13.refs_2_.refs_4_, ...), custom_call_target="tpu_custom_call" | custom-call | tf_op jit(solution)/shard_map/outer_product/pallas_call | solution.py:501
  96.0 1.0 collective-permute-done.20.refs_1_
  97.0 2.7 %collective-permute-done.21.refs_2_ = bf16[8,64,128]{2,1,0:T(8,128)(2,1)S(1)} collective-permute-done((bf16[8,64,128]{2,1,0:T(8,128)(2,1)S(1)}, bf16[8,64,128]{2,1,0:T(8,128)(2,1)S(1)}, u32[]{:S(2)}, u32[]{:S(2)}) %collective-permute-start.21) | collective-permute-done | bytes 131104 | tf_op jit(solution)/shard_map/ppermute | solution.py:549
  99.7 1.3 %finish.1 = bf16[8,256,128]{2,1,0:T(8,128)(2,1)} custom-call(s32[1]{0:T(128)} %bitcast.me_ref, bf16[8,256,128]{2,1,0:T(8,128)(2,1)S(1)} %copy-done, f32[256,8]{1,0:T(8,128)S(1)} %fusion.scale_ref, bf16[8,64,128]{2,1,0:T(8,128)(2,1)S(1)} %outer_product.2.refs_0_, bf16[8,64,128]{2,1,0:T(8,128)(2,1)S(1)} %collective-permute-done.20.refs_1_, ...), custom_call_target="tpu_custom_call" | custom-call | tf_op jit(solution)/shard_map/finish/pallas_call | solution.py:536
  (41 shorter events, 1.7 us)
Async XLA Ops:
  2.4 11.3 %collective-permute-start = (bf16[64,256]{1,0:T(8,128)(2,1)S(1)}, bf16[64,256]{1,0:T(8,128)(2,1)S(1)}, u32[]{:S(2)}, u32[]{:S(2)}) collective-permute-start(bf16[64,256]{1,0:T(8,128)(2,1)S(1)} %pair_bias.1), channel_id=1, source_target_pairs={{0,8},{1,9},{2,10},{3,11},{4,12},{5,13},{6,14},{7,15},{8,0},{9,1},... | collective-permute-start | bytes 98312 | tf_op jit(solution)/shard_map/ppermute | solution.py:549
  5.5 8.2 %collective-permute-start.1 = (bf16[64,256]{1,0:T(8,128)(2,1)S(1)}, bf16[64,256]{1,0:T(8,128)(2,1)S(1)}, u32[]{:S(2)}, u32[]{:S(2)}) collective-permute-start(bf16[64,256]{1,0:T(8,128)(2,1)S(1)} %pair_bias.1), channel_id=1, source_target_pairs={{0,16},{1,17},{2,18},{3,19},{4,20},{5,21},{6,22},{7,23},{8,24},{9,... | collective-permute-start | bytes 98312 | tf_op jit(solution)/shard_map/ppermute | solution.py:549
  8.1 5.7 %collective-permute-start.2 = (bf16[64,256]{1,0:T(8,128)(2,1)S(1)}, bf16[64,256]{1,0:T(8,128)(2,1)S(1)}, u32[]{:S(2)}, u32[]{:S(2)}) collective-permute-start(bf16[64,256]{1,0:T(8,128)(2,1)S(1)} %pair_bias.1), channel_id=1, source_target_pairs={{0,24},{1,25},{2,26},{3,27},{4,28},{5,29},{6,30},{7,31},{8,16},{9,... | collective-permute-start | bytes 98312 | tf_op jit(solution)/shard_map/ppermute | solution.py:549
  13.8 5.9 %collective-permute-start.3 = (bf16[4,64,256]{2,1,0:T(8,128)(2,1)S(1)}, bf16[4,64,256]{2,1,0:T(8,128)(2,1)S(1)}, u32[]{:S(2)}, u32[]{:S(2)}) collective-permute-start(bf16[4,64,256]{2,1,0:T(8,128)(2,1)S(1)} %pad_maximum_fusion.rest_0_), channel_id=1, source_target_pairs={{0,2},{1,3},{2,0},{3,1},{4,6},{5,7},{6,4},{7,5},{8,10},{9,11},{10,... | collective-permute-start | bytes 393224 | tf_op jit(solution)/shard_map/ppermute | solution.py:549
  15.5 7.7 %collective-permute-start.4 = (bf16[4,64,256]{2,1,0:T(8,128)(2,1)S(1)}, bf16[4,64,256]{2,1,0:T(8,128)(2,1)S(1)}, u32[]{:S(2)}, u32[]{:S(2)}) collective-permute-start(bf16[4,64,256]{2,1,0:T(8,128)(2,1)S(1)} %pad_maximum_fusion.rest_0_), channel_id=1, source_target_pairs={{0,4},{1,5},{2,6},{3,7},{4,0},{5,1},{6,2},{7,3},{8,12},{9,13},{10,... | collective-permute-start | bytes 393224 | tf_op jit(solution)/shard_map/ppermute | solution.py:549
  17.1 6.2 %collective-permute-start.5 = (bf16[4,64,256]{2,1,0:T(8,128)(2,1)S(1)}, bf16[4,64,256]{2,1,0:T(8,128)(2,1)S(1)}, u32[]{:S(2)}, u32[]{:S(2)}) collective-permute-start(bf16[4,64,256]{2,1,0:T(8,128)(2,1)S(1)} %pad_maximum_fusion.rest_0_), channel_id=1, source_target_pairs={{0,6},{1,7},{2,4},{3,5},{4,2},{5,3},{6,0},{7,1},{8,14},{9,15},{10,... | collective-permute-start | bytes 393224 | tf_op jit(solution)/shard_map/ppermute | solution.py:549
  17.4 6.4 %collective-permute-start.6 = (bf16[4,64,256]{2,1,0:T(8,128)(2,1)S(1)}, bf16[4,64,256]{2,1,0:T(8,128)(2,1)S(1)}, u32[]{:S(2)}, u32[]{:S(2)}) collective-permute-start(bf16[4,64,256]{2,1,0:T(8,128)(2,1)S(1)} %pad_maximum_fusion.rest_0_), channel_id=1, source_target_pairs={{0,1},{1,0},{2,3},{3,2},{4,5},{5,4},{6,7},{7,6},{8,9},{9,8},{10,11... | collective-permute-start | bytes 393224 | tf_op jit(solution)/shard_map/ppermute | solution.py:549
  19.7 4.1 %collective-permute-start.7 = (bf16[4,64,256]{2,1,0:T(8,128)(2,1)S(1)}, bf16[4,64,256]{2,1,0:T(8,128)(2,1)S(1)}, u32[]{:S(2)}, u32[]{:S(2)}) collective-permute-start(bf16[4,64,256]{2,1,0:T(8,128)(2,1)S(1)} %collective-permute-done.3.rest_1_), channel_id=1, source_target_pairs={{0,1},{1,0},{2,3},{3,2},{4,5},{5,4},{6,7},{7,6},{8,9},{9,8},{10,11... | collective-permute-start | bytes 393224 | tf_op jit(solution)/shard_map/ppermute | solution.py:549
  23.3 1.3 %collective-permute-start.8 = (bf16[4,64,256]{2,1,0:T(8,128)(2,1)S(1)}, bf16[4,64,256]{2,1,0:T(8,128)(2,1)S(1)}, u32[]{:S(2)}, u32[]{:S(2)}) collective-permute-start(bf16[4,64,256]{2,1,0:T(8,128)(2,1)S(1)} %collective-permute-done.4.rest_2_), channel_id=1, source_target_pairs={{0,1},{1,0},{2,3},{3,2},{4,5},{5,4},{6,7},{7,6},{8,9},{9,8},{10,11... | collective-permute-start | bytes 393224 | tf_op jit(solution)/shard_map/ppermute | solution.py:549
  23.3 1.5 %collective-permute-start.9 = (bf16[4,64,256]{2,1,0:T(8,128)(2,1)S(1)}, bf16[4,64,256]{2,1,0:T(8,128)(2,1)S(1)}, u32[]{:S(2)}, u32[]{:S(2)}) collective-permute-start(bf16[4,64,256]{2,1,0:T(8,128)(2,1)S(1)} %collective-permute-done.5.rest_3_), channel_id=1, source_target_pairs={{0,1},{1,0},{2,3},{3,2},{4,5},{5,4},{6,7},{7,6},{8,9},{9,8},{10,11... | collective-permute-start | bytes 393224 | tf_op jit(solution)/shard_map/ppermute | solution.py:549
  32.7 30.4 %copy-start.1 = (s32[256,256]{1,0:T(8,128)S(1)}, s32[256,256]{1,0:T(8,128)}, u32[]{:S(2)}) copy-start(s32[256,256]{1,0:T(8,128)} %mask_ref.3) | copy-start | bytes 786436
  32.7 30.4 %copy-start.3 = (bf16[4,256,256]{2,1,0:T(8,128)(2,1)S(1)}, bf16[4,256,256]{2,1,0:T(8,128)(2,1)}, u32[]{:S(2)}) copy-start(bf16[4,256,256]{2,1,0:T(8,128)(2,1)} %weight_ref.3) | copy-start | bytes 1572868
  32.7 30.4 %copy-start.4 = (bf16[256,256]{1,0:T(8,128)(2,1)S(1)}, bf16[256,256]{1,0:T(8,128)(2,1)}, u32[]{:S(2)}) copy-start(bf16[256,256]{1,0:T(8,128)(2,1)} %out_w_ref.3) | copy-start | bytes 393220
  32.7 30.4 %copy-start.5 = (bf16[256,64]{0,1:T(8,128)(2,1)S(1)}, bf16[256,64]{0,1:T(8,128)(2,1)}, u32[]{:S(2)}) copy-start(bf16[256,64]{0,1:T(8,128)(2,1)} %param.20) | copy-start | bytes 98308
  63.1 22.9 %copy-start.6 = (s32[256]{0:T(256)S(1)}, s32[256]{0:T(256)}, u32[]{:S(2)}) copy-start(s32[256]{0:T(256)} %param.14) | copy-start | bytes 3076
  63.1 23.9 %copy-start.2 = (bf16[1024,128]{1,0:T(8,128)(2,1)S(1)}, bf16[1024,128]{1,0:T(8,128)(2,1)}, u32[]{:S(2)}) copy-start(bf16[1024,128]{1,0:T(8,128)(2,1)} %refs_11_.1) | copy-start | bytes 786436
  71.2 7.4 %collective-permute-start.10 = (bf16[256,256]{1,0:T(8,128)(2,1)S(1)}, bf16[256,256]{1,0:T(8,128)(2,1)S(1)}, u32[]{:S(2)}, u32[]{:S(2)}) collective-permute-start(bf16[256,256]{1,0:T(8,128)(2,1)S(1)} %get-tuple-element.43.refs_1_.refs_3_), channel_id=1, source_target_pairs={{0,8},{1,9},{2,10},{3,11},{4,12},{5,13},{6,14},{7,15},{8,0},{9,1},... | collective-permute-start | bytes 393224 | tf_op jit(solution)/shard_map/ppermute | solution.py:549
  72.0 12.9 %collective-permute-start.11 = (bf16[256,256]{1,0:T(8,128)(2,1)S(1)}, bf16[256,256]{1,0:T(8,128)(2,1)S(1)}, u32[]{:S(2)}, u32[]{:S(2)}) collective-permute-start(bf16[256,256]{1,0:T(8,128)(2,1)S(1)} %get-tuple-element.43.refs_1_.refs_3_), channel_id=1, source_target_pairs={{0,16},{1,17},{2,18},{3,19},{4,20},{5,21},{6,22},{7,23},{8,24},{9,... | collective-permute-start | bytes 393224 | tf_op jit(solution)/shard_map/ppermute | solution.py:549
  73.1 11.8 %collective-permute-start.12 = (bf16[256,256]{1,0:T(8,128)(2,1)S(1)}, bf16[256,256]{1,0:T(8,128)(2,1)S(1)}, u32[]{:S(2)}, u32[]{:S(2)}) collective-permute-start(bf16[256,256]{1,0:T(8,128)(2,1)S(1)} %get-tuple-element.43.refs_1_.refs_3_), channel_id=1, source_target_pairs={{0,24},{1,25},{2,26},{3,27},{4,28},{5,29},{6,30},{7,31},{8,16},{9,... | collective-permute-start | bytes 393224 | tf_op jit(solution)/shard_map/ppermute | solution.py:549
  75.7 9.8 %collective-permute-start.17 = (bf16[256,256]{1,0:T(8,128)(2,1)S(1)}, bf16[256,256]{1,0:T(8,128)(2,1)S(1)}, u32[]{:S(2)}, u32[]{:S(2)}) collective-permute-start(bf16[256,256]{1,0:T(8,128)(2,1)S(1)} %get-tuple-element.42.refs_0_), channel_id=1, source_target_pairs={{0,2},{1,3},{2,0},{3,1},{4,6},{5,7},{6,4},{7,5},{8,10},{9,11},{10,... | collective-permute-start | bytes 393224 | tf_op jit(solution)/shard_map/ppermute | solution.py:549
  77.1 8.3 %collective-permute-start.18 = (bf16[256,256]{1,0:T(8,128)(2,1)S(1)}, bf16[256,256]{1,0:T(8,128)(2,1)S(1)}, u32[]{:S(2)}, u32[]{:S(2)}) collective-permute-start(bf16[256,256]{1,0:T(8,128)(2,1)S(1)} %get-tuple-element.42.refs_0_), channel_id=1, source_target_pairs={{0,4},{1,5},{2,6},{3,7},{4,0},{5,1},{6,2},{7,3},{8,12},{9,13},{10,... | collective-permute-start | bytes 393224 | tf_op jit(solution)/shard_map/ppermute | solution.py:549
  78.6 7.4 %collective-permute-start.19 = (bf16[256,256]{1,0:T(8,128)(2,1)S(1)}, bf16[256,256]{1,0:T(8,128)(2,1)S(1)}, u32[]{:S(2)}, u32[]{:S(2)}) collective-permute-start(bf16[256,256]{1,0:T(8,128)(2,1)S(1)} %get-tuple-element.42.refs_0_), channel_id=1, source_target_pairs={{0,6},{1,7},{2,4},{3,5},{4,2},{5,3},{6,0},{7,1},{8,14},{9,15},{10,... | collective-permute-start | bytes 393224 | tf_op jit(solution)/shard_map/ppermute | solution.py:549
  82.1 17.6 %copy-start = (bf16[8,256,128]{2,1,0:T(8,128)(2,1)S(1)}, bf16[8,256,128]{2,1,0:T(8,128)(2,1)}, u32[]{:S(2)}) copy-start(bf16[8,256,128]{2,1,0:T(8,128)(2,1)} %pair_ref.3) | copy-start | bytes 1572868
  84.9 1.3 %collective-permute-start.13 = (bf16[256,256]{1,0:T(8,128)(2,1)S(1)}, bf16[256,256]{1,0:T(8,128)(2,1)S(1)}, u32[]{:S(2)}, u32[]{:S(2)}) collective-permute-start(bf16[256,256]{1,0:T(8,128)(2,1)S(1)} %get-tuple-element.43.refs_1_.refs_3_), channel_id=1, source_target_pairs={{0,1},{1,0},{2,3},{3,2},{4,5},{5,4},{6,7},{7,6},{8,9},{9,8},{10,11... | collective-permute-start | bytes 393224 | tf_op jit(solution)/shard_map/ppermute | solution.py:549
  84.9 1.5 %collective-permute-start.14 = (bf16[256,256]{1,0:T(8,128)(2,1)S(1)}, bf16[256,256]{1,0:T(8,128)(2,1)S(1)}, u32[]{:S(2)}, u32[]{:S(2)}) collective-permute-start(bf16[256,256]{1,0:T(8,128)(2,1)S(1)} %collective-permute-done.10.refs_3_.refs_5_), channel_id=1, source_target_pairs={{0,1},{1,0},{2,3},{3,2},{4,5},{5,4},{6,7},{7,6},{8,9},{9,8},{10,11... | collective-permute-start | bytes 393224 | tf_op jit(solution)/shard_map/ppermute | solution.py:549
  85.4 1.3 %collective-permute-start.15 = (bf16[256,256]{1,0:T(8,128)(2,1)S(1)}, bf16[256,256]{1,0:T(8,128)(2,1)S(1)}, u32[]{:S(2)}, u32[]{:S(2)}) collective-permute-start(bf16[256,256]{1,0:T(8,128)(2,1)S(1)} %collective-permute-done.11.refs_5_.refs_7_), channel_id=1, source_target_pairs={{0,1},{1,0},{2,3},{3,2},{4,5},{5,4},{6,7},{7,6},{8,9},{9,8},{10,11... | collective-permute-start | bytes 393224 | tf_op jit(solution)/shard_map/ppermute | solution.py:549
  85.4 1.5 %collective-permute-start.16 = (bf16[256,256]{1,0:T(8,128)(2,1)S(1)}, bf16[256,256]{1,0:T(8,128)(2,1)S(1)}, u32[]{:S(2)}, u32[]{:S(2)}) collective-permute-start(bf16[256,256]{1,0:T(8,128)(2,1)S(1)} %collective-permute-done.12.refs_7_.refs_9_), channel_id=1, source_target_pairs={{0,1},{1,0},{2,3},{3,2},{4,5},{5,4},{6,7},{7,6},{8,9},{9,8},{10,11... | collective-permute-start | bytes 393224 | tf_op jit(solution)/shard_map/ppermute | solution.py:549
  90.6 6.4 %collective-permute-start.20 = (bf16[8,64,128]{2,1,0:T(8,128)(2,1)S(1)}, bf16[8,64,128]{2,1,0:T(8,128)(2,1)S(1)}, u32[]{:S(2)}, u32[]{:S(2)}) collective-permute-start(bf16[8,64,128]{2,1,0:T(8,128)(2,1)S(1)} %get-tuple-element.47), channel_id=1, source_target_pairs={{0,2},{1,3},{2,0},{3,1},{4,6},{5,7},{6,4},{7,5},{8,10},{9,11},{10,... | collective-permute-start | bytes 393224 | tf_op jit(solution)/shard_map/ppermute | solution.py:549
  91.5 8.3 %collective-permute-start.21 = (bf16[8,64,128]{2,1,0:T(8,128)(2,1)S(1)}, bf16[8,64,128]{2,1,0:T(8,128)(2,1)S(1)}, u32[]{:S(2)}, u32[]{:S(2)}) collective-permute-start(bf16[8,64,128]{2,1,0:T(8,128)(2,1)S(1)} %get-tuple-element.48), channel_id=1, source_target_pairs={{0,4},{1,5},{2,6},{3,7},{4,0},{5,1},{6,2},{7,3},{8,12},{9,13},{10,... | collective-permute-start | bytes 393224 | tf_op jit(solution)/shard_map/ppermute | solution.py:549
  92.9 6.9 %collective-permute-start.22 = (bf16[8,64,128]{2,1,0:T(8,128)(2,1)S(1)}, bf16[8,64,128]{2,1,0:T(8,128)(2,1)S(1)}, u32[]{:S(2)}, u32[]{:S(2)}) collective-permute-start(bf16[8,64,128]{2,1,0:T(8,128)(2,1)S(1)} %get-tuple-element.49), channel_id=1, source_target_pairs={{0,6},{1,7},{2,4},{3,5},{4,2},{5,3},{6,0},{7,1},{8,14},{9,15},{10,... | collective-permute-start | bytes 393224 | tf_op jit(solution)/shard_map/ppermute | solution.py:549

commit v12 on v11

--- a/solution.py
+++ b/solution.py
@@ -335,10 +335,11 @@
             own, spot, (((0,), (0,)), ((), ())), preferred_element_type=F32
         ).astype(BF16)
         items.append((q_ref[s], k_ref[s], v_ref[s], live))
+    heads = attend_all(items, lanes, lambda h: bias_all[h])
+    gated = [(heads[s] * g_ref[s]).astype(BF16) for s in range(step)]
     results = []
-    for s, heads_out in enumerate(attend_all(items, lanes, lambda h: bias_all[h])):
-        heads_out = (heads_out * g_ref[s]).astype(BF16)
-        total = x_ref[s].astype(F32) + nn_dot(heads_out, out_w_ref[...])
+    for s in range(step):
+        total = x_ref[s].astype(F32) + nn_dot(gated[s], out_w_ref[...])
         results.append(total.reshape(parts, 1, rows // step, total.shape[1]))
     joined = jnp.concatenate(results, axis=1)
     out_ref[...] = joined.reshape(out_ref.shape).astype(BF16)
@@ -347,7 +348,7 @@
 def row_attend(me, alignment, projected, mask, out_weight, bias_parts, plan, parts):
     seqs, length, width = alignment.shape
     rows = length // parts
-    step = 2
+    step = 4
     vmem = pl.BlockSpec(memory_space=pltpu.VMEM)
     block = pl.BlockSpec((step, length, width), lambda i: (i, 0, 0))
     return pl.pallas_call(
@@ -360,7 +361,7 @@
         out_specs=pl.BlockSpec((parts, step * rows, width), lambda i: (0, i, 0)),
         out_shape=jax.ShapeDtypeStruct((parts, seqs * rows, width), BF16),
         scratch_shapes=[pltpu.VMEM((ATTN_HEAD_COUNT, length, length), F32)],
-        compiler_params=params(24),
+        compiler_params=params(40),
         name="row_attend",
     )(me, *in_hbm(alignment, *projected, mask, out_weight), *in_vmem(*bias_parts))
 
@@ -458,9 +459,8 @@
     outs = refs[group + outer + 1 : -3]
     weight_rows, weight, held = refs[-3:]
     feat = FACTOR_CHANNELS
-    half = LANES // 2
-    duo = half // feat
-    tiles = items * feat // half
+    quad = LANES // feat
+    tiles = items * feat // LANES
     cols = outer * items
     width = weight_ref.shape[1]
 
@@ -468,42 +468,43 @@
     weight[...] = jnp.zeros_like(weight)
     for e in range(feat):
         block = weight_rows[pl.ds(e, feat, stride=feat), :].astype(BF16)
-        for i in range(duo):
-            start = (e * duo + i) * feat
+        for i in range(quad):
+            start = e * LANES + i * feat
             weight[start : start + feat, i * width : (i + 1) * width] = block
 
     right = jnp.concatenate([r[...] for r in rights], axis=0)
+    def product(k):
+        return nt_dot(right, lefts[k][...])
+
+    later = product(0)
     for k in range(group):
-        sums = nt_dot(right, lefts[k][...])
+        sums, later = later, product(k + 1) if k + 1 < group else None
         sums = sums.reshape(outer, feat, items, sums.shape[1])
         sums = jnp.transpose(sums, (1, 0, 2, 3)).reshape(feat, cols, sums.shape[3]).astype(BF16)
-        for e in range(0, feat, 2):
-            for t in range(tiles):
-                at = slice((k * tiles + t) * cols, (k * tiles + t + 1) * cols)
-                cut = slice(t * half, (t + 1) * half)
-                both = jnp.concatenate([sums[e, :, cut], sums[e + 1, :, cut]], axis=1)
-                held[at, e * half : (e + 2) * half] = both
+        for t in range(tiles):
+            at = slice((k * tiles + t) * cols, (k * tiles + t + 1) * cols)
+            for e in range(feat):
+                held[at, e * LANES : (e + 1) * LANES] = sums[e, :, t * LANES : (t + 1) * LANES]
     update = nn_dot(held[...], weight[...])
     for k in range(group):
         for t in range(tiles):
             rows = update[(k * tiles + t) * cols : (k * tiles + t + 1) * cols]
-            for i in range(duo):
-                outs[k][t * duo + i] = rows[:, i * width : (i + 1) * width].astype(BF16)
+            for i in range(quad):
+                outs[k][t * quad + i] = rows[:, i * width : (i + 1) * width].astype(BF16)
 
 
 def outer_product(lefts, rights, weight, items):
     group, outer = len(lefts), len(rights)
     cols = outer * items
-    half = LANES // 2
-    tiles = items * FACTOR_CHANNELS // half
-    depth = FACTOR_CHANNELS * half
+    tiles = items * FACTOR_CHANNELS // LANES
+    depth = FACTOR_CHANNELS * LANES
     width = weight.shape[1]
     return pl.pallas_call(
         functools.partial(outer_kernel, group, outer, items),
         out_shape=[jax.ShapeDtypeStruct((items, cols, width), BF16)] * group,
         scratch_shapes=[
             pltpu.VMEM(weight.shape, F32),
-            pltpu.VMEM((depth, half // FACTOR_CHANNELS * width), BF16),
+            pltpu.VMEM((depth, LANES // FACTOR_CHANNELS * width), BF16),
             pltpu.VMEM((group * tiles * cols, depth), BF16),
         ],
         compiler_params=params(28),
@@ -512,13 +513,14 @@
 
 
 def finish_kernel(offsets, line, me_ref, pair_ref, scale_ref, *refs):
-    parts, out_ref = refs[:-1], refs[-1]
+    parts, (out_ref, done, sems) = refs[:-3], refs[-3:]
     here = me_ref[0]
     items, cols, width = parts[0].shape
     outer = cols // items
     odd = (here & 1) == 1
-    for k, offset in enumerate(offsets):
-        for i in range(items):
+    copies = []
+    for i in range(items):
+        for k, offset in enumerate(offsets):
             both = parts[k][i].astype(F32).reshape(outer // 2, 2, items, width)
             low, high = both[:, 0:1], both[:, 1:2]
             both = jnp.concatenate([jnp.where(odd, high, low), jnp.where(odd, low, high)], axis=1)
@@ -528,7 +530,11 @@
                 start = pl.multiple_of((owner >> 1) * (2 * items), 2 * items)
                 at = pl.ds(start, 2 * items)
                 update = both[z] * scale_ref[at, i : i + 1]
-                out_ref[i, at, :] = (pair_ref[i, at, :].astype(F32) + update).astype(BF16)
+                done[i, at, :] = (pair_ref[i, at, :].astype(F32) + update).astype(BF16)
+        copies.append(pltpu.make_async_copy(done.at[i], out_ref.at[i], sems.at[i]))
+        copies[i].start()
+    for copy in copies:
+        copy.wait()
 
 
 def finish(me, pair_rep, scale, parts, offsets, line):
@@ -536,8 +542,12 @@
     return pl.pallas_call(
         functools.partial(finish_kernel, offsets, line),
         in_specs=[pl.BlockSpec(memory_space=pltpu.SMEM)] + [vmem] * (2 + len(parts)),
-        out_specs=vmem,
-        out_shape=jax.ShapeDtypeStruct(pair_rep.shape, BF16),
+        out_specs=pl.BlockSpec(memory_space=pltpu.HBM),
+        out_shape=pltpu.HBM(pair_rep.shape, BF16),
+        scratch_shapes=[
+            pltpu.VMEM(pair_rep.shape, BF16),
+            pltpu.SemaphoreType.DMA((pair_rep.shape[0],)),
+        ],
         compiler_params=params(16),
         name="finish",
     )(me, pair_rep, scale, *parts)

time: 101 us -> 101 us (level)
  no operation moved by 1% of the time
where the time goes in v12:
time: 101 us; the launch traced here: 100 us
  Pallas kernels  31.1 us (31%)
  blocking collectives  30.4 us (30%)
  starting transfers between devices  23.3 us (23%)
  waiting for transfers between devices  14.1 us (14%)
    all_to_all x1, blocking collectives, per_device_fast(): moved = lax.all_to_all(rows, 'dap', split_axis=0, concat_axis=0, tiled=True)  30.4 us
    ppermute x23, starting transfers between devices, exchange(): return lax.ppermute(block, 'dap', [(i, i ^ offset) for i in range(count)])  23.3 us
    ppermute x23, waiting for transfers between devices, exchange(): return lax.ppermute(block, 'dap', [(i, i ^ offset) for i in range(count)])  14.1 us
    pallas_call x1, Pallas kernels, column_attend(): pl.pallas_call(functools.partial(column_kernel, items), in_specs=[pl.Bloc...  8.07 us
    pallas_call x1, Pallas kernels, row_attend(): pl.pallas_call(functools.partial(row_attend_kernel, plan, step, seqs), gr...  7.88 us
    pallas_call x1, Pallas kernels, row_project(): pl.pallas_call(row_project_kernel, grid=(seqs // step,), in_specs=[block,...  5.58 us
    pallas_call x2, Pallas kernels, outer_product(): pl.pallas_call(functools.partial(outer_kernel, group, outer, items), out_...  4.79 us
  transfers between devices with their start and end apart: 23, of which 12 were waited for; matrix products, arithmetic and copies ran while one was open for 0% of the time, Pallas kernels for 9%

profile of v12, /device:TPU:0, one launch (start us, length us, event | category | flops | bytes accessed | tf_op | source)
XLA Modules:
  0.0 100.3 jit_solution(9176597954404309188)
XLA Ops:
  0.6 1.8 %pair_bias.1 = bf16[64,256]{1,0:T(8,128)(2,1)S(1)} custom-call(bf16[8,256,128]{2,1,0:T(8,128)(2,1)} %pair_ref.3, bf16[8,128]{1,0:T(8,128)(2,1)} %bitcast.12), custom_call_target="tpu_custom_call" | custom-call | tf_op jit(solution)/shard_map/pair_bias/pallas_call | solution.py:278
  2.4 3.1 %collective-permute-start = (bf16[64,256]{1,0:T(8,128)(2,1)S(1)}, bf16[64,256]{1,0:T(8,128)(2,1)S(1)}, u32[]{:S(2)}, u32[]{:S(2)}) collective-permute-start(bf16[64,256]{1,0:T(8,128)(2,1)S(1)} %pair_bias.1), channel_id=1, source_target_pairs={{0,8},{1,9},{2,10},{3,11},{4,12},{5,13},{6,14},{7,15},{8,0},{9,1},... | collective-permute-start | bytes 98312 | tf_op jit(solution)/shard_map/ppermute | solution.py:559
  5.5 2.6 %collective-permute-start.1 = (bf16[64,256]{1,0:T(8,128)(2,1)S(1)}, bf16[64,256]{1,0:T(8,128)(2,1)S(1)}, u32[]{:S(2)}, u32[]{:S(2)}) collective-permute-start(bf16[64,256]{1,0:T(8,128)(2,1)S(1)} %pair_bias.1), channel_id=1, source_target_pairs={{0,16},{1,17},{2,18},{3,19},{4,20},{5,21},{6,22},{7,23},{8,24},{9,... | collective-permute-start | bytes 98312 | tf_op jit(solution)/shard_map/ppermute | solution.py:559
  8.1 5.6 %row_project.1 = (bf16[8,256,256]{2,1,0:T(8,128)(2,1)}, bf16[8,256,256]{2,1,0:T(8,128)(2,1)}, bf16[8,256,256]{2,1,0:T(8,128)(2,1)}, f32[8,256,256]{2,1,0:T(8,128)}) custom-call(bf16[8,256,256]{2,1,0:T(8,128)(2,1)} %x_ref.3, bf16[4,256,256]{2,1,0:T(8,128)(2,1)} %weight_ref.2), custom_call_target="tpu_custom_call" | custom-call | tf_op jit(solution)/shard_map/row_project/pallas_call | solution.py:300
  13.8 1.7 %collective-permute-start.3 = (bf16[4,64,256]{2,1,0:T(8,128)(2,1)S(1)}, bf16[4,64,256]{2,1,0:T(8,128)(2,1)S(1)}, u32[]{:S(2)}, u32[]{:S(2)}) collective-permute-start(bf16[4,64,256]{2,1,0:T(8,128)(2,1)S(1)} %pad_maximum_fusion.rest_0_), channel_id=1, source_target_pairs={{0,2},{1,3},{2,0},{3,1},{4,6},{5,7},{6,4},{7,5},{8,10},{9,11},{10,... | collective-permute-start | bytes 393224 | tf_op jit(solution)/shard_map/ppermute | solution.py:559
  15.5 1.5 %collective-permute-start.4 = (bf16[4,64,256]{2,1,0:T(8,128)(2,1)S(1)}, bf16[4,64,256]{2,1,0:T(8,128)(2,1)S(1)}, u32[]{:S(2)}, u32[]{:S(2)}) collective-permute-start(bf16[4,64,256]{2,1,0:T(8,128)(2,1)S(1)} %pad_maximum_fusion.rest_0_), channel_id=1, source_target_pairs={{0,4},{1,5},{2,6},{3,7},{4,0},{5,1},{6,2},{7,3},{8,12},{9,13},{10,... | collective-permute-start | bytes 393224 | tf_op jit(solution)/shard_map/ppermute | solution.py:559
  17.1 0.3 collective-permute-start.5
  17.4 2.3 %collective-permute-done.3.rest_1_ = bf16[4,64,256]{2,1,0:T(8,128)(2,1)S(1)} collective-permute-done((bf16[4,64,256]{2,1,0:T(8,128)(2,1)S(1)}, bf16[4,64,256]{2,1,0:T(8,128)(2,1)S(1)}, u32[]{:S(2)}, u32[]{:S(2)}) %collective-permute-start.3) | collective-permute-done | bytes 131104 | tf_op jit(solution)/shard_map/ppermute | solution.py:559
  19.7 3.5 %collective-permute-done.4.rest_2_ = bf16[4,64,256]{2,1,0:T(8,128)(2,1)S(1)} collective-permute-done((bf16[4,64,256]{2,1,0:T(8,128)(2,1)S(1)}, bf16[4,64,256]{2,1,0:T(8,128)(2,1)S(1)}, u32[]{:S(2)}, u32[]{:S(2)}) %collective-permute-start.4) | collective-permute-done | bytes 131104 | tf_op jit(solution)/shard_map/ppermute | solution.py:559
  23.3 0.5 collective-permute-start.9
  23.8 0.8 collective-permute-done.8.rest_6_
  24.8 7.9 %row_attend.1 = bf16[32,64,256]{2,1,0:T(8,128)(2,1)S(1)} custom-call(s32[1]{0:T(128)} %bitcast.me_ref, bf16[8,256,256]{2,1,0:T(8,128)(2,1)} %x_ref.3, bf16[8,256,256]{2,1,0:T(8,128)(2,1)} %get-tuple-element.27.q_ref, bf16[8,256,256]{2,1,0:T(8,128)(2,1)} %get-tuple-element.28.k_ref, bf16[8,256,256]{2,1,0:T(8,128)(2,1)} %get-tuple-element.29.v_ref, ...), custom_call_target="tpu_custom_call" | custom-call | tf_op jit(solution)/shard_map/row_attend/pallas_call | solution.py:354
  32.7 30.4 %all_to_all.5.x_ref = bf16[32,64,256]{2,1,0:T(8,128)(2,1)S(1)} all-to-all(bf16[32,64,256]{2,1,0:T(8,128)(2,1)S(1)} %row_attend.1), channel_id=1, replica_groups=mesh['branch'=1,'dap'=32] {'dap'}, dimensions={0} | all-to-all | bytes 2097152 | tf_op jit(solution)/shard_map/all_to_all | solution.py:595
  63.2 8.1 %column_attend.1 = (bf16[8,256,256]{2,1,0:T(8,128)(2,1)S(1)}, bf16[256,256]{1,0:T(8,128)(2,1)S(1)}, bf16[256,256]{1,0:T(8,128)(2,1)S(1)}) custom-call(s32[1]{0:T(128)} %bitcast.me_ref, bf16[32,64,256]{2,1,0:T(8,128)(2,1)S(1)} %all_to_all.5.x_ref, s32[256,256]{1,0:T(8,128)S(1)} %copy-done.1, bf16[4,256,256]{2,1,0:T(8,128)(2,1)S(1)} %copy-done.3, ...), custom_call_target="tpu_custom_call" | custom-call | tf_op jit(solution)/shard_map/column_attend/pallas_call | solution.py:422
  71.2 0.8 collective-permute-start.10
  72.1 1.1 %collective-permute-start.11 = (bf16[256,256]{1,0:T(8,128)(2,1)S(1)}, bf16[256,256]{1,0:T(8,128)(2,1)S(1)}, u32[]{:S(2)}, u32[]{:S(2)}) collective-permute-start(bf16[256,256]{1,0:T(8,128)(2,1)S(1)} %get-tuple-element.43.refs_1_.refs_3_), channel_id=1, source_target_pairs={{0,16},{1,17},{2,18},{3,19},{4,20},{5,21},{6,22},{7,23},{8,24},{9,... | collective-permute-start | bytes 393224 | tf_op jit(solution)/shard_map/ppermute | solution.py:559
  73.2 2.5 %collective-permute-start.12 = (bf16[256,256]{1,0:T(8,128)(2,1)S(1)}, bf16[256,256]{1,0:T(8,128)(2,1)S(1)}, u32[]{:S(2)}, u32[]{:S(2)}) collective-permute-start(bf16[256,256]{1,0:T(8,128)(2,1)S(1)} %get-tuple-element.43.refs_1_.refs_3_), channel_id=1, source_target_pairs={{0,24},{1,25},{2,26},{3,27},{4,28},{5,29},{6,30},{7,31},{8,16},{9,... | collective-permute-start | bytes 393224 | tf_op jit(solution)/shard_map/ppermute | solution.py:559
  75.7 1.5 %collective-permute-start.17 = (bf16[256,256]{1,0:T(8,128)(2,1)S(1)}, bf16[256,256]{1,0:T(8,128)(2,1)S(1)}, u32[]{:S(2)}, u32[]{:S(2)}) collective-permute-start(bf16[256,256]{1,0:T(8,128)(2,1)S(1)} %get-tuple-element.42.refs_0_), channel_id=1, source_target_pairs={{0,2},{1,3},{2,0},{3,1},{4,6},{5,7},{6,4},{7,5},{8,10},{9,11},{10,... | collective-permute-start | bytes 393224 | tf_op jit(solution)/shard_map/ppermute | solution.py:559
  77.2 1.5 %collective-permute-start.18 = (bf16[256,256]{1,0:T(8,128)(2,1)S(1)}, bf16[256,256]{1,0:T(8,128)(2,1)S(1)}, u32[]{:S(2)}, u32[]{:S(2)}) collective-permute-start(bf16[256,256]{1,0:T(8,128)(2,1)S(1)} %get-tuple-element.42.refs_0_), channel_id=1, source_target_pairs={{0,4},{1,5},{2,6},{3,7},{4,0},{5,1},{6,2},{7,3},{8,12},{9,13},{10,... | collective-permute-start | bytes 393224 | tf_op jit(solution)/shard_map/ppermute | solution.py:559
  78.7 1.6 %collective-permute-start.19 = (bf16[256,256]{1,0:T(8,128)(2,1)S(1)}, bf16[256,256]{1,0:T(8,128)(2,1)S(1)}, u32[]{:S(2)}, u32[]{:S(2)}) collective-permute-start(bf16[256,256]{1,0:T(8,128)(2,1)S(1)} %get-tuple-element.42.refs_0_), channel_id=1, source_target_pairs={{0,6},{1,7},{2,4},{3,5},{4,2},{5,3},{6,0},{7,1},{8,14},{9,15},{10,... | collective-permute-start | bytes 393224 | tf_op jit(solution)/shard_map/ppermute | solution.py:559
  80.3 1.9 %interleave.1 = bf16[256,8,256]{2,1,0:T(8,128)(2,1)} custom-call(bf16[8,256,256]{2,1,0:T(8,128)(2,1)S(1)} %get-tuple-element.39.rows_ref), custom_call_target="tpu_custom_call" | custom-call | tf_op jit(solution)/shard_map/interleave/pallas_call | solution.py:444
  82.2 2.8 %collective-permute-done.11.refs_5_.refs_7_ = bf16[256,256]{1,0:T(8,128)(2,1)S(1)} collective-permute-done((bf16[256,256]{1,0:T(8,128)(2,1)S(1)}, bf16[256,256]{1,0:T(8,128)(2,1)S(1)}, u32[]{:S(2)}, u32[]{:S(2)}) %collective-permute-start.11) | collective-permute-done | bytes 131104 | tf_op jit(solution)/shard_map/ppermute | solution.py:559
  85.0 0.5 collective-permute-start.14
  85.5 0.5 collective-permute-start.16
  87.0 2.9 %outer_product.3 = (bf16[8,64,128]{2,1,0:T(8,128)(2,1)S(1)}, bf16[8,64,128]{2,1,0:T(8,128)(2,1)S(1)}, bf16[8,64,128]{2,1,0:T(8,128)(2,1)S(1)}) custom-call(bf16[256,256]{1,0:T(8,128)(2,1)S(1)} %collective-permute-done.17.refs_0_, bf16[256,256]{1,0:T(8,128)(2,1)S(1)} %collective-permute-done.18.refs_1_, bf16[256,256]{1,0:T(8,128)(2,1)S(1)} %collective-permute-done.19.refs_2_, ...), custom_call_target="tpu_custom_call" | custom-call | tf_op jit(solution)/shard_map/outer_product/pallas_call | solution.py:502
  89.9 0.9 collective-permute-start.20
  90.8 1.4 %collective-permute-start.21 = (bf16[8,64,128]{2,1,0:T(8,128)(2,1)S(1)}, bf16[8,64,128]{2,1,0:T(8,128)(2,1)S(1)}, u32[]{:S(2)}, u32[]{:S(2)}) collective-permute-start(bf16[8,64,128]{2,1,0:T(8,128)(2,1)S(1)} %get-tuple-element.48), channel_id=1, source_target_pairs={{0,4},{1,5},{2,6},{3,7},{4,0},{5,1},{6,2},{7,3},{8,12},{9,13},{10,... | collective-permute-start | bytes 393224 | tf_op jit(solution)/shard_map/ppermute | solution.py:559
  92.2 1.3 %collective-permute-start.22 = (bf16[8,64,128]{2,1,0:T(8,128)(2,1)S(1)}, bf16[8,64,128]{2,1,0:T(8,128)(2,1)S(1)}, u32[]{:S(2)}, u32[]{:S(2)}) collective-permute-start(bf16[8,64,128]{2,1,0:T(8,128)(2,1)S(1)} %get-tuple-element.49), channel_id=1, source_target_pairs={{0,6},{1,7},{2,4},{3,5},{4,2},{5,3},{6,0},{7,1},{8,14},{9,15},{10,... | collective-permute-start | bytes 393224 | tf_op jit(solution)/shard_map/ppermute | solution.py:559
  93.7 1.9 %outer_product.2.refs_0_ = bf16[8,64,128]{2,1,0:T(8,128)(2,1)S(1)} custom-call(bf16[256,256]{1,0:T(8,128)(2,1)S(1)} %get-tuple-element.42.refs_0_, bf16[256,256]{1,0:T(8,128)(2,1)S(1)} %get-tuple-element.43.refs_1_.refs_3_, bf16[256,256]{1,0:T(8,128)(2,1)S(1)} %collective-permute-done.13.refs_2_.refs_4_, ...), custom_call_target="tpu_custom_call" | custom-call | tf_op jit(solution)/shard_map/outer_product/pallas_call | solution.py:502
  95.7 0.6 collective-permute-done.20.refs_1_
  96.3 2.7 %collective-permute-done.21.refs_2_ = bf16[8,64,128]{2,1,0:T(8,128)(2,1)S(1)} collective-permute-done((bf16[8,64,128]{2,1,0:T(8,128)(2,1)S(1)}, bf16[8,64,128]{2,1,0:T(8,128)(2,1)S(1)}, u32[]{:S(2)}, u32[]{:S(2)}) %collective-permute-start.21) | collective-permute-done | bytes 131104 | tf_op jit(solution)/shard_map/ppermute | solution.py:559
  99.0 1.1 %finish.1 = bf16[8,256,128]{2,1,0:T(8,128)(2,1)} custom-call(s32[1]{0:T(128)} %bitcast.me_ref, bf16[8,256,128]{2,1,0:T(8,128)(2,1)S(1)} %copy-done, f32[256,8]{1,0:T(8,128)S(1)} %fusion.scale_ref, bf16[8,64,128]{2,1,0:T(8,128)(2,1)S(1)} %outer_product.2.refs_0_, bf16[8,64,128]{2,1,0:T(8,128)(2,1)S(1)} %collective-permute-done.20.refs_1_, ...), custom_call_target="tpu_custom_call" | custom-call | tf_op jit(solution)/shard_map/finish/pallas_call | solution.py:542
  (41 shorter events, 1.7 us)
Async XLA Ops:
  2.4 11.3 %collective-permute-start = (bf16[64,256]{1,0:T(8,128)(2,1)S(1)}, bf16[64,256]{1,0:T(8,128)(2,1)S(1)}, u32[]{:S(2)}, u32[]{:S(2)}) collective-permute-start(bf16[64,256]{1,0:T(8,128)(2,1)S(1)} %pair_bias.1), channel_id=1, source_target_pairs={{0,8},{1,9},{2,10},{3,11},{4,12},{5,13},{6,14},{7,15},{8,0},{9,1},... | collective-permute-start | bytes 98312 | tf_op jit(solution)/shard_map/ppermute | solution.py:559
  5.5 8.2 %collective-permute-start.1 = (bf16[64,256]{1,0:T(8,128)(2,1)S(1)}, bf16[64,256]{1,0:T(8,128)(2,1)S(1)}, u32[]{:S(2)}, u32[]{:S(2)}) collective-permute-start(bf16[64,256]{1,0:T(8,128)(2,1)S(1)} %pair_bias.1), channel_id=1, source_target_pairs={{0,16},{1,17},{2,18},{3,19},{4,20},{5,21},{6,22},{7,23},{8,24},{9,... | collective-permute-start | bytes 98312 | tf_op jit(solution)/shard_map/ppermute | solution.py:559
  8.1 5.7 %collective-permute-start.2 = (bf16[64,256]{1,0:T(8,128)(2,1)S(1)}, bf16[64,256]{1,0:T(8,128)(2,1)S(1)}, u32[]{:S(2)}, u32[]{:S(2)}) collective-permute-start(bf16[64,256]{1,0:T(8,128)(2,1)S(1)} %pair_bias.1), channel_id=1, source_target_pairs={{0,24},{1,25},{2,26},{3,27},{4,28},{5,29},{6,30},{7,31},{8,16},{9,... | collective-permute-start | bytes 98312 | tf_op jit(solution)/shard_map/ppermute | solution.py:559
  13.8 5.9 %collective-permute-start.3 = (bf16[4,64,256]{2,1,0:T(8,128)(2,1)S(1)}, bf16[4,64,256]{2,1,0:T(8,128)(2,1)S(1)}, u32[]{:S(2)}, u32[]{:S(2)}) collective-permute-start(bf16[4,64,256]{2,1,0:T(8,128)(2,1)S(1)} %pad_maximum_fusion.rest_0_), channel_id=1, source_target_pairs={{0,2},{1,3},{2,0},{3,1},{4,6},{5,7},{6,4},{7,5},{8,10},{9,11},{10,... | collective-permute-start | bytes 393224 | tf_op jit(solution)/shard_map/ppermute | solution.py:559
  15.5 7.7 %collective-permute-start.4 = (bf16[4,64,256]{2,1,0:T(8,128)(2,1)S(1)}, bf16[4,64,256]{2,1,0:T(8,128)(2,1)S(1)}, u32[]{:S(2)}, u32[]{:S(2)}) collective-permute-start(bf16[4,64,256]{2,1,0:T(8,128)(2,1)S(1)} %pad_maximum_fusion.rest_0_), channel_id=1, source_target_pairs={{0,4},{1,5},{2,6},{3,7},{4,0},{5,1},{6,2},{7,3},{8,12},{9,13},{10,... | collective-permute-start | bytes 393224 | tf_op jit(solution)/shard_map/ppermute | solution.py:559
  17.1 6.2 %collective-permute-start.5 = (bf16[4,64,256]{2,1,0:T(8,128)(2,1)S(1)}, bf16[4,64,256]{2,1,0:T(8,128)(2,1)S(1)}, u32[]{:S(2)}, u32[]{:S(2)}) collective-permute-start(bf16[4,64,256]{2,1,0:T(8,128)(2,1)S(1)} %pad_maximum_fusion.rest_0_), channel_id=1, source_target_pairs={{0,6},{1,7},{2,4},{3,5},{4,2},{5,3},{6,0},{7,1},{8,14},{9,15},{10,... | collective-permute-start | bytes 393224 | tf_op jit(solution)/shard_map/ppermute | solution.py:559
  17.4 6.4 %collective-permute-start.6 = (bf16[4,64,256]{2,1,0:T(8,128)(2,1)S(1)}, bf16[4,64,256]{2,1,0:T(8,128)(2,1)S(1)}, u32[]{:S(2)}, u32[]{:S(2)}) collective-permute-start(bf16[4,64,256]{2,1,0:T(8,128)(2,1)S(1)} %pad_maximum_fusion.rest_0_), channel_id=1, source_target_pairs={{0,1},{1,0},{2,3},{3,2},{4,5},{5,4},{6,7},{7,6},{8,9},{9,8},{10,11... | collective-permute-start | bytes 393224 | tf_op jit(solution)/shard_map/ppermute | solution.py:559
  19.7 4.1 %collective-permute-start.7 = (bf16[4,64,256]{2,1,0:T(8,128)(2,1)S(1)}, bf16[4,64,256]{2,1,0:T(8,128)(2,1)S(1)}, u32[]{:S(2)}, u32[]{:S(2)}) collective-permute-start(bf16[4,64,256]{2,1,0:T(8,128)(2,1)S(1)} %collective-permute-done.3.rest_1_), channel_id=1, source_target_pairs={{0,1},{1,0},{2,3},{3,2},{4,5},{5,4},{6,7},{7,6},{8,9},{9,8},{10,11... | collective-permute-start | bytes 393224 | tf_op jit(solution)/shard_map/ppermute | solution.py:559
  23.3 1.3 %collective-permute-start.8 = (bf16[4,64,256]{2,1,0:T(8,128)(2,1)S(1)}, bf16[4,64,256]{2,1,0:T(8,128)(2,1)S(1)}, u32[]{:S(2)}, u32[]{:S(2)}) collective-permute-start(bf16[4,64,256]{2,1,0:T(8,128)(2,1)S(1)} %collective-permute-done.4.rest_2_), channel_id=1, source_target_pairs={{0,1},{1,0},{2,3},{3,2},{4,5},{5,4},{6,7},{7,6},{8,9},{9,8},{10,11... | collective-permute-start | bytes 393224 | tf_op jit(solution)/shard_map/ppermute | solution.py:559
  23.3 1.5 %collective-permute-start.9 = (bf16[4,64,256]{2,1,0:T(8,128)(2,1)S(1)}, bf16[4,64,256]{2,1,0:T(8,128)(2,1)S(1)}, u32[]{:S(2)}, u32[]{:S(2)}) collective-permute-start(bf16[4,64,256]{2,1,0:T(8,128)(2,1)S(1)} %collective-permute-done.5.rest_3_), channel_id=1, source_target_pairs={{0,1},{1,0},{2,3},{3,2},{4,5},{5,4},{6,7},{7,6},{8,9},{9,8},{10,11... | collective-permute-start | bytes 393224 | tf_op jit(solution)/shard_map/ppermute | solution.py:559
  32.7 30.4 %copy-start.1 = (s32[256,256]{1,0:T(8,128)S(1)}, s32[256,256]{1,0:T(8,128)}, u32[]{:S(2)}) copy-start(s32[256,256]{1,0:T(8,128)} %mask_ref.3) | copy-start | bytes 786436
  32.7 30.4 %copy-start.3 = (bf16[4,256,256]{2,1,0:T(8,128)(2,1)S(1)}, bf16[4,256,256]{2,1,0:T(8,128)(2,1)}, u32[]{:S(2)}) copy-start(bf16[4,256,256]{2,1,0:T(8,128)(2,1)} %weight_ref.3) | copy-start | bytes 1572868
  32.7 30.4 %copy-start.4 = (bf16[256,256]{1,0:T(8,128)(2,1)S(1)}, bf16[256,256]{1,0:T(8,128)(2,1)}, u32[]{:S(2)}) copy-start(bf16[256,256]{1,0:T(8,128)(2,1)} %out_w_ref.3) | copy-start | bytes 393220
  32.7 30.4 %copy-start.5 = (bf16[256,64]{0,1:T(8,128)(2,1)S(1)}, bf16[256,64]{0,1:T(8,128)(2,1)}, u32[]{:S(2)}) copy-start(bf16[256,64]{0,1:T(8,128)(2,1)} %param.20) | copy-start | bytes 98308
  63.1 22.9 %copy-start.6 = (s32[256]{0:T(256)S(1)}, s32[256]{0:T(256)}, u32[]{:S(2)}) copy-start(s32[256]{0:T(256)} %param.14) | copy-start | bytes 3076
  63.1 23.9 %copy-start.2 = (bf16[1024,128]{1,0:T(8,128)(2,1)S(1)}, bf16[1024,128]{1,0:T(8,128)(2,1)}, u32[]{:S(2)}) copy-start(bf16[1024,128]{1,0:T(8,128)(2,1)} %refs_11_.1) | copy-start | bytes 786436
  71.2 7.4 %collective-permute-start.10 = (bf16[256,256]{1,0:T(8,128)(2,1)S(1)}, bf16[256,256]{1,0:T(8,128)(2,1)S(1)}, u32[]{:S(2)}, u32[]{:S(2)}) collective-permute-start(bf16[256,256]{1,0:T(8,128)(2,1)S(1)} %get-tuple-element.43.refs_1_.refs_3_), channel_id=1, source_target_pairs={{0,8},{1,9},{2,10},{3,11},{4,12},{5,13},{6,14},{7,15},{8,0},{9,1},... | collective-permute-start | bytes 393224 | tf_op jit(solution)/shard_map/ppermute | solution.py:559
  72.1 12.9 %collective-permute-start.11 = (bf16[256,256]{1,0:T(8,128)(2,1)S(1)}, bf16[256,256]{1,0:T(8,128)(2,1)S(1)}, u32[]{:S(2)}, u32[]{:S(2)}) collective-permute-start(bf16[256,256]{1,0:T(8,128)(2,1)S(1)} %get-tuple-element.43.refs_1_.refs_3_), channel_id=1, source_target_pairs={{0,16},{1,17},{2,18},{3,19},{4,20},{5,21},{6,22},{7,23},{8,24},{9,... | collective-permute-start | bytes 393224 | tf_op jit(solution)/shard_map/ppermute | solution.py:559
  73.2 11.8 %collective-permute-start.12 = (bf16[256,256]{1,0:T(8,128)(2,1)S(1)}, bf16[256,256]{1,0:T(8,128)(2,1)S(1)}, u32[]{:S(2)}, u32[]{:S(2)}) collective-permute-start(bf16[256,256]{1,0:T(8,128)(2,1)S(1)} %get-tuple-element.43.refs_1_.refs_3_), channel_id=1, source_target_pairs={{0,24},{1,25},{2,26},{3,27},{4,28},{5,29},{6,30},{7,31},{8,16},{9,... | collective-permute-start | bytes 393224 | tf_op jit(solution)/shard_map/ppermute | solution.py:559
  75.7 9.8 %collective-permute-start.17 = (bf16[256,256]{1,0:T(8,128)(2,1)S(1)}, bf16[256,256]{1,0:T(8,128)(2,1)S(1)}, u32[]{:S(2)}, u32[]{:S(2)}) collective-permute-start(bf16[256,256]{1,0:T(8,128)(2,1)S(1)} %get-tuple-element.42.refs_0_), channel_id=1, source_target_pairs={{0,2},{1,3},{2,0},{3,1},{4,6},{5,7},{6,4},{7,5},{8,10},{9,11},{10,... | collective-permute-start | bytes 393224 | tf_op jit(solution)/shard_map/ppermute | solution.py:559
  77.2 8.3 %collective-permute-start.18 = (bf16[256,256]{1,0:T(8,128)(2,1)S(1)}, bf16[256,256]{1,0:T(8,128)(2,1)S(1)}, u32[]{:S(2)}, u32[]{:S(2)}) collective-permute-start(bf16[256,256]{1,0:T(8,128)(2,1)S(1)} %get-tuple-element.42.refs_0_), channel_id=1, source_target_pairs={{0,4},{1,5},{2,6},{3,7},{4,0},{5,1},{6,2},{7,3},{8,12},{9,13},{10,... | collective-permute-start | bytes 393224 | tf_op jit(solution)/shard_map/ppermute | solution.py:559
  78.7 7.4 %collective-permute-start.19 = (bf16[256,256]{1,0:T(8,128)(2,1)S(1)}, bf16[256,256]{1,0:T(8,128)(2,1)S(1)}, u32[]{:S(2)}, u32[]{:S(2)}) collective-permute-start(bf16[256,256]{1,0:T(8,128)(2,1)S(1)} %get-tuple-element.42.refs_0_), channel_id=1, source_target_pairs={{0,6},{1,7},{2,4},{3,5},{4,2},{5,3},{6,0},{7,1},{8,14},{9,15},{10,... | collective-permute-start | bytes 393224 | tf_op jit(solution)/shard_map/ppermute | solution.py:559
  82.2 16.9 %copy-start = (bf16[8,256,128]{2,1,0:T(8,128)(2,1)S(1)}, bf16[8,256,128]{2,1,0:T(8,128)(2,1)}, u32[]{:S(2)}) copy-start(bf16[8,256,128]{2,1,0:T(8,128)(2,1)} %pair_ref.3) | copy-start | bytes 1572868
  85.0 1.3 %collective-permute-start.13 = (bf16[256,256]{1,0:T(8,128)(2,1)S(1)}, bf16[256,256]{1,0:T(8,128)(2,1)S(1)}, u32[]{:S(2)}, u32[]{:S(2)}) collective-permute-start(bf16[256,256]{1,0:T(8,128)(2,1)S(1)} %get-tuple-element.43.refs_1_.refs_3_), channel_id=1, source_target_pairs={{0,1},{1,0},{2,3},{3,2},{4,5},{5,4},{6,7},{7,6},{8,9},{9,8},{10,11... | collective-permute-start | bytes 393224 | tf_op jit(solution)/shard_map/ppermute | solution.py:559
  85.0 1.5 %collective-permute-start.14 = (bf16[256,256]{1,0:T(8,128)(2,1)S(1)}, bf16[256,256]{1,0:T(8,128)(2,1)S(1)}, u32[]{:S(2)}, u32[]{:S(2)}) collective-permute-start(bf16[256,256]{1,0:T(8,128)(2,1)S(1)} %collective-permute-done.10.refs_3_.refs_5_), channel_id=1, source_target_pairs={{0,1},{1,0},{2,3},{3,2},{4,5},{5,4},{6,7},{7,6},{8,9},{9,8},{10,11... | collective-permute-start | bytes 393224 | tf_op jit(solution)/shard_map/ppermute | solution.py:559
  85.5 1.3 %collective-permute-start.15 = (bf16[256,256]{1,0:T(8,128)(2,1)S(1)}, bf16[256,256]{1,0:T(8,128)(2,1)S(1)}, u32[]{:S(2)}, u32[]{:S(2)}) collective-permute-start(bf16[256,256]{1,0:T(8,128)(2,1)S(1)} %collective-permute-done.11.refs_5_.refs_7_), channel_id=1, source_target_pairs={{0,1},{1,0},{2,3},{3,2},{4,5},{5,4},{6,7},{7,6},{8,9},{9,8},{10,11... | collective-permute-start | bytes 393224 | tf_op jit(solution)/shard_map/ppermute | solution.py:559
  85.5 1.5 %collective-permute-start.16 = (bf16[256,256]{1,0:T(8,128)(2,1)S(1)}, bf16[256,256]{1,0:T(8,128)(2,1)S(1)}, u32[]{:S(2)}, u32[]{:S(2)}) collective-permute-start(bf16[256,256]{1,0:T(8,128)(2,1)S(1)} %collective-permute-done.12.refs_7_.refs_9_), channel_id=1, source_target_pairs={{0,1},{1,0},{2,3},{3,2},{4,5},{5,4},{6,7},{7,6},{8,9},{9,8},{10,11... | collective-permute-start | bytes 393224 | tf_op jit(solution)/shard_map/ppermute | solution.py:559
  89.9 6.4 %collective-permute-start.20 = (bf16[8,64,128]{2,1,0:T(8,128)(2,1)S(1)}, bf16[8,64,128]{2,1,0:T(8,128)(2,1)S(1)}, u32[]{:S(2)}, u32[]{:S(2)}) collective-permute-start(bf16[8,64,128]{2,1,0:T(8,128)(2,1)S(1)} %get-tuple-element.47), channel_id=1, source_target_pairs={{0,2},{1,3},{2,0},{3,1},{4,6},{5,7},{6,4},{7,5},{8,10},{9,11},{10,... | collective-permute-start | bytes 393224 | tf_op jit(solution)/shard_map/ppermute | solution.py:559
  90.8 8.2 %collective-permute-start.21 = (bf16[8,64,128]{2,1,0:T(8,128)(2,1)S(1)}, bf16[8,64,128]{2,1,0:T(8,128)(2,1)S(1)}, u32[]{:S(2)}, u32[]{:S(2)}) collective-permute-start(bf16[8,64,128]{2,1,0:T(8,128)(2,1)S(1)} %get-tuple-element.48), channel_id=1, source_target_pairs={{0,4},{1,5},{2,6},{3,7},{4,0},{5,1},{6,2},{7,3},{8,12},{9,13},{10,... | collective-permute-start | bytes 393224 | tf_op jit(solution)/shard_map/ppermute | solution.py:559
  92.2 6.9 %collective-permute-start.22 = (bf16[8,64,128]{2,1,0:T(8,128)(2,1)S(1)}, bf16[8,64,128]{2,1,0:T(8,128)(2,1)S(1)}, u32[]{:S(2)}, u32[]{:S(2)}) collective-permute-start(bf16[8,64,128]{2,1,0:T(8,128)(2,1)S(1)} %get-tuple-element.49), channel_id=1, source_target_pairs={{0,6},{1,7},{2,4},{3,5},{4,2},{5,3},{6,0},{7,1},{8,14},{9,15},{10,... | collective-permute-start | bytes 393224 | tf_op jit(solution)/shard_map/ppermute | solution.py:559

commit v13 on v12

--- a/solution.py
+++ b/solution.py
@@ -287,83 +287,109 @@
     )(*in_hbm(pair_rep, weight))
 
 
-def row_project_kernel(x_ref, weight_ref, q_ref, k_ref, v_ref, g_ref):
-    for s in range(x_ref.shape[0]):
+def row_project_kernel(
+    me_ref, x_ref, weight_ref, mask_ref, out_w_ref, q_ref, k_ref, v_ref, g_ref, own_ref, out_w_out
+):
+    step = x_ref.shape[0]
+    seqs = own_ref.shape[0]
+
+    @pl.when(pl.program_id(0) == 0)
+    def _():
+        rows = pl.ds(pl.multiple_of(me_ref[0] * seqs, seqs), seqs)
+        own_ref[...] = mask_ref[rows, :].astype(F32)
+        out_w_out[...] = out_w_ref[...]
+
+    for s in range(step):
+        at = pl.program_id(0) * step + s
         normed = layer_normalize(x_ref[s].astype(F32)).astype(BF16)
-        q_ref[s], k_ref[s], v_ref[s], g_ref[s] = project(normed, weight_ref)
-
-
-def row_project(alignment, weight):
+        q_ref[at], k_ref[at], v_ref[at], g_ref[s] = project(normed, weight_ref)
+
+
+def row_project(me, alignment, weight, mask, out_weight):
     seqs, length, width = alignment.shape
     step = 2
+    vmem = pl.BlockSpec(memory_space=pltpu.VMEM)
     block = pl.BlockSpec((step, length, width), lambda i: (i, 0, 0))
     return pl.pallas_call(
         row_project_kernel,
         grid=(seqs // step,),
-        in_specs=[block, full_spec(weight.shape)],
-        out_specs=[block] * 4,
-        out_shape=[pltpu.HBM(alignment.shape, BF16)] * 3 + [pltpu.HBM(alignment.shape, F32)],
+        in_specs=[pl.BlockSpec(memory_space=pltpu.SMEM), block]
+        + [full_spec(a.shape) for a in (weight, mask, out_weight)],
+        out_specs=[vmem] * 3 + [block] + [vmem] * 2,
+        out_shape=[pltpu.VMEM(alignment.shape, BF16)] * 3
+        + [
+            pltpu.HBM(alignment.shape, F32),
+            pltpu.VMEM((seqs, mask.shape[1]), F32),
+            pltpu.VMEM(out_weight.shape, BF16),
+        ],
         compiler_params=params(24),
         name="row_project",
-    )(*in_hbm(alignment, weight))
-
-
-def row_attend_kernel(
-    plan, step, seqs, me_ref, x_ref, q_ref, k_ref, v_ref, g_ref, mask_ref, out_w_ref, *rest
-):
-    bias_refs, out_ref, bias_all = rest[: len(plan)], rest[-2], rest[-1]
+    )(me, *in_hbm(alignment, weight, mask, out_weight))
+
+
+def row_attend_kernel(plan, me_ref, x_hbm, g_hbm, q_ref, k_ref, v_ref, own_ref, out_w_ref, *rest):
+    bias_refs = rest[: len(plan)]
+    out_ref, bias_all, x_ref, g_ref, sems = rest[len(plan) :]
     heads, length, _ = bias_all.shape
-
-    @pl.when(pl.program_id(0) == 0)
-    def _():
-        for bias_ref, offsets in zip(bias_refs, plan):
-            for z, offset in enumerate(offsets):
-                block = bias_ref[z].astype(F32).reshape(heads, -1, length)
-                rows = block.shape[1]
-                owner = me_ref[0] ^ offset
-                bias_all[:, pl.ds(pl.multiple_of(owner * rows, rows), rows), :] = block
+    seqs = q_ref.shape[0]
+    parts = out_ref.shape[0]
+
+    copies = [
+        pltpu.make_async_copy(x_hbm, x_ref, sems.at[0]),
+        pltpu.make_async_copy(g_hbm, g_ref, sems.at[1]),
+    ]
+    for copy in copies:
+        copy.start()
+    for bias_ref, offsets in zip(bias_refs, plan):
+        for z, offset in enumerate(offsets):
+            block = bias_ref[z].astype(F32).reshape(heads, -1, length)
+            rows = block.shape[1]
+            owner = me_ref[0] ^ offset
+            bias_all[:, pl.ds(pl.multiple_of(owner * rows, rows), rows), :] = block
 
     lanes = head_lanes(length)
-    parts, rows = out_ref.shape[0], out_ref.shape[1]
-    own = mask_ref[pl.ds(pl.multiple_of(me_ref[0] * seqs, seqs), seqs), :]
-    own = own.astype(F32).astype(BF16)
+    own = own_ref[...].astype(BF16)
     items = []
-    for s in range(step):
-        place = pl.program_id(0) * step + s
-        spot = one_hot((seqs, LANES), 0, place, LIVE_SCALE)
+    for s in range(seqs):
+        spot = one_hot((seqs, LANES), 0, s, LIVE_SCALE)
         live = lax.dot_general(
             own, spot, (((0,), (0,)), ((), ())), preferred_element_type=F32
         ).astype(BF16)
         items.append((q_ref[s], k_ref[s], v_ref[s], live))
-    heads = attend_all(items, lanes, lambda h: bias_all[h])
-    gated = [(heads[s] * g_ref[s]).astype(BF16) for s in range(step)]
-    results = []
-    for s in range(step):
-        total = x_ref[s].astype(F32) + nn_dot(gated[s], out_w_ref[...])
-        results.append(total.reshape(parts, 1, rows // step, total.shape[1]))
-    joined = jnp.concatenate(results, axis=1)
-    out_ref[...] = joined.reshape(out_ref.shape).astype(BF16)
-
-
-def row_attend(me, alignment, projected, mask, out_weight, bias_parts, plan, parts):
+    attended = attend_all(items, lanes, lambda h: bias_all[h])
+    for copy in copies:
+        copy.wait()
+    for pair in range(0, seqs, 2):
+        results = []
+        for s in (pair, pair + 1):
+            gated = (attended[s] * g_ref[s]).astype(BF16)
+            total = x_ref[s].astype(F32) + nn_dot(gated, out_w_ref[...])
+            results.append(total.reshape(parts, 1, length // parts, total.shape[1]))
+        joined = jnp.concatenate(results, axis=1)
+        height = 2 * length // parts
+        rows = slice(pair // 2 * height, (pair // 2 + 1) * height)
+        out_ref[:, rows, :] = joined.reshape(parts, height, joined.shape[3]).astype(BF16)
+
+
+def row_attend(me, alignment, gate, pinned, bias_parts, plan, parts):
     seqs, length, width = alignment.shape
-    rows = length // parts
-    step = 4
     vmem = pl.BlockSpec(memory_space=pltpu.VMEM)
-    block = pl.BlockSpec((step, length, width), lambda i: (i, 0, 0))
+    hbm = pl.BlockSpec(memory_space=pltpu.HBM)
+    held = in_vmem(*pinned, *bias_parts)
     return pl.pallas_call(
-        functools.partial(row_attend_kernel, plan, step, seqs),
-        grid=(seqs // step,),
-        in_specs=[pl.BlockSpec(memory_space=pltpu.SMEM)]
-        + [block] * 5
-        + [full_spec(mask.shape), full_spec(out_weight.shape)]
-        + [vmem] * len(bias_parts),
-        out_specs=pl.BlockSpec((parts, step * rows, width), lambda i: (0, i, 0)),
-        out_shape=jax.ShapeDtypeStruct((parts, seqs * rows, width), BF16),
-        scratch_shapes=[pltpu.VMEM((ATTN_HEAD_COUNT, length, length), F32)],
-        compiler_params=params(40),
+        functools.partial(row_attend_kernel, plan),
+        in_specs=[pl.BlockSpec(memory_space=pltpu.SMEM), hbm, hbm] + [vmem] * len(held),
+        out_specs=vmem,
+        out_shape=jax.ShapeDtypeStruct((parts, seqs * length // parts, width), BF16),
+        scratch_shapes=[
+            pltpu.VMEM((ATTN_HEAD_COUNT, length, length), F32),
+            pltpu.VMEM(alignment.shape, BF16),
+            pltpu.VMEM(alignment.shape, F32),
+            pltpu.SemaphoreType.DMA((2,)),
+        ],
+        compiler_params=params(44),
         name="row_attend",
-    )(me, *in_hbm(alignment, *projected, mask, out_weight), *in_vmem(*bias_parts))
+    )(me, *in_hbm(alignment, gate), *held)
 
 
 def column_kernel(
@@ -579,18 +605,19 @@
     items = pair_rep.shape[0]
 
     bias = pair_bias_block(pair_rep, bias_weight)
-    projected = list(row_project(alignment, row_proj_weight))
+    query, key, value, gate, own_mask, out_weight = row_project(
+        me, alignment, row_proj_weight, align_mask, row_out_weight
+    )
     column = [exchange(bias, count, z) for z in line]
-    *column, projected[0] = lax.optimization_barrier((*column, projected[0]))
+    *column, gate = lax.optimization_barrier((*column, gate))
     column = jnp.stack(column)
     bias_parts = [exchange(column, count, k) for k in plane]
     plan = [[k | z for z in line] for k in plane]
     bias_parts += [exchange(part, count, 1) for part in bias_parts]
     plan += [[offset | 1 for offset in offsets] for offsets in plan]
 
-    rows = row_attend(
-        me, alignment, projected, align_mask, row_out_weight, bias_parts, plan, count
-    )
+    pinned = (query, key, value, own_mask, out_weight)
+    rows = row_attend(me, alignment, gate, pinned, bias_parts, plan, count)
     rows, late_mask = lax.optimization_barrier((rows, align_mask))
     moved = lax.all_to_all(rows, "dap", split_axis=0, concat_axis=0, tiled=True)
     own_res = lax.dynamic_slice_in_dim(late_mask, dap_index * items, items, 1)

time: 101 us -> 99.4 us (0.984)
  Pallas kernels: 31.1 us -> 30 us
    pallas_call x2, Pallas kernels: 13.5 us -> 12.4 us  [the longest x1 7 us: row_attend(): pl.pallas_call(functools.partial(row_attend_kernel, plan), in_specs=[pl.B...]
where the time goes in v13:
time: 99.4 us; the launch traced here: 99.2 us
  blocking collectives  30.4 us (31%)
  Pallas kernels  30 us (30%)
  starting transfers between devices  23.3 us (23%)
  waiting for transfers between devices  14.1 us (14%)
    all_to_all x1, blocking collectives, per_device_fast(): moved = lax.all_to_all(rows, 'dap', split_axis=0, concat_axis=0, tiled=True)  30.4 us
    ppermute x23, starting transfers between devices, exchange(): return lax.ppermute(block, 'dap', [(i, i ^ offset) for i in range(count)])  23.3 us
    ppermute x23, waiting for transfers between devices, exchange(): return lax.ppermute(block, 'dap', [(i, i ^ offset) for i in range(count)])  14.1 us
    pallas_call x1, Pallas kernels, column_attend(): pl.pallas_call(functools.partial(column_kernel, items), in_specs=[pl.Bloc...  8.06 us
    pallas_call x1, Pallas kernels, row_attend(): pl.pallas_call(functools.partial(row_attend_kernel, plan), in_specs=[pl.B...  7 us
    pallas_call x1, Pallas kernels, row_project(): pl.pallas_call(row_project_kernel, grid=(seqs // step,), in_specs=[pl.Blo...  5.38 us
    pallas_call x2, Pallas kernels, outer_product(): pl.pallas_call(functools.partial(outer_kernel, group, outer, items), out_...  4.79 us
  transfers between devices with their start and end apart: 23, of which 12 were waited for; matrix products, arithmetic and copies ran while one was open for 0% of the time, Pallas kernels for 9%

profile of v13, /device:TPU:0, one launch (start us, length us, event | category | flops | bytes accessed | tf_op | source)
XLA Modules:
  0.0 99.2 jit_solution(4643107209651436405)
XLA Ops:
  0.6 1.8 %pair_bias.1 = bf16[64,256]{1,0:T(8,128)(2,1)S(1)} custom-call(bf16[8,256,128]{2,1,0:T(8,128)(2,1)} %pair_ref.3, bf16[8,128]{1,0:T(8,128)(2,1)} %bitcast.12), custom_call_target="tpu_custom_call" | custom-call | tf_op jit(solution)/shard_map/pair_bias/pallas_call | solution.py:278
  2.4 3.1 %collective-permute-start = (bf16[64,256]{1,0:T(8,128)(2,1)S(1)}, bf16[64,256]{1,0:T(8,128)(2,1)S(1)}, u32[]{:S(2)}, u32[]{:S(2)}) collective-permute-start(bf16[64,256]{1,0:T(8,128)(2,1)S(1)} %pair_bias.1), channel_id=1, source_target_pairs={{0,8},{1,9},{2,10},{3,11},{4,12},{5,13},{6,14},{7,15},{8,0},{9,1},... | collective-permute-start | bytes 98312 | tf_op jit(solution)/shard_map/ppermute | solution.py:585
  5.5 2.6 %collective-permute-start.1 = (bf16[64,256]{1,0:T(8,128)(2,1)S(1)}, bf16[64,256]{1,0:T(8,128)(2,1)S(1)}, u32[]{:S(2)}, u32[]{:S(2)}) collective-permute-start(bf16[64,256]{1,0:T(8,128)(2,1)S(1)} %pair_bias.1), channel_id=1, source_target_pairs={{0,16},{1,17},{2,18},{3,19},{4,20},{5,21},{6,22},{7,23},{8,24},{9,... | collective-permute-start | bytes 98312 | tf_op jit(solution)/shard_map/ppermute | solution.py:585
  8.1 5.4 %row_project.1 = (bf16[8,256,256]{2,1,0:T(8,128)(2,1)S(1)}, bf16[8,256,256]{2,1,0:T(8,128)(2,1)S(1)}, bf16[8,256,256]{2,1,0:T(8,128)(2,1)S(1)}, f32[8,256,256]{2...) custom-call(s32[1]{0:T(128)} %bitcast.me_ref, bf16[8,256,256]{2,1,0:T(8,128)(2,1)} %x_hbm.1, ...), custom_call_target="tpu_custom_call" | custom-call | tf_op jit(solution)/shard_map/row_project/pallas_call | solution.py:313
  13.8 1.6 %collective-permute-start.3 = (bf16[4,64,256]{2,1,0:T(8,128)(2,1)S(1)}, bf16[4,64,256]{2,1,0:T(8,128)(2,1)S(1)}, u32[]{:S(2)}, u32[]{:S(2)}) collective-permute-start(bf16[4,64,256]{2,1,0:T(8,128)(2,1)S(1)} %pad_maximum_fusion.rest_0_), channel_id=1, source_target_pairs={{0,2},{1,3},{2,0},{3,1},{4,6},{5,7},{6,4},{7,5},{8,10},{9,11},{10,... | collective-permute-start | bytes 393224 | tf_op jit(solution)/shard_map/ppermute | solution.py:585
  15.4 1.5 %collective-permute-start.4 = (bf16[4,64,256]{2,1,0:T(8,128)(2,1)S(1)}, bf16[4,64,256]{2,1,0:T(8,128)(2,1)S(1)}, u32[]{:S(2)}, u32[]{:S(2)}) collective-permute-start(bf16[4,64,256]{2,1,0:T(8,128)(2,1)S(1)} %pad_maximum_fusion.rest_0_), channel_id=1, source_target_pairs={{0,4},{1,5},{2,6},{3,7},{4,0},{5,1},{6,2},{7,3},{8,12},{9,13},{10,... | collective-permute-start | bytes 393224 | tf_op jit(solution)/shard_map/ppermute | solution.py:585
  16.9 0.5 collective-permute-start.5
  17.4 2.6 %collective-permute-done.3.rest_1_ = bf16[4,64,256]{2,1,0:T(8,128)(2,1)S(1)} collective-permute-done((bf16[4,64,256]{2,1,0:T(8,128)(2,1)S(1)}, bf16[4,64,256]{2,1,0:T(8,128)(2,1)S(1)}, u32[]{:S(2)}, u32[]{:S(2)}) %collective-permute-start.3) | collective-permute-done | bytes 131104 | tf_op jit(solution)/shard_map/ppermute | solution.py:585
  20.0 3.1 %collective-permute-done.4.rest_2_ = bf16[4,64,256]{2,1,0:T(8,128)(2,1)S(1)} collective-permute-done((bf16[4,64,256]{2,1,0:T(8,128)(2,1)S(1)}, bf16[4,64,256]{2,1,0:T(8,128)(2,1)S(1)}, u32[]{:S(2)}, u32[]{:S(2)}) %collective-permute-start.4) | collective-permute-done | bytes 131104 | tf_op jit(solution)/shard_map/ppermute | solution.py:585
  23.1 0.5 collective-permute-start.9
  23.6 0.8 collective-permute-done.8.rest_6_
  24.6 7.0 %row_attend.1 = bf16[32,64,256]{2,1,0:T(8,128)(2,1)S(1)} custom-call(s32[1]{0:T(128)} %bitcast.me_ref, bf16[8,256,256]{2,1,0:T(8,128)(2,1)} %x_hbm.1, f32[8,256,256]{2,1,0:T(8,128)} %get-tuple-element.29.g_hbm, bf16[8,256,256]{2,1,0:T(8,128)(2,1)S(1)} %get-tuple-element.30.q_ref, bf16[8,256,256]{2,1,0:T(8,128)(2,1)S(1)} %get-tuple-element.31.k_ref, ...), custom_call_target="tpu_custom_call" | custom-call | tf_op jit(solution)/shard_map/row_attend/pallas_call | solution.py:379
  31.7 30.4 %all_to_all.5.x_ref = bf16[32,64,256]{2,1,0:T(8,128)(2,1)S(1)} all-to-all(bf16[32,64,256]{2,1,0:T(8,128)(2,1)S(1)} %row_attend.1), channel_id=1, replica_groups=mesh['branch'=1,'dap'=32] {'dap'}, dimensions={0} | all-to-all | bytes 2097152 | tf_op jit(solution)/shard_map/all_to_all | solution.py:622
  62.1 8.1 %column_attend.1 = (bf16[8,256,256]{2,1,0:T(8,128)(2,1)S(1)}, bf16[256,256]{1,0:T(8,128)(2,1)S(1)}, bf16[256,256]{1,0:T(8,128)(2,1)S(1)}) custom-call(s32[1]{0:T(128)} %bitcast.me_ref, bf16[32,64,256]{2,1,0:T(8,128)(2,1)S(1)} %all_to_all.5.x_ref, s32[256,256]{1,0:T(8,128)S(1)} %copy-done.1, bf16[4,256,256]{2,1,0:T(8,128)(2,1)S(1)} %copy-done.3, ...), custom_call_target="tpu_custom_call" | custom-call | tf_op jit(solution)/shard_map/column_attend/pallas_call | solution.py:448
  70.1 0.8 collective-permute-start.10
  71.0 1.1 %collective-permute-start.11 = (bf16[256,256]{1,0:T(8,128)(2,1)S(1)}, bf16[256,256]{1,0:T(8,128)(2,1)S(1)}, u32[]{:S(2)}, u32[]{:S(2)}) collective-permute-start(bf16[256,256]{1,0:T(8,128)(2,1)S(1)} %get-tuple-element.47.refs_1_.refs_3_), channel_id=1, source_target_pairs={{0,16},{1,17},{2,18},{3,19},{4,20},{5,21},{6,22},{7,23},{8,24},{9,... | collective-permute-start | bytes 393224 | tf_op jit(solution)/shard_map/ppermute | solution.py:585
  72.1 2.5 %collective-permute-start.12 = (bf16[256,256]{1,0:T(8,128)(2,1)S(1)}, bf16[256,256]{1,0:T(8,128)(2,1)S(1)}, u32[]{:S(2)}, u32[]{:S(2)}) collective-permute-start(bf16[256,256]{1,0:T(8,128)(2,1)S(1)} %get-tuple-element.47.refs_1_.refs_3_), channel_id=1, source_target_pairs={{0,24},{1,25},{2,26},{3,27},{4,28},{5,29},{6,30},{7,31},{8,16},{9,... | collective-permute-start | bytes 393224 | tf_op jit(solution)/shard_map/ppermute | solution.py:585
  74.6 1.5 %collective-permute-start.17 = (bf16[256,256]{1,0:T(8,128)(2,1)S(1)}, bf16[256,256]{1,0:T(8,128)(2,1)S(1)}, u32[]{:S(2)}, u32[]{:S(2)}) collective-permute-start(bf16[256,256]{1,0:T(8,128)(2,1)S(1)} %get-tuple-element.46.refs_0_), channel_id=1, source_target_pairs={{0,2},{1,3},{2,0},{3,1},{4,6},{5,7},{6,4},{7,5},{8,10},{9,11},{10,... | collective-permute-start | bytes 393224 | tf_op jit(solution)/shard_map/ppermute | solution.py:585
  76.1 1.5 %collective-permute-start.18 = (bf16[256,256]{1,0:T(8,128)(2,1)S(1)}, bf16[256,256]{1,0:T(8,128)(2,1)S(1)}, u32[]{:S(2)}, u32[]{:S(2)}) collective-permute-start(bf16[256,256]{1,0:T(8,128)(2,1)S(1)} %get-tuple-element.46.refs_0_), channel_id=1, source_target_pairs={{0,4},{1,5},{2,6},{3,7},{4,0},{5,1},{6,2},{7,3},{8,12},{9,13},{10,... | collective-permute-start | bytes 393224 | tf_op jit(solution)/shard_map/ppermute | solution.py:585
  77.6 1.6 %collective-permute-start.19 = (bf16[256,256]{1,0:T(8,128)(2,1)S(1)}, bf16[256,256]{1,0:T(8,128)(2,1)S(1)}, u32[]{:S(2)}, u32[]{:S(2)}) collective-permute-start(bf16[256,256]{1,0:T(8,128)(2,1)S(1)} %get-tuple-element.46.refs_0_), channel_id=1, source_target_pairs={{0,6},{1,7},{2,4},{3,5},{4,2},{5,3},{6,0},{7,1},{8,14},{9,15},{10,... | collective-permute-start | bytes 393224 | tf_op jit(solution)/shard_map/ppermute | solution.py:585
  79.2 1.9 %interleave.1 = bf16[256,8,256]{2,1,0:T(8,128)(2,1)} custom-call(bf16[8,256,256]{2,1,0:T(8,128)(2,1)S(1)} %get-tuple-element.43.rows_ref), custom_call_target="tpu_custom_call" | custom-call | tf_op jit(solution)/shard_map/interleave/pallas_call | solution.py:470
  81.1 2.8 %collective-permute-done.11.refs_5_.refs_7_ = bf16[256,256]{1,0:T(8,128)(2,1)S(1)} collective-permute-done((bf16[256,256]{1,0:T(8,128)(2,1)S(1)}, bf16[256,256]{1,0:T(8,128)(2,1)S(1)}, u32[]{:S(2)}, u32[]{:S(2)}) %collective-permute-start.11) | collective-permute-done | bytes 131104 | tf_op jit(solution)/shard_map/ppermute | solution.py:585
  83.9 0.5 collective-permute-start.14
  84.4 0.5 collective-permute-start.16
  85.9 2.9 %outer_product.3 = (bf16[8,64,128]{2,1,0:T(8,128)(2,1)S(1)}, bf16[8,64,128]{2,1,0:T(8,128)(2,1)S(1)}, bf16[8,64,128]{2,1,0:T(8,128)(2,1)S(1)}) custom-call(bf16[256,256]{1,0:T(8,128)(2,1)S(1)} %collective-permute-done.17.refs_0_, bf16[256,256]{1,0:T(8,128)(2,1)S(1)} %collective-permute-done.18.refs_1_, bf16[256,256]{1,0:T(8,128)(2,1)S(1)} %collective-permute-done.19.refs_2_, ...), custom_call_target="tpu_custom_call" | custom-call | tf_op jit(solution)/shard_map/outer_product/pallas_call | solution.py:528
  88.8 0.9 collective-permute-start.20
  89.7 1.4 %collective-permute-start.21 = (bf16[8,64,128]{2,1,0:T(8,128)(2,1)S(1)}, bf16[8,64,128]{2,1,0:T(8,128)(2,1)S(1)}, u32[]{:S(2)}, u32[]{:S(2)}) collective-permute-start(bf16[8,64,128]{2,1,0:T(8,128)(2,1)S(1)} %get-tuple-element.52), channel_id=1, source_target_pairs={{0,4},{1,5},{2,6},{3,7},{4,0},{5,1},{6,2},{7,3},{8,12},{9,13},{10,... | collective-permute-start | bytes 393224 | tf_op jit(solution)/shard_map/ppermute | solution.py:585
  91.1 1.3 %collective-permute-start.22 = (bf16[8,64,128]{2,1,0:T(8,128)(2,1)S(1)}, bf16[8,64,128]{2,1,0:T(8,128)(2,1)S(1)}, u32[]{:S(2)}, u32[]{:S(2)}) collective-permute-start(bf16[8,64,128]{2,1,0:T(8,128)(2,1)S(1)} %get-tuple-element.53), channel_id=1, source_target_pairs={{0,6},{1,7},{2,4},{3,5},{4,2},{5,3},{6,0},{7,1},{8,14},{9,15},{10,... | collective-permute-start | bytes 393224 | tf_op jit(solution)/shard_map/ppermute | solution.py:585
  92.7 1.9 %outer_product.2.refs_0_ = bf16[8,64,128]{2,1,0:T(8,128)(2,1)S(1)} custom-call(bf16[256,256]{1,0:T(8,128)(2,1)S(1)} %get-tuple-element.46.refs_0_, bf16[256,256]{1,0:T(8,128)(2,1)S(1)} %get-tuple-element.47.refs_1_.refs_3_, bf16[256,256]{1,0:T(8,128)(2,1)S(1)} %collective-permute-done.13.refs_2_.refs_4_, ...), custom_call_target="tpu_custom_call" | custom-call | tf_op jit(solution)/shard_map/outer_product/pallas_call | solution.py:528
  94.6 0.6 collective-permute-done.20.refs_1_
  95.2 2.7 %collective-permute-done.21.refs_2_ = bf16[8,64,128]{2,1,0:T(8,128)(2,1)S(1)} collective-permute-done((bf16[8,64,128]{2,1,0:T(8,128)(2,1)S(1)}, bf16[8,64,128]{2,1,0:T(8,128)(2,1)S(1)}, u32[]{:S(2)}, u32[]{:S(2)}) %collective-permute-start.21) | collective-permute-done | bytes 131104 | tf_op jit(solution)/shard_map/ppermute | solution.py:585
  97.9 1.1 %finish.1 = bf16[8,256,128]{2,1,0:T(8,128)(2,1)} custom-call(s32[1]{0:T(128)} %bitcast.me_ref, bf16[8,256,128]{2,1,0:T(8,128)(2,1)S(1)} %copy-done, f32[256,8]{1,0:T(8,128)S(1)} %fusion.scale_ref, bf16[8,64,128]{2,1,0:T(8,128)(2,1)S(1)} %outer_product.2.refs_0_, bf16[8,64,128]{2,1,0:T(8,128)(2,1)S(1)} %collective-permute-done.20.refs_1_, ...), custom_call_target="tpu_custom_call" | custom-call | tf_op jit(solution)/shard_map/finish/pallas_call | solution.py:568
  (41 shorter events, 1.9 us)
Async XLA Ops:
  2.4 11.1 %collective-permute-start = (bf16[64,256]{1,0:T(8,128)(2,1)S(1)}, bf16[64,256]{1,0:T(8,128)(2,1)S(1)}, u32[]{:S(2)}, u32[]{:S(2)}) collective-permute-start(bf16[64,256]{1,0:T(8,128)(2,1)S(1)} %pair_bias.1), channel_id=1, source_target_pairs={{0,8},{1,9},{2,10},{3,11},{4,12},{5,13},{6,14},{7,15},{8,0},{9,1},... | collective-permute-start | bytes 98312 | tf_op jit(solution)/shard_map/ppermute | solution.py:585
  5.5 8.0 %collective-permute-start.1 = (bf16[64,256]{1,0:T(8,128)(2,1)S(1)}, bf16[64,256]{1,0:T(8,128)(2,1)S(1)}, u32[]{:S(2)}, u32[]{:S(2)}) collective-permute-start(bf16[64,256]{1,0:T(8,128)(2,1)S(1)} %pair_bias.1), channel_id=1, source_target_pairs={{0,16},{1,17},{2,18},{3,19},{4,20},{5,21},{6,22},{7,23},{8,24},{9,... | collective-permute-start | bytes 98312 | tf_op jit(solution)/shard_map/ppermute | solution.py:585
  8.1 5.7 %collective-permute-start.2 = (bf16[64,256]{1,0:T(8,128)(2,1)S(1)}, bf16[64,256]{1,0:T(8,128)(2,1)S(1)}, u32[]{:S(2)}, u32[]{:S(2)}) collective-permute-start(bf16[64,256]{1,0:T(8,128)(2,1)S(1)} %pair_bias.1), channel_id=1, source_target_pairs={{0,24},{1,25},{2,26},{3,27},{4,28},{5,29},{6,30},{7,31},{8,16},{9,... | collective-permute-start | bytes 98312 | tf_op jit(solution)/shard_map/ppermute | solution.py:585
  13.8 6.1 %collective-permute-start.3 = (bf16[4,64,256]{2,1,0:T(8,128)(2,1)S(1)}, bf16[4,64,256]{2,1,0:T(8,128)(2,1)S(1)}, u32[]{:S(2)}, u32[]{:S(2)}) collective-permute-start(bf16[4,64,256]{2,1,0:T(8,128)(2,1)S(1)} %pad_maximum_fusion.rest_0_), channel_id=1, source_target_pairs={{0,2},{1,3},{2,0},{3,1},{4,6},{5,7},{6,4},{7,5},{8,10},{9,11},{10,... | collective-permute-start | bytes 393224 | tf_op jit(solution)/shard_map/ppermute | solution.py:585
  15.4 7.7 %collective-permute-start.4 = (bf16[4,64,256]{2,1,0:T(8,128)(2,1)S(1)}, bf16[4,64,256]{2,1,0:T(8,128)(2,1)S(1)}, u32[]{:S(2)}, u32[]{:S(2)}) collective-permute-start(bf16[4,64,256]{2,1,0:T(8,128)(2,1)S(1)} %pad_maximum_fusion.rest_0_), channel_id=1, source_target_pairs={{0,4},{1,5},{2,6},{3,7},{4,0},{5,1},{6,2},{7,3},{8,12},{9,13},{10,... | collective-permute-start | bytes 393224 | tf_op jit(solution)/shard_map/ppermute | solution.py:585
  16.9 6.2 %collective-permute-start.5 = (bf16[4,64,256]{2,1,0:T(8,128)(2,1)S(1)}, bf16[4,64,256]{2,1,0:T(8,128)(2,1)S(1)}, u32[]{:S(2)}, u32[]{:S(2)}) collective-permute-start(bf16[4,64,256]{2,1,0:T(8,128)(2,1)S(1)} %pad_maximum_fusion.rest_0_), channel_id=1, source_target_pairs={{0,6},{1,7},{2,4},{3,5},{4,2},{5,3},{6,0},{7,1},{8,14},{9,15},{10,... | collective-permute-start | bytes 393224 | tf_op jit(solution)/shard_map/ppermute | solution.py:585
  17.4 6.2 %collective-permute-start.6 = (bf16[4,64,256]{2,1,0:T(8,128)(2,1)S(1)}, bf16[4,64,256]{2,1,0:T(8,128)(2,1)S(1)}, u32[]{:S(2)}, u32[]{:S(2)}) collective-permute-start(bf16[4,64,256]{2,1,0:T(8,128)(2,1)S(1)} %pad_maximum_fusion.rest_0_), channel_id=1, source_target_pairs={{0,1},{1,0},{2,3},{3,2},{4,5},{5,4},{6,7},{7,6},{8,9},{9,8},{10,11... | collective-permute-start | bytes 393224 | tf_op jit(solution)/shard_map/ppermute | solution.py:585
  20.0 3.6 %collective-permute-start.7 = (bf16[4,64,256]{2,1,0:T(8,128)(2,1)S(1)}, bf16[4,64,256]{2,1,0:T(8,128)(2,1)S(1)}, u32[]{:S(2)}, u32[]{:S(2)}) collective-permute-start(bf16[4,64,256]{2,1,0:T(8,128)(2,1)S(1)} %collective-permute-done.3.rest_1_), channel_id=1, source_target_pairs={{0,1},{1,0},{2,3},{3,2},{4,5},{5,4},{6,7},{7,6},{8,9},{9,8},{10,11... | collective-permute-start | bytes 393224 | tf_op jit(solution)/shard_map/ppermute | solution.py:585
  23.1 1.3 %collective-permute-start.8 = (bf16[4,64,256]{2,1,0:T(8,128)(2,1)S(1)}, bf16[4,64,256]{2,1,0:T(8,128)(2,1)S(1)}, u32[]{:S(2)}, u32[]{:S(2)}) collective-permute-start(bf16[4,64,256]{2,1,0:T(8,128)(2,1)S(1)} %collective-permute-done.4.rest_2_), channel_id=1, source_target_pairs={{0,1},{1,0},{2,3},{3,2},{4,5},{5,4},{6,7},{7,6},{8,9},{9,8},{10,11... | collective-permute-start | bytes 393224 | tf_op jit(solution)/shard_map/ppermute | solution.py:585
  23.1 1.5 %collective-permute-start.9 = (bf16[4,64,256]{2,1,0:T(8,128)(2,1)S(1)}, bf16[4,64,256]{2,1,0:T(8,128)(2,1)S(1)}, u32[]{:S(2)}, u32[]{:S(2)}) collective-permute-start(bf16[4,64,256]{2,1,0:T(8,128)(2,1)S(1)} %collective-permute-done.5.rest_3_), channel_id=1, source_target_pairs={{0,1},{1,0},{2,3},{3,2},{4,5},{5,4},{6,7},{7,6},{8,9},{9,8},{10,11... | collective-permute-start | bytes 393224 | tf_op jit(solution)/shard_map/ppermute | solution.py:585
  31.6 30.4 %copy-start.1 = (s32[256,256]{1,0:T(8,128)S(1)}, s32[256,256]{1,0:T(8,128)}, u32[]{:S(2)}) copy-start(s32[256,256]{1,0:T(8,128)} %mask_ref.3) | copy-start | bytes 786436
  31.6 30.4 %copy-start.3 = (bf16[4,256,256]{2,1,0:T(8,128)(2,1)S(1)}, bf16[4,256,256]{2,1,0:T(8,128)(2,1)}, u32[]{:S(2)}) copy-start(bf16[4,256,256]{2,1,0:T(8,128)(2,1)} %weight_ref.3) | copy-start | bytes 1572868
  31.6 30.4 %copy-start.4 = (bf16[256,256]{1,0:T(8,128)(2,1)S(1)}, bf16[256,256]{1,0:T(8,128)(2,1)}, u32[]{:S(2)}) copy-start(bf16[256,256]{1,0:T(8,128)(2,1)} %out_w_ref.3) | copy-start | bytes 393220
  31.6 30.4 %copy-start.5 = (bf16[256,64]{0,1:T(8,128)(2,1)S(1)}, bf16[256,64]{0,1:T(8,128)(2,1)}, u32[]{:S(2)}) copy-start(bf16[256,64]{0,1:T(8,128)(2,1)} %param.20) | copy-start | bytes 98308
  62.0 22.9 %copy-start.6 = (s32[256]{0:T(256)S(1)}, s32[256]{0:T(256)}, u32[]{:S(2)}) copy-start(s32[256]{0:T(256)} %param.14) | copy-start | bytes 3076
  62.0 23.9 %copy-start.2 = (bf16[1024,128]{1,0:T(8,128)(2,1)S(1)}, bf16[1024,128]{1,0:T(8,128)(2,1)}, u32[]{:S(2)}) copy-start(bf16[1024,128]{1,0:T(8,128)(2,1)} %refs_11_.1) | copy-start | bytes 786436
  70.1 7.4 %collective-permute-start.10 = (bf16[256,256]{1,0:T(8,128)(2,1)S(1)}, bf16[256,256]{1,0:T(8,128)(2,1)S(1)}, u32[]{:S(2)}, u32[]{:S(2)}) collective-permute-start(bf16[256,256]{1,0:T(8,128)(2,1)S(1)} %get-tuple-element.47.refs_1_.refs_3_), channel_id=1, source_target_pairs={{0,8},{1,9},{2,10},{3,11},{4,12},{5,13},{6,14},{7,15},{8,0},{9,1},... | collective-permute-start | bytes 393224 | tf_op jit(solution)/shard_map/ppermute | solution.py:585
  71.0 12.9 %collective-permute-start.11 = (bf16[256,256]{1,0:T(8,128)(2,1)S(1)}, bf16[256,256]{1,0:T(8,128)(2,1)S(1)}, u32[]{:S(2)}, u32[]{:S(2)}) collective-permute-start(bf16[256,256]{1,0:T(8,128)(2,1)S(1)} %get-tuple-element.47.refs_1_.refs_3_), channel_id=1, source_target_pairs={{0,16},{1,17},{2,18},{3,19},{4,20},{5,21},{6,22},{7,23},{8,24},{9,... | collective-permute-start | bytes 393224 | tf_op jit(solution)/shard_map/ppermute | solution.py:585
  72.1 11.8 %collective-permute-start.12 = (bf16[256,256]{1,0:T(8,128)(2,1)S(1)}, bf16[256,256]{1,0:T(8,128)(2,1)S(1)}, u32[]{:S(2)}, u32[]{:S(2)}) collective-permute-start(bf16[256,256]{1,0:T(8,128)(2,1)S(1)} %get-tuple-element.47.refs_1_.refs_3_), channel_id=1, source_target_pairs={{0,24},{1,25},{2,26},{3,27},{4,28},{5,29},{6,30},{7,31},{8,16},{9,... | collective-permute-start | bytes 393224 | tf_op jit(solution)/shard_map/ppermute | solution.py:585
  74.6 9.8 %collective-permute-start.17 = (bf16[256,256]{1,0:T(8,128)(2,1)S(1)}, bf16[256,256]{1,0:T(8,128)(2,1)S(1)}, u32[]{:S(2)}, u32[]{:S(2)}) collective-permute-start(bf16[256,256]{1,0:T(8,128)(2,1)S(1)} %get-tuple-element.46.refs_0_), channel_id=1, source_target_pairs={{0,2},{1,3},{2,0},{3,1},{4,6},{5,7},{6,4},{7,5},{8,10},{9,11},{10,... | collective-permute-start | bytes 393224 | tf_op jit(solution)/shard_map/ppermute | solution.py:585
  76.1 8.3 %collective-permute-start.18 = (bf16[256,256]{1,0:T(8,128)(2,1)S(1)}, bf16[256,256]{1,0:T(8,128)(2,1)S(1)}, u32[]{:S(2)}, u32[]{:S(2)}) collective-permute-start(bf16[256,256]{1,0:T(8,128)(2,1)S(1)} %get-tuple-element.46.refs_0_), channel_id=1, source_target_pairs={{0,4},{1,5},{2,6},{3,7},{4,0},{5,1},{6,2},{7,3},{8,12},{9,13},{10,... | collective-permute-start | bytes 393224 | tf_op jit(solution)/shard_map/ppermute | solution.py:585
  77.6 7.4 %collective-permute-start.19 = (bf16[256,256]{1,0:T(8,128)(2,1)S(1)}, bf16[256,256]{1,0:T(8,128)(2,1)S(1)}, u32[]{:S(2)}, u32[]{:S(2)}) collective-permute-start(bf16[256,256]{1,0:T(8,128)(2,1)S(1)} %get-tuple-element.46.refs_0_), channel_id=1, source_target_pairs={{0,6},{1,7},{2,4},{3,5},{4,2},{5,3},{6,0},{7,1},{8,14},{9,15},{10,... | collective-permute-start | bytes 393224 | tf_op jit(solution)/shard_map/ppermute | solution.py:585
  81.1 16.9 %copy-start = (bf16[8,256,128]{2,1,0:T(8,128)(2,1)S(1)}, bf16[8,256,128]{2,1,0:T(8,128)(2,1)}, u32[]{:S(2)}) copy-start(bf16[8,256,128]{2,1,0:T(8,128)(2,1)} %pair_ref.3) | copy-start | bytes 1572868
  83.9 1.3 %collective-permute-start.13 = (bf16[256,256]{1,0:T(8,128)(2,1)S(1)}, bf16[256,256]{1,0:T(8,128)(2,1)S(1)}, u32[]{:S(2)}, u32[]{:S(2)}) collective-permute-start(bf16[256,256]{1,0:T(8,128)(2,1)S(1)} %get-tuple-element.47.refs_1_.refs_3_), channel_id=1, source_target_pairs={{0,1},{1,0},{2,3},{3,2},{4,5},{5,4},{6,7},{7,6},{8,9},{9,8},{10,11... | collective-permute-start | bytes 393224 | tf_op jit(solution)/shard_map/ppermute | solution.py:585
  83.9 1.5 %collective-permute-start.14 = (bf16[256,256]{1,0:T(8,128)(2,1)S(1)}, bf16[256,256]{1,0:T(8,128)(2,1)S(1)}, u32[]{:S(2)}, u32[]{:S(2)}) collective-permute-start(bf16[256,256]{1,0:T(8,128)(2,1)S(1)} %collective-permute-done.10.refs_3_.refs_5_), channel_id=1, source_target_pairs={{0,1},{1,0},{2,3},{3,2},{4,5},{5,4},{6,7},{7,6},{8,9},{9,8},{10,11... | collective-permute-start | bytes 393224 | tf_op jit(solution)/shard_map/ppermute | solution.py:585
  84.4 1.3 %collective-permute-start.15 = (bf16[256,256]{1,0:T(8,128)(2,1)S(1)}, bf16[256,256]{1,0:T(8,128)(2,1)S(1)}, u32[]{:S(2)}, u32[]{:S(2)}) collective-permute-start(bf16[256,256]{1,0:T(8,128)(2,1)S(1)} %collective-permute-done.11.refs_5_.refs_7_), channel_id=1, source_target_pairs={{0,1},{1,0},{2,3},{3,2},{4,5},{5,4},{6,7},{7,6},{8,9},{9,8},{10,11... | collective-permute-start | bytes 393224 | tf_op jit(solution)/shard_map/ppermute | solution.py:585
  84.4 1.5 %collective-permute-start.16 = (bf16[256,256]{1,0:T(8,128)(2,1)S(1)}, bf16[256,256]{1,0:T(8,128)(2,1)S(1)}, u32[]{:S(2)}, u32[]{:S(2)}) collective-permute-start(bf16[256,256]{1,0:T(8,128)(2,1)S(1)} %collective-permute-done.12.refs_7_.refs_9_), channel_id=1, source_target_pairs={{0,1},{1,0},{2,3},{3,2},{4,5},{5,4},{6,7},{7,6},{8,9},{9,8},{10,11... | collective-permute-start | bytes 393224 | tf_op jit(solution)/shard_map/ppermute | solution.py:585
  88.8 6.4 %collective-permute-start.20 = (bf16[8,64,128]{2,1,0:T(8,128)(2,1)S(1)}, bf16[8,64,128]{2,1,0:T(8,128)(2,1)S(1)}, u32[]{:S(2)}, u32[]{:S(2)}) collective-permute-start(bf16[8,64,128]{2,1,0:T(8,128)(2,1)S(1)} %get-tuple-element.51), channel_id=1, source_target_pairs={{0,2},{1,3},{2,0},{3,1},{4,6},{5,7},{6,4},{7,5},{8,10},{9,11},{10,... | collective-permute-start | bytes 393224 | tf_op jit(solution)/shard_map/ppermute | solution.py:585
  89.7 8.2 %collective-permute-start.21 = (bf16[8,64,128]{2,1,0:T(8,128)(2,1)S(1)}, bf16[8,64,128]{2,1,0:T(8,128)(2,1)S(1)}, u32[]{:S(2)}, u32[]{:S(2)}) collective-permute-start(bf16[8,64,128]{2,1,0:T(8,128)(2,1)S(1)} %get-tuple-element.52), channel_id=1, source_target_pairs={{0,4},{1,5},{2,6},{3,7},{4,0},{5,1},{6,2},{7,3},{8,12},{9,13},{10,... | collective-permute-start | bytes 393224 | tf_op jit(solution)/shard_map/ppermute | solution.py:585
  91.1 6.9 %collective-permute-start.22 = (bf16[8,64,128]{2,1,0:T(8,128)(2,1)S(1)}, bf16[8,64,128]{2,1,0:T(8,128)(2,1)S(1)}, u32[]{:S(2)}, u32[]{:S(2)}) collective-permute-start(bf16[8,64,128]{2,1,0:T(8,128)(2,1)S(1)} %get-tuple-element.53), channel_id=1, source_target_pairs={{0,6},{1,7},{2,4},{3,5},{4,2},{5,3},{6,0},{7,1},{8,14},{9,15},{10,... | collective-permute-start | bytes 393224 | tf_op jit(solution)/shard_map/ppermute | solution.py:585

commit v14 on v13

--- a/solution.py
+++ b/solution.py
@@ -479,17 +479,10 @@
     )(*in_vmem(rows))
 
 
-def outer_kernel(group, outer, items, *refs):
-    lefts, rights = refs[:group], refs[group : group + outer]
-    weight_ref = refs[group + outer]
-    outs = refs[group + outer + 1 : -3]
-    weight_rows, weight, held = refs[-3:]
+def spread_kernel(weight_ref, weight, weight_rows):
     feat = FACTOR_CHANNELS
     quad = LANES // feat
-    tiles = items * feat // LANES
-    cols = outer * items
     width = weight_ref.shape[1]
-
     weight_rows[...] = weight_ref[...].astype(F32)
     weight[...] = jnp.zeros_like(weight)
     for e in range(feat):
@@ -497,6 +490,31 @@
         for i in range(quad):
             start = e * LANES + i * feat
             weight[start : start + feat, i * width : (i + 1) * width] = block
+
+
+def spread_weight(outer_out):
+    shape = (FACTOR_CHANNELS * LANES, LANES // FACTOR_CHANNELS * outer_out.shape[1])
+    return pl.pallas_call(
+        spread_kernel,
+        grid=(1,),
+        in_specs=[full_spec(outer_out.shape)],
+        out_specs=pl.BlockSpec(memory_space=pltpu.VMEM),
+        out_shape=pltpu.VMEM(shape, BF16),
+        scratch_shapes=[pltpu.VMEM(outer_out.shape, F32)],
+        compiler_params=params(8),
+        name="spread_weight",
+    )(*in_hbm(outer_out))
+
+
+def outer_kernel(group, outer, items, *refs):
+    lefts, rights = refs[:group], refs[group : group + outer]
+    weight_ref = refs[group + outer]
+    outs, held = refs[group + outer + 1 : -1], refs[-1]
+    feat = FACTOR_CHANNELS
+    quad = LANES // feat
+    tiles = items * feat // LANES
+    cols = outer * items
+    width = weight_ref.shape[1] // quad
 
     right = jnp.concatenate([r[...] for r in rights], axis=0)
     def product(k):
@@ -511,7 +529,7 @@
             at = slice((k * tiles + t) * cols, (k * tiles + t + 1) * cols)
             for e in range(feat):
                 held[at, e * LANES : (e + 1) * LANES] = sums[e, :, t * LANES : (t + 1) * LANES]
-    update = nn_dot(held[...], weight[...])
+    update = nn_dot(held[...], weight_ref[...])
     for k in range(group):
         for t in range(tiles):
             rows = update[(k * tiles + t) * cols : (k * tiles + t + 1) * cols]
@@ -523,19 +541,16 @@
     group, outer = len(lefts), len(rights)
     cols = outer * items
     tiles = items * FACTOR_CHANNELS // LANES
-    depth = FACTOR_CHANNELS * LANES
-    width = weight.shape[1]
+    width = weight.shape[1] * FACTOR_CHANNELS // LANES
+    vmem = pl.BlockSpec(memory_space=pltpu.VMEM)
     return pl.pallas_call(
         functools.partial(outer_kernel, group, outer, items),
+        in_specs=[vmem] * (group + outer + 1),
         out_shape=[jax.ShapeDtypeStruct((items, cols, width), BF16)] * group,
-        scratch_shapes=[
-            pltpu.VMEM(weight.shape, F32),
-            pltpu.VMEM((depth, LANES // FACTOR_CHANNELS * width), BF16),
-            pltpu.VMEM((group * tiles * cols, depth), BF16),
-        ],
+        scratch_shapes=[pltpu.VMEM((group * tiles * cols, weight.shape[0]), BF16)],
         compiler_params=params(28),
         name="outer_product",
-    )(*lefts, *rights, weight)
+    )(*lefts, *rights, *in_vmem(weight))
 
 
 def finish_kernel(offsets, line, me_ref, pair_ref, scale_ref, *refs):
@@ -639,12 +654,14 @@
     rights = [exchange(right, count, z) for z in line]
     rights[1], updated = lax.optimization_barrier((rights[1], updated))
     updated = interleave(updated)
-    *rights, updated = lax.optimization_barrier((*rights, updated))
+    updated, outer_out = lax.optimization_barrier((updated, outer_out))
+    spread = spread_weight(outer_out)
+    *rights, updated, spread = lax.optimization_barrier((*rights, updated, spread))
     rights = [part for own in rights for part in (own, exchange(own, count, 1))]
     lefts = [exchange(left, count, k) for k in plane]
-    sent = outer_product(lefts[1:], rights, outer_out, items)
+    sent = outer_product(lefts[1:], rights, spread, items)
     parts = [exchange(part, count, k) for part, k in zip(sent, plane[1:])]
-    own = outer_product([left], rights, outer_out, items)
+    own = outer_product([left], rights, spread, items)
     parts = list(own) + parts
     pair_out = finish(me, pair_rep, scale, parts, plane, line)
     return updated, pair_out
@@ -653,7 +670,8 @@
 def offset_groups(count):
     bits = count.bit_length() - 1
     near = (bits - 1) // 2
-    plane = [k << 1 for k in range(1 << near)]
+    plane = [k << 1 for k in sorted(range(1, 1 << near), key=lambda k: (-k.bit_count(), k))]
+    plane = [0] + plane
     line = [z << (1 + near) for z in range(1 << (bits - 1 - near))]
     return plane, line
 

time: 99.4 us -> 102 us (1.026)
  local copies, waits for them, and re-layouts: 0.11 us -> 4.25 us
  waiting for transfers between devices: 14.1 us -> 11.2 us
  blocking collectives: 30.4 us -> 31.6 us
  Pallas kernels: 30 us -> 31.2 us
    unnamed x14 -> x18, local copies, waits for them, and re-layouts: 0.04 us -> 4.17 us
    ppermute x23, waiting for transfers between devices: 14.1 us -> 11.2 us  [exchange(): return lax.ppermute(block, 'dap', [(i, i ^ offset) for i in range(count)])]
    all_to_all x1, blocking collectives: 30.4 us -> 31.6 us  [per_device_fast(): moved = lax.all_to_all(rows, 'dap', split_axis=0, concat_axis=0, tiled=True)]
    pallas_call x2 -> x3, Pallas kernels: 4.79 us -> 5.97 us  [the longest x2 4.31 us: outer_product(): pl.pallas_call(functools.partial(outer_kernel, group, outer, items), in_s...]
    ppermute x23, starting transfers between devices: 23.3 us -> 22.3 us  [exchange(): return lax.ppermute(block, 'dap', [(i, i ^ offset) for i in range(count)])]
  transfers between devices with their start and end apart: 23 -> 23, of which waited for: 12 -> 14; matrix products, arithmetic and copies ran while one was open for 0% -> 0% of each run, Pallas kernels for 9% -> 10%
where the time goes in v14:
time: 102 us
  blocking collectives  31.6 us (31%)
  Pallas kernels  31.2 us (31%)
  starting transfers between devices  22.3 us (22%)
  waiting for transfers between devices  11.2 us (11%)
  local copies, waits for them, and re-layouts  4.25 us (4%)
    all_to_all x1, blocking collectives, per_device_fast(): moved = lax.all_to_all(rows, 'dap', split_axis=0, concat_axis=0, tiled=True)  31.6 us
    ppermute x23, starting transfers between devices, exchange(): return lax.ppermute(block, 'dap', [(i, i ^ offset) for i in range(count)])  22.3 us
    ppermute x23, waiting for transfers between devices, exchange(): return lax.ppermute(block, 'dap', [(i, i ^ offset) for i in range(count)])  11.2 us
    pallas_call x1, Pallas kernels, column_attend(): pl.pallas_call(functools.partial(column_kernel, items), in_specs=[pl.Bloc...  8.06 us
    pallas_call x1, Pallas kernels, row_attend(): pl.pallas_call(functools.partial(row_attend_kernel, plan), in_specs=[pl.B...  7.01 us
    pallas_call x1, Pallas kernels, row_project(): pl.pallas_call(row_project_kernel, grid=(seqs // step,), in_specs=[pl.Blo...  5.37 us
    pallas_call x2, Pallas kernels, outer_product(): pl.pallas_call(functools.partial(outer_kernel, group, outer, items), in_s...  4.31 us
    unnamed x18, local copies, waits for them, and re-layouts  4.17 us
  transfers between devices with their start and end apart: 23, of which 14 were waited for; matrix products, arithmetic and copies ran while one was open for 0% of the time, Pallas kernels for 10%

profile of v14, /device:TPU:0, one launch (start us, length us, event | category | flops | bytes accessed | tf_op | source)
XLA Modules:
  0.0 101.7 jit_solution(2019713633654147217)
XLA Ops:
  0.6 1.8 %pair_bias.1 = bf16[64,256]{1,0:T(8,128)(2,1)S(1)} custom-call(bf16[8,256,128]{2,1,0:T(8,128)(2,1)} %pair_ref.3, bf16[8,128]{1,0:T(8,128)(2,1)} %bitcast.12), custom_call_target="tpu_custom_call" | custom-call | tf_op jit(solution)/shard_map/pair_bias/pallas_call | solution.py:278
  2.4 3.1 %collective-permute-start = (bf16[64,256]{1,0:T(8,128)(2,1)S(1)}, bf16[64,256]{1,0:T(8,128)(2,1)S(1)}, u32[]{:S(2)}, u32[]{:S(2)}) collective-permute-start(bf16[64,256]{1,0:T(8,128)(2,1)S(1)} %pair_bias.1), channel_id=1, source_target_pairs={{0,8},{1,9},{2,10},{3,11},{4,12},{5,13},{6,14},{7,15},{8,0},{9,1},... | collective-permute-start | bytes 98312 | tf_op jit(solution)/shard_map/ppermute | solution.py:600
  5.5 2.6 %collective-permute-start.1 = (bf16[64,256]{1,0:T(8,128)(2,1)S(1)}, bf16[64,256]{1,0:T(8,128)(2,1)S(1)}, u32[]{:S(2)}, u32[]{:S(2)}) collective-permute-start(bf16[64,256]{1,0:T(8,128)(2,1)S(1)} %pair_bias.1), channel_id=1, source_target_pairs={{0,16},{1,17},{2,18},{3,19},{4,20},{5,21},{6,22},{7,23},{8,24},{9,... | collective-permute-start | bytes 98312 | tf_op jit(solution)/shard_map/ppermute | solution.py:600
  8.1 5.4 %row_project.1 = (bf16[8,256,256]{2,1,0:T(8,128)(2,1)S(1)}, bf16[8,256,256]{2,1,0:T(8,128)(2,1)S(1)}, bf16[8,256,256]{2,1,0:T(8,128)(2,1)S(1)}, f32[8,256,256]{2...) custom-call(s32[1]{0:T(128)} %bitcast.me_ref, bf16[8,256,256]{2,1,0:T(8,128)(2,1)} %x_hbm.1, ...), custom_call_target="tpu_custom_call" | custom-call | tf_op jit(solution)/shard_map/row_project/pallas_call | solution.py:313
  13.8 2.5 %collective-permute-start.3 = (bf16[4,64,256]{2,1,0:T(8,128)(2,1)S(1)}, bf16[4,64,256]{2,1,0:T(8,128)(2,1)S(1)}, u32[]{:S(2)}, u32[]{:S(2)}) collective-permute-start(bf16[4,64,256]{2,1,0:T(8,128)(2,1)S(1)} %pad_maximum_fusion.rest_0_), channel_id=1, source_target_pairs={{0,6},{1,7},{2,4},{3,5},{4,2},{5,3},{6,0},{7,1},{8,14},{9,15},{10,... | collective-permute-start | bytes 393224 | tf_op jit(solution)/shard_map/ppermute | solution.py:600
  16.4 0.5 collective-permute-start.4
  16.9 0.5 collective-permute-start.5
  17.4 3.3 %collective-permute-done.3.rest_1_ = bf16[4,64,256]{2,1,0:T(8,128)(2,1)S(1)} collective-permute-done((bf16[4,64,256]{2,1,0:T(8,128)(2,1)S(1)}, bf16[4,64,256]{2,1,0:T(8,128)(2,1)S(1)}, u32[]{:S(2)}, u32[]{:S(2)}) %collective-permute-start.3) | collective-permute-done | bytes 131104 | tf_op jit(solution)/shard_map/ppermute | solution.py:600
  20.7 1.3 %collective-permute-done.4.rest_2_ = bf16[4,64,256]{2,1,0:T(8,128)(2,1)S(1)} collective-permute-done((bf16[4,64,256]{2,1,0:T(8,128)(2,1)S(1)}, bf16[4,64,256]{2,1,0:T(8,128)(2,1)S(1)}, u32[]{:S(2)}, u32[]{:S(2)}) %collective-permute-start.4) | collective-permute-done | bytes 131104 | tf_op jit(solution)/shard_map/ppermute | solution.py:600
  22.6 0.8 collective-permute-done.8.rest_6_
  23.6 7.0 %row_attend.1 = bf16[32,64,256]{2,1,0:T(8,128)(2,1)S(1)} custom-call(s32[1]{0:T(128)} %bitcast.me_ref, bf16[8,256,256]{2,1,0:T(8,128)(2,1)} %x_hbm.1, f32[8,256,256]{2,1,0:T(8,128)} %get-tuple-element.32.g_hbm, bf16[8,256,256]{2,1,0:T(8,128)(2,1)S(1)} %get-tuple-element.33.q_ref, bf16[8,256,256]{2,1,0:T(8,128)(2,1)S(1)} %get-tuple-element.34.k_ref, ...), custom_call_target="tpu_custom_call" | custom-call | tf_op jit(solution)/shard_map/row_attend/pallas_call | solution.py:379
  30.6 31.6 %all_to_all.5.x_ref = bf16[32,64,256]{2,1,0:T(8,128)(2,1)S(1)} all-to-all(bf16[32,64,256]{2,1,0:T(8,128)(2,1)S(1)} %row_attend.1), channel_id=1, replica_groups=mesh['branch'=1,'dap'=32] {'dap'}, dimensions={0} | all-to-all | bytes 2097152 | tf_op jit(solution)/shard_map/all_to_all | solution.py:637
  62.2 8.1 %column_attend.1 = (bf16[8,256,256]{2,1,0:T(8,128)(2,1)S(1)}, bf16[256,256]{1,0:T(8,128)(2,1)S(1)}, bf16[256,256]{1,0:T(8,128)(2,1)S(1)}) custom-call(s32[1]{0:T(128)} %bitcast.me_ref, bf16[32,64,256]{2,1,0:T(8,128)(2,1)S(1)} %all_to_all.5.x_ref, s32[256,256]{1,0:T(8,128)S(1)} %copy-done.4, bf16[4,256,256]{2,1,0:T(8,128)(2,1)S(1)} %copy-done.5, ...), custom_call_target="tpu_custom_call" | custom-call | tf_op jit(solution)/shard_map/column_attend/pallas_call | solution.py:448
  70.3 0.8 collective-permute-start.10
  71.1 1.1 %collective-permute-start.11 = (bf16[256,256]{1,0:T(8,128)(2,1)S(1)}, bf16[256,256]{1,0:T(8,128)(2,1)S(1)}, u32[]{:S(2)}, u32[]{:S(2)}) collective-permute-start(bf16[256,256]{1,0:T(8,128)(2,1)S(1)} %get-tuple-element.52.refs_1_.refs_3_), channel_id=1, source_target_pairs={{0,16},{1,17},{2,18},{3,19},{4,20},{5,21},{6,22},{7,23},{8,24},{9,... | collective-permute-start | bytes 393224 | tf_op jit(solution)/shard_map/ppermute | solution.py:600
  72.2 2.5 %collective-permute-start.12 = (bf16[256,256]{1,0:T(8,128)(2,1)S(1)}, bf16[256,256]{1,0:T(8,128)(2,1)S(1)}, u32[]{:S(2)}, u32[]{:S(2)}) collective-permute-start(bf16[256,256]{1,0:T(8,128)(2,1)S(1)} %get-tuple-element.52.refs_1_.refs_3_), channel_id=1, source_target_pairs={{0,24},{1,25},{2,26},{3,27},{4,28},{5,29},{6,30},{7,31},{8,16},{9,... | collective-permute-start | bytes 393224 | tf_op jit(solution)/shard_map/ppermute | solution.py:600
  74.7 2.4 %collective-permute-start.17 = (bf16[256,256]{1,0:T(8,128)(2,1)S(1)}, bf16[256,256]{1,0:T(8,128)(2,1)S(1)}, u32[]{:S(2)}, u32[]{:S(2)}) collective-permute-start(bf16[256,256]{1,0:T(8,128)(2,1)S(1)} %get-tuple-element.51.refs_0_), channel_id=1, source_target_pairs={{0,6},{1,7},{2,4},{3,5},{4,2},{5,3},{6,0},{7,1},{8,14},{9,15},{10,... | collective-permute-start | bytes 393224 | tf_op jit(solution)/shard_map/ppermute | solution.py:600
  77.1 0.5 collective-permute-start.18
  77.7 0.6 collective-permute-start.19
  78.3 1.9 %interleave.1 = bf16[256,8,256]{2,1,0:T(8,128)(2,1)} custom-call(bf16[8,256,256]{2,1,0:T(8,128)(2,1)S(1)} %get-tuple-element.46.rows_ref), custom_call_target="tpu_custom_call" | custom-call | tf_op jit(solution)/shard_map/interleave/pallas_call | solution.py:470
  80.2 1.7 %spread_weight.1.refs_9_.refs_11_ = bf16[4096,512]{1,0:T(8,128)(2,1)S(1)} custom-call(bf16[1024,128]{1,0:T(8,128)(2,1)} %weight_ref.4), custom_call_target="tpu_custom_call" | custom-call | tf_op jit(solution)/shard_map/spread_weight/pallas_call | solution.py:497
  81.9 1.9 %copy-done = bf16[4096,512]{1,0:T(8,128)(2,1)} copy-done((bf16[4096,512]{1,0:T(8,128)(2,1)}, bf16[4096,512]{1,0:T(8,128)(2,1)S(1)}, u32[]{:S(2)}) %copy-start) | copy-done | bytes 4194328
  84.0 0.5 collective-permute-start.14
  86.1 2.2 %copy-done.1 = bf16[4096,512]{1,0:T(8,128)(2,1)S(1)} copy-done((bf16[4096,512]{1,0:T(8,128)(2,1)S(1)}, bf16[4096,512]{1,0:T(8,128)(2,1)}, u32[]{:S(2)}) %copy-start.1) | copy-done | bytes 4194328
  88.3 2.6 %outer_product.3 = (bf16[8,64,128]{2,1,0:T(8,128)(2,1)S(1)}, bf16[8,64,128]{2,1,0:T(8,128)(2,1)S(1)}, bf16[8,64,128]{2,1,0:T(8,128)(2,1)S(1)}) custom-call(bf16[256,256]{1,0:T(8,128)(2,1)S(1)} %collective-permute-done.17.refs_0_, bf16[256,256]{1,0:T(8,128)(2,1)S(1)} %collective-permute-done.18.refs_1_, bf16[256,256]{1,0:T(8,128)(2,1)S(1)} %collective-permute-done.19.refs_2_, ...), custom_call_target="tpu_custom_call" | custom-call | tf_op jit(solution)/shard_map/outer_product/pallas_call | solution.py:546
  90.9 2.2 %collective-permute-start.20 = (bf16[8,64,128]{2,1,0:T(8,128)(2,1)S(1)}, bf16[8,64,128]{2,1,0:T(8,128)(2,1)S(1)}, u32[]{:S(2)}, u32[]{:S(2)}) collective-permute-start(bf16[8,64,128]{2,1,0:T(8,128)(2,1)S(1)} %get-tuple-element.57), channel_id=1, source_target_pairs={{0,6},{1,7},{2,4},{3,5},{4,2},{5,3},{6,0},{7,1},{8,14},{9,15},{10,... | collective-permute-start | bytes 393224 | tf_op jit(solution)/shard_map/ppermute | solution.py:600
  93.1 0.5 collective-permute-start.21
  93.7 0.8 collective-permute-start.22
  94.8 1.7 %outer_product.2.refs_0_ = bf16[8,64,128]{2,1,0:T(8,128)(2,1)S(1)} custom-call(bf16[256,256]{1,0:T(8,128)(2,1)S(1)} %get-tuple-element.51.refs_0_, bf16[256,256]{1,0:T(8,128)(2,1)S(1)} %get-tuple-element.52.refs_1_.refs_3_, bf16[256,256]{1,0:T(8,128)(2,1)S(1)} %collective-permute-done.13.refs_2_.refs_4_, ...), custom_call_target="tpu_custom_call" | custom-call | tf_op jit(solution)/shard_map/outer_product/pallas_call | solution.py:546
  96.5 1.7 %collective-permute-done.20.refs_1_ = bf16[8,64,128]{2,1,0:T(8,128)(2,1)S(1)} collective-permute-done((bf16[8,64,128]{2,1,0:T(8,128)(2,1)S(1)}, bf16[8,64,128]{2,1,0:T(8,128)(2,1)S(1)}, u32[]{:S(2)}, u32[]{:S(2)}) %collective-permute-start.20) | collective-permute-done | bytes 131104 | tf_op jit(solution)/shard_map/ppermute | solution.py:600
  98.2 2.0 %collective-permute-done.21.refs_2_ = bf16[8,64,128]{2,1,0:T(8,128)(2,1)S(1)} collective-permute-done((bf16[8,64,128]{2,1,0:T(8,128)(2,1)S(1)}, bf16[8,64,128]{2,1,0:T(8,128)(2,1)S(1)}, u32[]{:S(2)}, u32[]{:S(2)}) %collective-permute-start.21) | collective-permute-done | bytes 131104 | tf_op jit(solution)/shard_map/ppermute | solution.py:600
  100.4 1.1 %finish.1 = bf16[8,256,128]{2,1,0:T(8,128)(2,1)} custom-call(s32[1]{0:T(128)} %bitcast.me_ref, bf16[8,256,128]{2,1,0:T(8,128)(2,1)S(1)} %copy-done.3, f32[256,8]{1,0:T(8,128)S(1)} %fusion.scale_ref, bf16[8,64,128]{2,1,0:T(8,128)(2,1)S(1)} %outer_product.2.refs_0_, bf16[8,64,128]{2,1,0:T(8,128)(2,1)S(1)} %collective-permute-done.20.refs_1_, ...), custom_call_target="tpu_custom_call" | custom-call | tf_op jit(solution)/shard_map/finish/pallas_call | solution.py:583
  (46 shorter events, 3.3 us)
Async XLA Ops:
  2.4 11.1 %collective-permute-start = (bf16[64,256]{1,0:T(8,128)(2,1)S(1)}, bf16[64,256]{1,0:T(8,128)(2,1)S(1)}, u32[]{:S(2)}, u32[]{:S(2)}) collective-permute-start(bf16[64,256]{1,0:T(8,128)(2,1)S(1)} %pair_bias.1), channel_id=1, source_target_pairs={{0,8},{1,9},{2,10},{3,11},{4,12},{5,13},{6,14},{7,15},{8,0},{9,1},... | collective-permute-start | bytes 98312 | tf_op jit(solution)/shard_map/ppermute | solution.py:600
  5.5 8.0 %collective-permute-start.1 = (bf16[64,256]{1,0:T(8,128)(2,1)S(1)}, bf16[64,256]{1,0:T(8,128)(2,1)S(1)}, u32[]{:S(2)}, u32[]{:S(2)}) collective-permute-start(bf16[64,256]{1,0:T(8,128)(2,1)S(1)} %pair_bias.1), channel_id=1, source_target_pairs={{0,16},{1,17},{2,18},{3,19},{4,20},{5,21},{6,22},{7,23},{8,24},{9,... | collective-permute-start | bytes 98312 | tf_op jit(solution)/shard_map/ppermute | solution.py:600
  8.1 5.7 %collective-permute-start.2 = (bf16[64,256]{1,0:T(8,128)(2,1)S(1)}, bf16[64,256]{1,0:T(8,128)(2,1)S(1)}, u32[]{:S(2)}, u32[]{:S(2)}) collective-permute-start(bf16[64,256]{1,0:T(8,128)(2,1)S(1)} %pair_bias.1), channel_id=1, source_target_pairs={{0,24},{1,25},{2,26},{3,27},{4,28},{5,29},{6,30},{7,31},{8,16},{9,... | collective-permute-start | bytes 98312 | tf_op jit(solution)/shard_map/ppermute | solution.py:600
  13.8 6.9 %collective-permute-start.3 = (bf16[4,64,256]{2,1,0:T(8,128)(2,1)S(1)}, bf16[4,64,256]{2,1,0:T(8,128)(2,1)S(1)}, u32[]{:S(2)}, u32[]{:S(2)}) collective-permute-start(bf16[4,64,256]{2,1,0:T(8,128)(2,1)S(1)} %pad_maximum_fusion.rest_0_), channel_id=1, source_target_pairs={{0,6},{1,7},{2,4},{3,5},{4,2},{5,3},{6,0},{7,1},{8,14},{9,15},{10,... | collective-permute-start | bytes 393224 | tf_op jit(solution)/shard_map/ppermute | solution.py:600
  16.4 5.7 %collective-permute-start.4 = (bf16[4,64,256]{2,1,0:T(8,128)(2,1)S(1)}, bf16[4,64,256]{2,1,0:T(8,128)(2,1)S(1)}, u32[]{:S(2)}, u32[]{:S(2)}) collective-permute-start(bf16[4,64,256]{2,1,0:T(8,128)(2,1)S(1)} %pad_maximum_fusion.rest_0_), channel_id=1, source_target_pairs={{0,2},{1,3},{2,0},{3,1},{4,6},{5,7},{6,4},{7,5},{8,10},{9,11},{10,... | collective-permute-start | bytes 393224 | tf_op jit(solution)/shard_map/ppermute | solution.py:600
  16.9 5.2 %collective-permute-start.5 = (bf16[4,64,256]{2,1,0:T(8,128)(2,1)S(1)}, bf16[4,64,256]{2,1,0:T(8,128)(2,1)S(1)}, u32[]{:S(2)}, u32[]{:S(2)}) collective-permute-start(bf16[4,64,256]{2,1,0:T(8,128)(2,1)S(1)} %pad_maximum_fusion.rest_0_), channel_id=1, source_target_pairs={{0,4},{1,5},{2,6},{3,7},{4,0},{5,1},{6,2},{7,3},{8,12},{9,13},{10,... | collective-permute-start | bytes 393224 | tf_op jit(solution)/shard_map/ppermute | solution.py:600
  17.4 5.2 %collective-permute-start.6 = (bf16[4,64,256]{2,1,0:T(8,128)(2,1)S(1)}, bf16[4,64,256]{2,1,0:T(8,128)(2,1)S(1)}, u32[]{:S(2)}, u32[]{:S(2)}) collective-permute-start(bf16[4,64,256]{2,1,0:T(8,128)(2,1)S(1)} %pad_maximum_fusion.rest_0_), channel_id=1, source_target_pairs={{0,1},{1,0},{2,3},{3,2},{4,5},{5,4},{6,7},{7,6},{8,9},{9,8},{10,11... | collective-permute-start | bytes 393224 | tf_op jit(solution)/shard_map/ppermute | solution.py:600
  20.7 1.9 %collective-permute-start.7 = (bf16[4,64,256]{2,1,0:T(8,128)(2,1)S(1)}, bf16[4,64,256]{2,1,0:T(8,128)(2,1)S(1)}, u32[]{:S(2)}, u32[]{:S(2)}) collective-permute-start(bf16[4,64,256]{2,1,0:T(8,128)(2,1)S(1)} %collective-permute-done.3.rest_1_), channel_id=1, source_target_pairs={{0,1},{1,0},{2,3},{3,2},{4,5},{5,4},{6,7},{7,6},{8,9},{9,8},{10,11... | collective-permute-start | bytes 393224 | tf_op jit(solution)/shard_map/ppermute | solution.py:600
  22.1 1.3 %collective-permute-start.8 = (bf16[4,64,256]{2,1,0:T(8,128)(2,1)S(1)}, bf16[4,64,256]{2,1,0:T(8,128)(2,1)S(1)}, u32[]{:S(2)}, u32[]{:S(2)}) collective-permute-start(bf16[4,64,256]{2,1,0:T(8,128)(2,1)S(1)} %collective-permute-done.4.rest_2_), channel_id=1, source_target_pairs={{0,1},{1,0},{2,3},{3,2},{4,5},{5,4},{6,7},{7,6},{8,9},{9,8},{10,11... | collective-permute-start | bytes 393224 | tf_op jit(solution)/shard_map/ppermute | solution.py:600
  22.1 1.5 %collective-permute-start.9 = (bf16[4,64,256]{2,1,0:T(8,128)(2,1)S(1)}, bf16[4,64,256]{2,1,0:T(8,128)(2,1)S(1)}, u32[]{:S(2)}, u32[]{:S(2)}) collective-permute-start(bf16[4,64,256]{2,1,0:T(8,128)(2,1)S(1)} %collective-permute-done.5.rest_3_), channel_id=1, source_target_pairs={{0,1},{1,0},{2,3},{3,2},{4,5},{5,4},{6,7},{7,6},{8,9},{9,8},{10,11... | collective-permute-start | bytes 393224 | tf_op jit(solution)/shard_map/ppermute | solution.py:600
  23.6 38.6 %copy-start.4 = (s32[256,256]{1,0:T(8,128)S(1)}, s32[256,256]{1,0:T(8,128)}, u32[]{:S(2)}) copy-start(s32[256,256]{1,0:T(8,128)} %mask_ref.3) | copy-start | bytes 786436
  23.6 38.6 %copy-start.5 = (bf16[4,256,256]{2,1,0:T(8,128)(2,1)S(1)}, bf16[4,256,256]{2,1,0:T(8,128)(2,1)}, u32[]{:S(2)}) copy-start(bf16[4,256,256]{2,1,0:T(8,128)(2,1)} %weight_ref.3) | copy-start | bytes 1572868
  23.6 38.6 %copy-start.6 = (bf16[256,256]{1,0:T(8,128)(2,1)S(1)}, bf16[256,256]{1,0:T(8,128)(2,1)}, u32[]{:S(2)}) copy-start(bf16[256,256]{1,0:T(8,128)(2,1)} %out_w_ref.3) | copy-start | bytes 393220
  23.6 38.6 %copy-start.7 = (bf16[256,64]{0,1:T(8,128)(2,1)S(1)}, bf16[256,64]{0,1:T(8,128)(2,1)}, u32[]{:S(2)}) copy-start(bf16[256,64]{0,1:T(8,128)(2,1)} %param.20) | copy-start | bytes 98308
  62.2 22.8 %copy-start.8 = (s32[256]{0:T(256)S(1)}, s32[256]{0:T(256)}, u32[]{:S(2)}) copy-start(s32[256]{0:T(256)} %param.14) | copy-start | bytes 3076
  70.3 7.4 %collective-permute-start.10 = (bf16[256,256]{1,0:T(8,128)(2,1)S(1)}, bf16[256,256]{1,0:T(8,128)(2,1)S(1)}, u32[]{:S(2)}, u32[]{:S(2)}) collective-permute-start(bf16[256,256]{1,0:T(8,128)(2,1)S(1)} %get-tuple-element.52.refs_1_.refs_3_), channel_id=1, source_target_pairs={{0,8},{1,9},{2,10},{3,11},{4,12},{5,13},{6,14},{7,15},{8,0},{9,1},... | collective-permute-start | bytes 393224 | tf_op jit(solution)/shard_map/ppermute | solution.py:600
  71.1 12.9 %collective-permute-start.11 = (bf16[256,256]{1,0:T(8,128)(2,1)S(1)}, bf16[256,256]{1,0:T(8,128)(2,1)S(1)}, u32[]{:S(2)}, u32[]{:S(2)}) collective-permute-start(bf16[256,256]{1,0:T(8,128)(2,1)S(1)} %get-tuple-element.52.refs_1_.refs_3_), channel_id=1, source_target_pairs={{0,16},{1,17},{2,18},{3,19},{4,20},{5,21},{6,22},{7,23},{8,24},{9,... | collective-permute-start | bytes 393224 | tf_op jit(solution)/shard_map/ppermute | solution.py:600
  72.2 11.8 %collective-permute-start.12 = (bf16[256,256]{1,0:T(8,128)(2,1)S(1)}, bf16[256,256]{1,0:T(8,128)(2,1)S(1)}, u32[]{:S(2)}, u32[]{:S(2)}) collective-permute-start(bf16[256,256]{1,0:T(8,128)(2,1)S(1)} %get-tuple-element.52.refs_1_.refs_3_), channel_id=1, source_target_pairs={{0,24},{1,25},{2,26},{3,27},{4,28},{5,29},{6,30},{7,31},{8,16},{9,... | collective-permute-start | bytes 393224 | tf_op jit(solution)/shard_map/ppermute | solution.py:600
  74.7 9.8 %collective-permute-start.17 = (bf16[256,256]{1,0:T(8,128)(2,1)S(1)}, bf16[256,256]{1,0:T(8,128)(2,1)S(1)}, u32[]{:S(2)}, u32[]{:S(2)}) collective-permute-start(bf16[256,256]{1,0:T(8,128)(2,1)S(1)} %get-tuple-element.51.refs_0_), channel_id=1, source_target_pairs={{0,6},{1,7},{2,4},{3,5},{4,2},{5,3},{6,0},{7,1},{8,14},{9,15},{10,... | collective-permute-start | bytes 393224 | tf_op jit(solution)/shard_map/ppermute | solution.py:600
  77.1 7.4 %collective-permute-start.18 = (bf16[256,256]{1,0:T(8,128)(2,1)S(1)}, bf16[256,256]{1,0:T(8,128)(2,1)S(1)}, u32[]{:S(2)}, u32[]{:S(2)}) collective-permute-start(bf16[256,256]{1,0:T(8,128)(2,1)S(1)} %get-tuple-element.51.refs_0_), channel_id=1, source_target_pairs={{0,2},{1,3},{2,0},{3,1},{4,6},{5,7},{6,4},{7,5},{8,10},{9,11},{10,... | collective-permute-start | bytes 393224 | tf_op jit(solution)/shard_map/ppermute | solution.py:600
  77.7 7.4 %collective-permute-start.19 = (bf16[256,256]{1,0:T(8,128)(2,1)S(1)}, bf16[256,256]{1,0:T(8,128)(2,1)S(1)}, u32[]{:S(2)}, u32[]{:S(2)}) collective-permute-start(bf16[256,256]{1,0:T(8,128)(2,1)S(1)} %get-tuple-element.51.refs_0_), channel_id=1, source_target_pairs={{0,4},{1,5},{2,6},{3,7},{4,0},{5,1},{6,2},{7,3},{8,12},{9,13},{10,... | collective-permute-start | bytes 393224 | tf_op jit(solution)/shard_map/ppermute | solution.py:600
  81.9 2.0 %copy-start = (bf16[4096,512]{1,0:T(8,128)(2,1)}, bf16[4096,512]{1,0:T(8,128)(2,1)S(1)}, u32[]{:S(2)}) copy-start(bf16[4096,512]{1,0:T(8,128)(2,1)S(1)} %spread_weight.1.refs_9_.refs_11_) | copy-start | bytes 12582916
  84.0 1.3 %collective-permute-start.13 = (bf16[256,256]{1,0:T(8,128)(2,1)S(1)}, bf16[256,256]{1,0:T(8,128)(2,1)S(1)}, u32[]{:S(2)}, u32[]{:S(2)}) collective-permute-start(bf16[256,256]{1,0:T(8,128)(2,1)S(1)} %get-tuple-element.52.refs_1_.refs_3_), channel_id=1, source_target_pairs={{0,1},{1,0},{2,3},{3,2},{4,5},{5,4},{6,7},{7,6},{8,9},{9,8},{10,11... | collective-permute-start | bytes 393224 | tf_op jit(solution)/shard_map/ppermute | solution.py:600
  84.0 1.5 %collective-permute-start.14 = (bf16[256,256]{1,0:T(8,128)(2,1)S(1)}, bf16[256,256]{1,0:T(8,128)(2,1)S(1)}, u32[]{:S(2)}, u32[]{:S(2)}) collective-permute-start(bf16[256,256]{1,0:T(8,128)(2,1)S(1)} %collective-permute-done.10.refs_3_.refs_5_), channel_id=1, source_target_pairs={{0,1},{1,0},{2,3},{3,2},{4,5},{5,4},{6,7},{7,6},{8,9},{9,8},{10,11... | collective-permute-start | bytes 393224 | tf_op jit(solution)/shard_map/ppermute | solution.py:600
  84.5 1.3 %collective-permute-start.15 = (bf16[256,256]{1,0:T(8,128)(2,1)S(1)}, bf16[256,256]{1,0:T(8,128)(2,1)S(1)}, u32[]{:S(2)}, u32[]{:S(2)}) collective-permute-start(bf16[256,256]{1,0:T(8,128)(2,1)S(1)} %collective-permute-done.11.refs_5_.refs_7_), channel_id=1, source_target_pairs={{0,1},{1,0},{2,3},{3,2},{4,5},{5,4},{6,7},{7,6},{8,9},{9,8},{10,11... | collective-permute-start | bytes 393224 | tf_op jit(solution)/shard_map/ppermute | solution.py:600
  84.5 1.5 %collective-permute-start.16 = (bf16[256,256]{1,0:T(8,128)(2,1)S(1)}, bf16[256,256]{1,0:T(8,128)(2,1)S(1)}, u32[]{:S(2)}, u32[]{:S(2)}) collective-permute-start(bf16[256,256]{1,0:T(8,128)(2,1)S(1)} %collective-permute-done.12.refs_7_.refs_9_), channel_id=1, source_target_pairs={{0,1},{1,0},{2,3},{3,2},{4,5},{5,4},{6,7},{7,6},{8,9},{9,8},{10,11... | collective-permute-start | bytes 393224 | tf_op jit(solution)/shard_map/ppermute | solution.py:600
  86.1 2.2 %copy-start.1 = (bf16[4096,512]{1,0:T(8,128)(2,1)S(1)}, bf16[4096,512]{1,0:T(8,128)(2,1)}, u32[]{:S(2)}) copy-start(bf16[4096,512]{1,0:T(8,128)(2,1)} %copy-done) | copy-start | bytes 12582916
  88.3 6.5 %copy-start.2 = (bf16[4096,512]{1,0:T(8,128)(2,1)S(1)}, bf16[4096,512]{1,0:T(8,128)(2,1)}, u32[]{:S(2)}) copy-start(bf16[4096,512]{1,0:T(8,128)(2,1)} %copy-done) | copy-start | bytes 12582916
  90.9 9.5 %copy-start.3 = (bf16[8,256,128]{2,1,0:T(8,128)(2,1)S(1)}, bf16[8,256,128]{2,1,0:T(8,128)(2,1)}, u32[]{:S(2)}) copy-start(bf16[8,256,128]{2,1,0:T(8,128)(2,1)} %pair_ref.3) | copy-start | bytes 1572868
  90.9 7.3 %collective-permute-start.20 = (bf16[8,64,128]{2,1,0:T(8,128)(2,1)S(1)}, bf16[8,64,128]{2,1,0:T(8,128)(2,1)S(1)}, u32[]{:S(2)}, u32[]{:S(2)}) collective-permute-start(bf16[8,64,128]{2,1,0:T(8,128)(2,1)S(1)} %get-tuple-element.57), channel_id=1, source_target_pairs={{0,6},{1,7},{2,4},{3,5},{4,2},{5,3},{6,0},{7,1},{8,14},{9,15},{10,... | collective-permute-start | bytes 393224 | tf_op jit(solution)/shard_map/ppermute | solution.py:600
  93.1 7.1 %collective-permute-start.21 = (bf16[8,64,128]{2,1,0:T(8,128)(2,1)S(1)}, bf16[8,64,128]{2,1,0:T(8,128)(2,1)S(1)}, u32[]{:S(2)}, u32[]{:S(2)}) collective-permute-start(bf16[8,64,128]{2,1,0:T(8,128)(2,1)S(1)} %get-tuple-element.58), channel_id=1, source_target_pairs={{0,2},{1,3},{2,0},{3,1},{4,6},{5,7},{6,4},{7,5},{8,10},{9,11},{10,... | collective-permute-start | bytes 393224 | tf_op jit(solution)/shard_map/ppermute | solution.py:600
  93.7 6.7 %collective-permute-start.22 = (bf16[8,64,128]{2,1,0:T(8,128)(2,1)S(1)}, bf16[8,64,128]{2,1,0:T(8,128)(2,1)S(1)}, u32[]{:S(2)}, u32[]{:S(2)}) collective-permute-start(bf16[8,64,128]{2,1,0:T(8,128)(2,1)S(1)} %get-tuple-element.59), channel_id=1, source_target_pairs={{0,4},{1,5},{2,6},{3,7},{4,0},{5,1},{6,2},{7,3},{8,12},{9,13},{10,... | collective-permute-start | bytes 393224 | tf_op jit(solution)/shard_map/ppermute | solution.py:600

commit v15 on v13

--- a/solution.py
+++ b/solution.py
@@ -246,10 +246,10 @@
     for at in range(len(tasks) + 2):
         if at < len(tasks):
             score(at)
+        if 0 <= at - 1 < len(tasks):
+            raise_scores(at - 1)
         if 0 <= at - 2:
             gather(at - 2)
-        if 0 <= at - 1 < len(tasks):
-            raise_scores(at - 1)
     return [jnp.concatenate(p, axis=1) for p in pieces]
 
 

time: 99.4 us -> 99.4 us (level)
  no operation moved by 1% of the time
where the time goes in v15:
time: 99.4 us; the launch traced here: 99.2 us
  blocking collectives  30.4 us (31%)
  Pallas kernels  30 us (30%)
  starting transfers between devices  23.3 us (23%)
  waiting for transfers between devices  14.1 us (14%)
    all_to_all x1, blocking collectives, per_device_fast(): moved = lax.all_to_all(rows, 'dap', split_axis=0, concat_axis=0, tiled=True)  30.4 us
    ppermute x23, starting transfers between devices, exchange(): return lax.ppermute(block, 'dap', [(i, i ^ offset) for i in range(count)])  23.3 us
    ppermute x23, waiting for transfers between devices, exchange(): return lax.ppermute(block, 'dap', [(i, i ^ offset) for i in range(count)])  14.1 us
    pallas_call x1, Pallas kernels, column_attend(): pl.pallas_call(functools.partial(column_kernel, items), in_specs=[pl.Bloc...  8.06 us
    pallas_call x1, Pallas kernels, row_attend(): pl.pallas_call(functools.partial(row_attend_kernel, plan), in_specs=[pl.B...  7 us
    pallas_call x1, Pallas kernels, row_project(): pl.pallas_call(row_project_kernel, grid=(seqs // step,), in_specs=[pl.Blo...  5.38 us
    pallas_call x2, Pallas kernels, outer_product(): pl.pallas_call(functools.partial(outer_kernel, group, outer, items), out_...  4.79 us
  transfers between devices with their start and end apart: 23, of which 12 were waited for; matrix products, arithmetic and copies ran while one was open for 0% of the time, Pallas kernels for 9%

profile of v15, /device:TPU:0, one launch (start us, length us, event | category | flops | bytes accessed | tf_op | source)
XLA Modules:
  0.0 99.2 jit_solution(4643107209651436405)
XLA Ops:
  0.6 1.8 %pair_bias.1 = bf16[64,256]{1,0:T(8,128)(2,1)S(1)} custom-call(bf16[8,256,128]{2,1,0:T(8,128)(2,1)} %pair_ref.3, bf16[8,128]{1,0:T(8,128)(2,1)} %bitcast.12), custom_call_target="tpu_custom_call" | custom-call | tf_op jit(solution)/shard_map/pair_bias/pallas_call | solution.py:278
  2.4 3.1 %collective-permute-start = (bf16[64,256]{1,0:T(8,128)(2,1)S(1)}, bf16[64,256]{1,0:T(8,128)(2,1)S(1)}, u32[]{:S(2)}, u32[]{:S(2)}) collective-permute-start(bf16[64,256]{1,0:T(8,128)(2,1)S(1)} %pair_bias.1), channel_id=1, source_target_pairs={{0,8},{1,9},{2,10},{3,11},{4,12},{5,13},{6,14},{7,15},{8,0},{9,1},... | collective-permute-start | bytes 98312 | tf_op jit(solution)/shard_map/ppermute | solution.py:585
  5.5 2.6 %collective-permute-start.1 = (bf16[64,256]{1,0:T(8,128)(2,1)S(1)}, bf16[64,256]{1,0:T(8,128)(2,1)S(1)}, u32[]{:S(2)}, u32[]{:S(2)}) collective-permute-start(bf16[64,256]{1,0:T(8,128)(2,1)S(1)} %pair_bias.1), channel_id=1, source_target_pairs={{0,16},{1,17},{2,18},{3,19},{4,20},{5,21},{6,22},{7,23},{8,24},{9,... | collective-permute-start | bytes 98312 | tf_op jit(solution)/shard_map/ppermute | solution.py:585
  8.1 5.4 %row_project.1 = (bf16[8,256,256]{2,1,0:T(8,128)(2,1)S(1)}, bf16[8,256,256]{2,1,0:T(8,128)(2,1)S(1)}, bf16[8,256,256]{2,1,0:T(8,128)(2,1)S(1)}, f32[8,256,256]{2...) custom-call(s32[1]{0:T(128)} %bitcast.me_ref, bf16[8,256,256]{2,1,0:T(8,128)(2,1)} %x_hbm.1, ...), custom_call_target="tpu_custom_call" | custom-call | tf_op jit(solution)/shard_map/row_project/pallas_call | solution.py:313
  13.8 1.6 %collective-permute-start.3 = (bf16[4,64,256]{2,1,0:T(8,128)(2,1)S(1)}, bf16[4,64,256]{2,1,0:T(8,128)(2,1)S(1)}, u32[]{:S(2)}, u32[]{:S(2)}) collective-permute-start(bf16[4,64,256]{2,1,0:T(8,128)(2,1)S(1)} %pad_maximum_fusion.rest_0_), channel_id=1, source_target_pairs={{0,2},{1,3},{2,0},{3,1},{4,6},{5,7},{6,4},{7,5},{8,10},{9,11},{10,... | collective-permute-start | bytes 393224 | tf_op jit(solution)/shard_map/ppermute | solution.py:585
  15.4 1.5 %collective-permute-start.4 = (bf16[4,64,256]{2,1,0:T(8,128)(2,1)S(1)}, bf16[4,64,256]{2,1,0:T(8,128)(2,1)S(1)}, u32[]{:S(2)}, u32[]{:S(2)}) collective-permute-start(bf16[4,64,256]{2,1,0:T(8,128)(2,1)S(1)} %pad_maximum_fusion.rest_0_), channel_id=1, source_target_pairs={{0,4},{1,5},{2,6},{3,7},{4,0},{5,1},{6,2},{7,3},{8,12},{9,13},{10,... | collective-permute-start | bytes 393224 | tf_op jit(solution)/shard_map/ppermute | solution.py:585
  16.9 0.5 collective-permute-start.5
  17.4 2.6 %collective-permute-done.3.rest_1_ = bf16[4,64,256]{2,1,0:T(8,128)(2,1)S(1)} collective-permute-done((bf16[4,64,256]{2,1,0:T(8,128)(2,1)S(1)}, bf16[4,64,256]{2,1,0:T(8,128)(2,1)S(1)}, u32[]{:S(2)}, u32[]{:S(2)}) %collective-permute-start.3) | collective-permute-done | bytes 131104 | tf_op jit(solution)/shard_map/ppermute | solution.py:585
  20.0 3.1 %collective-permute-done.4.rest_2_ = bf16[4,64,256]{2,1,0:T(8,128)(2,1)S(1)} collective-permute-done((bf16[4,64,256]{2,1,0:T(8,128)(2,1)S(1)}, bf16[4,64,256]{2,1,0:T(8,128)(2,1)S(1)}, u32[]{:S(2)}, u32[]{:S(2)}) %collective-permute-start.4) | collective-permute-done | bytes 131104 | tf_op jit(solution)/shard_map/ppermute | solution.py:585
  23.1 0.5 collective-permute-start.9
  23.6 0.8 collective-permute-done.8.rest_6_
  24.6 7.0 %row_attend.1 = bf16[32,64,256]{2,1,0:T(8,128)(2,1)S(1)} custom-call(s32[1]{0:T(128)} %bitcast.me_ref, bf16[8,256,256]{2,1,0:T(8,128)(2,1)} %x_hbm.1, f32[8,256,256]{2,1,0:T(8,128)} %get-tuple-element.29.g_hbm, bf16[8,256,256]{2,1,0:T(8,128)(2,1)S(1)} %get-tuple-element.30.q_ref, bf16[8,256,256]{2,1,0:T(8,128)(2,1)S(1)} %get-tuple-element.31.k_ref, ...), custom_call_target="tpu_custom_call" | custom-call | tf_op jit(solution)/shard_map/row_attend/pallas_call | solution.py:379
  31.7 30.4 %all_to_all.5.x_ref = bf16[32,64,256]{2,1,0:T(8,128)(2,1)S(1)} all-to-all(bf16[32,64,256]{2,1,0:T(8,128)(2,1)S(1)} %row_attend.1), channel_id=1, replica_groups=mesh['branch'=1,'dap'=32] {'dap'}, dimensions={0} | all-to-all | bytes 2097152 | tf_op jit(solution)/shard_map/all_to_all | solution.py:622
  62.1 8.1 %column_attend.1 = (bf16[8,256,256]{2,1,0:T(8,128)(2,1)S(1)}, bf16[256,256]{1,0:T(8,128)(2,1)S(1)}, bf16[256,256]{1,0:T(8,128)(2,1)S(1)}) custom-call(s32[1]{0:T(128)} %bitcast.me_ref, bf16[32,64,256]{2,1,0:T(8,128)(2,1)S(1)} %all_to_all.5.x_ref, s32[256,256]{1,0:T(8,128)S(1)} %copy-done.1, bf16[4,256,256]{2,1,0:T(8,128)(2,1)S(1)} %copy-done.3, ...), custom_call_target="tpu_custom_call" | custom-call | tf_op jit(solution)/shard_map/column_attend/pallas_call | solution.py:448
  70.1 0.8 collective-permute-start.10
  71.0 1.1 %collective-permute-start.11 = (bf16[256,256]{1,0:T(8,128)(2,1)S(1)}, bf16[256,256]{1,0:T(8,128)(2,1)S(1)}, u32[]{:S(2)}, u32[]{:S(2)}) collective-permute-start(bf16[256,256]{1,0:T(8,128)(2,1)S(1)} %get-tuple-element.47.refs_1_.refs_3_), channel_id=1, source_target_pairs={{0,16},{1,17},{2,18},{3,19},{4,20},{5,21},{6,22},{7,23},{8,24},{9,... | collective-permute-start | bytes 393224 | tf_op jit(solution)/shard_map/ppermute | solution.py:585
  72.1 2.5 %collective-permute-start.12 = (bf16[256,256]{1,0:T(8,128)(2,1)S(1)}, bf16[256,256]{1,0:T(8,128)(2,1)S(1)}, u32[]{:S(2)}, u32[]{:S(2)}) collective-permute-start(bf16[256,256]{1,0:T(8,128)(2,1)S(1)} %get-tuple-element.47.refs_1_.refs_3_), channel_id=1, source_target_pairs={{0,24},{1,25},{2,26},{3,27},{4,28},{5,29},{6,30},{7,31},{8,16},{9,... | collective-permute-start | bytes 393224 | tf_op jit(solution)/shard_map/ppermute | solution.py:585
  74.6 1.5 %collective-permute-start.17 = (bf16[256,256]{1,0:T(8,128)(2,1)S(1)}, bf16[256,256]{1,0:T(8,128)(2,1)S(1)}, u32[]{:S(2)}, u32[]{:S(2)}) collective-permute-start(bf16[256,256]{1,0:T(8,128)(2,1)S(1)} %get-tuple-element.46.refs_0_), channel_id=1, source_target_pairs={{0,2},{1,3},{2,0},{3,1},{4,6},{5,7},{6,4},{7,5},{8,10},{9,11},{10,... | collective-permute-start | bytes 393224 | tf_op jit(solution)/shard_map/ppermute | solution.py:585
  76.1 1.5 %collective-permute-start.18 = (bf16[256,256]{1,0:T(8,128)(2,1)S(1)}, bf16[256,256]{1,0:T(8,128)(2,1)S(1)}, u32[]{:S(2)}, u32[]{:S(2)}) collective-permute-start(bf16[256,256]{1,0:T(8,128)(2,1)S(1)} %get-tuple-element.46.refs_0_), channel_id=1, source_target_pairs={{0,4},{1,5},{2,6},{3,7},{4,0},{5,1},{6,2},{7,3},{8,12},{9,13},{10,... | collective-permute-start | bytes 393224 | tf_op jit(solution)/shard_map/ppermute | solution.py:585
  77.6 1.6 %collective-permute-start.19 = (bf16[256,256]{1,0:T(8,128)(2,1)S(1)}, bf16[256,256]{1,0:T(8,128)(2,1)S(1)}, u32[]{:S(2)}, u32[]{:S(2)}) collective-permute-start(bf16[256,256]{1,0:T(8,128)(2,1)S(1)} %get-tuple-element.46.refs_0_), channel_id=1, source_target_pairs={{0,6},{1,7},{2,4},{3,5},{4,2},{5,3},{6,0},{7,1},{8,14},{9,15},{10,... | collective-permute-start | bytes 393224 | tf_op jit(solution)/shard_map/ppermute | solution.py:585
  79.2 1.9 %interleave.1 = bf16[256,8,256]{2,1,0:T(8,128)(2,1)} custom-call(bf16[8,256,256]{2,1,0:T(8,128)(2,1)S(1)} %get-tuple-element.43.rows_ref), custom_call_target="tpu_custom_call" | custom-call | tf_op jit(solution)/shard_map/interleave/pallas_call | solution.py:470
  81.1 2.8 %collective-permute-done.11.refs_5_.refs_7_ = bf16[256,256]{1,0:T(8,128)(2,1)S(1)} collective-permute-done((bf16[256,256]{1,0:T(8,128)(2,1)S(1)}, bf16[256,256]{1,0:T(8,128)(2,1)S(1)}, u32[]{:S(2)}, u32[]{:S(2)}) %collective-permute-start.11) | collective-permute-done | bytes 131104 | tf_op jit(solution)/shard_map/ppermute | solution.py:585
  83.9 0.5 collective-permute-start.14
  84.4 0.5 collective-permute-start.16
  85.9 2.9 %outer_product.3 = (bf16[8,64,128]{2,1,0:T(8,128)(2,1)S(1)}, bf16[8,64,128]{2,1,0:T(8,128)(2,1)S(1)}, bf16[8,64,128]{2,1,0:T(8,128)(2,1)S(1)}) custom-call(bf16[256,256]{1,0:T(8,128)(2,1)S(1)} %collective-permute-done.17.refs_0_, bf16[256,256]{1,0:T(8,128)(2,1)S(1)} %collective-permute-done.18.refs_1_, bf16[256,256]{1,0:T(8,128)(2,1)S(1)} %collective-permute-done.19.refs_2_, ...), custom_call_target="tpu_custom_call" | custom-call | tf_op jit(solution)/shard_map/outer_product/pallas_call | solution.py:528
  88.8 0.9 collective-permute-start.20
  89.7 1.4 %collective-permute-start.21 = (bf16[8,64,128]{2,1,0:T(8,128)(2,1)S(1)}, bf16[8,64,128]{2,1,0:T(8,128)(2,1)S(1)}, u32[]{:S(2)}, u32[]{:S(2)}) collective-permute-start(bf16[8,64,128]{2,1,0:T(8,128)(2,1)S(1)} %get-tuple-element.52), channel_id=1, source_target_pairs={{0,4},{1,5},{2,6},{3,7},{4,0},{5,1},{6,2},{7,3},{8,12},{9,13},{10,... | collective-permute-start | bytes 393224 | tf_op jit(solution)/shard_map/ppermute | solution.py:585
  91.1 1.3 %collective-permute-start.22 = (bf16[8,64,128]{2,1,0:T(8,128)(2,1)S(1)}, bf16[8,64,128]{2,1,0:T(8,128)(2,1)S(1)}, u32[]{:S(2)}, u32[]{:S(2)}) collective-permute-start(bf16[8,64,128]{2,1,0:T(8,128)(2,1)S(1)} %get-tuple-element.53), channel_id=1, source_target_pairs={{0,6},{1,7},{2,4},{3,5},{4,2},{5,3},{6,0},{7,1},{8,14},{9,15},{10,... | collective-permute-start | bytes 393224 | tf_op jit(solution)/shard_map/ppermute | solution.py:585
  92.7 1.9 %outer_product.2.refs_0_ = bf16[8,64,128]{2,1,0:T(8,128)(2,1)S(1)} custom-call(bf16[256,256]{1,0:T(8,128)(2,1)S(1)} %get-tuple-element.46.refs_0_, bf16[256,256]{1,0:T(8,128)(2,1)S(1)} %get-tuple-element.47.refs_1_.refs_3_, bf16[256,256]{1,0:T(8,128)(2,1)S(1)} %collective-permute-done.13.refs_2_.refs_4_, ...), custom_call_target="tpu_custom_call" | custom-call | tf_op jit(solution)/shard_map/outer_product/pallas_call | solution.py:528
  94.6 0.6 collective-permute-done.20.refs_1_
  95.2 2.7 %collective-permute-done.21.refs_2_ = bf16[8,64,128]{2,1,0:T(8,128)(2,1)S(1)} collective-permute-done((bf16[8,64,128]{2,1,0:T(8,128)(2,1)S(1)}, bf16[8,64,128]{2,1,0:T(8,128)(2,1)S(1)}, u32[]{:S(2)}, u32[]{:S(2)}) %collective-permute-start.21) | collective-permute-done | bytes 131104 | tf_op jit(solution)/shard_map/ppermute | solution.py:585
  97.9 1.1 %finish.1 = bf16[8,256,128]{2,1,0:T(8,128)(2,1)} custom-call(s32[1]{0:T(128)} %bitcast.me_ref, bf16[8,256,128]{2,1,0:T(8,128)(2,1)S(1)} %copy-done, f32[256,8]{1,0:T(8,128)S(1)} %fusion.scale_ref, bf16[8,64,128]{2,1,0:T(8,128)(2,1)S(1)} %outer_product.2.refs_0_, bf16[8,64,128]{2,1,0:T(8,128)(2,1)S(1)} %collective-permute-done.20.refs_1_, ...), custom_call_target="tpu_custom_call" | custom-call | tf_op jit(solution)/shard_map/finish/pallas_call | solution.py:568
  (41 shorter events, 1.9 us)
Async XLA Ops:
  2.4 11.1 %collective-permute-start = (bf16[64,256]{1,0:T(8,128)(2,1)S(1)}, bf16[64,256]{1,0:T(8,128)(2,1)S(1)}, u32[]{:S(2)}, u32[]{:S(2)}) collective-permute-start(bf16[64,256]{1,0:T(8,128)(2,1)S(1)} %pair_bias.1), channel_id=1, source_target_pairs={{0,8},{1,9},{2,10},{3,11},{4,12},{5,13},{6,14},{7,15},{8,0},{9,1},... | collective-permute-start | bytes 98312 | tf_op jit(solution)/shard_map/ppermute | solution.py:585
  5.5 8.0 %collective-permute-start.1 = (bf16[64,256]{1,0:T(8,128)(2,1)S(1)}, bf16[64,256]{1,0:T(8,128)(2,1)S(1)}, u32[]{:S(2)}, u32[]{:S(2)}) collective-permute-start(bf16[64,256]{1,0:T(8,128)(2,1)S(1)} %pair_bias.1), channel_id=1, source_target_pairs={{0,16},{1,17},{2,18},{3,19},{4,20},{5,21},{6,22},{7,23},{8,24},{9,... | collective-permute-start | bytes 98312 | tf_op jit(solution)/shard_map/ppermute | solution.py:585
  8.1 5.7 %collective-permute-start.2 = (bf16[64,256]{1,0:T(8,128)(2,1)S(1)}, bf16[64,256]{1,0:T(8,128)(2,1)S(1)}, u32[]{:S(2)}, u32[]{:S(2)}) collective-permute-start(bf16[64,256]{1,0:T(8,128)(2,1)S(1)} %pair_bias.1), channel_id=1, source_target_pairs={{0,24},{1,25},{2,26},{3,27},{4,28},{5,29},{6,30},{7,31},{8,16},{9,... | collective-permute-start | bytes 98312 | tf_op jit(solution)/shard_map/ppermute | solution.py:585
  13.8 6.1 %collective-permute-start.3 = (bf16[4,64,256]{2,1,0:T(8,128)(2,1)S(1)}, bf16[4,64,256]{2,1,0:T(8,128)(2,1)S(1)}, u32[]{:S(2)}, u32[]{:S(2)}) collective-permute-start(bf16[4,64,256]{2,1,0:T(8,128)(2,1)S(1)} %pad_maximum_fusion.rest_0_), channel_id=1, source_target_pairs={{0,2},{1,3},{2,0},{3,1},{4,6},{5,7},{6,4},{7,5},{8,10},{9,11},{10,... | collective-permute-start | bytes 393224 | tf_op jit(solution)/shard_map/ppermute | solution.py:585
  15.4 7.7 %collective-permute-start.4 = (bf16[4,64,256]{2,1,0:T(8,128)(2,1)S(1)}, bf16[4,64,256]{2,1,0:T(8,128)(2,1)S(1)}, u32[]{:S(2)}, u32[]{:S(2)}) collective-permute-start(bf16[4,64,256]{2,1,0:T(8,128)(2,1)S(1)} %pad_maximum_fusion.rest_0_), channel_id=1, source_target_pairs={{0,4},{1,5},{2,6},{3,7},{4,0},{5,1},{6,2},{7,3},{8,12},{9,13},{10,... | collective-permute-start | bytes 393224 | tf_op jit(solution)/shard_map/ppermute | solution.py:585
  16.9 6.2 %collective-permute-start.5 = (bf16[4,64,256]{2,1,0:T(8,128)(2,1)S(1)}, bf16[4,64,256]{2,1,0:T(8,128)(2,1)S(1)}, u32[]{:S(2)}, u32[]{:S(2)}) collective-permute-start(bf16[4,64,256]{2,1,0:T(8,128)(2,1)S(1)} %pad_maximum_fusion.rest_0_), channel_id=1, source_target_pairs={{0,6},{1,7},{2,4},{3,5},{4,2},{5,3},{6,0},{7,1},{8,14},{9,15},{10,... | collective-permute-start | bytes 393224 | tf_op jit(solution)/shard_map/ppermute | solution.py:585
  17.4 6.2 %collective-permute-start.6 = (bf16[4,64,256]{2,1,0:T(8,128)(2,1)S(1)}, bf16[4,64,256]{2,1,0:T(8,128)(2,1)S(1)}, u32[]{:S(2)}, u32[]{:S(2)}) collective-permute-start(bf16[4,64,256]{2,1,0:T(8,128)(2,1)S(1)} %pad_maximum_fusion.rest_0_), channel_id=1, source_target_pairs={{0,1},{1,0},{2,3},{3,2},{4,5},{5,4},{6,7},{7,6},{8,9},{9,8},{10,11... | collective-permute-start | bytes 393224 | tf_op jit(solution)/shard_map/ppermute | solution.py:585
  20.0 3.6 %collective-permute-start.7 = (bf16[4,64,256]{2,1,0:T(8,128)(2,1)S(1)}, bf16[4,64,256]{2,1,0:T(8,128)(2,1)S(1)}, u32[]{:S(2)}, u32[]{:S(2)}) collective-permute-start(bf16[4,64,256]{2,1,0:T(8,128)(2,1)S(1)} %collective-permute-done.3.rest_1_), channel_id=1, source_target_pairs={{0,1},{1,0},{2,3},{3,2},{4,5},{5,4},{6,7},{7,6},{8,9},{9,8},{10,11... | collective-permute-start | bytes 393224 | tf_op jit(solution)/shard_map/ppermute | solution.py:585
  23.1 1.3 %collective-permute-start.8 = (bf16[4,64,256]{2,1,0:T(8,128)(2,1)S(1)}, bf16[4,64,256]{2,1,0:T(8,128)(2,1)S(1)}, u32[]{:S(2)}, u32[]{:S(2)}) collective-permute-start(bf16[4,64,256]{2,1,0:T(8,128)(2,1)S(1)} %collective-permute-done.4.rest_2_), channel_id=1, source_target_pairs={{0,1},{1,0},{2,3},{3,2},{4,5},{5,4},{6,7},{7,6},{8,9},{9,8},{10,11... | collective-permute-start | bytes 393224 | tf_op jit(solution)/shard_map/ppermute | solution.py:585
  23.1 1.5 %collective-permute-start.9 = (bf16[4,64,256]{2,1,0:T(8,128)(2,1)S(1)}, bf16[4,64,256]{2,1,0:T(8,128)(2,1)S(1)}, u32[]{:S(2)}, u32[]{:S(2)}) collective-permute-start(bf16[4,64,256]{2,1,0:T(8,128)(2,1)S(1)} %collective-permute-done.5.rest_3_), channel_id=1, source_target_pairs={{0,1},{1,0},{2,3},{3,2},{4,5},{5,4},{6,7},{7,6},{8,9},{9,8},{10,11... | collective-permute-start | bytes 393224 | tf_op jit(solution)/shard_map/ppermute | solution.py:585
  31.6 30.4 %copy-start.1 = (s32[256,256]{1,0:T(8,128)S(1)}, s32[256,256]{1,0:T(8,128)}, u32[]{:S(2)}) copy-start(s32[256,256]{1,0:T(8,128)} %mask_ref.3) | copy-start | bytes 786436
  31.6 30.4 %copy-start.3 = (bf16[4,256,256]{2,1,0:T(8,128)(2,1)S(1)}, bf16[4,256,256]{2,1,0:T(8,128)(2,1)}, u32[]{:S(2)}) copy-start(bf16[4,256,256]{2,1,0:T(8,128)(2,1)} %weight_ref.3) | copy-start | bytes 1572868
  31.6 30.4 %copy-start.4 = (bf16[256,256]{1,0:T(8,128)(2,1)S(1)}, bf16[256,256]{1,0:T(8,128)(2,1)}, u32[]{:S(2)}) copy-start(bf16[256,256]{1,0:T(8,128)(2,1)} %out_w_ref.3) | copy-start | bytes 393220
  31.6 30.4 %copy-start.5 = (bf16[256,64]{0,1:T(8,128)(2,1)S(1)}, bf16[256,64]{0,1:T(8,128)(2,1)}, u32[]{:S(2)}) copy-start(bf16[256,64]{0,1:T(8,128)(2,1)} %param.20) | copy-start | bytes 98308
  62.0 22.9 %copy-start.6 = (s32[256]{0:T(256)S(1)}, s32[256]{0:T(256)}, u32[]{:S(2)}) copy-start(s32[256]{0:T(256)} %param.14) | copy-start | bytes 3076
  62.0 23.9 %copy-start.2 = (bf16[1024,128]{1,0:T(8,128)(2,1)S(1)}, bf16[1024,128]{1,0:T(8,128)(2,1)}, u32[]{:S(2)}) copy-start(bf16[1024,128]{1,0:T(8,128)(2,1)} %refs_11_.1) | copy-start | bytes 786436
  70.1 7.4 %collective-permute-start.10 = (bf16[256,256]{1,0:T(8,128)(2,1)S(1)}, bf16[256,256]{1,0:T(8,128)(2,1)S(1)}, u32[]{:S(2)}, u32[]{:S(2)}) collective-permute-start(bf16[256,256]{1,0:T(8,128)(2,1)S(1)} %get-tuple-element.47.refs_1_.refs_3_), channel_id=1, source_target_pairs={{0,8},{1,9},{2,10},{3,11},{4,12},{5,13},{6,14},{7,15},{8,0},{9,1},... | collective-permute-start | bytes 393224 | tf_op jit(solution)/shard_map/ppermute | solution.py:585
  71.0 12.9 %collective-permute-start.11 = (bf16[256,256]{1,0:T(8,128)(2,1)S(1)}, bf16[256,256]{1,0:T(8,128)(2,1)S(1)}, u32[]{:S(2)}, u32[]{:S(2)}) collective-permute-start(bf16[256,256]{1,0:T(8,128)(2,1)S(1)} %get-tuple-element.47.refs_1_.refs_3_), channel_id=1, source_target_pairs={{0,16},{1,17},{2,18},{3,19},{4,20},{5,21},{6,22},{7,23},{8,24},{9,... | collective-permute-start | bytes 393224 | tf_op jit(solution)/shard_map/ppermute | solution.py:585
  72.1 11.8 %collective-permute-start.12 = (bf16[256,256]{1,0:T(8,128)(2,1)S(1)}, bf16[256,256]{1,0:T(8,128)(2,1)S(1)}, u32[]{:S(2)}, u32[]{:S(2)}) collective-permute-start(bf16[256,256]{1,0:T(8,128)(2,1)S(1)} %get-tuple-element.47.refs_1_.refs_3_), channel_id=1, source_target_pairs={{0,24},{1,25},{2,26},{3,27},{4,28},{5,29},{6,30},{7,31},{8,16},{9,... | collective-permute-start | bytes 393224 | tf_op jit(solution)/shard_map/ppermute | solution.py:585
  74.6 9.8 %collective-permute-start.17 = (bf16[256,256]{1,0:T(8,128)(2,1)S(1)}, bf16[256,256]{1,0:T(8,128)(2,1)S(1)}, u32[]{:S(2)}, u32[]{:S(2)}) collective-permute-start(bf16[256,256]{1,0:T(8,128)(2,1)S(1)} %get-tuple-element.46.refs_0_), channel_id=1, source_target_pairs={{0,2},{1,3},{2,0},{3,1},{4,6},{5,7},{6,4},{7,5},{8,10},{9,11},{10,... | collective-permute-start | bytes 393224 | tf_op jit(solution)/shard_map/ppermute | solution.py:585
  76.1 8.3 %collective-permute-start.18 = (bf16[256,256]{1,0:T(8,128)(2,1)S(1)}, bf16[256,256]{1,0:T(8,128)(2,1)S(1)}, u32[]{:S(2)}, u32[]{:S(2)}) collective-permute-start(bf16[256,256]{1,0:T(8,128)(2,1)S(1)} %get-tuple-element.46.refs_0_), channel_id=1, source_target_pairs={{0,4},{1,5},{2,6},{3,7},{4,0},{5,1},{6,2},{7,3},{8,12},{9,13},{10,... | collective-permute-start | bytes 393224 | tf_op jit(solution)/shard_map/ppermute | solution.py:585
  77.6 7.4 %collective-permute-start.19 = (bf16[256,256]{1,0:T(8,128)(2,1)S(1)}, bf16[256,256]{1,0:T(8,128)(2,1)S(1)}, u32[]{:S(2)}, u32[]{:S(2)}) collective-permute-start(bf16[256,256]{1,0:T(8,128)(2,1)S(1)} %get-tuple-element.46.refs_0_), channel_id=1, source_target_pairs={{0,6},{1,7},{2,4},{3,5},{4,2},{5,3},{6,0},{7,1},{8,14},{9,15},{10,... | collective-permute-start | bytes 393224 | tf_op jit(solution)/shard_map/ppermute | solution.py:585
  81.1 16.9 %copy-start = (bf16[8,256,128]{2,1,0:T(8,128)(2,1)S(1)}, bf16[8,256,128]{2,1,0:T(8,128)(2,1)}, u32[]{:S(2)}) copy-start(bf16[8,256,128]{2,1,0:T(8,128)(2,1)} %pair_ref.3) | copy-start | bytes 1572868
  83.9 1.3 %collective-permute-start.13 = (bf16[256,256]{1,0:T(8,128)(2,1)S(1)}, bf16[256,256]{1,0:T(8,128)(2,1)S(1)}, u32[]{:S(2)}, u32[]{:S(2)}) collective-permute-start(bf16[256,256]{1,0:T(8,128)(2,1)S(1)} %get-tuple-element.47.refs_1_.refs_3_), channel_id=1, source_target_pairs={{0,1},{1,0},{2,3},{3,2},{4,5},{5,4},{6,7},{7,6},{8,9},{9,8},{10,11... | collective-permute-start | bytes 393224 | tf_op jit(solution)/shard_map/ppermute | solution.py:585
  83.9 1.5 %collective-permute-start.14 = (bf16[256,256]{1,0:T(8,128)(2,1)S(1)}, bf16[256,256]{1,0:T(8,128)(2,1)S(1)}, u32[]{:S(2)}, u32[]{:S(2)}) collective-permute-start(bf16[256,256]{1,0:T(8,128)(2,1)S(1)} %collective-permute-done.10.refs_3_.refs_5_), channel_id=1, source_target_pairs={{0,1},{1,0},{2,3},{3,2},{4,5},{5,4},{6,7},{7,6},{8,9},{9,8},{10,11... | collective-permute-start | bytes 393224 | tf_op jit(solution)/shard_map/ppermute | solution.py:585
  84.4 1.3 %collective-permute-start.15 = (bf16[256,256]{1,0:T(8,128)(2,1)S(1)}, bf16[256,256]{1,0:T(8,128)(2,1)S(1)}, u32[]{:S(2)}, u32[]{:S(2)}) collective-permute-start(bf16[256,256]{1,0:T(8,128)(2,1)S(1)} %collective-permute-done.11.refs_5_.refs_7_), channel_id=1, source_target_pairs={{0,1},{1,0},{2,3},{3,2},{4,5},{5,4},{6,7},{7,6},{8,9},{9,8},{10,11... | collective-permute-start | bytes 393224 | tf_op jit(solution)/shard_map/ppermute | solution.py:585
  84.4 1.5 %collective-permute-start.16 = (bf16[256,256]{1,0:T(8,128)(2,1)S(1)}, bf16[256,256]{1,0:T(8,128)(2,1)S(1)}, u32[]{:S(2)}, u32[]{:S(2)}) collective-permute-start(bf16[256,256]{1,0:T(8,128)(2,1)S(1)} %collective-permute-done.12.refs_7_.refs_9_), channel_id=1, source_target_pairs={{0,1},{1,0},{2,3},{3,2},{4,5},{5,4},{6,7},{7,6},{8,9},{9,8},{10,11... | collective-permute-start | bytes 393224 | tf_op jit(solution)/shard_map/ppermute | solution.py:585
  88.8 6.4 %collective-permute-start.20 = (bf16[8,64,128]{2,1,0:T(8,128)(2,1)S(1)}, bf16[8,64,128]{2,1,0:T(8,128)(2,1)S(1)}, u32[]{:S(2)}, u32[]{:S(2)}) collective-permute-start(bf16[8,64,128]{2,1,0:T(8,128)(2,1)S(1)} %get-tuple-element.51), channel_id=1, source_target_pairs={{0,2},{1,3},{2,0},{3,1},{4,6},{5,7},{6,4},{7,5},{8,10},{9,11},{10,... | collective-permute-start | bytes 393224 | tf_op jit(solution)/shard_map/ppermute | solution.py:585
  89.7 8.2 %collective-permute-start.21 = (bf16[8,64,128]{2,1,0:T(8,128)(2,1)S(1)}, bf16[8,64,128]{2,1,0:T(8,128)(2,1)S(1)}, u32[]{:S(2)}, u32[]{:S(2)}) collective-permute-start(bf16[8,64,128]{2,1,0:T(8,128)(2,1)S(1)} %get-tuple-element.52), channel_id=1, source_target_pairs={{0,4},{1,5},{2,6},{3,7},{4,0},{5,1},{6,2},{7,3},{8,12},{9,13},{10,... | collective-permute-start | bytes 393224 | tf_op jit(solution)/shard_map/ppermute | solution.py:585
  91.1 6.9 %collective-permute-start.22 = (bf16[8,64,128]{2,1,0:T(8,128)(2,1)S(1)}, bf16[8,64,128]{2,1,0:T(8,128)(2,1)S(1)}, u32[]{:S(2)}, u32[]{:S(2)}) collective-permute-start(bf16[8,64,128]{2,1,0:T(8,128)(2,1)S(1)} %get-tuple-element.53), channel_id=1, source_target_pairs={{0,6},{1,7},{2,4},{3,5},{4,2},{5,3},{6,0},{7,1},{8,14},{9,15},{10,... | collective-permute-start | bytes 393224 | tf_op jit(solution)/shard_map/ppermute | solution.py:585
